TPU v7x, 32 devices: a whole 2x2x4 slice. The times are simulated.
32 devices in a mesh: dp: 8 (over z, core), comp: 4 (over y, x).
Axes of the slice: x: 2, y: 2, z: 4, core: 2. Of those that a mesh axis runs over, the one named last changes fastest.
Arguments:
- embeddings: float32 [8192, 768], P('dp'), may hold values from -6 to 6
- comp_means: float32 [2048, 768], P(('comp', 'dp')), may hold values from -1.2 to 1.2
- comp_variances: float32 [2048, 768], P(('comp', 'dp')), may hold values from 0.8 to 1.25
- comp_mass: float32 [2048], P(('comp', 'dp')), may hold values from 0.3 to 3
Outputs:
- new_means: float32 [2048, 768], P(('comp', 'dp'))
- new_variances: float32 [2048, 768], P(('comp', 'dp'))
- new_mass: float32 [2048], P(('comp', 'dp'))
All inputs are finite; a program needn't handle non-finite values.
Results may differ from a plain program's by a relative error of at most 0.0003.
Values sent between devices are 32-bit elements; how exact they have to be, the bound alone decides.
No kernel may reach another device: no remote copies, remote signals or barrier semaphores. Data moves between devices by JAX's collectives and lax.ppermute only.
A program may use at most 64 MiB of HBM per device.

v0:
```python
import functools

import jax
import jax.numpy as jnp
from jax import lax
from jax.experimental import pallas as pl
from jax.experimental.pallas import tpu as pltpu
from jax.sharding import PartitionSpec as P

F32 = jnp.float32
BF16 = jnp.bfloat16
LANES = 128
HEAVY = pl.CostEstimate(flops=10**10, bytes_accessed=10**8, transcendentals=0)
ACROSS = (((1,), (1,)), ((), ()))
WITHIN = (((1,), (0,)), ((), ()))


def params(megabytes):
    return pltpu.CompilerParams(vmem_limit_bytes=megabytes * 1024 * 1024)


def split(value):
    high = value.astype(BF16)
    return high, (value - high.astype(F32)).astype(BF16)


def diagonal(rows, columns):
    shape = (rows, columns)
    return lax.broadcasted_iota(jnp.int32, shape, 0) == lax.broadcasted_iota(jnp.int32, shape, 1)


def to_row(column, lanes):
    return jnp.sum(jnp.where(diagonal(column.shape[0], lanes), column, 0.0), axis=0, keepdims=True)


def to_column(row, rows):
    return jnp.sum(jnp.where(diagonal(rows, row.shape[1]), row, 0.0), axis=1, keepdims=True)


def coefficient_kernel(means_ref, variances_ref, mass_ref, pack_ref):
    n, width = means_ref.shape
    means, variances = means_ref[...], variances_ref[...]
    mean_prec = means * (1.0 / variances)
    sums = jnp.sum(jnp.log(variances) + means * mean_prec, axis=1, keepdims=True)
    offset = to_column(jnp.log(mass_ref[...]), n) - 0.5 * sums
    for c in range(width // LANES):
        pack_ref[c * n : (c + 1) * n, :] = mean_prec[:, c * LANES : (c + 1) * LANES]
    pack_ref[width // LANES * n :, :] = jnp.broadcast_to(to_row(offset, LANES), (8, LANES))


def coefficients(means, variances, mass):
    n, width = means.shape
    return pl.pallas_call(
        coefficient_kernel,
        out_shape=jax.ShapeDtypeStruct((width // LANES * n + 8, LANES), F32),
        cost_estimate=HEAVY,
        compiler_params=params(16),
        name="coefficients",
    )(means, variances, mass.reshape(1, n))


def halves_kernel(own_ref, other_ref, xh_ref, xl_ref, sh_ref, sl_ref):
    def put(block):
        xh_ref[...], xl_ref[...] = split(block)
        sh_ref[...], sl_ref[...] = split(block * block)

    first = pl.program_id(0) < pl.num_programs(0) // 2

    @pl.when(first)
    def _():
        put(own_ref[...])

    @pl.when(jnp.logical_not(first))
    def _():
        put(other_ref[...])


def halves(own, other):
    rows, width = own.shape
    tile = min(256, rows)
    steps = rows // tile
    out = jax.ShapeDtypeStruct((2 * rows, width), BF16)
    return pl.pallas_call(
        halves_kernel,
        grid=(2 * steps,),
        in_specs=[
            pl.BlockSpec((tile, width), lambda i: (jnp.minimum(i, steps - 1), 0)),
            pl.BlockSpec((tile, width), lambda i: (jnp.maximum(i - steps, 0), 0)),
        ],
        out_specs=[pl.BlockSpec((tile, width), lambda i: (i, 0))] * 4,
        out_shape=[out] * 4,
        cost_estimate=HEAVY,
        compiler_params=params(16),
        name="halves",
    )(own, other)


def load_packs(packs, weights, n):
    comps, tiles = n * len(packs), weights.shape[1] // LANES
    for q, pack in enumerate(packs):
        for c in range(tiles):
            lanes = slice(c * LANES, (c + 1) * LANES)
            high, low = split(pack[c * n : (c + 1) * n, :])
            weights[q * n : (q + 1) * n, lanes] = high
            weights[comps + q * n : comps + (q + 1) * n, lanes] = low
    return jnp.concatenate([to_column(pack[tiles * n : tiles * n + 1, :], n) for pack in packs])


def load_variances(variances, weights, n):
    comps = n * len(variances)
    for q, ref in enumerate(variances):
        high, low = split(-0.5 * (1.0 / ref[...]))
        weights[q * n : (q + 1) * n, :] = high
        weights[comps + q * n : comps + (q + 1) * n, :] = low


def product(weights, high, low, dims):
    comps = weights.shape[0] // 2
    both = lax.dot_general(weights, high, dims, preferred_element_type=F32)
    rest = lax.dot_general(weights[:comps], low, dims, preferred_element_type=F32)
    return both[:comps] + (both[comps:] + rest)


def row_tiles(rows, tile=256):
    tile = min(tile, rows)
    return [slice(i, i + tile) for i in range(0, rows, tile)]


def quad_kernel(n, *refs):
    *variances, high_ref, low_ref, out_ref, weights = refs
    load_variances(variances, weights, n)
    for tile in row_tiles(high_ref.shape[0]):
        out_ref[:, tile] = product(weights[...], high_ref[tile, :], low_ref[tile, :], ACROSS)


def stats_of(scores):
    peak = jnp.max(scores, axis=0, keepdims=True)
    return peak, jnp.sum(jnp.exp(scores - peak), axis=0, keepdims=True)


def joined(one, other):
    peak = jnp.maximum(one[0], other[0])
    return peak, one[1] * jnp.exp(one[0] - peak) + other[1] * jnp.exp(other[0] - peak)


def early_kernel(n, *refs):
    *linear, high_ref, low_ref, quad_ref, out_ref, stats_ref, weights = refs
    offset = load_packs(linear, weights, n)
    for tile in row_tiles(high_ref.shape[0]):
        scores = product(weights[...], high_ref[tile, :], low_ref[tile, :], ACROSS)
        scores = quad_ref[:, tile] + scores + offset
        out_ref[:, tile] = scores
        stats_ref[0:1, tile], stats_ref[1:2, tile] = stats_of(scores)


def half_tiles(half):
    for block in range(2):
        for part in row_tiles(half):
            yield slice(block * half + part.start, block * half + part.stop), block, part


def last_kernel(n, *refs):
    *linear, xh_ref, xl_ref, quad_ref, early_ref, out_ref, stats_ref, weights = refs
    offset = load_packs(linear, weights, n)
    for tile, block, part in half_tiles(stats_ref.shape[2]):
        scores = product(weights[...], xh_ref[tile, :], xl_ref[tile, :], ACROSS)
        scores = quad_ref[:, tile] + scores + offset
        out_ref[:, tile] = scores
        early = early_ref[0:1, tile], early_ref[1:2, tile]
        peak, total = joined(stats_of(scores), early)
        stats_ref[block, 0:1, part] = peak
        stats_ref[block, 1:2, part] = total


def score_call(body, out_shape, scratch, name, *operands):
    return pl.pallas_call(
        body,
        out_shape=[jax.ShapeDtypeStruct(shape, F32) for shape in out_shape],
        scratch_shapes=[pltpu.VMEM(shape, BF16) for shape in scratch],
        cost_estimate=HEAVY,
        compiler_params=params(24),
        name=name,
    )(*operands)


def moment_tiles(resp_ref, high_ref, low_ref, packs, n):
    for c in range(0, high_ref.shape[1], 2 * LANES):
        columns = slice(c, c + 2 * LANES)
        total = product(resp_ref[...], high_ref[:, columns], low_ref[:, columns], WITHIN)
        for q, pack in enumerate(packs):
            for k in range(2):
                place = (c // LANES + k) * n
                pack[place : place + n, :] = total[q * n : (q + 1) * n, k * LANES : (k + 1) * LANES]


def first_kernel(n, early_ref, late_ref, stats_ref, high_ref, low_ref, *refs):
    *packs, resp_ref = refs
    comps = resp_ref.shape[0] // 2
    counts = jnp.zeros((comps, LANES), F32)
    for tile, block, part in half_tiles(stats_ref.shape[2]):
        peak, total = stats_ref[block, 0:1, part], stats_ref[block, 1:2, part]
        scores = jnp.concatenate([early_ref[:, tile], late_ref[:, tile]])
        resp = jnp.exp(scores - peak) * (1.0 / total)
        resp_ref[:comps, tile], resp_ref[comps:, tile] = split(resp)
        counts += sum(resp[:, c : c + LANES] for c in range(0, resp.shape[1], LANES))
    moment_tiles(resp_ref, high_ref, low_ref, packs, n)
    column = jnp.sum(counts, axis=1, keepdims=True)
    for q, pack in enumerate(packs):
        row = to_row(column[q * n : (q + 1) * n], LANES)
        pack[-8:, :] = jnp.broadcast_to(row, (8, LANES))


def first_moments(early, late, stats, high, low, n):
    rows, width = high.shape
    comps = early.shape[0] + late.shape[0]
    pack = jax.ShapeDtypeStruct((width // LANES * n + 8, LANES), F32)
    return pl.pallas_call(
        functools.partial(first_kernel, n),
        out_shape=[pack] * (comps // n) + [jax.ShapeDtypeStruct((2 * comps, rows), BF16)],
        cost_estimate=HEAVY,
        compiler_params=params(24),
        name="first_moments",
    )(early, late, stats, high, low)


def second_kernel(n, resp_ref, high_ref, low_ref, *packs):
    moment_tiles(resp_ref, high_ref, low_ref, packs, n)


def second_moments(resp, high, low, n):
    pack = jax.ShapeDtypeStruct((high.shape[1] // LANES * n, LANES), F32)
    return pl.pallas_call(
        functools.partial(second_kernel, n),
        out_shape=[pack] * (resp.shape[0] // 2 // n),
        cost_estimate=HEAVY,
        compiler_params=params(24),
        name="second_moments",
    )(resp, high, low)


def update_kernel(
    scale,
    means_ref,
    variances_ref,
    mass_ref,
    first_ref,
    second_ref,
    near_first_ref,
    near_second_ref,
    new_means_ref,
    new_variances_ref,
    new_mass_ref,
):
    n, width = means_ref.shape
    tiles = width // LANES * n
    row = first_ref[tiles : tiles + 1, :n] + near_first_ref[tiles : tiles + 1, :n]
    new_row = 0.4 * mass_ref[...] + scale * row
    new_mass_ref[...] = new_row
    inverse = 1.0 / to_column(new_row, n)
    kept = 0.4 * to_column(mass_ref[...], n)
    for c in range(width // LANES):
        lanes, tile = slice(c * LANES, (c + 1) * LANES), slice(c * n, (c + 1) * n)
        means, variances = means_ref[:, lanes], variances_ref[:, lanes]
        first = first_ref[tile, :] + near_first_ref[tile, :]
        second = second_ref[tile, :] + near_second_ref[tile, :]
        new_means = (kept * means + scale * first) * inverse
        new_means_ref[:, lanes] = new_means
        second_moment = kept * (variances + means * means) + scale * second
        new_variances_ref[:, lanes] = second_moment * inverse - new_means * new_means


def update(scale, means, variances, mass, *sums):
    n = mass.shape[0]
    block = jax.ShapeDtypeStruct(means.shape, F32)
    new_means, new_variances, new_mass = pl.pallas_call(
        functools.partial(update_kernel, scale),
        out_shape=(block, block, jax.ShapeDtypeStruct((1, n), F32)),
        cost_estimate=HEAVY,
        compiler_params=params(16),
        name="update",
    )(means, variances, mass.reshape(1, n), *sums)
    return new_means, new_variances, new_mass.reshape(n)


def swap(value, axis, bit):
    size = lax.axis_size(axis)
    return lax.ppermute(value, axis, [(i, i ^ bit) for i in range(size)])


def vmem(value):
    return pltpu.with_memory_space_constraint(value, pltpu.VMEM)


def after(value, *others):
    return lax.optimization_barrier((value, *others))[0]


def gather_early(piece):
    bit = lax.axis_size("dp") // 4
    held = {0: piece}
    while bit > 1:
        held.update({q ^ bit: swap(value, "dp", 2 * bit) for q, value in held.items()})
        bit //= 2
    held[1] = swap(piece, "dp", 2)
    return held


def scatter_planes(first, second):
    held = [dict(enumerate(parts)) for parts in (first, second)]
    totals, near = [[parts.pop(0)] for parts in held], []
    planes, bit = len(first), 1
    while bit < planes:
        ready = []
        for parts in held:
            for q in sorted((q for q in parts if q & bit and q != bit), reverse=True):
                parts[q ^ bit] = parts[q ^ bit] + swap(after(parts.pop(q), *ready), "dp", 2 * bit)
                ready = [parts[q ^ bit]]
        for total, parts in zip(totals, held):
            part = swap(after(parts.pop(bit), *ready), "dp", 2 * bit)
            (near if bit == 1 else total).append(part)
        bit *= 2
    return *lax.optimization_barrier(tuple(sum(t[1:], t[0]) for t in totals)), *near


def merge(stats):
    peak = functools.reduce(jnp.maximum, [s[:, 0] for s in stats])
    total = sum(s[:, 1] * jnp.exp(s[:, 0] - peak) for s in stats)
    return jnp.stack([peak, total], axis=1)


def per_device(embeddings, comp_means, comp_variances, comp_mass):
    n = comp_means.shape[0]
    rows, width = embeddings.shape
    planes = lax.axis_size("dp") // 2
    variances = gather_early(comp_variances)
    linear = gather_early(coefficients(comp_means, comp_variances, comp_mass))
    other = swap(embeddings, "dp", 1)
    order = sorted(linear)
    late = [q for q in range(planes) if q not in linear]
    x_high, x_low, s_high, s_low = halves(embeddings, other)
    for q in late:
        variances[q] = swap(after(variances[q ^ 1], x_high), "dp", 2)
    n_early, n_late = n * len(order), n * len(late)

    def quad_scores(group, name):
        comps = n * len(group)
        operands = (*(vmem(variances[q]) for q in group), s_high, s_low)
        body = functools.partial(quad_kernel, n)
        return score_call(body, [(comps, 2 * rows)], [(2 * comps, width)], name, *operands)[0]

    quad = quad_scores(order, "early_quad")
    for q in late:
        linear[q] = swap(after(linear[q ^ 1], quad, linear[1]), "dp", 2)
    early, early_stats = score_call(
        functools.partial(early_kernel, n),
        [(n_early, 2 * rows), (2, 2 * rows)],
        [(2 * n_early, width)],
        "early_scores",
        *(vmem(linear[q]) for q in order),
        x_high,
        x_low,
        quad,
    )
    last, stats = score_call(
        functools.partial(last_kernel, n),
        [(n_late, 2 * rows), (2, 2, rows)],
        [(2 * n_late, width)],
        "last_scores",
        *(vmem(linear[q]) for q in late),
        x_high,
        x_low,
        quad_scores(late, "late_quad"),
        early_stats,
    )
    stats = merge([stats, swap(stats, "dp", 1)[::-1]])
    stats = merge([stats] + [swap(stats, "comp", q) for q in range(1, lax.axis_size("comp"))])

    *first, resp = first_moments(early, last, stats, x_high, x_low, n)
    second = second_moments(resp, s_high, s_low, n)
    place = {q: i for i, q in enumerate(order + late)}
    first, second = ([parts[place[q]] for q in range(planes)] for parts in (first, second))
    sums = scatter_planes(first, second)

    total_comps = n * lax.axis_size("dp") * lax.axis_size("comp")
    total_rows = embeddings.shape[0] * lax.axis_size("dp")
    scale = 0.6 * (total_comps / total_rows)
    return update(scale, comp_means, comp_variances, comp_mass, *sums)


def solution(mesh):
    placed = (P("dp", None), P(("comp", "dp"), None), P(("comp", "dp"), None), P(("comp", "dp")))
    return jax.shard_map(
        per_device,
        mesh=mesh,
        in_specs=placed,
        out_specs=(P(("comp", "dp"), None), P(("comp", "dp"), None), P(("comp", "dp"))),
        check_vma=False,
    )
```

profile of v0, /device:TPU:0, one launch (start us, length us, event | category | flops | bytes accessed | tf_op | source)
XLA Modules:
  0.0 73.4 jit_solution(7141389326615089327)
XLA Ops:
  1.1 3.7 %collective-permute-start.4 = (f32[64,768]{1,0:T(8,128)}, f32[64,768]{1,0:T(8,128)S(1)}, u32[]{:S(2)}, u32[]{:S(2)}) collective-permute-start(f32[64,768]{1,0:T(8,128)} %variances_ref.3), channel_id=1, source_target_pairs={{0,16},{4,20},{8,24},{12,28},{16,0},{20,4},{24,8},{28,12},{1,17},{... | collective-permute-start | bytes 589832 | tf_op jit(solution)/shard_map/ppermute | solution.py:287
  4.8 1.6 %collective-permute-start.3 = (f32[64,768]{1,0:T(8,128)}, f32[64,768]{1,0:T(8,128)S(1)}, u32[]{:S(2)}, u32[]{:S(2)}) collective-permute-start(f32[64,768]{1,0:T(8,128)} %variances_ref.3), channel_id=1, source_target_pairs={{0,8},{4,12},{8,0},{12,4},{16,24},{20,28},{24,16},{28,20},{1,9},{5... | collective-permute-start | bytes 589832 | tf_op jit(solution)/shard_map/ppermute | solution.py:287
  10.8 2.2 %halves.1 = (bf16[2048,768]{1,0:T(8,128)(2,1)S(1)}, bf16[2048,768]{1,0:T(8,128)(2,1)S(1)}, bf16[2048,768]{1,0:T(8,128)(2,1)S(1)}, bf16[2048,768]{1,0:T(8,128)(2,1)S(1)}) custom-call(f32[1024,768]{1,0:T(8,128)S(1)} %copy-done, f32[1024,768]{1,0:T(8,128)S(1)} %collective-permute-done.2.other_ref), custom_call_target="tpu_custom_call" | custom-call | flops 10000000000 | bytes 100000000 | tf_op jit(solution)/shard_map/halves/pallas_call | solution.py:83
  13.0 2.0 %collective-permute-done.4.refs_2_ = f32[64,768]{1,0:T(8,128)S(1)} collective-permute-done((f32[64,768]{1,0:T(8,128)}, f32[64,768]{1,0:T(8,128)S(1)}, u32[]{:S(2)}, u32[]{:S(2)}) %collective-permute-start.4) | collective-permute-done | bytes 196640 | tf_op jit(solution)/shard_map/ppermute | solution.py:287
  16.6 2.4 %early_quad.1.refs_5_ = f32[192,2048]{1,0:T(8,128)S(1)} custom-call(f32[64,768]{1,0:T(8,128)S(1)} %copy-done.4, f32[64,768]{1,0:T(8,128)S(1)} %collective-permute-done.3.refs_1_, f32[64,768]{1,0:T(8,128)S(1)} %collective-permute-done.4.refs_2_, bf16[2048,768]{1,0:T(8,128)(2,1)S(1)} %get-tuple-element.32.refs_3_.refs_1_.high_ref, ...), custom_call_target="tpu_custom_call" | custom-call | flops 10000000000 | bytes 100000000 | tf_op jit(solution)/shard_map/early_quad/pallas_call | solution.py:176
  19.1 4.4 %collective-permute-done.1.refs_2_ = f32[392,128]{1,0:T(8,128)S(1)} collective-permute-done((f32[392,128]{1,0:T(8,128)S(1)}, f32[392,128]{1,0:T(8,128)S(1)}, u32[]{:S(2)}, u32[]{:S(2)}) %collective-permute-start.1) | collective-permute-done | bytes 200736 | tf_op jit(solution)/shard_map/ppermute | solution.py:287
  24.1 1.6 %collective-permute-start.5 = (f32[392,128]{1,0:T(8,128)S(1)}, f32[392,128]{1,0:T(8,128)S(1)}, u32[]{:S(2)}, u32[]{:S(2)}) collective-permute-start(f32[392,128]{1,0:T(8,128)S(1)} %collective-permute-done.1.refs_2_), channel_id=1, source_target_pairs={{0,8},{4,12},{8,0},{12,4},{16,24},{20,28},{24,16},{28,20},{1,9},{5... | collective-permute-start | bytes 602120 | tf_op jit(solution)/shard_map/ppermute | solution.py:287
  25.6 2.5 %early_scores.1 = (f32[192,2048]{1,0:T(8,128)S(1)}, f32[2,2048]{1,0:T(2,128)S(1)}) custom-call(f32[392,128]{1,0:T(8,128)S(1)} %coefficients.1.refs_0_, f32[392,128]{1,0:T(8,128)S(1)} %collective-permute-done.refs_1_, f32[392,128]{1,0:T(8,128)S(1)} %collective-permute-done.1.refs_2_, bf16[2048,768]{1,0:T(8,128)(2,1)S(1)} %get-tuple-element.30.refs_3_.refs_1_.high_ref, ...), custom_call_target="tpu_custom_call" | custom-call | flops 10000000000 | bytes 100000000 | tf_op jit(solution)/shard_map/early_scores/pallas_call | solution.py:176
  28.3 2.0 %late_quad.1.refs_3_ = f32[64,2048]{1,0:T(8,128)S(1)} custom-call(f32[64,768]{1,0:T(8,128)S(1)} %collective-permute-done.6.refs_0_, bf16[2048,768]{1,0:T(8,128)(2,1)S(1)} %get-tuple-element.32.refs_3_.refs_1_.high_ref, bf16[2048,768]{1,0:T(8,128)(2,1)S(1)} %get-tuple-element.33.refs_4_.refs_2_.low_ref), custom_call_target="tpu_custom_call" | custom-call | flops 10000000000 | bytes 100000000 | tf_op jit(solution)/shard_map/late_quad/pallas_call | solution.py:176
  30.3 1.8 %collective-permute-done.5.refs_0_ = f32[392,128]{1,0:T(8,128)S(1)} collective-permute-done((f32[392,128]{1,0:T(8,128)S(1)}, f32[392,128]{1,0:T(8,128)S(1)}, u32[]{:S(2)}, u32[]{:S(2)}) %collective-permute-start.5) | collective-permute-done | bytes 200736 | tf_op jit(solution)/shard_map/ppermute | solution.py:287
  32.1 2.1 %last_scores.1 = (f32[64,2048]{1,0:T(8,128)S(1)}, f32[2,2,1024]{2,1,0:T(2,128)S(1)}) custom-call(f32[392,128]{1,0:T(8,128)S(1)} %collective-permute-done.5.refs_0_, bf16[2048,768]{1,0:T(8,128)(2,1)S(1)} %get-tuple-element.30.refs_3_.refs_1_.high_ref, bf16[2048,768]{1,0:T(8,128)(2,1)S(1)} %get-tuple-element.31.refs_4_.refs_2_.low_ref, ...), custom_call_target="tpu_custom_call" | custom-call | flops 10000000000 | bytes 100000000 | tf_op jit(solution)/shard_map/last_scores/pallas_call | solution.py:176
  34.4 1.2 %collective-permute-done.7 = f32[2,2,1024]{2,1,0:T(2,128)S(1)} collective-permute-done((f32[2,2,1024]{2,1,0:T(2,128)S(1)}, f32[2,2,1024]{2,1,0:T(2,128)S(1)}, u32[]{:S(2)}, u32[]{:S(2)}) %collective-permute-start.7) | collective-permute-done | bytes 16416 | tf_op jit(solution)/shard_map/ppermute | solution.py:287
  35.6 2.6 %collective-permute-start.10 = (f32[2,2,1024]{2,1,0:T(2,128)S(1)}, f32[2,2,1024]{2,1,0:T(2,128)S(1)}, u32[]{:S(2)}, u32[]{:S(2)}) collective-permute-start(f32[2,2,1024]{2,1,0:T(2,128)S(1)} %pad_maximum_fusion), channel_id=1, source_target_pairs={{0,3},{1,2},{2,1},{3,0},{4,7},{5,6},{6,5},{7,4},{8,11},{9,10},{10,... | collective-permute-start | bytes 49160 | tf_op jit(solution)/shard_map/ppermute | solution.py:287
  40.3 1.6 %collective-permute-done.9 = f32[2,2,1024]{2,1,0:T(2,128)S(1)} collective-permute-done((f32[2,2,1024]{2,1,0:T(2,128)S(1)}, f32[2,2,1024]{2,1,0:T(2,128)S(1)}, u32[]{:S(2)}, u32[]{:S(2)}) %collective-permute-start.9) | collective-permute-done | bytes 16416 | tf_op jit(solution)/shard_map/ppermute | solution.py:287
  42.5 2.7 %first_moments.1 = (f32[392,128]{1,0:T(8,128)S(1)}, f32[392,128]{1,0:T(8,128)S(1)}, f32[392,128]{1,0:T(8,128)S(1)}, f32[392,128]{1,0:T(8,128)S(1)}, bf16[512,2048]{1,0:T(8,128)(2,1)S(1)}) custom-call(f32[192,2048]{1,0:T(8,128)S(1)} %get-tuple-element.34.early_ref, f32[64,2048]{1,0:T(8,128)S(1)} %get-tuple-element.38.late_ref, ...), custom_call_target="tpu_custom_call" | custom-call | flops 10000000000 | bytes 100000000 | tf_op jit(solution)/shard_map/first_moments/pallas_call | solution.py:217
  45.2 1.5 %collective-permute-start.11 = (f32[392,128]{1,0:T(8,128)S(1)}, f32[392,128]{1,0:T(8,128)S(1)}, u32[]{:S(2)}, u32[]{:S(2)}) collective-permute-start(f32[392,128]{1,0:T(8,128)S(1)} %get-tuple-element.42), channel_id=1, source_target_pairs={{0,8},{4,12},{8,0},{12,4},{16,24},{20,28},{24,16},{28,20},{1,9},{5... | collective-permute-start | bytes 602120 | tf_op jit(solution)/shard_map/ppermute | solution.py:287
  46.8 2.6 %second_moments.1 = (f32[384,128]{1,0:T(8,128)S(1)}, f32[384,128]{1,0:T(8,128)S(1)}, f32[384,128]{1,0:T(8,128)S(1)}, f32[384,128]{1,0:T(8,128)S(1)}) custom-call(bf16[512,2048]{1,0:T(8,128)(2,1)S(1)} %get-tuple-element.43.resp_ref, bf16[2048,768]{1,0:T(8,128)(2,1)S(1)} %get-tuple-element.32.refs_3_.refs_1_.high_ref, ...), custom_call_target="tpu_custom_call" | custom-call | flops 10000000000 | bytes 100000000 | tf_op jit(solution)/shard_map/second_moments/pallas_call | solution.py:232
  49.4 1.6 %collective-permute-done.11 = f32[392,128]{1,0:T(8,128)S(1)} collective-permute-done((f32[392,128]{1,0:T(8,128)S(1)}, f32[392,128]{1,0:T(8,128)S(1)}, u32[]{:S(2)}, u32[]{:S(2)}) %collective-permute-start.11) | collective-permute-done | bytes 200736 | tf_op jit(solution)/shard_map/ppermute | solution.py:287
  51.1 1.5 %collective-permute-start.13 = (f32[384,128]{1,0:T(8,128)S(1)}, f32[384,128]{1,0:T(8,128)S(1)}, u32[]{:S(2)}, u32[]{:S(2)}) collective-permute-start(f32[384,128]{1,0:T(8,128)S(1)} %get-tuple-element.47), channel_id=1, source_target_pairs={{0,8},{4,12},{8,0},{12,4},{16,24},{20,28},{24,16},{28,20},{1,9},{5... | collective-permute-start | bytes 589832 | tf_op jit(solution)/shard_map/ppermute | solution.py:287
  52.6 2.1 %collective-permute-start.12 = (f32[392,128]{1,0:T(8,128)S(1)}, f32[392,128]{1,0:T(8,128)S(1)}, u32[]{:S(2)}, u32[]{:S(2)}) collective-permute-start(f32[392,128]{1,0:T(8,128)S(1)} %add.33), channel_id=1, source_target_pairs={{0,16},{4,20},{8,24},{12,28},{16,0},{20,4},{24,8},{28,12},{1,17},{... | collective-permute-start | bytes 602120 | tf_op jit(solution)/shard_map/ppermute | solution.py:287
  54.7 6.8 %collective-permute-done.13 = f32[384,128]{1,0:T(8,128)S(1)} collective-permute-done((f32[384,128]{1,0:T(8,128)S(1)}, f32[384,128]{1,0:T(8,128)S(1)}, u32[]{:S(2)}, u32[]{:S(2)}) %collective-permute-start.13) | collective-permute-done | bytes 196640 | tf_op jit(solution)/shard_map/ppermute | solution.py:287
  61.6 4.1 %collective-permute-start.14 = (f32[384,128]{1,0:T(8,128)S(1)}, f32[384,128]{1,0:T(8,128)S(1)}, u32[]{:S(2)}, u32[]{:S(2)}) collective-permute-start(f32[384,128]{1,0:T(8,128)S(1)} %add.35), channel_id=1, source_target_pairs={{0,16},{4,20},{8,24},{12,28},{16,0},{20,4},{24,8},{28,12},{1,17},{... | collective-permute-start | bytes 589832 | tf_op jit(solution)/shard_map/ppermute | solution.py:287
  65.7 3.6 %collective-permute-done.14 = f32[384,128]{1,0:T(8,128)S(1)} collective-permute-done((f32[384,128]{1,0:T(8,128)S(1)}, f32[384,128]{1,0:T(8,128)S(1)}, u32[]{:S(2)}, u32[]{:S(2)}) %collective-permute-start.14) | collective-permute-done | bytes 196640 | tf_op jit(solution)/shard_map/ppermute | solution.py:287
  69.4 3.1 %collective-permute-done.16.near_second_ref = f32[384,128]{1,0:T(8,128)S(1)} collective-permute-done((f32[384,128]{1,0:T(8,128)S(1)}, f32[384,128]{1,0:T(8,128)S(1)}, u32[]{:S(2)}, u32[]{:S(2)}) %collective-permute-start.16) | collective-permute-done | bytes 196640 | tf_op jit(solution)/shard_map/ppermute | solution.py:287
  (42 shorter events, 11.2 us)
Async XLA Ops:
  0.6 9.0 %collective-permute-start.2 = (f32[1024,768]{1,0:T(8,128)}, f32[1024,768]{1,0:T(8,128)S(1)}, u32[]{:S(2)}, u32[]{:S(2)}) collective-permute-start(f32[1024,768]{1,0:T(8,128)} %own_ref.1), channel_id=1, source_target_pairs={{0,4},{4,0},{8,12},{12,8},{16,20},{20,16},{24,28},{28,24},{1,5},{5... | collective-permute-start | bytes 9437192 | tf_op jit(solution)/shard_map/ppermute | solution.py:287
  1.1 13.9 %collective-permute-start.4 = (f32[64,768]{1,0:T(8,128)}, f32[64,768]{1,0:T(8,128)S(1)}, u32[]{:S(2)}, u32[]{:S(2)}) collective-permute-start(f32[64,768]{1,0:T(8,128)} %variances_ref.3), channel_id=1, source_target_pairs={{0,16},{4,20},{8,24},{12,28},{16,0},{20,4},{24,8},{28,12},{1,17},{... | collective-permute-start | bytes 589832 | tf_op jit(solution)/shard_map/ppermute | solution.py:287
  4.8 11.8 %collective-permute-start.3 = (f32[64,768]{1,0:T(8,128)}, f32[64,768]{1,0:T(8,128)S(1)}, u32[]{:S(2)}, u32[]{:S(2)}) collective-permute-start(f32[64,768]{1,0:T(8,128)} %variances_ref.3), channel_id=1, source_target_pairs={{0,8},{4,12},{8,0},{12,4},{16,24},{20,28},{24,16},{28,20},{1,9},{5... | collective-permute-start | bytes 589832 | tf_op jit(solution)/shard_map/ppermute | solution.py:287
  6.4 0.9 %copy-start.1 = (f32[64,768]{1,0:T(8,128)S(1)}, f32[64,768]{1,0:T(8,128)}, u32[]{:S(2)}) copy-start(f32[64,768]{1,0:T(8,128)} %means_ref.3) | copy-start | bytes 589828
  7.3 0.9 %copy-start.3 = (f32[64,768]{1,0:T(8,128)S(1)}, f32[64,768]{1,0:T(8,128)}, u32[]{:S(2)}) copy-start(f32[64,768]{1,0:T(8,128)} %variances_ref.3) | copy-start | bytes 589828
  8.2 0.7 copy-start.5
  8.9 1.9 %copy-start = (f32[1024,768]{1,0:T(8,128)S(1)}, f32[1024,768]{1,0:T(8,128)}, u32[]{:S(2)}) copy-start(f32[1024,768]{1,0:T(8,128)} %own_ref.1) | copy-start | bytes 9437188
  9.0 7.6 %copy-start.4 = (f32[64,768]{1,0:T(8,128)S(1)}, f32[64,768]{1,0:T(8,128)}, u32[]{:S(2)}) copy-start(f32[64,768]{1,0:T(8,128)} %variances_ref.3) | copy-start | bytes 589828
  9.1 14.4 %collective-permute-start.1 = (f32[392,128]{1,0:T(8,128)S(1)}, f32[392,128]{1,0:T(8,128)S(1)}, u32[]{:S(2)}, u32[]{:S(2)}) collective-permute-start(f32[392,128]{1,0:T(8,128)S(1)} %coefficients.1.refs_0_), channel_id=1, source_target_pairs={{0,16},{4,20},{8,24},{12,28},{16,0},{20,4},{24,8},{28,12},{1,17},{... | collective-permute-start | bytes 602120 | tf_op jit(solution)/shard_map/ppermute | solution.py:287
  9.5 14.6 %collective-permute-start = (f32[392,128]{1,0:T(8,128)S(1)}, f32[392,128]{1,0:T(8,128)S(1)}, u32[]{:S(2)}, u32[]{:S(2)}) collective-permute-start(f32[392,128]{1,0:T(8,128)S(1)} %coefficients.1.refs_0_), channel_id=1, source_target_pairs={{0,8},{4,12},{8,0},{12,4},{16,24},{20,28},{24,16},{28,20},{1,9},{5... | collective-permute-start | bytes 602120 | tf_op jit(solution)/shard_map/ppermute | solution.py:287
  15.1 13.2 %collective-permute-start.6 = (f32[64,768]{1,0:T(8,128)S(1)}, f32[64,768]{1,0:T(8,128)S(1)}, u32[]{:S(2)}, u32[]{:S(2)}) collective-permute-start(f32[64,768]{1,0:T(8,128)S(1)} %collective-permute-done.4.refs_2_), channel_id=1, source_target_pairs={{0,8},{4,12},{8,0},{12,4},{16,24},{20,28},{24,16},{28,20},{1,9},{5... | collective-permute-start | bytes 589832 | tf_op jit(solution)/shard_map/ppermute | solution.py:287
  24.1 8.1 %collective-permute-start.5 = (f32[392,128]{1,0:T(8,128)S(1)}, f32[392,128]{1,0:T(8,128)S(1)}, u32[]{:S(2)}, u32[]{:S(2)}) collective-permute-start(f32[392,128]{1,0:T(8,128)S(1)} %collective-permute-done.1.refs_2_), channel_id=1, source_target_pairs={{0,8},{4,12},{8,0},{12,4},{16,24},{20,28},{24,16},{28,20},{1,9},{5... | collective-permute-start | bytes 602120 | tf_op jit(solution)/shard_map/ppermute | solution.py:287
  34.3 1.2 %collective-permute-start.7 = (f32[2,2,1024]{2,1,0:T(2,128)S(1)}, f32[2,2,1024]{2,1,0:T(2,128)S(1)}, u32[]{:S(2)}, u32[]{:S(2)}) collective-permute-start(f32[2,2,1024]{2,1,0:T(2,128)S(1)} %get-tuple-element.39), channel_id=1, source_target_pairs={{0,4},{4,0},{8,12},{12,8},{16,20},{20,16},{24,28},{28,24},{1,5},{5... | collective-permute-start | bytes 49160 | tf_op jit(solution)/shard_map/ppermute | solution.py:287
  35.6 4.7 %collective-permute-start.10 = (f32[2,2,1024]{2,1,0:T(2,128)S(1)}, f32[2,2,1024]{2,1,0:T(2,128)S(1)}, u32[]{:S(2)}, u32[]{:S(2)}) collective-permute-start(f32[2,2,1024]{2,1,0:T(2,128)S(1)} %pad_maximum_fusion), channel_id=1, source_target_pairs={{0,3},{1,2},{2,1},{3,0},{4,7},{5,6},{6,5},{7,4},{8,11},{9,10},{10,... | collective-permute-start | bytes 49160 | tf_op jit(solution)/shard_map/ppermute | solution.py:287
  38.2 3.7 %collective-permute-start.9 = (f32[2,2,1024]{2,1,0:T(2,128)S(1)}, f32[2,2,1024]{2,1,0:T(2,128)S(1)}, u32[]{:S(2)}, u32[]{:S(2)}) collective-permute-start(f32[2,2,1024]{2,1,0:T(2,128)S(1)} %pad_maximum_fusion), channel_id=1, source_target_pairs={{0,2},{1,3},{2,0},{3,1},{4,6},{5,7},{6,4},{7,5},{8,10},{9,11},{10,... | collective-permute-start | bytes 49160 | tf_op jit(solution)/shard_map/ppermute | solution.py:287
  38.7 3.7 %collective-permute-start.8 = (f32[2,2,1024]{2,1,0:T(2,128)S(1)}, f32[2,2,1024]{2,1,0:T(2,128)S(1)}, u32[]{:S(2)}, u32[]{:S(2)}) collective-permute-start(f32[2,2,1024]{2,1,0:T(2,128)S(1)} %pad_maximum_fusion), channel_id=1, source_target_pairs={{0,1},{1,0},{2,3},{3,2},{4,5},{5,4},{6,7},{7,6},{8,9},{9,8},{10,11... | collective-permute-start | bytes 49160 | tf_op jit(solution)/shard_map/ppermute | solution.py:287
  45.2 5.8 %collective-permute-start.11 = (f32[392,128]{1,0:T(8,128)S(1)}, f32[392,128]{1,0:T(8,128)S(1)}, u32[]{:S(2)}, u32[]{:S(2)}) collective-permute-start(f32[392,128]{1,0:T(8,128)S(1)} %get-tuple-element.42), channel_id=1, source_target_pairs={{0,8},{4,12},{8,0},{12,4},{16,24},{20,28},{24,16},{28,20},{1,9},{5... | collective-permute-start | bytes 602120 | tf_op jit(solution)/shard_map/ppermute | solution.py:287
  46.8 25.7 %copy-start.2 = (f32[64,768]{1,0:T(8,128)S(1)}, f32[64,768]{1,0:T(8,128)}, u32[]{:S(2)}) copy-start(f32[64,768]{1,0:T(8,128)} %means_ref.3) | copy-start | bytes 589828
  46.8 25.7 %copy-start.6 = (f32[64]{0:T(128)S(1)}, f32[64]{0:T(128)}, u32[]{:S(2)}) copy-start(f32[64]{0:T(128)} %param.7) | copy-start | bytes 772
  51.1 10.4 %collective-permute-start.13 = (f32[384,128]{1,0:T(8,128)S(1)}, f32[384,128]{1,0:T(8,128)S(1)}, u32[]{:S(2)}, u32[]{:S(2)}) collective-permute-start(f32[384,128]{1,0:T(8,128)S(1)} %get-tuple-element.47), channel_id=1, source_target_pairs={{0,8},{4,12},{8,0},{12,4},{16,24},{20,28},{24,16},{28,20},{1,9},{5... | collective-permute-start | bytes 589832 | tf_op jit(solution)/shard_map/ppermute | solution.py:287
  52.6 13.1 %collective-permute-start.12 = (f32[392,128]{1,0:T(8,128)S(1)}, f32[392,128]{1,0:T(8,128)S(1)}, u32[]{:S(2)}, u32[]{:S(2)}) collective-permute-start(f32[392,128]{1,0:T(8,128)S(1)} %add.33), channel_id=1, source_target_pairs={{0,16},{4,20},{8,24},{12,28},{16,0},{20,4},{24,8},{28,12},{1,17},{... | collective-permute-start | bytes 602120 | tf_op jit(solution)/shard_map/ppermute | solution.py:287
  61.5 11.0 %collective-permute-start.15 = (f32[392,128]{1,0:T(8,128)S(1)}, f32[392,128]{1,0:T(8,128)S(1)}, u32[]{:S(2)}, u32[]{:S(2)}) collective-permute-start(f32[392,128]{1,0:T(8,128)S(1)} %get-tuple-element.51), channel_id=1, source_target_pairs={{0,8},{4,12},{8,0},{12,4},{16,24},{20,28},{24,16},{28,20},{1,9},{5... | collective-permute-start | bytes 602120 | tf_op jit(solution)/shard_map/ppermute | solution.py:287
  61.6 7.8 %collective-permute-start.14 = (f32[384,128]{1,0:T(8,128)S(1)}, f32[384,128]{1,0:T(8,128)S(1)}, u32[]{:S(2)}, u32[]{:S(2)}) collective-permute-start(f32[384,128]{1,0:T(8,128)S(1)} %add.35), channel_id=1, source_target_pairs={{0,16},{4,20},{8,24},{12,28},{16,0},{20,4},{24,8},{28,12},{1,17},{... | collective-permute-start | bytes 589832 | tf_op jit(solution)/shard_map/ppermute | solution.py:287
  65.6 6.9 %collective-permute-start.16 = (f32[384,128]{1,0:T(8,128)S(1)}, f32[384,128]{1,0:T(8,128)S(1)}, u32[]{:S(2)}, u32[]{:S(2)}) collective-permute-start(f32[384,128]{1,0:T(8,128)S(1)} %get-tuple-element.53), channel_id=1, source_target_pairs={{0,8},{4,12},{8,0},{12,4},{16,24},{20,28},{24,16},{28,20},{1,9},{5... | collective-permute-start | bytes 589832 | tf_op jit(solution)/shard_map/ppermute | solution.py:287
where the time goes:
time: 73.6 us; the launch traced here: 73.4 us
  waiting for transfers between devices  29.3 us (40%)
  starting transfers between devices  21.7 us (29%)
  Pallas kernels  17.7 us (24%)
  local copies, waits for them, and re-layouts  3.67 us (5%)
  between operations  0.74 us (1%)
    ppermute x17, waiting for transfers between devices, swap(): return lax.ppermute(value, axis, [(i, i ^ bit) for i in range(size)])  29.3 us
    ppermute x17, starting transfers between devices, swap(): return lax.ppermute(value, axis, [(i, i ^ bit) for i in range(size)])  21.7 us
    pallas_call x4, Pallas kernels, score_call(): pl.pallas_call(body, out_shape=[jax.ShapeDtypeStruct(shape, F32) for shap...  9.13 us
    unnamed x14, local copies, waits for them, and re-layouts  3.66 us
    pallas_call x1, Pallas kernels, first_moments(): pl.pallas_call(functools.partial(first_kernel, n), out_shape=[pack] * (co...  2.7 us
    pallas_call x1, Pallas kernels, second_moments(): pl.pallas_call(functools.partial(second_kernel, n), out_shape=[pack] * (r...  2.6 us
    pallas_call x1, Pallas kernels, halves(): pl.pallas_call(halves_kernel, grid=(2 * steps,), in_specs=[pl.BlockSpec((...  2.25 us
  transfers between devices with their start and end apart: 17, of which 14 were waited for; matrix products, arithmetic and copies ran while one was open for 0% of the time, Pallas kernels for 16%

commit v1 on v0

--- a/solution.py
+++ b/solution.py
@@ -313,7 +313,7 @@
         ready = []
         for parts in held:
             for q in sorted((q for q in parts if q & bit and q != bit), reverse=True):
-                parts[q ^ bit] = parts[q ^ bit] + swap(after(parts.pop(q), *ready), "dp", 2 * bit)
+                parts[q ^ bit] = parts[q ^ bit] + swap(parts.pop(q), "dp", 2 * bit)
                 ready = [parts[q ^ bit]]
         for total, parts in zip(totals, held):
             part = swap(after(parts.pop(bit), *ready), "dp", 2 * bit)
@@ -350,7 +350,7 @@
 
     quad = quad_scores(order, "early_quad")
     for q in late:
-        linear[q] = swap(after(linear[q ^ 1], quad, linear[1]), "dp", 2)
+        linear[q] = swap(after(linear[q ^ 1], quad), "dp", 2)
     early, early_stats = score_call(
         functools.partial(early_kernel, n),
         [(n_early, 2 * rows), (2, 2 * rows)],

time: 73.6 us -> 73.8 us (level)
  transfers between devices with their start and end apart: 17 -> 17, of which waited for: 14 -> 13; matrix products, arithmetic and copies ran while one was open for 0% -> 0% of each run, Pallas kernels for 16% -> 16%
where the time goes in v1:
time: 73.8 us; the launch traced here: 73.6 us
  waiting for transfers between devices  29.6 us (40%)
  starting transfers between devices  21.6 us (29%)
  Pallas kernels  17.7 us (24%)
  local copies, waits for them, and re-layouts  3.67 us (5%)
  between operations  0.75 us (1%)
    ppermute x17, waiting for transfers between devices, swap(): return lax.ppermute(value, axis, [(i, i ^ bit) for i in range(size)])  29.6 us
    ppermute x17, starting transfers between devices, swap(): return lax.ppermute(value, axis, [(i, i ^ bit) for i in range(size)])  21.6 us
    pallas_call x4, Pallas kernels, score_call(): pl.pallas_call(body, out_shape=[jax.ShapeDtypeStruct(shape, F32) for shap...  9.12 us
    unnamed x14, local copies, waits for them, and re-layouts  3.66 us
    pallas_call x1, Pallas kernels, first_moments(): pl.pallas_call(functools.partial(first_kernel, n), out_shape=[pack] * (co...  2.7 us
    pallas_call x1, Pallas kernels, second_moments(): pl.pallas_call(functools.partial(second_kernel, n), out_shape=[pack] * (r...  2.6 us
    pallas_call x1, Pallas kernels, halves(): pl.pallas_call(halves_kernel, grid=(2 * steps,), in_specs=[pl.BlockSpec((...  2.25 us
  transfers between devices with their start and end apart: 17, of which 13 were waited for; matrix products, arithmetic and copies ran while one was open for 0% of the time, Pallas kernels for 16%

profile of v1, /device:TPU:0, one launch (start us, length us, event | category | flops | bytes accessed | tf_op | source)
XLA Modules:
  0.0 73.6 jit_solution(12439106685668284753)
XLA Ops:
  1.1 3.7 %collective-permute-start.4 = (f32[64,768]{1,0:T(8,128)}, f32[64,768]{1,0:T(8,128)S(1)}, u32[]{:S(2)}, u32[]{:S(2)}) collective-permute-start(f32[64,768]{1,0:T(8,128)} %variances_ref.3), channel_id=1, source_target_pairs={{0,16},{4,20},{8,24},{12,28},{16,0},{20,4},{24,8},{28,12},{1,17},{... | collective-permute-start | bytes 589832 | tf_op jit(solution)/shard_map/ppermute | solution.py:287
  4.8 1.6 %collective-permute-start.3 = (f32[64,768]{1,0:T(8,128)}, f32[64,768]{1,0:T(8,128)S(1)}, u32[]{:S(2)}, u32[]{:S(2)}) collective-permute-start(f32[64,768]{1,0:T(8,128)} %variances_ref.3), channel_id=1, source_target_pairs={{0,8},{4,12},{8,0},{12,4},{16,24},{20,28},{24,16},{28,20},{1,9},{5... | collective-permute-start | bytes 589832 | tf_op jit(solution)/shard_map/ppermute | solution.py:287
  10.8 2.2 %halves.1 = (bf16[2048,768]{1,0:T(8,128)(2,1)S(1)}, bf16[2048,768]{1,0:T(8,128)(2,1)S(1)}, bf16[2048,768]{1,0:T(8,128)(2,1)S(1)}, bf16[2048,768]{1,0:T(8,128)(2,1)S(1)}) custom-call(f32[1024,768]{1,0:T(8,128)S(1)} %copy-done, f32[1024,768]{1,0:T(8,128)S(1)} %collective-permute-done.2.other_ref), custom_call_target="tpu_custom_call" | custom-call | flops 10000000000 | bytes 100000000 | tf_op jit(solution)/shard_map/halves/pallas_call | solution.py:83
  13.0 2.0 %collective-permute-done.4.refs_2_ = f32[64,768]{1,0:T(8,128)S(1)} collective-permute-done((f32[64,768]{1,0:T(8,128)}, f32[64,768]{1,0:T(8,128)S(1)}, u32[]{:S(2)}, u32[]{:S(2)}) %collective-permute-start.4) | collective-permute-done | bytes 196640 | tf_op jit(solution)/shard_map/ppermute | solution.py:287
  16.6 2.4 %early_quad.1.refs_5_ = f32[192,2048]{1,0:T(8,128)S(1)} custom-call(f32[64,768]{1,0:T(8,128)S(1)} %copy-done.4, f32[64,768]{1,0:T(8,128)S(1)} %collective-permute-done.3.refs_1_, f32[64,768]{1,0:T(8,128)S(1)} %collective-permute-done.4.refs_2_, bf16[2048,768]{1,0:T(8,128)(2,1)S(1)} %get-tuple-element.31.refs_3_.refs_1_.high_ref, ...), custom_call_target="tpu_custom_call" | custom-call | flops 10000000000 | bytes 100000000 | tf_op jit(solution)/shard_map/early_quad/pallas_call | solution.py:176
  19.1 4.4 %collective-permute-done.1.refs_2_ = f32[392,128]{1,0:T(8,128)S(1)} collective-permute-done((f32[392,128]{1,0:T(8,128)S(1)}, f32[392,128]{1,0:T(8,128)S(1)}, u32[]{:S(2)}, u32[]{:S(2)}) %collective-permute-start.1) | collective-permute-done | bytes 200736 | tf_op jit(solution)/shard_map/ppermute | solution.py:287
  24.2 2.5 %early_scores.1 = (f32[192,2048]{1,0:T(8,128)S(1)}, f32[2,2048]{1,0:T(2,128)S(1)}) custom-call(f32[392,128]{1,0:T(8,128)S(1)} %coefficients.1.refs_0_, f32[392,128]{1,0:T(8,128)S(1)} %collective-permute-done.refs_1_, f32[392,128]{1,0:T(8,128)S(1)} %collective-permute-done.1.refs_2_, bf16[2048,768]{1,0:T(8,128)(2,1)S(1)} %get-tuple-element.29.refs_3_.refs_1_.high_ref, ...), custom_call_target="tpu_custom_call" | custom-call | flops 10000000000 | bytes 100000000 | tf_op jit(solution)/shard_map/early_scores/pallas_call | solution.py:176
  26.7 1.6 %collective-permute-done.6.refs_0_ = f32[64,768]{1,0:T(8,128)S(1)} collective-permute-done((f32[64,768]{1,0:T(8,128)S(1)}, f32[64,768]{1,0:T(8,128)S(1)}, u32[]{:S(2)}, u32[]{:S(2)}) %collective-permute-start.6) | collective-permute-done | bytes 196640 | tf_op jit(solution)/shard_map/ppermute | solution.py:287
  28.3 2.0 %late_quad.1.refs_3_ = f32[64,2048]{1,0:T(8,128)S(1)} custom-call(f32[64,768]{1,0:T(8,128)S(1)} %collective-permute-done.6.refs_0_, bf16[2048,768]{1,0:T(8,128)(2,1)S(1)} %get-tuple-element.31.refs_3_.refs_1_.high_ref, bf16[2048,768]{1,0:T(8,128)(2,1)S(1)} %get-tuple-element.32.refs_4_.refs_2_.low_ref), custom_call_target="tpu_custom_call" | custom-call | flops 10000000000 | bytes 100000000 | tf_op jit(solution)/shard_map/late_quad/pallas_call | solution.py:176
  30.3 1.8 %collective-permute-done.5.refs_0_ = f32[392,128]{1,0:T(8,128)S(1)} collective-permute-done((f32[392,128]{1,0:T(8,128)S(1)}, f32[392,128]{1,0:T(8,128)S(1)}, u32[]{:S(2)}, u32[]{:S(2)}) %collective-permute-start.5) | collective-permute-done | bytes 200736 | tf_op jit(solution)/shard_map/ppermute | solution.py:287
  32.1 2.1 %last_scores.1 = (f32[64,2048]{1,0:T(8,128)S(1)}, f32[2,2,1024]{2,1,0:T(2,128)S(1)}) custom-call(f32[392,128]{1,0:T(8,128)S(1)} %collective-permute-done.5.refs_0_, bf16[2048,768]{1,0:T(8,128)(2,1)S(1)} %get-tuple-element.29.refs_3_.refs_1_.high_ref, bf16[2048,768]{1,0:T(8,128)(2,1)S(1)} %get-tuple-element.30.refs_4_.refs_2_.low_ref, ...), custom_call_target="tpu_custom_call" | custom-call | flops 10000000000 | bytes 100000000 | tf_op jit(solution)/shard_map/last_scores/pallas_call | solution.py:176
  34.4 1.2 %collective-permute-done.7 = f32[2,2,1024]{2,1,0:T(2,128)S(1)} collective-permute-done((f32[2,2,1024]{2,1,0:T(2,128)S(1)}, f32[2,2,1024]{2,1,0:T(2,128)S(1)}, u32[]{:S(2)}, u32[]{:S(2)}) %collective-permute-start.7) | collective-permute-done | bytes 16416 | tf_op jit(solution)/shard_map/ppermute | solution.py:287
  35.6 2.6 %collective-permute-start.10 = (f32[2,2,1024]{2,1,0:T(2,128)S(1)}, f32[2,2,1024]{2,1,0:T(2,128)S(1)}, u32[]{:S(2)}, u32[]{:S(2)}) collective-permute-start(f32[2,2,1024]{2,1,0:T(2,128)S(1)} %pad_maximum_fusion), channel_id=1, source_target_pairs={{0,3},{1,2},{2,1},{3,0},{4,7},{5,6},{6,5},{7,4},{8,11},{9,10},{10,... | collective-permute-start | bytes 49160 | tf_op jit(solution)/shard_map/ppermute | solution.py:287
  40.3 1.6 %collective-permute-done.9 = f32[2,2,1024]{2,1,0:T(2,128)S(1)} collective-permute-done((f32[2,2,1024]{2,1,0:T(2,128)S(1)}, f32[2,2,1024]{2,1,0:T(2,128)S(1)}, u32[]{:S(2)}, u32[]{:S(2)}) %collective-permute-start.9) | collective-permute-done | bytes 16416 | tf_op jit(solution)/shard_map/ppermute | solution.py:287
  42.5 2.7 %first_moments.1 = (f32[392,128]{1,0:T(8,128)S(1)}, f32[392,128]{1,0:T(8,128)S(1)}, f32[392,128]{1,0:T(8,128)S(1)}, f32[392,128]{1,0:T(8,128)S(1)}, bf16[512,2048]{1,0:T(8,128)(2,1)S(1)}) custom-call(f32[192,2048]{1,0:T(8,128)S(1)} %get-tuple-element.33.early_ref, f32[64,2048]{1,0:T(8,128)S(1)} %get-tuple-element.37.late_ref, ...), custom_call_target="tpu_custom_call" | custom-call | flops 10000000000 | bytes 100000000 | tf_op jit(solution)/shard_map/first_moments/pallas_call | solution.py:217
  45.2 1.5 %collective-permute-start.11 = (f32[392,128]{1,0:T(8,128)S(1)}, f32[392,128]{1,0:T(8,128)S(1)}, u32[]{:S(2)}, u32[]{:S(2)}) collective-permute-start(f32[392,128]{1,0:T(8,128)S(1)} %get-tuple-element.41), channel_id=1, source_target_pairs={{0,8},{4,12},{8,0},{12,4},{16,24},{20,28},{24,16},{28,20},{1,9},{5... | collective-permute-start | bytes 602120 | tf_op jit(solution)/shard_map/ppermute | solution.py:287
  46.8 2.6 %second_moments.1 = (f32[384,128]{1,0:T(8,128)S(1)}, f32[384,128]{1,0:T(8,128)S(1)}, f32[384,128]{1,0:T(8,128)S(1)}, f32[384,128]{1,0:T(8,128)S(1)}) custom-call(bf16[512,2048]{1,0:T(8,128)(2,1)S(1)} %get-tuple-element.42.resp_ref, bf16[2048,768]{1,0:T(8,128)(2,1)S(1)} %get-tuple-element.31.refs_3_.refs_1_.high_ref, ...), custom_call_target="tpu_custom_call" | custom-call | flops 10000000000 | bytes 100000000 | tf_op jit(solution)/shard_map/second_moments/pallas_call | solution.py:232
  50.0 1.8 %collective-permute-done.11 = f32[392,128]{1,0:T(8,128)S(1)} collective-permute-done((f32[392,128]{1,0:T(8,128)S(1)}, f32[392,128]{1,0:T(8,128)S(1)}, u32[]{:S(2)}, u32[]{:S(2)}) %collective-permute-start.11) | collective-permute-done | bytes 200736 | tf_op jit(solution)/shard_map/ppermute | solution.py:287
  51.8 4.3 %collective-permute-start.12 = (f32[392,128]{1,0:T(8,128)S(1)}, f32[392,128]{1,0:T(8,128)S(1)}, u32[]{:S(2)}, u32[]{:S(2)}) collective-permute-start(f32[392,128]{1,0:T(8,128)S(1)} %add.33), channel_id=1, source_target_pairs={{0,16},{4,20},{8,24},{12,28},{16,0},{20,4},{24,8},{28,12},{1,17},{... | collective-permute-start | bytes 602120 | tf_op jit(solution)/shard_map/ppermute | solution.py:287
  56.1 1.3 %collective-permute-done.13 = f32[384,128]{1,0:T(8,128)S(1)} collective-permute-done((f32[384,128]{1,0:T(8,128)S(1)}, f32[384,128]{1,0:T(8,128)S(1)}, u32[]{:S(2)}, u32[]{:S(2)}) %collective-permute-start.13) | collective-permute-done | bytes 196640 | tf_op jit(solution)/shard_map/ppermute | solution.py:287
  57.4 1.4 %collective-permute-start.15 = (f32[392,128]{1,0:T(8,128)S(1)}, f32[392,128]{1,0:T(8,128)S(1)}, u32[]{:S(2)}, u32[]{:S(2)}) collective-permute-start(f32[392,128]{1,0:T(8,128)S(1)} %get-tuple-element.49), channel_id=1, source_target_pairs={{0,8},{4,12},{8,0},{12,4},{16,24},{20,28},{24,16},{28,20},{1,9},{5... | collective-permute-start | bytes 602120 | tf_op jit(solution)/shard_map/ppermute | solution.py:287
  58.8 2.2 %collective-permute-start.14 = (f32[384,128]{1,0:T(8,128)S(1)}, f32[384,128]{1,0:T(8,128)S(1)}, u32[]{:S(2)}, u32[]{:S(2)}) collective-permute-start(f32[384,128]{1,0:T(8,128)S(1)} %add.35), channel_id=1, source_target_pairs={{0,16},{4,20},{8,24},{12,28},{16,0},{20,4},{24,8},{28,12},{1,17},{... | collective-permute-start | bytes 589832 | tf_op jit(solution)/shard_map/ppermute | solution.py:287
  61.1 8.6 %collective-permute-done.14 = f32[384,128]{1,0:T(8,128)S(1)} collective-permute-done((f32[384,128]{1,0:T(8,128)S(1)}, f32[384,128]{1,0:T(8,128)S(1)}, u32[]{:S(2)}, u32[]{:S(2)}) %collective-permute-start.14) | collective-permute-done | bytes 196640 | tf_op jit(solution)/shard_map/ppermute | solution.py:287
  69.8 2.9 %collective-permute-done.16.near_second_ref = f32[384,128]{1,0:T(8,128)S(1)} collective-permute-done((f32[384,128]{1,0:T(8,128)S(1)}, f32[384,128]{1,0:T(8,128)S(1)}, u32[]{:S(2)}, u32[]{:S(2)}) %collective-permute-start.16) | collective-permute-done | bytes 196640 | tf_op jit(solution)/shard_map/ppermute | solution.py:287
  (42 shorter events, 11.7 us)
Async XLA Ops:
  0.6 9.0 %collective-permute-start.2 = (f32[1024,768]{1,0:T(8,128)}, f32[1024,768]{1,0:T(8,128)S(1)}, u32[]{:S(2)}, u32[]{:S(2)}) collective-permute-start(f32[1024,768]{1,0:T(8,128)} %own_ref.1), channel_id=1, source_target_pairs={{0,4},{4,0},{8,12},{12,8},{16,20},{20,16},{24,28},{28,24},{1,5},{5... | collective-permute-start | bytes 9437192 | tf_op jit(solution)/shard_map/ppermute | solution.py:287
  1.1 13.9 %collective-permute-start.4 = (f32[64,768]{1,0:T(8,128)}, f32[64,768]{1,0:T(8,128)S(1)}, u32[]{:S(2)}, u32[]{:S(2)}) collective-permute-start(f32[64,768]{1,0:T(8,128)} %variances_ref.3), channel_id=1, source_target_pairs={{0,16},{4,20},{8,24},{12,28},{16,0},{20,4},{24,8},{28,12},{1,17},{... | collective-permute-start | bytes 589832 | tf_op jit(solution)/shard_map/ppermute | solution.py:287
  4.8 11.8 %collective-permute-start.3 = (f32[64,768]{1,0:T(8,128)}, f32[64,768]{1,0:T(8,128)S(1)}, u32[]{:S(2)}, u32[]{:S(2)}) collective-permute-start(f32[64,768]{1,0:T(8,128)} %variances_ref.3), channel_id=1, source_target_pairs={{0,8},{4,12},{8,0},{12,4},{16,24},{20,28},{24,16},{28,20},{1,9},{5... | collective-permute-start | bytes 589832 | tf_op jit(solution)/shard_map/ppermute | solution.py:287
  6.4 0.9 %copy-start.1 = (f32[64,768]{1,0:T(8,128)S(1)}, f32[64,768]{1,0:T(8,128)}, u32[]{:S(2)}) copy-start(f32[64,768]{1,0:T(8,128)} %means_ref.3) | copy-start | bytes 589828
  7.3 0.9 %copy-start.3 = (f32[64,768]{1,0:T(8,128)S(1)}, f32[64,768]{1,0:T(8,128)}, u32[]{:S(2)}) copy-start(f32[64,768]{1,0:T(8,128)} %variances_ref.3) | copy-start | bytes 589828
  8.2 0.7 copy-start.5
  8.9 1.9 %copy-start = (f32[1024,768]{1,0:T(8,128)S(1)}, f32[1024,768]{1,0:T(8,128)}, u32[]{:S(2)}) copy-start(f32[1024,768]{1,0:T(8,128)} %own_ref.1) | copy-start | bytes 9437188
  9.0 7.6 %copy-start.4 = (f32[64,768]{1,0:T(8,128)S(1)}, f32[64,768]{1,0:T(8,128)}, u32[]{:S(2)}) copy-start(f32[64,768]{1,0:T(8,128)} %variances_ref.3) | copy-start | bytes 589828
  9.1 14.4 %collective-permute-start.1 = (f32[392,128]{1,0:T(8,128)S(1)}, f32[392,128]{1,0:T(8,128)S(1)}, u32[]{:S(2)}, u32[]{:S(2)}) collective-permute-start(f32[392,128]{1,0:T(8,128)S(1)} %coefficients.1.refs_0_), channel_id=1, source_target_pairs={{0,16},{4,20},{8,24},{12,28},{16,0},{20,4},{24,8},{28,12},{1,17},{... | collective-permute-start | bytes 602120 | tf_op jit(solution)/shard_map/ppermute | solution.py:287
  9.5 14.7 %collective-permute-start = (f32[392,128]{1,0:T(8,128)S(1)}, f32[392,128]{1,0:T(8,128)S(1)}, u32[]{:S(2)}, u32[]{:S(2)}) collective-permute-start(f32[392,128]{1,0:T(8,128)S(1)} %coefficients.1.refs_0_), channel_id=1, source_target_pairs={{0,8},{4,12},{8,0},{12,4},{16,24},{20,28},{24,16},{28,20},{1,9},{5... | collective-permute-start | bytes 602120 | tf_op jit(solution)/shard_map/ppermute | solution.py:287
  15.1 13.2 %collective-permute-start.6 = (f32[64,768]{1,0:T(8,128)S(1)}, f32[64,768]{1,0:T(8,128)S(1)}, u32[]{:S(2)}, u32[]{:S(2)}) collective-permute-start(f32[64,768]{1,0:T(8,128)S(1)} %collective-permute-done.4.refs_2_), channel_id=1, source_target_pairs={{0,8},{4,12},{8,0},{12,4},{16,24},{20,28},{24,16},{28,20},{1,9},{5... | collective-permute-start | bytes 589832 | tf_op jit(solution)/shard_map/ppermute | solution.py:287
  23.5 8.7 %collective-permute-start.5 = (f32[392,128]{1,0:T(8,128)S(1)}, f32[392,128]{1,0:T(8,128)S(1)}, u32[]{:S(2)}, u32[]{:S(2)}) collective-permute-start(f32[392,128]{1,0:T(8,128)S(1)} %collective-permute-done.1.refs_2_), channel_id=1, source_target_pairs={{0,8},{4,12},{8,0},{12,4},{16,24},{20,28},{24,16},{28,20},{1,9},{5... | collective-permute-start | bytes 602120 | tf_op jit(solution)/shard_map/ppermute | solution.py:287
  34.3 1.2 %collective-permute-start.7 = (f32[2,2,1024]{2,1,0:T(2,128)S(1)}, f32[2,2,1024]{2,1,0:T(2,128)S(1)}, u32[]{:S(2)}, u32[]{:S(2)}) collective-permute-start(f32[2,2,1024]{2,1,0:T(2,128)S(1)} %get-tuple-element.38), channel_id=1, source_target_pairs={{0,4},{4,0},{8,12},{12,8},{16,20},{20,16},{24,28},{28,24},{1,5},{5... | collective-permute-start | bytes 49160 | tf_op jit(solution)/shard_map/ppermute | solution.py:287
  35.6 4.7 %collective-permute-start.10 = (f32[2,2,1024]{2,1,0:T(2,128)S(1)}, f32[2,2,1024]{2,1,0:T(2,128)S(1)}, u32[]{:S(2)}, u32[]{:S(2)}) collective-permute-start(f32[2,2,1024]{2,1,0:T(2,128)S(1)} %pad_maximum_fusion), channel_id=1, source_target_pairs={{0,3},{1,2},{2,1},{3,0},{4,7},{5,6},{6,5},{7,4},{8,11},{9,10},{10,... | collective-permute-start | bytes 49160 | tf_op jit(solution)/shard_map/ppermute | solution.py:287
  38.2 3.7 %collective-permute-start.9 = (f32[2,2,1024]{2,1,0:T(2,128)S(1)}, f32[2,2,1024]{2,1,0:T(2,128)S(1)}, u32[]{:S(2)}, u32[]{:S(2)}) collective-permute-start(f32[2,2,1024]{2,1,0:T(2,128)S(1)} %pad_maximum_fusion), channel_id=1, source_target_pairs={{0,2},{1,3},{2,0},{3,1},{4,6},{5,7},{6,4},{7,5},{8,10},{9,11},{10,... | collective-permute-start | bytes 49160 | tf_op jit(solution)/shard_map/ppermute | solution.py:287
  38.7 3.7 %collective-permute-start.8 = (f32[2,2,1024]{2,1,0:T(2,128)S(1)}, f32[2,2,1024]{2,1,0:T(2,128)S(1)}, u32[]{:S(2)}, u32[]{:S(2)}) collective-permute-start(f32[2,2,1024]{2,1,0:T(2,128)S(1)} %pad_maximum_fusion), channel_id=1, source_target_pairs={{0,1},{1,0},{2,3},{3,2},{4,5},{5,4},{6,7},{7,6},{8,9},{9,8},{10,11... | collective-permute-start | bytes 49160 | tf_op jit(solution)/shard_map/ppermute | solution.py:287
  45.2 6.6 %collective-permute-start.11 = (f32[392,128]{1,0:T(8,128)S(1)}, f32[392,128]{1,0:T(8,128)S(1)}, u32[]{:S(2)}, u32[]{:S(2)}) collective-permute-start(f32[392,128]{1,0:T(8,128)S(1)} %get-tuple-element.41), channel_id=1, source_target_pairs={{0,8},{4,12},{8,0},{12,4},{16,24},{20,28},{24,16},{28,20},{1,9},{5... | collective-permute-start | bytes 602120 | tf_op jit(solution)/shard_map/ppermute | solution.py:287
  46.8 25.9 %copy-start.2 = (f32[64,768]{1,0:T(8,128)S(1)}, f32[64,768]{1,0:T(8,128)}, u32[]{:S(2)}) copy-start(f32[64,768]{1,0:T(8,128)} %means_ref.3) | copy-start | bytes 589828
  46.8 25.9 %copy-start.6 = (f32[64]{0:T(128)S(1)}, f32[64]{0:T(128)}, u32[]{:S(2)}) copy-start(f32[64]{0:T(128)} %param.7) | copy-start | bytes 772
  49.4 8.0 %collective-permute-start.13 = (f32[384,128]{1,0:T(8,128)S(1)}, f32[384,128]{1,0:T(8,128)S(1)}, u32[]{:S(2)}, u32[]{:S(2)}) collective-permute-start(f32[384,128]{1,0:T(8,128)S(1)} %get-tuple-element.45), channel_id=1, source_target_pairs={{0,8},{4,12},{8,0},{12,4},{16,24},{20,28},{24,16},{28,20},{1,9},{5... | collective-permute-start | bytes 589832 | tf_op jit(solution)/shard_map/ppermute | solution.py:287
  51.8 17.9 %collective-permute-start.12 = (f32[392,128]{1,0:T(8,128)S(1)}, f32[392,128]{1,0:T(8,128)S(1)}, u32[]{:S(2)}, u32[]{:S(2)}) collective-permute-start(f32[392,128]{1,0:T(8,128)S(1)} %add.33), channel_id=1, source_target_pairs={{0,16},{4,20},{8,24},{12,28},{16,0},{20,4},{24,8},{28,12},{1,17},{... | collective-permute-start | bytes 602120 | tf_op jit(solution)/shard_map/ppermute | solution.py:287
  57.4 15.2 %collective-permute-start.15 = (f32[392,128]{1,0:T(8,128)S(1)}, f32[392,128]{1,0:T(8,128)S(1)}, u32[]{:S(2)}, u32[]{:S(2)}) collective-permute-start(f32[392,128]{1,0:T(8,128)S(1)} %get-tuple-element.49), channel_id=1, source_target_pairs={{0,8},{4,12},{8,0},{12,4},{16,24},{20,28},{24,16},{28,20},{1,9},{5... | collective-permute-start | bytes 602120 | tf_op jit(solution)/shard_map/ppermute | solution.py:287
  58.8 10.9 %collective-permute-start.14 = (f32[384,128]{1,0:T(8,128)S(1)}, f32[384,128]{1,0:T(8,128)S(1)}, u32[]{:S(2)}, u32[]{:S(2)}) collective-permute-start(f32[384,128]{1,0:T(8,128)S(1)} %add.35), channel_id=1, source_target_pairs={{0,16},{4,20},{8,24},{12,28},{16,0},{20,4},{24,8},{28,12},{1,17},{... | collective-permute-start | bytes 589832 | tf_op jit(solution)/shard_map/ppermute | solution.py:287
  61.0 11.6 %collective-permute-start.16 = (f32[384,128]{1,0:T(8,128)S(1)}, f32[384,128]{1,0:T(8,128)S(1)}, u32[]{:S(2)}, u32[]{:S(2)}) collective-permute-start(f32[384,128]{1,0:T(8,128)S(1)} %get-tuple-element.51), channel_id=1, source_target_pairs={{0,8},{4,12},{8,0},{12,4},{16,24},{20,28},{24,16},{28,20},{1,9},{5... | collective-permute-start | bytes 589832 | tf_op jit(solution)/shard_map/ppermute | solution.py:287

commit v2 on v1

--- a/solution.py
+++ b/solution.py
@@ -37,7 +37,16 @@
     return jnp.sum(jnp.where(diagonal(rows, row.shape[1]), row, 0.0), axis=1, keepdims=True)
 
 
-def coefficient_kernel(means_ref, variances_ref, mass_ref, pack_ref):
+def coefficient_kernel(
+    means_hbm, variances_hbm, mass_hbm, pack_ref, means_ref, variances_ref, mass_ref, sems
+):
+    sources = (variances_hbm, means_hbm, mass_hbm)
+    targets = (variances_ref, means_ref, mass_ref)
+    copies = [pltpu.make_async_copy(s, t, sems.at[i]) for i, (s, t) in enumerate(zip(sources, targets))]
+    for copy in copies:
+        copy.start()
+    for copy in copies:
+        copy.wait()
     n, width = means_ref.shape
     means, variances = means_ref[...], variances_ref[...]
     mean_prec = means * (1.0 / variances)
@@ -50,13 +59,21 @@
 
 def coefficients(means, variances, mass):
     n, width = means.shape
+    operands = (means, variances, mass.reshape(1, n))
     return pl.pallas_call(
         coefficient_kernel,
+        in_specs=[pl.BlockSpec(memory_space=pl.ANY)] * 3,
         out_shape=jax.ShapeDtypeStruct((width // LANES * n + 8, LANES), F32),
+        scratch_shapes=[
+            pltpu.VMEM((n, width), F32),
+            pltpu.VMEM((n, width), F32),
+            pltpu.VMEM((1, n), F32),
+            pltpu.SemaphoreType.DMA((3,)),
+        ],
         cost_estimate=HEAVY,
         compiler_params=params(16),
         name="coefficients",
-    )(means, variances, mass.reshape(1, n))
+    )(*(pltpu.with_memory_space_constraint(x, pltpu.HBM) for x in operands))
 
 
 def halves_kernel(own_ref, other_ref, xh_ref, xl_ref, sh_ref, sl_ref):

time: 73.8 us -> 73.6 us (level)
  local copies, waits for them, and re-layouts: 3.67 us -> 0.15 us
  waiting for transfers between devices: 29.6 us -> 32.5 us
  Pallas kernels: 17.7 us -> 19 us
  starting transfers between devices: 21.6 us -> 20.8 us
    unnamed x14 -> x8, local copies, waits for them, and re-layouts: 3.66 us -> 0.14 us
    ppermute x17, waiting for transfers between devices: 29.6 us -> 32.5 us  [swap(): return lax.ppermute(value, axis, [(i, i ^ bit) for i in range(size)])]
    pallas_call x1, Pallas kernels: 0.14 us -> 1.35 us  [coefficients(): pl.pallas_call(coefficient_kernel, in_specs=[pl.BlockSpec(memory_space=pl...]
    ppermute x17, starting transfers between devices: 21.6 us -> 20.8 us  [swap(): return lax.ppermute(value, axis, [(i, i ^ bit) for i in range(size)])]
  transfers between devices with their start and end apart: 17 -> 17, of which waited for: 13 -> 14; matrix products, arithmetic and copies ran while one was open for 0% -> 0% of each run, Pallas kernels for 16% -> 18%
where the time goes in v2:
time: 73.6 us; the launch traced here: 73.5 us
  waiting for transfers between devices  32.5 us (44%)
  starting transfers between devices  20.8 us (28%)
  Pallas kernels  19 us (26%)
  between operations  0.75 us (1%)
    ppermute x17, waiting for transfers between devices, swap(): return lax.ppermute(value, axis, [(i, i ^ bit) for i in range(size)])  32.5 us
    ppermute x17, starting transfers between devices, swap(): return lax.ppermute(value, axis, [(i, i ^ bit) for i in range(size)])  20.8 us
    pallas_call x4, Pallas kernels, score_call(): pl.pallas_call(body, out_shape=[jax.ShapeDtypeStruct(shape, F32) for shap...  9.14 us
    pallas_call x1, Pallas kernels, first_moments(): pl.pallas_call(functools.partial(first_kernel, n), out_shape=[pack] * (co...  2.7 us
    pallas_call x1, Pallas kernels, second_moments(): pl.pallas_call(functools.partial(second_kernel, n), out_shape=[pack] * (r...  2.6 us
    pallas_call x1, Pallas kernels, halves(): pl.pallas_call(halves_kernel, grid=(2 * steps,), in_specs=[pl.BlockSpec((...  2.25 us
  transfers between devices with their start and end apart: 17, of which 14 were waited for; matrix products, arithmetic and copies ran while one was open for 0% of the time, Pallas kernels for 18%

profile of v2, /device:TPU:0, one launch (start us, length us, event | category | flops | bytes accessed | tf_op | source)
XLA Modules:
  0.0 73.5 jit_solution(12642133953558176540)
XLA Ops:
  1.1 3.7 %collective-permute-start.4 = (f32[64,768]{1,0:T(8,128)}, f32[64,768]{1,0:T(8,128)S(1)}, u32[]{:S(2)}, u32[]{:S(2)}) collective-permute-start(f32[64,768]{1,0:T(8,128)} %variances_ref.1), channel_id=1, source_target_pairs={{0,16},{4,20},{8,24},{12,28},{16,0},{20,4},{24,8},{28,12},{1,17},{... | collective-permute-start | bytes 589832 | tf_op jit(solution)/shard_map/ppermute | solution.py:304
  4.8 1.6 %collective-permute-start.3 = (f32[64,768]{1,0:T(8,128)}, f32[64,768]{1,0:T(8,128)S(1)}, u32[]{:S(2)}, u32[]{:S(2)}) collective-permute-start(f32[64,768]{1,0:T(8,128)} %variances_ref.1), channel_id=1, source_target_pairs={{0,8},{4,12},{8,0},{12,4},{16,24},{20,28},{24,16},{28,20},{1,9},{5... | collective-permute-start | bytes 589832 | tf_op jit(solution)/shard_map/ppermute | solution.py:304
  6.4 1.3 %coefficients.1.refs_0_ = f32[392,128]{1,0:T(8,128)S(1)} custom-call(f32[64,768]{1,0:T(8,128)} %means_ref.1, f32[64,768]{1,0:T(8,128)} %variances_ref.1, f32[1,64]{1,0:T(1,128)} %bitcast.2), custom_call_target="tpu_custom_call" | custom-call | flops 10000000000 | bytes 100000000 | tf_op jit(solution)/shard_map/coefficients/pallas_call | solution.py:63
  8.5 2.2 %halves.1 = (bf16[2048,768]{1,0:T(8,128)(2,1)S(1)}, bf16[2048,768]{1,0:T(8,128)(2,1)S(1)}, bf16[2048,768]{1,0:T(8,128)(2,1)S(1)}, bf16[2048,768]{1,0:T(8,128)(2,1)S(1)}) custom-call(f32[1024,768]{1,0:T(8,128)S(1)} %copy-done, f32[1024,768]{1,0:T(8,128)S(1)} %collective-permute-done.2.other_ref), custom_call_target="tpu_custom_call" | custom-call | flops 10000000000 | bytes 100000000 | tf_op jit(solution)/shard_map/halves/pallas_call | solution.py:100
  10.7 4.4 %collective-permute-done.4.refs_2_ = f32[64,768]{1,0:T(8,128)S(1)} collective-permute-done((f32[64,768]{1,0:T(8,128)}, f32[64,768]{1,0:T(8,128)S(1)}, u32[]{:S(2)}, u32[]{:S(2)}) %collective-permute-start.4) | collective-permute-done | bytes 196640 | tf_op jit(solution)/shard_map/ppermute | solution.py:304
  17.0 2.4 %early_quad.1.refs_5_ = f32[192,2048]{1,0:T(8,128)S(1)} custom-call(f32[64,768]{1,0:T(8,128)S(1)} %copy-done.2, f32[64,768]{1,0:T(8,128)S(1)} %collective-permute-done.3.refs_1_, f32[64,768]{1,0:T(8,128)S(1)} %collective-permute-done.4.refs_2_, bf16[2048,768]{1,0:T(8,128)(2,1)S(1)} %get-tuple-element.31.refs_3_.refs_1_.high_ref, ...), custom_call_target="tpu_custom_call" | custom-call | flops 10000000000 | bytes 100000000 | tf_op jit(solution)/shard_map/early_quad/pallas_call | solution.py:193
  19.4 4.1 %collective-permute-done.1.refs_2_ = f32[392,128]{1,0:T(8,128)S(1)} collective-permute-done((f32[392,128]{1,0:T(8,128)S(1)}, f32[392,128]{1,0:T(8,128)S(1)}, u32[]{:S(2)}, u32[]{:S(2)}) %collective-permute-start.1) | collective-permute-done | bytes 200736 | tf_op jit(solution)/shard_map/ppermute | solution.py:304
  24.4 2.5 %early_scores.1 = (f32[192,2048]{1,0:T(8,128)S(1)}, f32[2,2048]{1,0:T(2,128)S(1)}) custom-call(f32[392,128]{1,0:T(8,128)S(1)} %coefficients.1.refs_0_, f32[392,128]{1,0:T(8,128)S(1)} %collective-permute-done.refs_1_, f32[392,128]{1,0:T(8,128)S(1)} %collective-permute-done.1.refs_2_, bf16[2048,768]{1,0:T(8,128)(2,1)S(1)} %get-tuple-element.29.refs_3_.refs_1_.high_ref, ...), custom_call_target="tpu_custom_call" | custom-call | flops 10000000000 | bytes 100000000 | tf_op jit(solution)/shard_map/early_scores/pallas_call | solution.py:193
  26.9 1.7 %collective-permute-done.6.refs_0_ = f32[64,768]{1,0:T(8,128)S(1)} collective-permute-done((f32[64,768]{1,0:T(8,128)S(1)}, f32[64,768]{1,0:T(8,128)S(1)}, u32[]{:S(2)}, u32[]{:S(2)}) %collective-permute-start.6) | collective-permute-done | bytes 196640 | tf_op jit(solution)/shard_map/ppermute | solution.py:304
  28.6 2.1 %late_quad.1.refs_3_ = f32[64,2048]{1,0:T(8,128)S(1)} custom-call(f32[64,768]{1,0:T(8,128)S(1)} %collective-permute-done.6.refs_0_, bf16[2048,768]{1,0:T(8,128)(2,1)S(1)} %get-tuple-element.31.refs_3_.refs_1_.high_ref, bf16[2048,768]{1,0:T(8,128)(2,1)S(1)} %get-tuple-element.32.refs_4_.refs_2_.low_ref), custom_call_target="tpu_custom_call" | custom-call | flops 10000000000 | bytes 100000000 | tf_op jit(solution)/shard_map/late_quad/pallas_call | solution.py:193
  30.7 1.5 %collective-permute-done.5.refs_0_ = f32[392,128]{1,0:T(8,128)S(1)} collective-permute-done((f32[392,128]{1,0:T(8,128)S(1)}, f32[392,128]{1,0:T(8,128)S(1)}, u32[]{:S(2)}, u32[]{:S(2)}) %collective-permute-start.5) | collective-permute-done | bytes 200736 | tf_op jit(solution)/shard_map/ppermute | solution.py:304
  32.1 2.1 %last_scores.1 = (f32[64,2048]{1,0:T(8,128)S(1)}, f32[2,2,1024]{2,1,0:T(2,128)S(1)}) custom-call(f32[392,128]{1,0:T(8,128)S(1)} %collective-permute-done.5.refs_0_, bf16[2048,768]{1,0:T(8,128)(2,1)S(1)} %get-tuple-element.29.refs_3_.refs_1_.high_ref, bf16[2048,768]{1,0:T(8,128)(2,1)S(1)} %get-tuple-element.30.refs_4_.refs_2_.low_ref, ...), custom_call_target="tpu_custom_call" | custom-call | flops 10000000000 | bytes 100000000 | tf_op jit(solution)/shard_map/last_scores/pallas_call | solution.py:193
  34.4 1.2 %collective-permute-done.7 = f32[2,2,1024]{2,1,0:T(2,128)S(1)} collective-permute-done((f32[2,2,1024]{2,1,0:T(2,128)S(1)}, f32[2,2,1024]{2,1,0:T(2,128)S(1)}, u32[]{:S(2)}, u32[]{:S(2)}) %collective-permute-start.7) | collective-permute-done | bytes 16416 | tf_op jit(solution)/shard_map/ppermute | solution.py:304
  35.6 2.6 %collective-permute-start.10 = (f32[2,2,1024]{2,1,0:T(2,128)S(1)}, f32[2,2,1024]{2,1,0:T(2,128)S(1)}, u32[]{:S(2)}, u32[]{:S(2)}) collective-permute-start(f32[2,2,1024]{2,1,0:T(2,128)S(1)} %pad_maximum_fusion), channel_id=1, source_target_pairs={{0,3},{1,2},{2,1},{3,0},{4,7},{5,6},{6,5},{7,4},{8,11},{9,10},{10,... | collective-permute-start | bytes 49160 | tf_op jit(solution)/shard_map/ppermute | solution.py:304
  40.3 1.6 %collective-permute-done.9 = f32[2,2,1024]{2,1,0:T(2,128)S(1)} collective-permute-done((f32[2,2,1024]{2,1,0:T(2,128)S(1)}, f32[2,2,1024]{2,1,0:T(2,128)S(1)}, u32[]{:S(2)}, u32[]{:S(2)}) %collective-permute-start.9) | collective-permute-done | bytes 16416 | tf_op jit(solution)/shard_map/ppermute | solution.py:304
  42.5 2.7 %first_moments.1 = (f32[392,128]{1,0:T(8,128)S(1)}, f32[392,128]{1,0:T(8,128)S(1)}, f32[392,128]{1,0:T(8,128)S(1)}, f32[392,128]{1,0:T(8,128)S(1)}, bf16[512,2048]{1,0:T(8,128)(2,1)S(1)}) custom-call(f32[192,2048]{1,0:T(8,128)S(1)} %get-tuple-element.33.early_ref, f32[64,2048]{1,0:T(8,128)S(1)} %get-tuple-element.37.late_ref, ...), custom_call_target="tpu_custom_call" | custom-call | flops 10000000000 | bytes 100000000 | tf_op jit(solution)/shard_map/first_moments/pallas_call | solution.py:234
  45.2 1.5 %collective-permute-start.11 = (f32[392,128]{1,0:T(8,128)S(1)}, f32[392,128]{1,0:T(8,128)S(1)}, u32[]{:S(2)}, u32[]{:S(2)}) collective-permute-start(f32[392,128]{1,0:T(8,128)S(1)} %get-tuple-element.41), channel_id=1, source_target_pairs={{0,8},{4,12},{8,0},{12,4},{16,24},{20,28},{24,16},{28,20},{1,9},{5... | collective-permute-start | bytes 602120 | tf_op jit(solution)/shard_map/ppermute | solution.py:304
  46.8 2.6 %second_moments.1 = (f32[384,128]{1,0:T(8,128)S(1)}, f32[384,128]{1,0:T(8,128)S(1)}, f32[384,128]{1,0:T(8,128)S(1)}, f32[384,128]{1,0:T(8,128)S(1)}) custom-call(bf16[512,2048]{1,0:T(8,128)(2,1)S(1)} %get-tuple-element.42.resp_ref, bf16[2048,768]{1,0:T(8,128)(2,1)S(1)} %get-tuple-element.31.refs_3_.refs_1_.high_ref, ...), custom_call_target="tpu_custom_call" | custom-call | flops 10000000000 | bytes 100000000 | tf_op jit(solution)/shard_map/second_moments/pallas_call | solution.py:249
  50.0 1.8 %collective-permute-done.11 = f32[392,128]{1,0:T(8,128)S(1)} collective-permute-done((f32[392,128]{1,0:T(8,128)S(1)}, f32[392,128]{1,0:T(8,128)S(1)}, u32[]{:S(2)}, u32[]{:S(2)}) %collective-permute-start.11) | collective-permute-done | bytes 200736 | tf_op jit(solution)/shard_map/ppermute | solution.py:304
  51.8 3.9 %collective-permute-start.12 = (f32[392,128]{1,0:T(8,128)S(1)}, f32[392,128]{1,0:T(8,128)S(1)}, u32[]{:S(2)}, u32[]{:S(2)}) collective-permute-start(f32[392,128]{1,0:T(8,128)S(1)} %add.33), channel_id=1, source_target_pairs={{0,16},{4,20},{8,24},{12,28},{16,0},{20,4},{24,8},{28,12},{1,17},{... | collective-permute-start | bytes 602120 | tf_op jit(solution)/shard_map/ppermute | solution.py:304
  55.7 1.8 %collective-permute-done.13 = f32[384,128]{1,0:T(8,128)S(1)} collective-permute-done((f32[384,128]{1,0:T(8,128)S(1)}, f32[384,128]{1,0:T(8,128)S(1)}, u32[]{:S(2)}, u32[]{:S(2)}) %collective-permute-start.13) | collective-permute-done | bytes 196640 | tf_op jit(solution)/shard_map/ppermute | solution.py:304
  58.6 1.9 %collective-permute-start.14 = (f32[384,128]{1,0:T(8,128)S(1)}, f32[384,128]{1,0:T(8,128)S(1)}, u32[]{:S(2)}, u32[]{:S(2)}) collective-permute-start(f32[384,128]{1,0:T(8,128)S(1)} %add.35), channel_id=1, source_target_pairs={{0,16},{4,20},{8,24},{12,28},{16,0},{20,4},{24,8},{28,12},{1,17},{... | collective-permute-start | bytes 589832 | tf_op jit(solution)/shard_map/ppermute | solution.py:304
  60.9 8.6 %collective-permute-done.14 = f32[384,128]{1,0:T(8,128)S(1)} collective-permute-done((f32[384,128]{1,0:T(8,128)S(1)}, f32[384,128]{1,0:T(8,128)S(1)}, u32[]{:S(2)}, u32[]{:S(2)}) %collective-permute-start.14) | collective-permute-done | bytes 196640 | tf_op jit(solution)/shard_map/ppermute | solution.py:304
  69.5 3.0 %collective-permute-done.16.near_second_ref = f32[384,128]{1,0:T(8,128)S(1)} collective-permute-done((f32[384,128]{1,0:T(8,128)S(1)}, f32[384,128]{1,0:T(8,128)S(1)}, u32[]{:S(2)}, u32[]{:S(2)}) %collective-permute-start.16) | collective-permute-done | bytes 196640 | tf_op jit(solution)/shard_map/ppermute | solution.py:304
  (36 shorter events, 10.0 us)
Async XLA Ops:
  0.6 7.7 %collective-permute-start.2 = (f32[1024,768]{1,0:T(8,128)}, f32[1024,768]{1,0:T(8,128)S(1)}, u32[]{:S(2)}, u32[]{:S(2)}) collective-permute-start(f32[1024,768]{1,0:T(8,128)} %own_ref.1), channel_id=1, source_target_pairs={{0,4},{4,0},{8,12},{12,8},{16,20},{20,16},{24,28},{28,24},{1,5},{5... | collective-permute-start | bytes 9437192 | tf_op jit(solution)/shard_map/ppermute | solution.py:304
  1.1 13.9 %collective-permute-start.4 = (f32[64,768]{1,0:T(8,128)}, f32[64,768]{1,0:T(8,128)S(1)}, u32[]{:S(2)}, u32[]{:S(2)}) collective-permute-start(f32[64,768]{1,0:T(8,128)} %variances_ref.1), channel_id=1, source_target_pairs={{0,16},{4,20},{8,24},{12,28},{16,0},{20,4},{24,8},{28,12},{1,17},{... | collective-permute-start | bytes 589832 | tf_op jit(solution)/shard_map/ppermute | solution.py:304
  4.8 12.2 %collective-permute-start.3 = (f32[64,768]{1,0:T(8,128)}, f32[64,768]{1,0:T(8,128)S(1)}, u32[]{:S(2)}, u32[]{:S(2)}) collective-permute-start(f32[64,768]{1,0:T(8,128)} %variances_ref.1), channel_id=1, source_target_pairs={{0,8},{4,12},{8,0},{12,4},{16,24},{20,28},{24,16},{28,20},{1,9},{5... | collective-permute-start | bytes 589832 | tf_op jit(solution)/shard_map/ppermute | solution.py:304
  6.4 2.1 %copy-start = (f32[1024,768]{1,0:T(8,128)S(1)}, f32[1024,768]{1,0:T(8,128)}, u32[]{:S(2)}) copy-start(f32[1024,768]{1,0:T(8,128)} %own_ref.1) | copy-start | bytes 9437188
  7.7 9.2 %copy-start.2 = (f32[64,768]{1,0:T(8,128)S(1)}, f32[64,768]{1,0:T(8,128)}, u32[]{:S(2)}) copy-start(f32[64,768]{1,0:T(8,128)} %variances_ref.1) | copy-start | bytes 589828
  7.8 15.7 %collective-permute-start.1 = (f32[392,128]{1,0:T(8,128)S(1)}, f32[392,128]{1,0:T(8,128)S(1)}, u32[]{:S(2)}, u32[]{:S(2)}) collective-permute-start(f32[392,128]{1,0:T(8,128)S(1)} %coefficients.1.refs_0_), channel_id=1, source_target_pairs={{0,16},{4,20},{8,24},{12,28},{16,0},{20,4},{24,8},{28,12},{1,17},{... | collective-permute-start | bytes 602120 | tf_op jit(solution)/shard_map/ppermute | solution.py:304
  8.2 16.2 %collective-permute-start = (f32[392,128]{1,0:T(8,128)S(1)}, f32[392,128]{1,0:T(8,128)S(1)}, u32[]{:S(2)}, u32[]{:S(2)}) collective-permute-start(f32[392,128]{1,0:T(8,128)S(1)} %coefficients.1.refs_0_), channel_id=1, source_target_pairs={{0,8},{4,12},{8,0},{12,4},{16,24},{20,28},{24,16},{28,20},{1,9},{5... | collective-permute-start | bytes 602120 | tf_op jit(solution)/shard_map/ppermute | solution.py:304
  15.1 13.5 %collective-permute-start.6 = (f32[64,768]{1,0:T(8,128)S(1)}, f32[64,768]{1,0:T(8,128)S(1)}, u32[]{:S(2)}, u32[]{:S(2)}) collective-permute-start(f32[64,768]{1,0:T(8,128)S(1)} %collective-permute-done.4.refs_2_), channel_id=1, source_target_pairs={{0,8},{4,12},{8,0},{12,4},{16,24},{20,28},{24,16},{28,20},{1,9},{5... | collective-permute-start | bytes 589832 | tf_op jit(solution)/shard_map/ppermute | solution.py:304
  23.5 8.7 %collective-permute-start.5 = (f32[392,128]{1,0:T(8,128)S(1)}, f32[392,128]{1,0:T(8,128)S(1)}, u32[]{:S(2)}, u32[]{:S(2)}) collective-permute-start(f32[392,128]{1,0:T(8,128)S(1)} %collective-permute-done.1.refs_2_), channel_id=1, source_target_pairs={{0,8},{4,12},{8,0},{12,4},{16,24},{20,28},{24,16},{28,20},{1,9},{5... | collective-permute-start | bytes 602120 | tf_op jit(solution)/shard_map/ppermute | solution.py:304
  34.3 1.2 %collective-permute-start.7 = (f32[2,2,1024]{2,1,0:T(2,128)S(1)}, f32[2,2,1024]{2,1,0:T(2,128)S(1)}, u32[]{:S(2)}, u32[]{:S(2)}) collective-permute-start(f32[2,2,1024]{2,1,0:T(2,128)S(1)} %get-tuple-element.38), channel_id=1, source_target_pairs={{0,4},{4,0},{8,12},{12,8},{16,20},{20,16},{24,28},{28,24},{1,5},{5... | collective-permute-start | bytes 49160 | tf_op jit(solution)/shard_map/ppermute | solution.py:304
  35.6 4.7 %collective-permute-start.10 = (f32[2,2,1024]{2,1,0:T(2,128)S(1)}, f32[2,2,1024]{2,1,0:T(2,128)S(1)}, u32[]{:S(2)}, u32[]{:S(2)}) collective-permute-start(f32[2,2,1024]{2,1,0:T(2,128)S(1)} %pad_maximum_fusion), channel_id=1, source_target_pairs={{0,3},{1,2},{2,1},{3,0},{4,7},{5,6},{6,5},{7,4},{8,11},{9,10},{10,... | collective-permute-start | bytes 49160 | tf_op jit(solution)/shard_map/ppermute | solution.py:304
  38.2 3.7 %collective-permute-start.9 = (f32[2,2,1024]{2,1,0:T(2,128)S(1)}, f32[2,2,1024]{2,1,0:T(2,128)S(1)}, u32[]{:S(2)}, u32[]{:S(2)}) collective-permute-start(f32[2,2,1024]{2,1,0:T(2,128)S(1)} %pad_maximum_fusion), channel_id=1, source_target_pairs={{0,2},{1,3},{2,0},{3,1},{4,6},{5,7},{6,4},{7,5},{8,10},{9,11},{10,... | collective-permute-start | bytes 49160 | tf_op jit(solution)/shard_map/ppermute | solution.py:304
  38.7 3.7 %collective-permute-start.8 = (f32[2,2,1024]{2,1,0:T(2,128)S(1)}, f32[2,2,1024]{2,1,0:T(2,128)S(1)}, u32[]{:S(2)}, u32[]{:S(2)}) collective-permute-start(f32[2,2,1024]{2,1,0:T(2,128)S(1)} %pad_maximum_fusion), channel_id=1, source_target_pairs={{0,1},{1,0},{2,3},{3,2},{4,5},{5,4},{6,7},{7,6},{8,9},{9,8},{10,11... | collective-permute-start | bytes 49160 | tf_op jit(solution)/shard_map/ppermute | solution.py:304
  45.2 6.6 %collective-permute-start.11 = (f32[392,128]{1,0:T(8,128)S(1)}, f32[392,128]{1,0:T(8,128)S(1)}, u32[]{:S(2)}, u32[]{:S(2)}) collective-permute-start(f32[392,128]{1,0:T(8,128)S(1)} %get-tuple-element.41), channel_id=1, source_target_pairs={{0,8},{4,12},{8,0},{12,4},{16,24},{20,28},{24,16},{28,20},{1,9},{5... | collective-permute-start | bytes 602120 | tf_op jit(solution)/shard_map/ppermute | solution.py:304
  46.8 25.8 %copy-start.1 = (f32[64,768]{1,0:T(8,128)S(1)}, f32[64,768]{1,0:T(8,128)}, u32[]{:S(2)}) copy-start(f32[64,768]{1,0:T(8,128)} %means_ref.1) | copy-start | bytes 589828
  46.8 25.8 %copy-start.3 = (f32[64]{0:T(128)S(1)}, f32[64]{0:T(128)}, u32[]{:S(2)}) copy-start(f32[64]{0:T(128)} %param.7) | copy-start | bytes 772
  49.4 8.1 %collective-permute-start.13 = (f32[384,128]{1,0:T(8,128)S(1)}, f32[384,128]{1,0:T(8,128)S(1)}, u32[]{:S(2)}, u32[]{:S(2)}) collective-permute-start(f32[384,128]{1,0:T(8,128)S(1)} %get-tuple-element.45), channel_id=1, source_target_pairs={{0,8},{4,12},{8,0},{12,4},{16,24},{20,28},{24,16},{28,20},{1,9},{5... | collective-permute-start | bytes 589832 | tf_op jit(solution)/shard_map/ppermute | solution.py:304
  51.8 17.6 %collective-permute-start.12 = (f32[392,128]{1,0:T(8,128)S(1)}, f32[392,128]{1,0:T(8,128)S(1)}, u32[]{:S(2)}, u32[]{:S(2)}) collective-permute-start(f32[392,128]{1,0:T(8,128)S(1)} %add.33), channel_id=1, source_target_pairs={{0,16},{4,20},{8,24},{12,28},{16,0},{20,4},{24,8},{28,12},{1,17},{... | collective-permute-start | bytes 602120 | tf_op jit(solution)/shard_map/ppermute | solution.py:304
  57.6 15.0 %collective-permute-start.15 = (f32[392,128]{1,0:T(8,128)S(1)}, f32[392,128]{1,0:T(8,128)S(1)}, u32[]{:S(2)}, u32[]{:S(2)}) collective-permute-start(f32[392,128]{1,0:T(8,128)S(1)} %get-tuple-element.49), channel_id=1, source_target_pairs={{0,8},{4,12},{8,0},{12,4},{16,24},{20,28},{24,16},{28,20},{1,9},{5... | collective-permute-start | bytes 602120 | tf_op jit(solution)/shard_map/ppermute | solution.py:304
  58.6 10.9 %collective-permute-start.14 = (f32[384,128]{1,0:T(8,128)S(1)}, f32[384,128]{1,0:T(8,128)S(1)}, u32[]{:S(2)}, u32[]{:S(2)}) collective-permute-start(f32[384,128]{1,0:T(8,128)S(1)} %add.35), channel_id=1, source_target_pairs={{0,16},{4,20},{8,24},{12,28},{16,0},{20,4},{24,8},{28,12},{1,17},{... | collective-permute-start | bytes 589832 | tf_op jit(solution)/shard_map/ppermute | solution.py:304
  60.5 12.0 %collective-permute-start.16 = (f32[384,128]{1,0:T(8,128)S(1)}, f32[384,128]{1,0:T(8,128)S(1)}, u32[]{:S(2)}, u32[]{:S(2)}) collective-permute-start(f32[384,128]{1,0:T(8,128)S(1)} %get-tuple-element.51), channel_id=1, source_target_pairs={{0,8},{4,12},{8,0},{12,4},{16,24},{20,28},{24,16},{28,20},{1,9},{5... | collective-permute-start | bytes 589832 | tf_op jit(solution)/shard_map/ppermute | solution.py:304

commit v3 on v2

--- a/solution.py
+++ b/solution.py
@@ -11,6 +11,7 @@
 BF16 = jnp.bfloat16
 LANES = 128
 HEAVY = pl.CostEstimate(flops=10**10, bytes_accessed=10**8, transcendentals=0)
+LIGHT = pl.CostEstimate(flops=10**8, bytes_accessed=10**6, transcendentals=0)
 ACROSS = (((1,), (1,)), ((), ()))
 WITHIN = (((1,), (0,)), ((), ()))
 
@@ -120,6 +121,8 @@
             high, low = split(pack[c * n : (c + 1) * n, :])
             weights[q * n : (q + 1) * n, lanes] = high
             weights[comps + q * n : comps + (q + 1) * n, lanes] = low
+    if packs[0].shape[0] == tiles * n:
+        return None
     return jnp.concatenate([to_column(pack[tiles * n : tiles * n + 1, :], n) for pack in packs])
 
 
@@ -176,11 +179,21 @@
             yield slice(block * half + part.start, block * half + part.stop), block, part
 
 
+def head_kernel(n, *refs):
+    *linear, high_ref, low_ref, quad_ref, out_ref, weights = refs
+    load_packs(linear, weights, n)
+    columns = slice(0, weights.shape[1])
+    for tile in row_tiles(high_ref.shape[0]):
+        scores = product(weights[...], high_ref[tile, columns], low_ref[tile, columns], ACROSS)
+        out_ref[:, tile] = quad_ref[:, tile] + scores
+
+
 def last_kernel(n, *refs):
-    *linear, xh_ref, xl_ref, quad_ref, early_ref, out_ref, stats_ref, weights = refs
+    *linear, high_ref, low_ref, quad_ref, early_ref, out_ref, stats_ref, weights = refs
     offset = load_packs(linear, weights, n)
+    columns = slice(high_ref.shape[1] - weights.shape[1], high_ref.shape[1])
     for tile, block, part in half_tiles(stats_ref.shape[2]):
-        scores = product(weights[...], xh_ref[tile, :], xl_ref[tile, :], ACROSS)
+        scores = product(weights[...], high_ref[tile, columns], low_ref[tile, columns], ACROSS)
         scores = quad_ref[:, tile] + scores + offset
         out_ref[:, tile] = scores
         early = early_ref[0:1, tile], early_ref[1:2, tile]
@@ -189,12 +202,12 @@
         stats_ref[block, 1:2, part] = total
 
 
-def score_call(body, out_shape, scratch, name, *operands):
+def score_call(body, out_shape, scratch, name, *operands, cost=None):
     return pl.pallas_call(
         body,
         out_shape=[jax.ShapeDtypeStruct(shape, F32) for shape in out_shape],
         scratch_shapes=[pltpu.VMEM(shape, BF16) for shape in scratch],
-        cost_estimate=HEAVY,
+        cost_estimate=cost or HEAVY,
         compiler_params=params(24),
         name=name,
     )(*operands)
@@ -359,15 +372,19 @@
         variances[q] = swap(after(variances[q ^ 1], x_high), "dp", 2)
     n_early, n_late = n * len(order), n * len(late)
 
-    def quad_scores(group, name):
+    def quad_scores(group, name, cost=None):
         comps = n * len(group)
         operands = (*(vmem(variances[q]) for q in group), s_high, s_low)
         body = functools.partial(quad_kernel, n)
-        return score_call(body, [(comps, 2 * rows)], [(2 * comps, width)], name, *operands)[0]
+        return score_call(body, [(comps, 2 * rows)], [(2 * comps, width)], name, *operands, cost=cost)[0]
 
     quad = quad_scores(order, "early_quad")
+    head = width // LANES * 2 // 3
+    heads, tails = [], []
     for q in late:
-        linear[q] = swap(after(linear[q ^ 1], quad), "dp", 2)
+        source = after(linear[q ^ 1], quad)
+        heads.append(vmem(swap(source[: head * n], "dp", 2)))
+        tails.append(source[head * n :])
     early, early_stats = score_call(
         functools.partial(early_kernel, n),
         [(n_early, 2 * rows), (2, 2 * rows)],
@@ -377,16 +394,29 @@
         x_high,
         x_low,
         quad,
+        cost=LIGHT,
+    )
+    tails = [vmem(swap(after(tail, early), "dp", 2)) for tail in tails]
+    (part,) = score_call(
+        functools.partial(head_kernel, n),
+        [(n_late, 2 * rows)],
+        [(2 * n_late, head * LANES)],
+        "late_head",
+        *heads,
+        x_high,
+        x_low,
+        quad_scores(late, "late_quad", LIGHT),
+        cost=LIGHT,
     )
     last, stats = score_call(
         functools.partial(last_kernel, n),
         [(n_late, 2 * rows), (2, 2, rows)],
-        [(2 * n_late, width)],
+        [(2 * n_late, width - head * LANES)],
         "last_scores",
-        *(vmem(linear[q]) for q in late),
+        *tails,
         x_high,
         x_low,
-        quad_scores(late, "late_quad"),
+        part,
         early_stats,
     )
     stats = merge([stats, swap(stats, "dp", 1)[::-1]])

time: 73.6 us -> 74.4 us (1.011)
  waiting for transfers between devices: 32.5 us -> 34.7 us
  starting transfers between devices: 20.8 us -> 19.3 us
    ppermute x17 -> x18, waiting for transfers between devices: 32.5 us -> 34.7 us  [swap(): return lax.ppermute(value, axis, [(i, i ^ bit) for i in range(size)])]
    ppermute x17 -> x18, starting transfers between devices: 20.8 us -> 19.3 us  [swap(): return lax.ppermute(value, axis, [(i, i ^ bit) for i in range(size)])]
    pallas_call x4 -> x5, Pallas kernels: 9.14 us -> 9.25 us  [score_call(): pl.pallas_call(body, out_shape=[jax.ShapeDtypeStruct(shape, F32) for shap...]
  transfers between devices with their start and end apart: 17 -> 18, of which waited for: 14 -> 14; matrix products, arithmetic and copies ran while one was open for 0% -> 0% of each run, Pallas kernels for 18% -> 20%
where the time goes in v3:
time: 74.4 us; the launch traced here: 74.2 us
  waiting for transfers between devices  34.7 us (47%)
  starting transfers between devices  19.3 us (26%)
  Pallas kernels  19 us (26%)
  between operations  0.76 us (1%)
    ppermute x18, waiting for transfers between devices, swap(): return lax.ppermute(value, axis, [(i, i ^ bit) for i in range(size)])  34.7 us
    ppermute x18, starting transfers between devices, swap(): return lax.ppermute(value, axis, [(i, i ^ bit) for i in range(size)])  19.3 us
    pallas_call x5, Pallas kernels, score_call(): pl.pallas_call(body, out_shape=[jax.ShapeDtypeStruct(shape, F32) for shap...  9.25 us
    pallas_call x1, Pallas kernels, first_moments(): pl.pallas_call(functools.partial(first_kernel, n), out_shape=[pack] * (co...  2.67 us
    pallas_call x1, Pallas kernels, second_moments(): pl.pallas_call(functools.partial(second_kernel, n), out_shape=[pack] * (r...  2.59 us
    pallas_call x1, Pallas kernels, halves(): pl.pallas_call(halves_kernel, grid=(2 * steps,), in_specs=[pl.BlockSpec((...  2.25 us
  transfers between devices with their start and end apart: 18, of which 14 were waited for; matrix products, arithmetic and copies ran while one was open for 0% of the time, Pallas kernels for 20%

profile of v3, /device:TPU:0, one launch (start us, length us, event | category | flops | bytes accessed | tf_op | source)
XLA Modules:
  0.0 74.2 jit_solution(9077012802686793160)
XLA Ops:
  1.1 3.7 %collective-permute-start.4 = (f32[64,768]{1,0:T(8,128)}, f32[64,768]{1,0:T(8,128)S(1)}, u32[]{:S(2)}, u32[]{:S(2)}) collective-permute-start(f32[64,768]{1,0:T(8,128)} %variances_ref.1), channel_id=1, source_target_pairs={{0,16},{4,20},{8,24},{12,28},{16,0},{20,4},{24,8},{28,12},{1,17},{... | collective-permute-start | bytes 589832 | tf_op jit(solution)/shard_map/ppermute | solution.py:317
  4.8 1.6 %collective-permute-start.3 = (f32[64,768]{1,0:T(8,128)}, f32[64,768]{1,0:T(8,128)S(1)}, u32[]{:S(2)}, u32[]{:S(2)}) collective-permute-start(f32[64,768]{1,0:T(8,128)} %variances_ref.1), channel_id=1, source_target_pairs={{0,8},{4,12},{8,0},{12,4},{16,24},{20,28},{24,16},{28,20},{1,9},{5... | collective-permute-start | bytes 589832 | tf_op jit(solution)/shard_map/ppermute | solution.py:317
  6.4 1.3 %coefficients.1.refs_0_ = f32[392,128]{1,0:T(8,128)S(1)} custom-call(f32[64,768]{1,0:T(8,128)} %means_ref.1, f32[64,768]{1,0:T(8,128)} %variances_ref.1, f32[1,64]{1,0:T(1,128)} %bitcast.2), custom_call_target="tpu_custom_call" | custom-call | flops 10000000000 | bytes 100000000 | tf_op jit(solution)/shard_map/coefficients/pallas_call | solution.py:64
  8.5 2.2 %halves.1 = (bf16[2048,768]{1,0:T(8,128)(2,1)S(1)}, bf16[2048,768]{1,0:T(8,128)(2,1)S(1)}, bf16[2048,768]{1,0:T(8,128)(2,1)S(1)}, bf16[2048,768]{1,0:T(8,128)(2,1)S(1)}) custom-call(f32[1024,768]{1,0:T(8,128)S(1)} %copy-done, f32[1024,768]{1,0:T(8,128)S(1)} %collective-permute-done.2.other_ref), custom_call_target="tpu_custom_call" | custom-call | flops 10000000000 | bytes 100000000 | tf_op jit(solution)/shard_map/halves/pallas_call | solution.py:101
  10.7 4.4 %collective-permute-done.4.refs_2_ = f32[64,768]{1,0:T(8,128)S(1)} collective-permute-done((f32[64,768]{1,0:T(8,128)}, f32[64,768]{1,0:T(8,128)S(1)}, u32[]{:S(2)}, u32[]{:S(2)}) %collective-permute-start.4) | collective-permute-done | bytes 196640 | tf_op jit(solution)/shard_map/ppermute | solution.py:317
  15.9 1.1 %collective-permute-done.3.refs_1_ = f32[64,768]{1,0:T(8,128)S(1)} collective-permute-done((f32[64,768]{1,0:T(8,128)}, f32[64,768]{1,0:T(8,128)S(1)}, u32[]{:S(2)}, u32[]{:S(2)}) %collective-permute-start.3) | collective-permute-done | bytes 196640 | tf_op jit(solution)/shard_map/ppermute | solution.py:317
  17.0 2.4 %early_quad.1.refs_5_ = f32[192,2048]{1,0:T(8,128)S(1)} custom-call(f32[64,768]{1,0:T(8,128)S(1)} %copy-done.2, f32[64,768]{1,0:T(8,128)S(1)} %collective-permute-done.3.refs_1_, f32[64,768]{1,0:T(8,128)S(1)} %collective-permute-done.4.refs_2_, bf16[2048,768]{1,0:T(8,128)(2,1)S(1)} %get-tuple-element.32.refs_3_.refs_1_.high_ref, ...), custom_call_target="tpu_custom_call" | custom-call | flops 10000000000 | bytes 100000000 | tf_op jit(solution)/shard_map/early_quad/pallas_call | solution.py:206
  19.4 4.1 %collective-permute-done.1.refs_2_ = f32[392,128]{1,0:T(8,128)S(1)} collective-permute-done((f32[392,128]{1,0:T(8,128)S(1)}, f32[392,128]{1,0:T(8,128)S(1)}, u32[]{:S(2)}, u32[]{:S(2)}) %collective-permute-start.1) | collective-permute-done | bytes 200736 | tf_op jit(solution)/shard_map/ppermute | solution.py:317
  24.4 2.5 %early_scores.1 = (f32[192,2048]{1,0:T(8,128)S(1)}, f32[2,2048]{1,0:T(2,128)S(1)}) custom-call(f32[392,128]{1,0:T(8,128)S(1)} %coefficients.1.refs_0_, f32[392,128]{1,0:T(8,128)S(1)} %collective-permute-done.refs_1_, f32[392,128]{1,0:T(8,128)S(1)} %collective-permute-done.1.refs_2_, bf16[2048,768]{1,0:T(8,128)(2,1)S(1)} %get-tuple-element.30.refs_3_.refs_1_.high_ref, ...), custom_call_target="tpu_custom_call" | custom-call | flops 100000000 | bytes 1000000 | tf_op jit(solution)/shard_map/early_scores/pallas_call | solution.py:206
  26.9 1.3 %collective-permute-start.5 = (f32[136,128]{1,0:T(8,128)S(1)}, f32[136,128]{1,0:T(8,128)S(1)}, u32[]{:S(2)}, u32[]{:S(2)}) collective-permute-start(f32[136,128]{1,0:T(8,128)S(1)} %slice.47), channel_id=1, source_target_pairs={{0,8},{4,12},{8,0},{12,4},{16,24},{20,28},{24,16},{28,20},{1,9},{5... | collective-permute-start | bytes 208904 | tf_op jit(solution)/shard_map/ppermute | solution.py:317
  28.6 2.1 %late_quad.1.refs_3_ = f32[64,2048]{1,0:T(8,128)S(1)} custom-call(f32[64,768]{1,0:T(8,128)S(1)} %collective-permute-done.7.refs_0_, bf16[2048,768]{1,0:T(8,128)(2,1)S(1)} %get-tuple-element.32.refs_3_.refs_1_.high_ref, bf16[2048,768]{1,0:T(8,128)(2,1)S(1)} %get-tuple-element.33.refs_4_.refs_2_.low_ref), custom_call_target="tpu_custom_call" | custom-call | flops 100000000 | bytes 1000000 | tf_op jit(solution)/shard_map/late_quad/pallas_call | solution.py:206
  31.4 1.4 %late_head.1.refs_3_ = f32[64,2048]{1,0:T(8,128)S(1)} custom-call(f32[256,128]{1,0:T(8,128)S(1)} %collective-permute-done.6.refs_0_, bf16[2048,768]{1,0:T(8,128)(2,1)S(1)} %get-tuple-element.30.refs_3_.refs_1_.high_ref, bf16[2048,768]{1,0:T(8,128)(2,1)S(1)} %get-tuple-element.31.refs_4_.refs_2_.low_ref, f32[64,2048]{1,0:T(8,128)S(1)} %late_quad.1.refs_3_), custom_call_target="tpu_custom_call" | custom-call | flops 100000000 | bytes 1000000 | tf_op jit(solution)/shard_map/late_head/pallas_call | solution.py:206
  33.7 1.2 %collective-permute-done.8 = f32[2,2,1024]{2,1,0:T(2,128)S(1)} collective-permute-done((f32[2,2,1024]{2,1,0:T(2,128)S(1)}, f32[2,2,1024]{2,1,0:T(2,128)S(1)}, u32[]{:S(2)}, u32[]{:S(2)}) %collective-permute-start.8) | collective-permute-done | bytes 16416 | tf_op jit(solution)/shard_map/ppermute | solution.py:317
  35.0 2.6 %collective-permute-start.11 = (f32[2,2,1024]{2,1,0:T(2,128)S(1)}, f32[2,2,1024]{2,1,0:T(2,128)S(1)}, u32[]{:S(2)}, u32[]{:S(2)}) collective-permute-start(f32[2,2,1024]{2,1,0:T(2,128)S(1)} %pad_maximum_fusion), channel_id=1, source_target_pairs={{0,3},{1,2},{2,1},{3,0},{4,7},{5,6},{6,5},{7,4},{8,11},{9,10},{10,... | collective-permute-start | bytes 49160 | tf_op jit(solution)/shard_map/ppermute | solution.py:317
  38.5 1.1 %collective-permute-done.11 = f32[2,2,1024]{2,1,0:T(2,128)S(1)} collective-permute-done((f32[2,2,1024]{2,1,0:T(2,128)S(1)}, f32[2,2,1024]{2,1,0:T(2,128)S(1)}, u32[]{:S(2)}, u32[]{:S(2)}) %collective-permute-start.11) | collective-permute-done | bytes 16416 | tf_op jit(solution)/shard_map/ppermute | solution.py:317
  39.7 1.6 %collective-permute-done.10 = f32[2,2,1024]{2,1,0:T(2,128)S(1)} collective-permute-done((f32[2,2,1024]{2,1,0:T(2,128)S(1)}, f32[2,2,1024]{2,1,0:T(2,128)S(1)}, u32[]{:S(2)}, u32[]{:S(2)}) %collective-permute-start.10) | collective-permute-done | bytes 16416 | tf_op jit(solution)/shard_map/ppermute | solution.py:317
  41.9 2.7 %first_moments.1 = (f32[392,128]{1,0:T(8,128)S(1)}, f32[392,128]{1,0:T(8,128)S(1)}, f32[392,128]{1,0:T(8,128)S(1)}, f32[392,128]{1,0:T(8,128)S(1)}, bf16[512,2048]{1,0:T(8,128)(2,1)S(1)}) custom-call(f32[192,2048]{1,0:T(8,128)S(1)} %get-tuple-element.34.early_ref, f32[64,2048]{1,0:T(8,128)S(1)} %get-tuple-element.39.late_ref, ...), custom_call_target="tpu_custom_call" | custom-call | flops 10000000000 | bytes 100000000 | tf_op jit(solution)/shard_map/first_moments/pallas_call | solution.py:247
  44.6 1.2 %collective-permute-start.12 = (f32[392,128]{1,0:T(8,128)S(1)}, f32[392,128]{1,0:T(8,128)S(1)}, u32[]{:S(2)}, u32[]{:S(2)}) collective-permute-start(f32[392,128]{1,0:T(8,128)S(1)} %get-tuple-element.43), channel_id=1, source_target_pairs={{0,8},{4,12},{8,0},{12,4},{16,24},{20,28},{24,16},{28,20},{1,9},{5... | collective-permute-start | bytes 602120 | tf_op jit(solution)/shard_map/ppermute | solution.py:317
  45.8 2.6 %second_moments.1 = (f32[384,128]{1,0:T(8,128)S(1)}, f32[384,128]{1,0:T(8,128)S(1)}, f32[384,128]{1,0:T(8,128)S(1)}, f32[384,128]{1,0:T(8,128)S(1)}) custom-call(bf16[512,2048]{1,0:T(8,128)(2,1)S(1)} %get-tuple-element.44.resp_ref, bf16[2048,768]{1,0:T(8,128)(2,1)S(1)} %get-tuple-element.32.refs_3_.refs_1_.high_ref, ...), custom_call_target="tpu_custom_call" | custom-call | flops 10000000000 | bytes 100000000 | tf_op jit(solution)/shard_map/second_moments/pallas_call | solution.py:262
  49.3 4.3 %collective-permute-done.12 = f32[392,128]{1,0:T(8,128)S(1)} collective-permute-done((f32[392,128]{1,0:T(8,128)S(1)}, f32[392,128]{1,0:T(8,128)S(1)}, u32[]{:S(2)}, u32[]{:S(2)}) %collective-permute-start.12) | collective-permute-done | bytes 200736 | tf_op jit(solution)/shard_map/ppermute | solution.py:317
  54.4 2.3 %collective-permute-done.14 = f32[384,128]{1,0:T(8,128)S(1)} collective-permute-done((f32[384,128]{1,0:T(8,128)S(1)}, f32[384,128]{1,0:T(8,128)S(1)}, u32[]{:S(2)}, u32[]{:S(2)}) %collective-permute-start.14) | collective-permute-done | bytes 196640 | tf_op jit(solution)/shard_map/ppermute | solution.py:317
  57.3 2.4 %collective-permute-start.15 = (f32[384,128]{1,0:T(8,128)S(1)}, f32[384,128]{1,0:T(8,128)S(1)}, u32[]{:S(2)}, u32[]{:S(2)}) collective-permute-start(f32[384,128]{1,0:T(8,128)S(1)} %add.35), channel_id=1, source_target_pairs={{0,16},{4,20},{8,24},{12,28},{16,0},{20,4},{24,8},{28,12},{1,17},{... | collective-permute-start | bytes 589832 | tf_op jit(solution)/shard_map/ppermute | solution.py:317
  60.2 10.6 %collective-permute-done.15 = f32[384,128]{1,0:T(8,128)S(1)} collective-permute-done((f32[384,128]{1,0:T(8,128)S(1)}, f32[384,128]{1,0:T(8,128)S(1)}, u32[]{:S(2)}, u32[]{:S(2)}) %collective-permute-start.15) | collective-permute-done | bytes 196640 | tf_op jit(solution)/shard_map/ppermute | solution.py:317
  70.9 2.4 %collective-permute-done.17.near_second_ref = f32[384,128]{1,0:T(8,128)S(1)} collective-permute-done((f32[384,128]{1,0:T(8,128)S(1)}, f32[384,128]{1,0:T(8,128)S(1)}, u32[]{:S(2)}, u32[]{:S(2)}) %collective-permute-start.17) | collective-permute-done | bytes 196640 | tf_op jit(solution)/shard_map/ppermute | solution.py:317
  (41 shorter events, 10.4 us)
Async XLA Ops:
  0.6 7.7 %collective-permute-start.2 = (f32[1024,768]{1,0:T(8,128)}, f32[1024,768]{1,0:T(8,128)S(1)}, u32[]{:S(2)}, u32[]{:S(2)}) collective-permute-start(f32[1024,768]{1,0:T(8,128)} %own_ref.1), channel_id=1, source_target_pairs={{0,4},{4,0},{8,12},{12,8},{16,20},{20,16},{24,28},{28,24},{1,5},{5... | collective-permute-start | bytes 9437192 | tf_op jit(solution)/shard_map/ppermute | solution.py:317
  1.1 13.9 %collective-permute-start.4 = (f32[64,768]{1,0:T(8,128)}, f32[64,768]{1,0:T(8,128)S(1)}, u32[]{:S(2)}, u32[]{:S(2)}) collective-permute-start(f32[64,768]{1,0:T(8,128)} %variances_ref.1), channel_id=1, source_target_pairs={{0,16},{4,20},{8,24},{12,28},{16,0},{20,4},{24,8},{28,12},{1,17},{... | collective-permute-start | bytes 589832 | tf_op jit(solution)/shard_map/ppermute | solution.py:317
  4.8 12.2 %collective-permute-start.3 = (f32[64,768]{1,0:T(8,128)}, f32[64,768]{1,0:T(8,128)S(1)}, u32[]{:S(2)}, u32[]{:S(2)}) collective-permute-start(f32[64,768]{1,0:T(8,128)} %variances_ref.1), channel_id=1, source_target_pairs={{0,8},{4,12},{8,0},{12,4},{16,24},{20,28},{24,16},{28,20},{1,9},{5... | collective-permute-start | bytes 589832 | tf_op jit(solution)/shard_map/ppermute | solution.py:317
  6.4 2.1 %copy-start = (f32[1024,768]{1,0:T(8,128)S(1)}, f32[1024,768]{1,0:T(8,128)}, u32[]{:S(2)}) copy-start(f32[1024,768]{1,0:T(8,128)} %own_ref.1) | copy-start | bytes 9437188
  7.7 9.2 %copy-start.2 = (f32[64,768]{1,0:T(8,128)S(1)}, f32[64,768]{1,0:T(8,128)}, u32[]{:S(2)}) copy-start(f32[64,768]{1,0:T(8,128)} %variances_ref.1) | copy-start | bytes 589828
  7.8 15.7 %collective-permute-start.1 = (f32[392,128]{1,0:T(8,128)S(1)}, f32[392,128]{1,0:T(8,128)S(1)}, u32[]{:S(2)}, u32[]{:S(2)}) collective-permute-start(f32[392,128]{1,0:T(8,128)S(1)} %coefficients.1.refs_0_), channel_id=1, source_target_pairs={{0,16},{4,20},{8,24},{12,28},{16,0},{20,4},{24,8},{28,12},{1,17},{... | collective-permute-start | bytes 602120 | tf_op jit(solution)/shard_map/ppermute | solution.py:317
  8.2 16.2 %collective-permute-start = (f32[392,128]{1,0:T(8,128)S(1)}, f32[392,128]{1,0:T(8,128)S(1)}, u32[]{:S(2)}, u32[]{:S(2)}) collective-permute-start(f32[392,128]{1,0:T(8,128)S(1)} %coefficients.1.refs_0_), channel_id=1, source_target_pairs={{0,8},{4,12},{8,0},{12,4},{16,24},{20,28},{24,16},{28,20},{1,9},{5... | collective-permute-start | bytes 602120 | tf_op jit(solution)/shard_map/ppermute | solution.py:317
  15.1 13.5 %collective-permute-start.7 = (f32[64,768]{1,0:T(8,128)S(1)}, f32[64,768]{1,0:T(8,128)S(1)}, u32[]{:S(2)}, u32[]{:S(2)}) collective-permute-start(f32[64,768]{1,0:T(8,128)S(1)} %collective-permute-done.4.refs_2_), channel_id=1, source_target_pairs={{0,8},{4,12},{8,0},{12,4},{16,24},{20,28},{24,16},{28,20},{1,9},{5... | collective-permute-start | bytes 589832 | tf_op jit(solution)/shard_map/ppermute | solution.py:317
  23.5 7.9 %collective-permute-start.6 = (f32[256,128]{1,0:T(8,128)S(1)}, f32[256,128]{1,0:T(8,128)S(1)}, u32[]{:S(2)}, u32[]{:S(2)}) collective-permute-start(f32[256,128]{1,0:T(8,128)S(1)} %slice.48), channel_id=1, source_target_pairs={{0,8},{4,12},{8,0},{12,4},{16,24},{20,28},{24,16},{28,20},{1,9},{5... | collective-permute-start | bytes 393224 | tf_op jit(solution)/shard_map/ppermute | solution.py:317
  26.9 5.9 %collective-permute-start.5 = (f32[136,128]{1,0:T(8,128)S(1)}, f32[136,128]{1,0:T(8,128)S(1)}, u32[]{:S(2)}, u32[]{:S(2)}) collective-permute-start(f32[136,128]{1,0:T(8,128)S(1)} %slice.47), channel_id=1, source_target_pairs={{0,8},{4,12},{8,0},{12,4},{16,24},{20,28},{24,16},{28,20},{1,9},{5... | collective-permute-start | bytes 208904 | tf_op jit(solution)/shard_map/ppermute | solution.py:317
  33.6 1.2 %collective-permute-start.8 = (f32[2,2,1024]{2,1,0:T(2,128)S(1)}, f32[2,2,1024]{2,1,0:T(2,128)S(1)}, u32[]{:S(2)}, u32[]{:S(2)}) collective-permute-start(f32[2,2,1024]{2,1,0:T(2,128)S(1)} %get-tuple-element.40), channel_id=1, source_target_pairs={{0,4},{4,0},{8,12},{12,8},{16,20},{20,16},{24,28},{28,24},{1,5},{5... | collective-permute-start | bytes 49160 | tf_op jit(solution)/shard_map/ppermute | solution.py:317
  35.0 4.7 %collective-permute-start.11 = (f32[2,2,1024]{2,1,0:T(2,128)S(1)}, f32[2,2,1024]{2,1,0:T(2,128)S(1)}, u32[]{:S(2)}, u32[]{:S(2)}) collective-permute-start(f32[2,2,1024]{2,1,0:T(2,128)S(1)} %pad_maximum_fusion), channel_id=1, source_target_pairs={{0,3},{1,2},{2,1},{3,0},{4,7},{5,6},{6,5},{7,4},{8,11},{9,10},{10,... | collective-permute-start | bytes 49160 | tf_op jit(solution)/shard_map/ppermute | solution.py:317
  37.6 3.7 %collective-permute-start.10 = (f32[2,2,1024]{2,1,0:T(2,128)S(1)}, f32[2,2,1024]{2,1,0:T(2,128)S(1)}, u32[]{:S(2)}, u32[]{:S(2)}) collective-permute-start(f32[2,2,1024]{2,1,0:T(2,128)S(1)} %pad_maximum_fusion), channel_id=1, source_target_pairs={{0,2},{1,3},{2,0},{3,1},{4,6},{5,7},{6,4},{7,5},{8,10},{9,11},{10,... | collective-permute-start | bytes 49160 | tf_op jit(solution)/shard_map/ppermute | solution.py:317
  38.1 3.7 %collective-permute-start.9 = (f32[2,2,1024]{2,1,0:T(2,128)S(1)}, f32[2,2,1024]{2,1,0:T(2,128)S(1)}, u32[]{:S(2)}, u32[]{:S(2)}) collective-permute-start(f32[2,2,1024]{2,1,0:T(2,128)S(1)} %pad_maximum_fusion), channel_id=1, source_target_pairs={{0,1},{1,0},{2,3},{3,2},{4,5},{5,4},{6,7},{7,6},{8,9},{9,8},{10,11... | collective-permute-start | bytes 49160 | tf_op jit(solution)/shard_map/ppermute | solution.py:317
  44.6 9.0 %collective-permute-start.12 = (f32[392,128]{1,0:T(8,128)S(1)}, f32[392,128]{1,0:T(8,128)S(1)}, u32[]{:S(2)}, u32[]{:S(2)}) collective-permute-start(f32[392,128]{1,0:T(8,128)S(1)} %get-tuple-element.43), channel_id=1, source_target_pairs={{0,8},{4,12},{8,0},{12,4},{16,24},{20,28},{24,16},{28,20},{1,9},{5... | collective-permute-start | bytes 602120 | tf_op jit(solution)/shard_map/ppermute | solution.py:317
  45.8 27.5 %copy-start.1 = (f32[64,768]{1,0:T(8,128)S(1)}, f32[64,768]{1,0:T(8,128)}, u32[]{:S(2)}) copy-start(f32[64,768]{1,0:T(8,128)} %means_ref.1) | copy-start | bytes 589828
  45.8 27.5 %copy-start.3 = (f32[64]{0:T(128)S(1)}, f32[64]{0:T(128)}, u32[]{:S(2)}) copy-start(f32[64]{0:T(128)} %param.7) | copy-start | bytes 772
  48.4 8.3 %collective-permute-start.14 = (f32[384,128]{1,0:T(8,128)S(1)}, f32[384,128]{1,0:T(8,128)S(1)}, u32[]{:S(2)}, u32[]{:S(2)}) collective-permute-start(f32[384,128]{1,0:T(8,128)S(1)} %get-tuple-element.47), channel_id=1, source_target_pairs={{0,8},{4,12},{8,0},{12,4},{16,24},{20,28},{24,16},{28,20},{1,9},{5... | collective-permute-start | bytes 589832 | tf_op jit(solution)/shard_map/ppermute | solution.py:317
  53.6 17.3 %collective-permute-start.13 = (f32[392,128]{1,0:T(8,128)S(1)}, f32[392,128]{1,0:T(8,128)S(1)}, u32[]{:S(2)}, u32[]{:S(2)}) collective-permute-start(f32[392,128]{1,0:T(8,128)S(1)} %add.33), channel_id=1, source_target_pairs={{0,16},{4,20},{8,24},{12,28},{16,0},{20,4},{24,8},{28,12},{1,17},{... | collective-permute-start | bytes 602120 | tf_op jit(solution)/shard_map/ppermute | solution.py:317
  56.8 16.5 %collective-permute-start.16 = (f32[392,128]{1,0:T(8,128)S(1)}, f32[392,128]{1,0:T(8,128)S(1)}, u32[]{:S(2)}, u32[]{:S(2)}) collective-permute-start(f32[392,128]{1,0:T(8,128)S(1)} %get-tuple-element.51), channel_id=1, source_target_pairs={{0,8},{4,12},{8,0},{12,4},{16,24},{20,28},{24,16},{28,20},{1,9},{5... | collective-permute-start | bytes 602120 | tf_op jit(solution)/shard_map/ppermute | solution.py:317
  57.3 13.5 %collective-permute-start.15 = (f32[384,128]{1,0:T(8,128)S(1)}, f32[384,128]{1,0:T(8,128)S(1)}, u32[]{:S(2)}, u32[]{:S(2)}) collective-permute-start(f32[384,128]{1,0:T(8,128)S(1)} %add.35), channel_id=1, source_target_pairs={{0,16},{4,20},{8,24},{12,28},{16,0},{20,4},{24,8},{28,12},{1,17},{... | collective-permute-start | bytes 589832 | tf_op jit(solution)/shard_map/ppermute | solution.py:317
  59.7 13.5 %collective-permute-start.17 = (f32[384,128]{1,0:T(8,128)S(1)}, f32[384,128]{1,0:T(8,128)S(1)}, u32[]{:S(2)}, u32[]{:S(2)}) collective-permute-start(f32[384,128]{1,0:T(8,128)S(1)} %get-tuple-element.53), channel_id=1, source_target_pairs={{0,8},{4,12},{8,0},{12,4},{16,24},{20,28},{24,16},{28,20},{1,9},{5... | collective-permute-start | bytes 589832 | tf_op jit(solution)/shard_map/ppermute | solution.py:317

commit v4 on v3

--- a/solution.py
+++ b/solution.py
@@ -343,7 +343,7 @@
         ready = []
         for parts in held:
             for q in sorted((q for q in parts if q & bit and q != bit), reverse=True):
-                parts[q ^ bit] = parts[q ^ bit] + swap(parts.pop(q), "dp", 2 * bit)
+                parts[q ^ bit] = parts[q ^ bit] + swap(after(parts.pop(q), *ready), "dp", 2 * bit)
                 ready = [parts[q ^ bit]]
         for total, parts in zip(totals, held):
             part = swap(after(parts.pop(bit), *ready), "dp", 2 * bit)

time: 74.4 us -> 72.7 us (0.977)
  waiting for transfers between devices: 34.7 us -> 30.6 us
  starting transfers between devices: 19.3 us -> 21.8 us
    ppermute x18, waiting for transfers between devices: 34.7 us -> 30.6 us  [swap(): return lax.ppermute(value, axis, [(i, i ^ bit) for i in range(size)])]
    ppermute x18, starting transfers between devices: 19.3 us -> 21.8 us  [swap(): return lax.ppermute(value, axis, [(i, i ^ bit) for i in range(size)])]
where the time goes in v4:
time: 72.7 us; the launch traced here: 72.6 us
  waiting for transfers between devices  30.6 us (42%)
  starting transfers between devices  21.8 us (30%)
  Pallas kernels  19 us (26%)
  between operations  0.75 us (1%)
    ppermute x18, waiting for transfers between devices, swap(): return lax.ppermute(value, axis, [(i, i ^ bit) for i in range(size)])  30.6 us
    ppermute x18, starting transfers between devices, swap(): return lax.ppermute(value, axis, [(i, i ^ bit) for i in range(size)])  21.8 us
    pallas_call x5, Pallas kernels, score_call(): pl.pallas_call(body, out_shape=[jax.ShapeDtypeStruct(shape, F32) for shap...  9.25 us
    pallas_call x1, Pallas kernels, first_moments(): pl.pallas_call(functools.partial(first_kernel, n), out_shape=[pack] * (co...  2.67 us
    pallas_call x1, Pallas kernels, second_moments(): pl.pallas_call(functools.partial(second_kernel, n), out_shape=[pack] * (r...  2.59 us
    pallas_call x1, Pallas kernels, halves(): pl.pallas_call(halves_kernel, grid=(2 * steps,), in_specs=[pl.BlockSpec((...  2.25 us
  transfers between devices with their start and end apart: 18, of which 14 were waited for; matrix products, arithmetic and copies ran while one was open for 0% of the time, Pallas kernels for 20%

profile of v4, /device:TPU:0, one launch (start us, length us, event | category | flops | bytes accessed | tf_op | source)
XLA Modules:
  0.0 72.6 jit_solution(13340136597204851134)
XLA Ops:
  1.1 3.7 %collective-permute-start.4 = (f32[64,768]{1,0:T(8,128)}, f32[64,768]{1,0:T(8,128)S(1)}, u32[]{:S(2)}, u32[]{:S(2)}) collective-permute-start(f32[64,768]{1,0:T(8,128)} %variances_ref.1), channel_id=1, source_target_pairs={{0,16},{4,20},{8,24},{12,28},{16,0},{20,4},{24,8},{28,12},{1,17},{... | collective-permute-start | bytes 589832 | tf_op jit(solution)/shard_map/ppermute | solution.py:317
  4.8 1.6 %collective-permute-start.3 = (f32[64,768]{1,0:T(8,128)}, f32[64,768]{1,0:T(8,128)S(1)}, u32[]{:S(2)}, u32[]{:S(2)}) collective-permute-start(f32[64,768]{1,0:T(8,128)} %variances_ref.1), channel_id=1, source_target_pairs={{0,8},{4,12},{8,0},{12,4},{16,24},{20,28},{24,16},{28,20},{1,9},{5... | collective-permute-start | bytes 589832 | tf_op jit(solution)/shard_map/ppermute | solution.py:317
  6.4 1.3 %coefficients.1.refs_0_ = f32[392,128]{1,0:T(8,128)S(1)} custom-call(f32[64,768]{1,0:T(8,128)} %means_ref.1, f32[64,768]{1,0:T(8,128)} %variances_ref.1, f32[1,64]{1,0:T(1,128)} %bitcast.2), custom_call_target="tpu_custom_call" | custom-call | flops 10000000000 | bytes 100000000 | tf_op jit(solution)/shard_map/coefficients/pallas_call | solution.py:64
  8.5 2.2 %halves.1 = (bf16[2048,768]{1,0:T(8,128)(2,1)S(1)}, bf16[2048,768]{1,0:T(8,128)(2,1)S(1)}, bf16[2048,768]{1,0:T(8,128)(2,1)S(1)}, bf16[2048,768]{1,0:T(8,128)(2,1)S(1)}) custom-call(f32[1024,768]{1,0:T(8,128)S(1)} %copy-done, f32[1024,768]{1,0:T(8,128)S(1)} %collective-permute-done.2.other_ref), custom_call_target="tpu_custom_call" | custom-call | flops 10000000000 | bytes 100000000 | tf_op jit(solution)/shard_map/halves/pallas_call | solution.py:101
  10.7 4.4 %collective-permute-done.4.refs_2_ = f32[64,768]{1,0:T(8,128)S(1)} collective-permute-done((f32[64,768]{1,0:T(8,128)}, f32[64,768]{1,0:T(8,128)S(1)}, u32[]{:S(2)}, u32[]{:S(2)}) %collective-permute-start.4) | collective-permute-done | bytes 196640 | tf_op jit(solution)/shard_map/ppermute | solution.py:317
  17.0 2.4 %early_quad.1.refs_5_ = f32[192,2048]{1,0:T(8,128)S(1)} custom-call(f32[64,768]{1,0:T(8,128)S(1)} %copy-done.2, f32[64,768]{1,0:T(8,128)S(1)} %collective-permute-done.3.refs_1_, f32[64,768]{1,0:T(8,128)S(1)} %collective-permute-done.4.refs_2_, bf16[2048,768]{1,0:T(8,128)(2,1)S(1)} %get-tuple-element.33.refs_3_.refs_1_.high_ref, ...), custom_call_target="tpu_custom_call" | custom-call | flops 10000000000 | bytes 100000000 | tf_op jit(solution)/shard_map/early_quad/pallas_call | solution.py:206
  19.4 4.1 %collective-permute-done.1.refs_2_ = f32[392,128]{1,0:T(8,128)S(1)} collective-permute-done((f32[392,128]{1,0:T(8,128)S(1)}, f32[392,128]{1,0:T(8,128)S(1)}, u32[]{:S(2)}, u32[]{:S(2)}) %collective-permute-start.1) | collective-permute-done | bytes 200736 | tf_op jit(solution)/shard_map/ppermute | solution.py:317
  24.4 2.5 %early_scores.1 = (f32[192,2048]{1,0:T(8,128)S(1)}, f32[2,2048]{1,0:T(2,128)S(1)}) custom-call(f32[392,128]{1,0:T(8,128)S(1)} %coefficients.1.refs_0_, f32[392,128]{1,0:T(8,128)S(1)} %collective-permute-done.refs_1_, f32[392,128]{1,0:T(8,128)S(1)} %collective-permute-done.1.refs_2_, bf16[2048,768]{1,0:T(8,128)(2,1)S(1)} %get-tuple-element.31.refs_3_.refs_1_.high_ref, ...), custom_call_target="tpu_custom_call" | custom-call | flops 100000000 | bytes 1000000 | tf_op jit(solution)/shard_map/early_scores/pallas_call | solution.py:206
  26.9 1.3 %collective-permute-start.5 = (f32[136,128]{1,0:T(8,128)S(1)}, f32[136,128]{1,0:T(8,128)S(1)}, u32[]{:S(2)}, u32[]{:S(2)}) collective-permute-start(f32[136,128]{1,0:T(8,128)S(1)} %slice.47), channel_id=1, source_target_pairs={{0,8},{4,12},{8,0},{12,4},{16,24},{20,28},{24,16},{28,20},{1,9},{5... | collective-permute-start | bytes 208904 | tf_op jit(solution)/shard_map/ppermute | solution.py:317
  28.6 2.1 %late_quad.1.refs_3_ = f32[64,2048]{1,0:T(8,128)S(1)} custom-call(f32[64,768]{1,0:T(8,128)S(1)} %collective-permute-done.7.refs_0_, bf16[2048,768]{1,0:T(8,128)(2,1)S(1)} %get-tuple-element.33.refs_3_.refs_1_.high_ref, bf16[2048,768]{1,0:T(8,128)(2,1)S(1)} %get-tuple-element.34.refs_4_.refs_2_.low_ref), custom_call_target="tpu_custom_call" | custom-call | flops 100000000 | bytes 1000000 | tf_op jit(solution)/shard_map/late_quad/pallas_call | solution.py:206
  31.4 1.4 %late_head.1.refs_3_ = f32[64,2048]{1,0:T(8,128)S(1)} custom-call(f32[256,128]{1,0:T(8,128)S(1)} %collective-permute-done.6.refs_0_, bf16[2048,768]{1,0:T(8,128)(2,1)S(1)} %get-tuple-element.31.refs_3_.refs_1_.high_ref, bf16[2048,768]{1,0:T(8,128)(2,1)S(1)} %get-tuple-element.32.refs_4_.refs_2_.low_ref, f32[64,2048]{1,0:T(8,128)S(1)} %late_quad.1.refs_3_), custom_call_target="tpu_custom_call" | custom-call | flops 100000000 | bytes 1000000 | tf_op jit(solution)/shard_map/late_head/pallas_call | solution.py:206
  33.7 1.2 %collective-permute-done.8 = f32[2,2,1024]{2,1,0:T(2,128)S(1)} collective-permute-done((f32[2,2,1024]{2,1,0:T(2,128)S(1)}, f32[2,2,1024]{2,1,0:T(2,128)S(1)}, u32[]{:S(2)}, u32[]{:S(2)}) %collective-permute-start.8) | collective-permute-done | bytes 16416 | tf_op jit(solution)/shard_map/ppermute | solution.py:317
  35.0 2.6 %collective-permute-start.11 = (f32[2,2,1024]{2,1,0:T(2,128)S(1)}, f32[2,2,1024]{2,1,0:T(2,128)S(1)}, u32[]{:S(2)}, u32[]{:S(2)}) collective-permute-start(f32[2,2,1024]{2,1,0:T(2,128)S(1)} %pad_maximum_fusion), channel_id=1, source_target_pairs={{0,3},{1,2},{2,1},{3,0},{4,7},{5,6},{6,5},{7,4},{8,11},{9,10},{10,... | collective-permute-start | bytes 49160 | tf_op jit(solution)/shard_map/ppermute | solution.py:317
  39.7 1.6 %collective-permute-done.10 = f32[2,2,1024]{2,1,0:T(2,128)S(1)} collective-permute-done((f32[2,2,1024]{2,1,0:T(2,128)S(1)}, f32[2,2,1024]{2,1,0:T(2,128)S(1)}, u32[]{:S(2)}, u32[]{:S(2)}) %collective-permute-start.10) | collective-permute-done | bytes 16416 | tf_op jit(solution)/shard_map/ppermute | solution.py:317
  41.9 2.7 %first_moments.1 = (f32[392,128]{1,0:T(8,128)S(1)}, f32[392,128]{1,0:T(8,128)S(1)}, f32[392,128]{1,0:T(8,128)S(1)}, f32[392,128]{1,0:T(8,128)S(1)}, bf16[512,2048]{1,0:T(8,128)(2,1)S(1)}) custom-call(f32[192,2048]{1,0:T(8,128)S(1)} %get-tuple-element.35.early_ref, f32[64,2048]{1,0:T(8,128)S(1)} %get-tuple-element.40.late_ref, ...), custom_call_target="tpu_custom_call" | custom-call | flops 10000000000 | bytes 100000000 | tf_op jit(solution)/shard_map/first_moments/pallas_call | solution.py:247
  44.6 1.2 %collective-permute-start.12 = (f32[392,128]{1,0:T(8,128)S(1)}, f32[392,128]{1,0:T(8,128)S(1)}, u32[]{:S(2)}, u32[]{:S(2)}) collective-permute-start(f32[392,128]{1,0:T(8,128)S(1)} %get-tuple-element.44), channel_id=1, source_target_pairs={{0,8},{4,12},{8,0},{12,4},{16,24},{20,28},{24,16},{28,20},{1,9},{5... | collective-permute-start | bytes 602120 | tf_op jit(solution)/shard_map/ppermute | solution.py:317
  45.8 2.6 %second_moments.1 = (f32[384,128]{1,0:T(8,128)S(1)}, f32[384,128]{1,0:T(8,128)S(1)}, f32[384,128]{1,0:T(8,128)S(1)}, f32[384,128]{1,0:T(8,128)S(1)}) custom-call(bf16[512,2048]{1,0:T(8,128)(2,1)S(1)} %get-tuple-element.45.resp_ref, bf16[2048,768]{1,0:T(8,128)(2,1)S(1)} %get-tuple-element.33.refs_3_.refs_1_.high_ref, ...), custom_call_target="tpu_custom_call" | custom-call | flops 10000000000 | bytes 100000000 | tf_op jit(solution)/shard_map/second_moments/pallas_call | solution.py:262
  48.4 1.9 %collective-permute-done.12 = f32[392,128]{1,0:T(8,128)S(1)} collective-permute-done((f32[392,128]{1,0:T(8,128)S(1)}, f32[392,128]{1,0:T(8,128)S(1)}, u32[]{:S(2)}, u32[]{:S(2)}) %collective-permute-start.12) | collective-permute-done | bytes 200736 | tf_op jit(solution)/shard_map/ppermute | solution.py:317
  50.4 1.2 %collective-permute-start.14 = (f32[384,128]{1,0:T(8,128)S(1)}, f32[384,128]{1,0:T(8,128)S(1)}, u32[]{:S(2)}, u32[]{:S(2)}) collective-permute-start(f32[384,128]{1,0:T(8,128)S(1)} %get-tuple-element.49), channel_id=1, source_target_pairs={{0,8},{4,12},{8,0},{12,4},{16,24},{20,28},{24,16},{28,20},{1,9},{5... | collective-permute-start | bytes 589832 | tf_op jit(solution)/shard_map/ppermute | solution.py:317
  51.6 1.7 %collective-permute-start.13 = (f32[392,128]{1,0:T(8,128)S(1)}, f32[392,128]{1,0:T(8,128)S(1)}, u32[]{:S(2)}, u32[]{:S(2)}) collective-permute-start(f32[392,128]{1,0:T(8,128)S(1)} %add.33), channel_id=1, source_target_pairs={{0,16},{4,20},{8,24},{12,28},{16,0},{20,4},{24,8},{28,12},{1,17},{... | collective-permute-start | bytes 602120 | tf_op jit(solution)/shard_map/ppermute | solution.py:317
  53.4 6.0 %collective-permute-done.14 = f32[384,128]{1,0:T(8,128)S(1)} collective-permute-done((f32[384,128]{1,0:T(8,128)S(1)}, f32[384,128]{1,0:T(8,128)S(1)}, u32[]{:S(2)}, u32[]{:S(2)}) %collective-permute-start.14) | collective-permute-done | bytes 196640 | tf_op jit(solution)/shard_map/ppermute | solution.py:317
  59.5 4.5 %collective-permute-start.15 = (f32[384,128]{1,0:T(8,128)S(1)}, f32[384,128]{1,0:T(8,128)S(1)}, u32[]{:S(2)}, u32[]{:S(2)}) collective-permute-start(f32[384,128]{1,0:T(8,128)S(1)} %add.35), channel_id=1, source_target_pairs={{0,16},{4,20},{8,24},{12,28},{16,0},{20,4},{24,8},{28,12},{1,17},{... | collective-permute-start | bytes 589832 | tf_op jit(solution)/shard_map/ppermute | solution.py:317
  64.1 4.1 %collective-permute-done.15 = f32[384,128]{1,0:T(8,128)S(1)} collective-permute-done((f32[384,128]{1,0:T(8,128)S(1)}, f32[384,128]{1,0:T(8,128)S(1)}, u32[]{:S(2)}, u32[]{:S(2)}) %collective-permute-start.15) | collective-permute-done | bytes 196640 | tf_op jit(solution)/shard_map/ppermute | solution.py:317
  68.3 3.3 %collective-permute-done.17.near_second_ref = f32[384,128]{1,0:T(8,128)S(1)} collective-permute-done((f32[384,128]{1,0:T(8,128)S(1)}, f32[384,128]{1,0:T(8,128)S(1)}, u32[]{:S(2)}, u32[]{:S(2)}) %collective-permute-start.17) | collective-permute-done | bytes 196640 | tf_op jit(solution)/shard_map/ppermute | solution.py:317
  (41 shorter events, 10.0 us)
Async XLA Ops:
  0.6 7.7 %collective-permute-start.2 = (f32[1024,768]{1,0:T(8,128)}, f32[1024,768]{1,0:T(8,128)S(1)}, u32[]{:S(2)}, u32[]{:S(2)}) collective-permute-start(f32[1024,768]{1,0:T(8,128)} %own_ref.1), channel_id=1, source_target_pairs={{0,4},{4,0},{8,12},{12,8},{16,20},{20,16},{24,28},{28,24},{1,5},{5... | collective-permute-start | bytes 9437192 | tf_op jit(solution)/shard_map/ppermute | solution.py:317
  1.1 13.9 %collective-permute-start.4 = (f32[64,768]{1,0:T(8,128)}, f32[64,768]{1,0:T(8,128)S(1)}, u32[]{:S(2)}, u32[]{:S(2)}) collective-permute-start(f32[64,768]{1,0:T(8,128)} %variances_ref.1), channel_id=1, source_target_pairs={{0,16},{4,20},{8,24},{12,28},{16,0},{20,4},{24,8},{28,12},{1,17},{... | collective-permute-start | bytes 589832 | tf_op jit(solution)/shard_map/ppermute | solution.py:317
  4.8 12.2 %collective-permute-start.3 = (f32[64,768]{1,0:T(8,128)}, f32[64,768]{1,0:T(8,128)S(1)}, u32[]{:S(2)}, u32[]{:S(2)}) collective-permute-start(f32[64,768]{1,0:T(8,128)} %variances_ref.1), channel_id=1, source_target_pairs={{0,8},{4,12},{8,0},{12,4},{16,24},{20,28},{24,16},{28,20},{1,9},{5... | collective-permute-start | bytes 589832 | tf_op jit(solution)/shard_map/ppermute | solution.py:317
  6.4 2.1 %copy-start = (f32[1024,768]{1,0:T(8,128)S(1)}, f32[1024,768]{1,0:T(8,128)}, u32[]{:S(2)}) copy-start(f32[1024,768]{1,0:T(8,128)} %own_ref.1) | copy-start | bytes 9437188
  7.7 9.2 %copy-start.2 = (f32[64,768]{1,0:T(8,128)S(1)}, f32[64,768]{1,0:T(8,128)}, u32[]{:S(2)}) copy-start(f32[64,768]{1,0:T(8,128)} %variances_ref.1) | copy-start | bytes 589828
  7.8 15.7 %collective-permute-start.1 = (f32[392,128]{1,0:T(8,128)S(1)}, f32[392,128]{1,0:T(8,128)S(1)}, u32[]{:S(2)}, u32[]{:S(2)}) collective-permute-start(f32[392,128]{1,0:T(8,128)S(1)} %coefficients.1.refs_0_), channel_id=1, source_target_pairs={{0,16},{4,20},{8,24},{12,28},{16,0},{20,4},{24,8},{28,12},{1,17},{... | collective-permute-start | bytes 602120 | tf_op jit(solution)/shard_map/ppermute | solution.py:317
  8.2 16.2 %collective-permute-start = (f32[392,128]{1,0:T(8,128)S(1)}, f32[392,128]{1,0:T(8,128)S(1)}, u32[]{:S(2)}, u32[]{:S(2)}) collective-permute-start(f32[392,128]{1,0:T(8,128)S(1)} %coefficients.1.refs_0_), channel_id=1, source_target_pairs={{0,8},{4,12},{8,0},{12,4},{16,24},{20,28},{24,16},{28,20},{1,9},{5... | collective-permute-start | bytes 602120 | tf_op jit(solution)/shard_map/ppermute | solution.py:317
  15.1 13.5 %collective-permute-start.7 = (f32[64,768]{1,0:T(8,128)S(1)}, f32[64,768]{1,0:T(8,128)S(1)}, u32[]{:S(2)}, u32[]{:S(2)}) collective-permute-start(f32[64,768]{1,0:T(8,128)S(1)} %collective-permute-done.4.refs_2_), channel_id=1, source_target_pairs={{0,8},{4,12},{8,0},{12,4},{16,24},{20,28},{24,16},{28,20},{1,9},{5... | collective-permute-start | bytes 589832 | tf_op jit(solution)/shard_map/ppermute | solution.py:317
  23.5 7.9 %collective-permute-start.6 = (f32[256,128]{1,0:T(8,128)S(1)}, f32[256,128]{1,0:T(8,128)S(1)}, u32[]{:S(2)}, u32[]{:S(2)}) collective-permute-start(f32[256,128]{1,0:T(8,128)S(1)} %slice.48), channel_id=1, source_target_pairs={{0,8},{4,12},{8,0},{12,4},{16,24},{20,28},{24,16},{28,20},{1,9},{5... | collective-permute-start | bytes 393224 | tf_op jit(solution)/shard_map/ppermute | solution.py:317
  26.9 5.9 %collective-permute-start.5 = (f32[136,128]{1,0:T(8,128)S(1)}, f32[136,128]{1,0:T(8,128)S(1)}, u32[]{:S(2)}, u32[]{:S(2)}) collective-permute-start(f32[136,128]{1,0:T(8,128)S(1)} %slice.47), channel_id=1, source_target_pairs={{0,8},{4,12},{8,0},{12,4},{16,24},{20,28},{24,16},{28,20},{1,9},{5... | collective-permute-start | bytes 208904 | tf_op jit(solution)/shard_map/ppermute | solution.py:317
  33.6 1.2 %collective-permute-start.8 = (f32[2,2,1024]{2,1,0:T(2,128)S(1)}, f32[2,2,1024]{2,1,0:T(2,128)S(1)}, u32[]{:S(2)}, u32[]{:S(2)}) collective-permute-start(f32[2,2,1024]{2,1,0:T(2,128)S(1)} %get-tuple-element.41), channel_id=1, source_target_pairs={{0,4},{4,0},{8,12},{12,8},{16,20},{20,16},{24,28},{28,24},{1,5},{5... | collective-permute-start | bytes 49160 | tf_op jit(solution)/shard_map/ppermute | solution.py:317
  35.0 4.7 %collective-permute-start.11 = (f32[2,2,1024]{2,1,0:T(2,128)S(1)}, f32[2,2,1024]{2,1,0:T(2,128)S(1)}, u32[]{:S(2)}, u32[]{:S(2)}) collective-permute-start(f32[2,2,1024]{2,1,0:T(2,128)S(1)} %pad_maximum_fusion), channel_id=1, source_target_pairs={{0,3},{1,2},{2,1},{3,0},{4,7},{5,6},{6,5},{7,4},{8,11},{9,10},{10,... | collective-permute-start | bytes 49160 | tf_op jit(solution)/shard_map/ppermute | solution.py:317
  37.6 3.7 %collective-permute-start.10 = (f32[2,2,1024]{2,1,0:T(2,128)S(1)}, f32[2,2,1024]{2,1,0:T(2,128)S(1)}, u32[]{:S(2)}, u32[]{:S(2)}) collective-permute-start(f32[2,2,1024]{2,1,0:T(2,128)S(1)} %pad_maximum_fusion), channel_id=1, source_target_pairs={{0,2},{1,3},{2,0},{3,1},{4,6},{5,7},{6,4},{7,5},{8,10},{9,11},{10,... | collective-permute-start | bytes 49160 | tf_op jit(solution)/shard_map/ppermute | solution.py:317
  38.1 3.7 %collective-permute-start.9 = (f32[2,2,1024]{2,1,0:T(2,128)S(1)}, f32[2,2,1024]{2,1,0:T(2,128)S(1)}, u32[]{:S(2)}, u32[]{:S(2)}) collective-permute-start(f32[2,2,1024]{2,1,0:T(2,128)S(1)} %pad_maximum_fusion), channel_id=1, source_target_pairs={{0,1},{1,0},{2,3},{3,2},{4,5},{5,4},{6,7},{7,6},{8,9},{9,8},{10,11... | collective-permute-start | bytes 49160 | tf_op jit(solution)/shard_map/ppermute | solution.py:317
  44.6 5.8 %collective-permute-start.12 = (f32[392,128]{1,0:T(8,128)S(1)}, f32[392,128]{1,0:T(8,128)S(1)}, u32[]{:S(2)}, u32[]{:S(2)}) collective-permute-start(f32[392,128]{1,0:T(8,128)S(1)} %get-tuple-element.44), channel_id=1, source_target_pairs={{0,8},{4,12},{8,0},{12,4},{16,24},{20,28},{24,16},{28,20},{1,9},{5... | collective-permute-start | bytes 602120 | tf_op jit(solution)/shard_map/ppermute | solution.py:317
  45.8 25.8 %copy-start.1 = (f32[64,768]{1,0:T(8,128)S(1)}, f32[64,768]{1,0:T(8,128)}, u32[]{:S(2)}) copy-start(f32[64,768]{1,0:T(8,128)} %means_ref.1) | copy-start | bytes 589828
  45.8 25.8 %copy-start.3 = (f32[64]{0:T(128)S(1)}, f32[64]{0:T(128)}, u32[]{:S(2)}) copy-start(f32[64]{0:T(128)} %param.7) | copy-start | bytes 772
  50.4 9.0 %collective-permute-start.14 = (f32[384,128]{1,0:T(8,128)S(1)}, f32[384,128]{1,0:T(8,128)S(1)}, u32[]{:S(2)}, u32[]{:S(2)}) collective-permute-start(f32[384,128]{1,0:T(8,128)S(1)} %get-tuple-element.49), channel_id=1, source_target_pairs={{0,8},{4,12},{8,0},{12,4},{16,24},{20,28},{24,16},{28,20},{1,9},{5... | collective-permute-start | bytes 589832 | tf_op jit(solution)/shard_map/ppermute | solution.py:317
  51.6 12.5 %collective-permute-start.13 = (f32[392,128]{1,0:T(8,128)S(1)}, f32[392,128]{1,0:T(8,128)S(1)}, u32[]{:S(2)}, u32[]{:S(2)}) collective-permute-start(f32[392,128]{1,0:T(8,128)S(1)} %add.33), channel_id=1, source_target_pairs={{0,16},{4,20},{8,24},{12,28},{16,0},{20,4},{24,8},{28,12},{1,17},{... | collective-permute-start | bytes 602120 | tf_op jit(solution)/shard_map/ppermute | solution.py:317
  59.4 12.2 %collective-permute-start.16 = (f32[392,128]{1,0:T(8,128)S(1)}, f32[392,128]{1,0:T(8,128)S(1)}, u32[]{:S(2)}, u32[]{:S(2)}) collective-permute-start(f32[392,128]{1,0:T(8,128)S(1)} %get-tuple-element.53), channel_id=1, source_target_pairs={{0,8},{4,12},{8,0},{12,4},{16,24},{20,28},{24,16},{28,20},{1,9},{5... | collective-permute-start | bytes 602120 | tf_op jit(solution)/shard_map/ppermute | solution.py:317
  59.5 8.8 %collective-permute-start.15 = (f32[384,128]{1,0:T(8,128)S(1)}, f32[384,128]{1,0:T(8,128)S(1)}, u32[]{:S(2)}, u32[]{:S(2)}) collective-permute-start(f32[384,128]{1,0:T(8,128)S(1)} %add.35), channel_id=1, source_target_pairs={{0,16},{4,20},{8,24},{12,28},{16,0},{20,4},{24,8},{28,12},{1,17},{... | collective-permute-start | bytes 589832 | tf_op jit(solution)/shard_map/ppermute | solution.py:317
  64.0 7.6 %collective-permute-start.17 = (f32[384,128]{1,0:T(8,128)S(1)}, f32[384,128]{1,0:T(8,128)S(1)}, u32[]{:S(2)}, u32[]{:S(2)}) collective-permute-start(f32[384,128]{1,0:T(8,128)S(1)} %get-tuple-element.55), channel_id=1, source_target_pairs={{0,8},{4,12},{8,0},{12,4},{16,24},{20,28},{24,16},{28,20},{1,9},{5... | collective-permute-start | bytes 589832 | tf_op jit(solution)/shard_map/ppermute | solution.py:317

commit v5 on v4

--- a/solution.py
+++ b/solution.py
@@ -349,7 +349,8 @@
             part = swap(after(parts.pop(bit), *ready), "dp", 2 * bit)
             (near if bit == 1 else total).append(part)
         bit *= 2
-    return *lax.optimization_barrier(tuple(sum(t[1:], t[0]) for t in totals)), *near
+    one, other, *near = lax.optimization_barrier((sum(totals[0][1:], totals[0][0]), totals[1][0], *near))
+    return one, sum(totals[1][1:], other), *near
 
 
 def merge(stats):

time: 72.7 us -> 72.7 us (level)
  transfers between devices with their start and end apart: 18 -> 18, of which waited for: 14 -> 13; matrix products, arithmetic and copies ran while one was open for 0% -> 0% of each run, Pallas kernels for 20% -> 20%
where the time goes in v5:
time: 72.7 us; the launch traced here: 72.6 us
  waiting for transfers between devices  30.6 us (42%)
  starting transfers between devices  21.8 us (30%)
  Pallas kernels  19 us (26%)
  between operations  0.77 us (1%)
    ppermute x18, waiting for transfers between devices, swap(): return lax.ppermute(value, axis, [(i, i ^ bit) for i in range(size)])  30.6 us
    ppermute x18, starting transfers between devices, swap(): return lax.ppermute(value, axis, [(i, i ^ bit) for i in range(size)])  21.8 us
    pallas_call x5, Pallas kernels, score_call(): pl.pallas_call(body, out_shape=[jax.ShapeDtypeStruct(shape, F32) for shap...  9.25 us
    pallas_call x1, Pallas kernels, first_moments(): pl.pallas_call(functools.partial(first_kernel, n), out_shape=[pack] * (co...  2.67 us
    pallas_call x1, Pallas kernels, second_moments(): pl.pallas_call(functools.partial(second_kernel, n), out_shape=[pack] * (r...  2.59 us
    pallas_call x1, Pallas kernels, halves(): pl.pallas_call(halves_kernel, grid=(2 * steps,), in_specs=[pl.BlockSpec((...  2.25 us
  transfers between devices with their start and end apart: 18, of which 13 were waited for; matrix products, arithmetic and copies ran while one was open for 0% of the time, Pallas kernels for 20%

profile of v5, /device:TPU:0, one launch (start us, length us, event | category | flops | bytes accessed | tf_op | source)
XLA Modules:
  0.0 72.6 jit_solution(16084787558442318333)
XLA Ops:
  1.1 3.7 %collective-permute-start.4 = (f32[64,768]{1,0:T(8,128)}, f32[64,768]{1,0:T(8,128)S(1)}, u32[]{:S(2)}, u32[]{:S(2)}) collective-permute-start(f32[64,768]{1,0:T(8,128)} %variances_ref.1), channel_id=1, source_target_pairs={{0,16},{4,20},{8,24},{12,28},{16,0},{20,4},{24,8},{28,12},{1,17},{... | collective-permute-start | bytes 589832 | tf_op jit(solution)/shard_map/ppermute | solution.py:317
  4.8 1.6 %collective-permute-start.3 = (f32[64,768]{1,0:T(8,128)}, f32[64,768]{1,0:T(8,128)S(1)}, u32[]{:S(2)}, u32[]{:S(2)}) collective-permute-start(f32[64,768]{1,0:T(8,128)} %variances_ref.1), channel_id=1, source_target_pairs={{0,8},{4,12},{8,0},{12,4},{16,24},{20,28},{24,16},{28,20},{1,9},{5... | collective-permute-start | bytes 589832 | tf_op jit(solution)/shard_map/ppermute | solution.py:317
  6.4 1.3 %coefficients.1.refs_0_ = f32[392,128]{1,0:T(8,128)S(1)} custom-call(f32[64,768]{1,0:T(8,128)} %means_ref.1, f32[64,768]{1,0:T(8,128)} %variances_ref.1, f32[1,64]{1,0:T(1,128)} %bitcast.2), custom_call_target="tpu_custom_call" | custom-call | flops 10000000000 | bytes 100000000 | tf_op jit(solution)/shard_map/coefficients/pallas_call | solution.py:64
  8.5 2.2 %halves.1 = (bf16[2048,768]{1,0:T(8,128)(2,1)S(1)}, bf16[2048,768]{1,0:T(8,128)(2,1)S(1)}, bf16[2048,768]{1,0:T(8,128)(2,1)S(1)}, bf16[2048,768]{1,0:T(8,128)(2,1)S(1)}) custom-call(f32[1024,768]{1,0:T(8,128)S(1)} %copy-done, f32[1024,768]{1,0:T(8,128)S(1)} %collective-permute-done.2.other_ref), custom_call_target="tpu_custom_call" | custom-call | flops 10000000000 | bytes 100000000 | tf_op jit(solution)/shard_map/halves/pallas_call | solution.py:101
  10.7 4.4 %collective-permute-done.4.refs_2_ = f32[64,768]{1,0:T(8,128)S(1)} collective-permute-done((f32[64,768]{1,0:T(8,128)}, f32[64,768]{1,0:T(8,128)S(1)}, u32[]{:S(2)}, u32[]{:S(2)}) %collective-permute-start.4) | collective-permute-done | bytes 196640 | tf_op jit(solution)/shard_map/ppermute | solution.py:317
  17.0 2.4 %early_quad.1.refs_5_ = f32[192,2048]{1,0:T(8,128)S(1)} custom-call(f32[64,768]{1,0:T(8,128)S(1)} %copy-done.2, f32[64,768]{1,0:T(8,128)S(1)} %collective-permute-done.3.refs_1_, f32[64,768]{1,0:T(8,128)S(1)} %collective-permute-done.4.refs_2_, bf16[2048,768]{1,0:T(8,128)(2,1)S(1)} %get-tuple-element.35.refs_3_.refs_1_.high_ref, ...), custom_call_target="tpu_custom_call" | custom-call | flops 10000000000 | bytes 100000000 | tf_op jit(solution)/shard_map/early_quad/pallas_call | solution.py:206
  19.4 4.1 %collective-permute-done.1.refs_2_ = f32[392,128]{1,0:T(8,128)S(1)} collective-permute-done((f32[392,128]{1,0:T(8,128)S(1)}, f32[392,128]{1,0:T(8,128)S(1)}, u32[]{:S(2)}, u32[]{:S(2)}) %collective-permute-start.1) | collective-permute-done | bytes 200736 | tf_op jit(solution)/shard_map/ppermute | solution.py:317
  24.4 2.5 %early_scores.1 = (f32[192,2048]{1,0:T(8,128)S(1)}, f32[2,2048]{1,0:T(2,128)S(1)}) custom-call(f32[392,128]{1,0:T(8,128)S(1)} %coefficients.1.refs_0_, f32[392,128]{1,0:T(8,128)S(1)} %collective-permute-done.refs_1_, f32[392,128]{1,0:T(8,128)S(1)} %collective-permute-done.1.refs_2_, bf16[2048,768]{1,0:T(8,128)(2,1)S(1)} %get-tuple-element.33.refs_3_.refs_1_.high_ref, ...), custom_call_target="tpu_custom_call" | custom-call | flops 100000000 | bytes 1000000 | tf_op jit(solution)/shard_map/early_scores/pallas_call | solution.py:206
  26.9 1.3 %collective-permute-start.5 = (f32[136,128]{1,0:T(8,128)S(1)}, f32[136,128]{1,0:T(8,128)S(1)}, u32[]{:S(2)}, u32[]{:S(2)}) collective-permute-start(f32[136,128]{1,0:T(8,128)S(1)} %slice.47), channel_id=1, source_target_pairs={{0,8},{4,12},{8,0},{12,4},{16,24},{20,28},{24,16},{28,20},{1,9},{5... | collective-permute-start | bytes 208904 | tf_op jit(solution)/shard_map/ppermute | solution.py:317
  28.6 2.1 %late_quad.1.refs_3_ = f32[64,2048]{1,0:T(8,128)S(1)} custom-call(f32[64,768]{1,0:T(8,128)S(1)} %collective-permute-done.7.refs_0_, bf16[2048,768]{1,0:T(8,128)(2,1)S(1)} %get-tuple-element.35.refs_3_.refs_1_.high_ref, bf16[2048,768]{1,0:T(8,128)(2,1)S(1)} %get-tuple-element.36.refs_4_.refs_2_.low_ref), custom_call_target="tpu_custom_call" | custom-call | flops 100000000 | bytes 1000000 | tf_op jit(solution)/shard_map/late_quad/pallas_call | solution.py:206
  31.4 1.4 %late_head.1.refs_3_ = f32[64,2048]{1,0:T(8,128)S(1)} custom-call(f32[256,128]{1,0:T(8,128)S(1)} %collective-permute-done.6.refs_0_, bf16[2048,768]{1,0:T(8,128)(2,1)S(1)} %get-tuple-element.33.refs_3_.refs_1_.high_ref, bf16[2048,768]{1,0:T(8,128)(2,1)S(1)} %get-tuple-element.34.refs_4_.refs_2_.low_ref, f32[64,2048]{1,0:T(8,128)S(1)} %late_quad.1.refs_3_), custom_call_target="tpu_custom_call" | custom-call | flops 100000000 | bytes 1000000 | tf_op jit(solution)/shard_map/late_head/pallas_call | solution.py:206
  33.7 1.2 %collective-permute-done.8 = f32[2,2,1024]{2,1,0:T(2,128)S(1)} collective-permute-done((f32[2,2,1024]{2,1,0:T(2,128)S(1)}, f32[2,2,1024]{2,1,0:T(2,128)S(1)}, u32[]{:S(2)}, u32[]{:S(2)}) %collective-permute-start.8) | collective-permute-done | bytes 16416 | tf_op jit(solution)/shard_map/ppermute | solution.py:317
  35.0 2.6 %collective-permute-start.11 = (f32[2,2,1024]{2,1,0:T(2,128)S(1)}, f32[2,2,1024]{2,1,0:T(2,128)S(1)}, u32[]{:S(2)}, u32[]{:S(2)}) collective-permute-start(f32[2,2,1024]{2,1,0:T(2,128)S(1)} %pad_maximum_fusion), channel_id=1, source_target_pairs={{0,3},{1,2},{2,1},{3,0},{4,7},{5,6},{6,5},{7,4},{8,11},{9,10},{10,... | collective-permute-start | bytes 49160 | tf_op jit(solution)/shard_map/ppermute | solution.py:317
  39.7 1.6 %collective-permute-done.10 = f32[2,2,1024]{2,1,0:T(2,128)S(1)} collective-permute-done((f32[2,2,1024]{2,1,0:T(2,128)S(1)}, f32[2,2,1024]{2,1,0:T(2,128)S(1)}, u32[]{:S(2)}, u32[]{:S(2)}) %collective-permute-start.10) | collective-permute-done | bytes 16416 | tf_op jit(solution)/shard_map/ppermute | solution.py:317
  41.9 2.7 %first_moments.1 = (f32[392,128]{1,0:T(8,128)S(1)}, f32[392,128]{1,0:T(8,128)S(1)}, f32[392,128]{1,0:T(8,128)S(1)}, f32[392,128]{1,0:T(8,128)S(1)}, bf16[512,2048]{1,0:T(8,128)(2,1)S(1)}) custom-call(f32[192,2048]{1,0:T(8,128)S(1)} %get-tuple-element.37.early_ref, f32[64,2048]{1,0:T(8,128)S(1)} %get-tuple-element.42.late_ref, ...), custom_call_target="tpu_custom_call" | custom-call | flops 10000000000 | bytes 100000000 | tf_op jit(solution)/shard_map/first_moments/pallas_call | solution.py:247
  44.6 1.2 %collective-permute-start.12 = (f32[392,128]{1,0:T(8,128)S(1)}, f32[392,128]{1,0:T(8,128)S(1)}, u32[]{:S(2)}, u32[]{:S(2)}) collective-permute-start(f32[392,128]{1,0:T(8,128)S(1)} %get-tuple-element.46), channel_id=1, source_target_pairs={{0,8},{4,12},{8,0},{12,4},{16,24},{20,28},{24,16},{28,20},{1,9},{5... | collective-permute-start | bytes 602120 | tf_op jit(solution)/shard_map/ppermute | solution.py:317
  45.8 2.6 %second_moments.1 = (f32[384,128]{1,0:T(8,128)S(1)}, f32[384,128]{1,0:T(8,128)S(1)}, f32[384,128]{1,0:T(8,128)S(1)}, f32[384,128]{1,0:T(8,128)S(1)}) custom-call(bf16[512,2048]{1,0:T(8,128)(2,1)S(1)} %get-tuple-element.47.resp_ref, bf16[2048,768]{1,0:T(8,128)(2,1)S(1)} %get-tuple-element.35.refs_3_.refs_1_.high_ref, ...), custom_call_target="tpu_custom_call" | custom-call | flops 10000000000 | bytes 100000000 | tf_op jit(solution)/shard_map/second_moments/pallas_call | solution.py:262
  48.4 1.9 %collective-permute-done.12 = f32[392,128]{1,0:T(8,128)S(1)} collective-permute-done((f32[392,128]{1,0:T(8,128)S(1)}, f32[392,128]{1,0:T(8,128)S(1)}, u32[]{:S(2)}, u32[]{:S(2)}) %collective-permute-start.12) | collective-permute-done | bytes 200736 | tf_op jit(solution)/shard_map/ppermute | solution.py:317
  50.4 1.2 %collective-permute-start.14 = (f32[384,128]{1,0:T(8,128)S(1)}, f32[384,128]{1,0:T(8,128)S(1)}, u32[]{:S(2)}, u32[]{:S(2)}) collective-permute-start(f32[384,128]{1,0:T(8,128)S(1)} %get-tuple-element.52), channel_id=1, source_target_pairs={{0,8},{4,12},{8,0},{12,4},{16,24},{20,28},{24,16},{28,20},{1,9},{5... | collective-permute-start | bytes 589832 | tf_op jit(solution)/shard_map/ppermute | solution.py:317
  51.6 1.7 %collective-permute-start.13 = (f32[392,128]{1,0:T(8,128)S(1)}, f32[392,128]{1,0:T(8,128)S(1)}, u32[]{:S(2)}, u32[]{:S(2)}) collective-permute-start(f32[392,128]{1,0:T(8,128)S(1)} %add.33), channel_id=1, source_target_pairs={{0,16},{4,20},{8,24},{12,28},{16,0},{20,4},{24,8},{28,12},{1,17},{... | collective-permute-start | bytes 602120 | tf_op jit(solution)/shard_map/ppermute | solution.py:317
  53.4 5.7 %collective-permute-done.14 = f32[384,128]{1,0:T(8,128)S(1)} collective-permute-done((f32[384,128]{1,0:T(8,128)S(1)}, f32[384,128]{1,0:T(8,128)S(1)}, u32[]{:S(2)}, u32[]{:S(2)}) %collective-permute-start.14) | collective-permute-done | bytes 196640 | tf_op jit(solution)/shard_map/ppermute | solution.py:317
  59.2 2.0 %collective-permute-start.16 = (f32[384,128]{1,0:T(8,128)S(1)}, f32[384,128]{1,0:T(8,128)S(1)}, u32[]{:S(2)}, u32[]{:S(2)}) collective-permute-start(f32[384,128]{1,0:T(8,128)S(1)} %get-tuple-element.55), channel_id=1, source_target_pairs={{0,8},{4,12},{8,0},{12,4},{16,24},{20,28},{24,16},{28,20},{1,9},{5... | collective-permute-start | bytes 589832 | tf_op jit(solution)/shard_map/ppermute | solution.py:317
  61.2 2.6 %collective-permute-start.17 = (f32[384,128]{1,0:T(8,128)S(1)}, f32[384,128]{1,0:T(8,128)S(1)}, u32[]{:S(2)}, u32[]{:S(2)}) collective-permute-start(f32[384,128]{1,0:T(8,128)S(1)} %add.35), channel_id=1, source_target_pairs={{0,16},{4,20},{8,24},{12,28},{16,0},{20,4},{24,8},{28,12},{1,17},{... | collective-permute-start | bytes 589832 | tf_op jit(solution)/shard_map/ppermute | solution.py:317
  63.9 7.8 %collective-permute-done.16.near_second_ref = f32[384,128]{1,0:T(8,128)S(1)} collective-permute-done((f32[384,128]{1,0:T(8,128)S(1)}, f32[384,128]{1,0:T(8,128)S(1)}, u32[]{:S(2)}, u32[]{:S(2)}) %collective-permute-start.16) | collective-permute-done | bytes 196640 | tf_op jit(solution)/shard_map/ppermute | solution.py:317
  (41 shorter events, 10.0 us)
Async XLA Ops:
  0.6 7.7 %collective-permute-start.2 = (f32[1024,768]{1,0:T(8,128)}, f32[1024,768]{1,0:T(8,128)S(1)}, u32[]{:S(2)}, u32[]{:S(2)}) collective-permute-start(f32[1024,768]{1,0:T(8,128)} %own_ref.1), channel_id=1, source_target_pairs={{0,4},{4,0},{8,12},{12,8},{16,20},{20,16},{24,28},{28,24},{1,5},{5... | collective-permute-start | bytes 9437192 | tf_op jit(solution)/shard_map/ppermute | solution.py:317
  1.1 13.9 %collective-permute-start.4 = (f32[64,768]{1,0:T(8,128)}, f32[64,768]{1,0:T(8,128)S(1)}, u32[]{:S(2)}, u32[]{:S(2)}) collective-permute-start(f32[64,768]{1,0:T(8,128)} %variances_ref.1), channel_id=1, source_target_pairs={{0,16},{4,20},{8,24},{12,28},{16,0},{20,4},{24,8},{28,12},{1,17},{... | collective-permute-start | bytes 589832 | tf_op jit(solution)/shard_map/ppermute | solution.py:317
  4.8 12.2 %collective-permute-start.3 = (f32[64,768]{1,0:T(8,128)}, f32[64,768]{1,0:T(8,128)S(1)}, u32[]{:S(2)}, u32[]{:S(2)}) collective-permute-start(f32[64,768]{1,0:T(8,128)} %variances_ref.1), channel_id=1, source_target_pairs={{0,8},{4,12},{8,0},{12,4},{16,24},{20,28},{24,16},{28,20},{1,9},{5... | collective-permute-start | bytes 589832 | tf_op jit(solution)/shard_map/ppermute | solution.py:317
  6.4 2.1 %copy-start = (f32[1024,768]{1,0:T(8,128)S(1)}, f32[1024,768]{1,0:T(8,128)}, u32[]{:S(2)}) copy-start(f32[1024,768]{1,0:T(8,128)} %own_ref.1) | copy-start | bytes 9437188
  7.7 9.2 %copy-start.2 = (f32[64,768]{1,0:T(8,128)S(1)}, f32[64,768]{1,0:T(8,128)}, u32[]{:S(2)}) copy-start(f32[64,768]{1,0:T(8,128)} %variances_ref.1) | copy-start | bytes 589828
  7.8 15.7 %collective-permute-start.1 = (f32[392,128]{1,0:T(8,128)S(1)}, f32[392,128]{1,0:T(8,128)S(1)}, u32[]{:S(2)}, u32[]{:S(2)}) collective-permute-start(f32[392,128]{1,0:T(8,128)S(1)} %coefficients.1.refs_0_), channel_id=1, source_target_pairs={{0,16},{4,20},{8,24},{12,28},{16,0},{20,4},{24,8},{28,12},{1,17},{... | collective-permute-start | bytes 602120 | tf_op jit(solution)/shard_map/ppermute | solution.py:317
  8.2 16.2 %collective-permute-start = (f32[392,128]{1,0:T(8,128)S(1)}, f32[392,128]{1,0:T(8,128)S(1)}, u32[]{:S(2)}, u32[]{:S(2)}) collective-permute-start(f32[392,128]{1,0:T(8,128)S(1)} %coefficients.1.refs_0_), channel_id=1, source_target_pairs={{0,8},{4,12},{8,0},{12,4},{16,24},{20,28},{24,16},{28,20},{1,9},{5... | collective-permute-start | bytes 602120 | tf_op jit(solution)/shard_map/ppermute | solution.py:317
  15.1 13.5 %collective-permute-start.7 = (f32[64,768]{1,0:T(8,128)S(1)}, f32[64,768]{1,0:T(8,128)S(1)}, u32[]{:S(2)}, u32[]{:S(2)}) collective-permute-start(f32[64,768]{1,0:T(8,128)S(1)} %collective-permute-done.4.refs_2_), channel_id=1, source_target_pairs={{0,8},{4,12},{8,0},{12,4},{16,24},{20,28},{24,16},{28,20},{1,9},{5... | collective-permute-start | bytes 589832 | tf_op jit(solution)/shard_map/ppermute | solution.py:317
  23.5 7.9 %collective-permute-start.6 = (f32[256,128]{1,0:T(8,128)S(1)}, f32[256,128]{1,0:T(8,128)S(1)}, u32[]{:S(2)}, u32[]{:S(2)}) collective-permute-start(f32[256,128]{1,0:T(8,128)S(1)} %slice.48), channel_id=1, source_target_pairs={{0,8},{4,12},{8,0},{12,4},{16,24},{20,28},{24,16},{28,20},{1,9},{5... | collective-permute-start | bytes 393224 | tf_op jit(solution)/shard_map/ppermute | solution.py:317
  26.9 5.9 %collective-permute-start.5 = (f32[136,128]{1,0:T(8,128)S(1)}, f32[136,128]{1,0:T(8,128)S(1)}, u32[]{:S(2)}, u32[]{:S(2)}) collective-permute-start(f32[136,128]{1,0:T(8,128)S(1)} %slice.47), channel_id=1, source_target_pairs={{0,8},{4,12},{8,0},{12,4},{16,24},{20,28},{24,16},{28,20},{1,9},{5... | collective-permute-start | bytes 208904 | tf_op jit(solution)/shard_map/ppermute | solution.py:317
  33.6 1.2 %collective-permute-start.8 = (f32[2,2,1024]{2,1,0:T(2,128)S(1)}, f32[2,2,1024]{2,1,0:T(2,128)S(1)}, u32[]{:S(2)}, u32[]{:S(2)}) collective-permute-start(f32[2,2,1024]{2,1,0:T(2,128)S(1)} %get-tuple-element.43), channel_id=1, source_target_pairs={{0,4},{4,0},{8,12},{12,8},{16,20},{20,16},{24,28},{28,24},{1,5},{5... | collective-permute-start | bytes 49160 | tf_op jit(solution)/shard_map/ppermute | solution.py:317
  35.0 4.7 %collective-permute-start.11 = (f32[2,2,1024]{2,1,0:T(2,128)S(1)}, f32[2,2,1024]{2,1,0:T(2,128)S(1)}, u32[]{:S(2)}, u32[]{:S(2)}) collective-permute-start(f32[2,2,1024]{2,1,0:T(2,128)S(1)} %pad_maximum_fusion), channel_id=1, source_target_pairs={{0,3},{1,2},{2,1},{3,0},{4,7},{5,6},{6,5},{7,4},{8,11},{9,10},{10,... | collective-permute-start | bytes 49160 | tf_op jit(solution)/shard_map/ppermute | solution.py:317
  37.6 3.7 %collective-permute-start.10 = (f32[2,2,1024]{2,1,0:T(2,128)S(1)}, f32[2,2,1024]{2,1,0:T(2,128)S(1)}, u32[]{:S(2)}, u32[]{:S(2)}) collective-permute-start(f32[2,2,1024]{2,1,0:T(2,128)S(1)} %pad_maximum_fusion), channel_id=1, source_target_pairs={{0,2},{1,3},{2,0},{3,1},{4,6},{5,7},{6,4},{7,5},{8,10},{9,11},{10,... | collective-permute-start | bytes 49160 | tf_op jit(solution)/shard_map/ppermute | solution.py:317
  38.1 3.7 %collective-permute-start.9 = (f32[2,2,1024]{2,1,0:T(2,128)S(1)}, f32[2,2,1024]{2,1,0:T(2,128)S(1)}, u32[]{:S(2)}, u32[]{:S(2)}) collective-permute-start(f32[2,2,1024]{2,1,0:T(2,128)S(1)} %pad_maximum_fusion), channel_id=1, source_target_pairs={{0,1},{1,0},{2,3},{3,2},{4,5},{5,4},{6,7},{7,6},{8,9},{9,8},{10,11... | collective-permute-start | bytes 49160 | tf_op jit(solution)/shard_map/ppermute | solution.py:317
  44.6 5.8 %collective-permute-start.12 = (f32[392,128]{1,0:T(8,128)S(1)}, f32[392,128]{1,0:T(8,128)S(1)}, u32[]{:S(2)}, u32[]{:S(2)}) collective-permute-start(f32[392,128]{1,0:T(8,128)S(1)} %get-tuple-element.46), channel_id=1, source_target_pairs={{0,8},{4,12},{8,0},{12,4},{16,24},{20,28},{24,16},{28,20},{1,9},{5... | collective-permute-start | bytes 602120 | tf_op jit(solution)/shard_map/ppermute | solution.py:317
  45.8 25.8 %copy-start.1 = (f32[64,768]{1,0:T(8,128)S(1)}, f32[64,768]{1,0:T(8,128)}, u32[]{:S(2)}) copy-start(f32[64,768]{1,0:T(8,128)} %means_ref.1) | copy-start | bytes 589828
  45.8 25.8 %copy-start.3 = (f32[64]{0:T(128)S(1)}, f32[64]{0:T(128)}, u32[]{:S(2)}) copy-start(f32[64]{0:T(128)} %param.7) | copy-start | bytes 772
  50.4 8.7 %collective-permute-start.14 = (f32[384,128]{1,0:T(8,128)S(1)}, f32[384,128]{1,0:T(8,128)S(1)}, u32[]{:S(2)}, u32[]{:S(2)}) collective-permute-start(f32[384,128]{1,0:T(8,128)S(1)} %get-tuple-element.52), channel_id=1, source_target_pairs={{0,8},{4,12},{8,0},{12,4},{16,24},{20,28},{24,16},{28,20},{1,9},{5... | collective-permute-start | bytes 589832 | tf_op jit(solution)/shard_map/ppermute | solution.py:317
  51.6 12.2 %collective-permute-start.13 = (f32[392,128]{1,0:T(8,128)S(1)}, f32[392,128]{1,0:T(8,128)S(1)}, u32[]{:S(2)}, u32[]{:S(2)}) collective-permute-start(f32[392,128]{1,0:T(8,128)S(1)} %add.33), channel_id=1, source_target_pairs={{0,16},{4,20},{8,24},{12,28},{16,0},{20,4},{24,8},{28,12},{1,17},{... | collective-permute-start | bytes 602120 | tf_op jit(solution)/shard_map/ppermute | solution.py:317
  59.1 12.5 %collective-permute-start.15 = (f32[392,128]{1,0:T(8,128)S(1)}, f32[392,128]{1,0:T(8,128)S(1)}, u32[]{:S(2)}, u32[]{:S(2)}) collective-permute-start(f32[392,128]{1,0:T(8,128)S(1)} %get-tuple-element.53), channel_id=1, source_target_pairs={{0,8},{4,12},{8,0},{12,4},{16,24},{20,28},{24,16},{28,20},{1,9},{5... | collective-permute-start | bytes 602120 | tf_op jit(solution)/shard_map/ppermute | solution.py:317
  59.2 12.4 %collective-permute-start.16 = (f32[384,128]{1,0:T(8,128)S(1)}, f32[384,128]{1,0:T(8,128)S(1)}, u32[]{:S(2)}, u32[]{:S(2)}) collective-permute-start(f32[384,128]{1,0:T(8,128)S(1)} %get-tuple-element.55), channel_id=1, source_target_pairs={{0,8},{4,12},{8,0},{12,4},{16,24},{20,28},{24,16},{28,20},{1,9},{5... | collective-permute-start | bytes 589832 | tf_op jit(solution)/shard_map/ppermute | solution.py:317
  61.2 10.4 %collective-permute-start.17 = (f32[384,128]{1,0:T(8,128)S(1)}, f32[384,128]{1,0:T(8,128)S(1)}, u32[]{:S(2)}, u32[]{:S(2)}) collective-permute-start(f32[384,128]{1,0:T(8,128)S(1)} %add.35), channel_id=1, source_target_pairs={{0,16},{4,20},{8,24},{12,28},{16,0},{20,4},{24,8},{28,12},{1,17},{... | collective-permute-start | bytes 589832 | tf_op jit(solution)/shard_map/ppermute | solution.py:317

commit v6 on v5

--- a/solution.py
+++ b/solution.py
@@ -317,21 +317,16 @@
     return lax.ppermute(value, axis, [(i, i ^ bit) for i in range(size)])
 
 
-def vmem(value):
-    return pltpu.with_memory_space_constraint(value, pltpu.VMEM)
-
-
 def after(value, *others):
     return lax.optimization_barrier((value, *others))[0]
 
 
-def gather_early(piece):
+def gather_even(piece):
     bit = lax.axis_size("dp") // 4
     held = {0: piece}
     while bit > 1:
         held.update({q ^ bit: swap(value, "dp", 2 * bit) for q, value in held.items()})
         bit //= 2
-    held[1] = swap(piece, "dp", 2)
     return held
 
 
@@ -363,58 +358,54 @@
     n = comp_means.shape[0]
     rows, width = embeddings.shape
     planes = lax.axis_size("dp") // 2
-    variances = gather_early(comp_variances)
-    linear = gather_early(coefficients(comp_means, comp_variances, comp_mass))
+    variances = gather_even(comp_variances)
+    near = swap(comp_variances, "dp", 2)
+    pack = coefficients(comp_means, comp_variances, comp_mass)
+    linear = [pack] + [swap(pack, "dp", 2 * q) for q in reversed(range(2, planes))][::-1]
     other = swap(embeddings, "dp", 1)
-    order = sorted(linear)
-    late = [q for q in range(planes) if q not in linear]
     x_high, x_low, s_high, s_low = halves(embeddings, other)
-    for q in late:
-        variances[q] = swap(after(variances[q ^ 1], x_high), "dp", 2)
-    n_early, n_late = n * len(order), n * len(late)
-
-    def quad_scores(group, name, cost=None):
+    far = {q ^ 1: swap(after(variances[q], x_high), "dp", 2) for q in sorted(variances) if q}
+    variances = [{**variances, **far}[q] for q in range(planes) if q != 1]
+    n_early = n * len(linear)
+
+    def quad_scores(group, name):
         comps = n * len(group)
-        operands = (*(vmem(variances[q]) for q in group), s_high, s_low)
         body = functools.partial(quad_kernel, n)
-        return score_call(body, [(comps, 2 * rows)], [(2 * comps, width)], name, *operands, cost=cost)[0]
-
-    quad = quad_scores(order, "early_quad")
+        shapes = [(comps, 2 * rows)], [(2 * comps, width)]
+        return score_call(body, *shapes, name, *group, s_high, s_low)[0]
+
     head = width // LANES * 2 // 3
-    heads, tails = [], []
-    for q in late:
-        source = after(linear[q ^ 1], quad)
-        heads.append(vmem(swap(source[: head * n], "dp", 2)))
-        tails.append(source[head * n :])
+    late_head = swap(pack[: head * n], "dp", 2)
+    late_quad = quad_scores([near], "late_quad")
+    late_tail = swap(after(pack[head * n :], late_quad), "dp", 2)
     early, early_stats = score_call(
         functools.partial(early_kernel, n),
         [(n_early, 2 * rows), (2, 2 * rows)],
         [(2 * n_early, width)],
         "early_scores",
-        *(vmem(linear[q]) for q in order),
+        *linear,
         x_high,
         x_low,
-        quad,
+        quad_scores(variances, "early_quad"),
         cost=LIGHT,
     )
-    tails = [vmem(swap(after(tail, early), "dp", 2)) for tail in tails]
     (part,) = score_call(
         functools.partial(head_kernel, n),
-        [(n_late, 2 * rows)],
-        [(2 * n_late, head * LANES)],
+        [(n, 2 * rows)],
+        [(2 * n, head * LANES)],
         "late_head",
-        *heads,
+        late_head,
         x_high,
         x_low,
-        quad_scores(late, "late_quad", LIGHT),
+        late_quad,
         cost=LIGHT,
     )
     last, stats = score_call(
         functools.partial(last_kernel, n),
-        [(n_late, 2 * rows), (2, 2, rows)],
-        [(2 * n_late, width - head * LANES)],
+        [(n, 2 * rows), (2, 2, rows)],
+        [(2 * n, width - head * LANES)],
         "last_scores",
-        *tails,
+        late_tail,
         x_high,
         x_low,
         part,
@@ -425,7 +416,7 @@
 
     *first, resp = first_moments(early, last, stats, x_high, x_low, n)
     second = second_moments(resp, s_high, s_low, n)
-    place = {q: i for i, q in enumerate(order + late)}
+    place = {q: i for i, q in enumerate([0, *range(2, planes), 1])}
     first, second = ([parts[place[q]] for q in range(planes)] for parts in (first, second))
     sums = scatter_planes(first, second)
 

time: 72.7 us -> 76 us (1.045)
  starting transfers between devices: 21.8 us -> 24.5 us
    ppermute x18, starting transfers between devices: 21.8 us -> 24.5 us  [swap(): return lax.ppermute(value, axis, [(i, i ^ bit) for i in range(size)])]
  transfers between devices with their start and end apart: 18 -> 18, of which waited for: 13 -> 11; matrix products, arithmetic and copies ran while one was open for 0% -> 0% of each run, Pallas kernels for 20% -> 19%
where the time goes in v6:
time: 76 us; the launch traced here: 75.9 us
  waiting for transfers between devices  31.3 us (41%)
  starting transfers between devices  24.5 us (32%)
  Pallas kernels  19 us (25%)
  between operations  0.78 us (1%)
    ppermute x18, waiting for transfers between devices, swap(): return lax.ppermute(value, axis, [(i, i ^ bit) for i in range(size)])  31.3 us
    ppermute x18, starting transfers between devices, swap(): return lax.ppermute(value, axis, [(i, i ^ bit) for i in range(size)])  24.5 us
    pallas_call x5, Pallas kernels, score_call(): pl.pallas_call(body, out_shape=[jax.ShapeDtypeStruct(shape, F32) for shap...  9.21 us
    pallas_call x1, Pallas kernels, first_moments(): pl.pallas_call(functools.partial(first_kernel, n), out_shape=[pack] * (co...  2.65 us
    pallas_call x1, Pallas kernels, second_moments(): pl.pallas_call(functools.partial(second_kernel, n), out_shape=[pack] * (r...  2.63 us
    pallas_call x1, Pallas kernels, halves(): pl.pallas_call(halves_kernel, grid=(2 * steps,), in_specs=[pl.BlockSpec((...  2.25 us
  transfers between devices with their start and end apart: 18, of which 11 were waited for; matrix products, arithmetic and copies ran while one was open for 0% of the time, Pallas kernels for 19%

profile of v6, /device:TPU:0, one launch (start us, length us, event | category | flops | bytes accessed | tf_op | source)
XLA Modules:
  0.0 75.9 jit_solution(6198855249662095537)
XLA Ops:
  1.1 3.7 %collective-permute-start.3 = (f32[64,768]{1,0:T(8,128)}, f32[64,768]{1,0:T(8,128)S(1)}, u32[]{:S(2)}, u32[]{:S(2)}) collective-permute-start(f32[64,768]{1,0:T(8,128)} %variances_ref.1), channel_id=1, source_target_pairs={{0,16},{4,20},{8,24},{12,28},{16,0},{20,4},{24,8},{28,12},{1,17},{... | collective-permute-start | bytes 589832 | tf_op jit(solution)/shard_map/ppermute | solution.py:317
  4.8 1.6 %collective-permute-start.5 = (f32[64,768]{1,0:T(8,128)}, f32[64,768]{1,0:T(8,128)S(1)}, u32[]{:S(2)}, u32[]{:S(2)}) collective-permute-start(f32[64,768]{1,0:T(8,128)} %variances_ref.1), channel_id=1, source_target_pairs={{0,8},{4,12},{8,0},{12,4},{16,24},{20,28},{24,16},{28,20},{1,9},{5... | collective-permute-start | bytes 589832 | tf_op jit(solution)/shard_map/ppermute | solution.py:317
  6.4 1.3 %coefficients.1.refs_0_ = f32[392,128]{1,0:T(8,128)S(1)} custom-call(f32[64,768]{1,0:T(8,128)} %means_ref.1, f32[64,768]{1,0:T(8,128)} %variances_ref.1, f32[1,64]{1,0:T(1,128)} %bitcast.2), custom_call_target="tpu_custom_call" | custom-call | flops 10000000000 | bytes 100000000 | tf_op jit(solution)/shard_map/coefficients/pallas_call | solution.py:64
  7.8 1.9 %collective-permute-start = (f32[392,128]{1,0:T(8,128)S(1)}, f32[392,128]{1,0:T(8,128)S(1)}, u32[]{:S(2)}, u32[]{:S(2)}) collective-permute-start(f32[392,128]{1,0:T(8,128)S(1)} %coefficients.1.refs_0_), channel_id=1, source_target_pairs={{0,16},{4,20},{8,24},{12,28},{16,0},{20,4},{24,8},{28,12},{1,17},{... | collective-permute-start | bytes 602120 | tf_op jit(solution)/shard_map/ppermute | solution.py:317
  9.8 2.5 %collective-permute-start.7 = (f32[256,128]{1,0:T(8,128)S(1)}, f32[256,128]{1,0:T(8,128)S(1)}, u32[]{:S(2)}, u32[]{:S(2)}) collective-permute-start(f32[256,128]{1,0:T(8,128)S(1)} %slice.62), channel_id=1, source_target_pairs={{0,8},{4,12},{8,0},{12,4},{16,24},{20,28},{24,16},{28,20},{1,9},{5... | collective-permute-start | bytes 393224 | tf_op jit(solution)/shard_map/ppermute | solution.py:317
  12.3 2.2 %halves.1 = (bf16[2048,768]{1,0:T(8,128)(2,1)S(1)}, bf16[2048,768]{1,0:T(8,128)(2,1)S(1)}, bf16[2048,768]{1,0:T(8,128)(2,1)S(1)}, bf16[2048,768]{1,0:T(8,128)(2,1)S(1)}) custom-call(f32[1024,768]{1,0:T(8,128)S(1)} %copy-done, f32[1024,768]{1,0:T(8,128)S(1)} %collective-permute-done.2.other_ref), custom_call_target="tpu_custom_call" | custom-call | flops 10000000000 | bytes 100000000 | tf_op jit(solution)/shard_map/halves/pallas_call | solution.py:101
  15.9 2.1 %late_quad.1.refs_3_ = f32[64,2048]{1,0:T(8,128)S(1)} custom-call(f32[64,768]{1,0:T(8,128)S(1)} %collective-permute-done.5.refs_0_, bf16[2048,768]{1,0:T(8,128)(2,1)S(1)} %get-tuple-element.35.refs_3_.refs_1_.high_ref, bf16[2048,768]{1,0:T(8,128)(2,1)S(1)} %get-tuple-element.36.refs_4_.refs_2_.low_ref), custom_call_target="tpu_custom_call" | custom-call | flops 10000000000 | bytes 100000000 | tf_op jit(solution)/shard_map/late_quad/pallas_call | solution.py:206
  18.0 1.2 %collective-permute-start.6 = (f32[136,128]{1,0:T(8,128)S(1)}, f32[136,128]{1,0:T(8,128)S(1)}, u32[]{:S(2)}, u32[]{:S(2)}) collective-permute-start(f32[136,128]{1,0:T(8,128)S(1)} %slice.61), channel_id=1, source_target_pairs={{0,8},{4,12},{8,0},{12,4},{16,24},{20,28},{24,16},{28,20},{1,9},{5... | collective-permute-start | bytes 208904 | tf_op jit(solution)/shard_map/ppermute | solution.py:317
  19.2 6.8 %collective-permute-done.7.refs_0_ = f32[256,128]{1,0:T(8,128)S(1)} collective-permute-done((f32[256,128]{1,0:T(8,128)S(1)}, f32[256,128]{1,0:T(8,128)S(1)}, u32[]{:S(2)}, u32[]{:S(2)}) %collective-permute-start.7) | collective-permute-done | bytes 131104 | tf_op jit(solution)/shard_map/ppermute | solution.py:317
  26.0 1.4 %late_head.1.refs_3_ = f32[64,2048]{1,0:T(8,128)S(1)} custom-call(f32[256,128]{1,0:T(8,128)S(1)} %collective-permute-done.7.refs_0_, bf16[2048,768]{1,0:T(8,128)(2,1)S(1)} %get-tuple-element.32.refs_3_.refs_1_.high_ref, bf16[2048,768]{1,0:T(8,128)(2,1)S(1)} %get-tuple-element.33.refs_4_.refs_2_.low_ref, f32[64,2048]{1,0:T(8,128)S(1)} %late_quad.1.refs_3_), custom_call_target="tpu_custom_call" | custom-call | flops 100000000 | bytes 1000000 | tf_op jit(solution)/shard_map/late_head/pallas_call | solution.py:206
  27.4 2.8 %collective-permute-done.4.refs_2_ = f32[64,768]{1,0:T(8,128)S(1)} collective-permute-done((f32[64,768]{1,0:T(8,128)S(1)}, f32[64,768]{1,0:T(8,128)S(1)}, u32[]{:S(2)}, u32[]{:S(2)}) %collective-permute-start.4) | collective-permute-done | bytes 196640 | tf_op jit(solution)/shard_map/ppermute | solution.py:317
  30.2 2.4 %early_quad.1.refs_5_ = f32[192,2048]{1,0:T(8,128)S(1)} custom-call(f32[64,768]{1,0:T(8,128)S(1)} %copy-done.2, f32[64,768]{1,0:T(8,128)S(1)} %collective-permute-done.3.refs_1_, f32[64,768]{1,0:T(8,128)S(1)} %collective-permute-done.4.refs_2_, bf16[2048,768]{1,0:T(8,128)(2,1)S(1)} %get-tuple-element.35.refs_3_.refs_1_.high_ref, ...), custom_call_target="tpu_custom_call" | custom-call | flops 10000000000 | bytes 100000000 | tf_op jit(solution)/shard_map/early_quad/pallas_call | solution.py:206
  32.6 2.5 %early_scores.1 = (f32[192,2048]{1,0:T(8,128)S(1)}, f32[2,2048]{1,0:T(2,128)S(1)}) custom-call(f32[392,128]{1,0:T(8,128)S(1)} %coefficients.1.refs_0_, f32[392,128]{1,0:T(8,128)S(1)} %collective-permute-done.refs_1_, f32[392,128]{1,0:T(8,128)S(1)} %collective-permute-done.1.refs_2_, bf16[2048,768]{1,0:T(8,128)(2,1)S(1)} %get-tuple-element.32.refs_3_.refs_1_.high_ref, ...), custom_call_target="tpu_custom_call" | custom-call | flops 100000000 | bytes 1000000 | tf_op jit(solution)/shard_map/early_scores/pallas_call | solution.py:206
  36.0 1.2 %collective-permute-done.8 = f32[2,2,1024]{2,1,0:T(2,128)S(1)} collective-permute-done((f32[2,2,1024]{2,1,0:T(2,128)S(1)}, f32[2,2,1024]{2,1,0:T(2,128)S(1)}, u32[]{:S(2)}, u32[]{:S(2)}) %collective-permute-start.8) | collective-permute-done | bytes 16416 | tf_op jit(solution)/shard_map/ppermute | solution.py:317
  37.3 2.5 %collective-permute-start.11 = (f32[2,2,1024]{2,1,0:T(2,128)S(1)}, f32[2,2,1024]{2,1,0:T(2,128)S(1)}, u32[]{:S(2)}, u32[]{:S(2)}) collective-permute-start(f32[2,2,1024]{2,1,0:T(2,128)S(1)} %pad_maximum_fusion), channel_id=1, source_target_pairs={{0,3},{1,2},{2,1},{3,0},{4,7},{5,6},{6,5},{7,4},{8,11},{9,10},{10,... | collective-permute-start | bytes 49160 | tf_op jit(solution)/shard_map/ppermute | solution.py:317
  40.8 1.1 %collective-permute-done.11 = f32[2,2,1024]{2,1,0:T(2,128)S(1)} collective-permute-done((f32[2,2,1024]{2,1,0:T(2,128)S(1)}, f32[2,2,1024]{2,1,0:T(2,128)S(1)}, u32[]{:S(2)}, u32[]{:S(2)}) %collective-permute-start.11) | collective-permute-done | bytes 16416 | tf_op jit(solution)/shard_map/ppermute | solution.py:317
  42.0 1.5 %collective-permute-done.10 = f32[2,2,1024]{2,1,0:T(2,128)S(1)} collective-permute-done((f32[2,2,1024]{2,1,0:T(2,128)S(1)}, f32[2,2,1024]{2,1,0:T(2,128)S(1)}, u32[]{:S(2)}, u32[]{:S(2)}) %collective-permute-start.10) | collective-permute-done | bytes 16416 | tf_op jit(solution)/shard_map/ppermute | solution.py:317
  44.1 2.7 %first_moments.1 = (f32[392,128]{1,0:T(8,128)S(1)}, f32[392,128]{1,0:T(8,128)S(1)}, f32[392,128]{1,0:T(8,128)S(1)}, f32[392,128]{1,0:T(8,128)S(1)}, bf16[512,2048]{1,0:T(8,128)(2,1)S(1)}) custom-call(f32[192,2048]{1,0:T(8,128)S(1)} %get-tuple-element.37.early_ref, f32[64,2048]{1,0:T(8,128)S(1)} %get-tuple-element.40.late_ref, ...), custom_call_target="tpu_custom_call" | custom-call | flops 10000000000 | bytes 100000000 | tf_op jit(solution)/shard_map/first_moments/pallas_call | solution.py:247
  46.8 2.6 %collective-permute-start.12 = (f32[392,128]{1,0:T(8,128)S(1)}, f32[392,128]{1,0:T(8,128)S(1)}, u32[]{:S(2)}, u32[]{:S(2)}) collective-permute-start(f32[392,128]{1,0:T(8,128)S(1)} %get-tuple-element.44), channel_id=1, source_target_pairs={{0,8},{4,12},{8,0},{12,4},{16,24},{20,28},{24,16},{28,20},{1,9},{5... | collective-permute-start | bytes 602120 | tf_op jit(solution)/shard_map/ppermute | solution.py:317
  49.4 2.6 %second_moments.1 = (f32[384,128]{1,0:T(8,128)S(1)}, f32[384,128]{1,0:T(8,128)S(1)}, f32[384,128]{1,0:T(8,128)S(1)}, f32[384,128]{1,0:T(8,128)S(1)}) custom-call(bf16[512,2048]{1,0:T(8,128)(2,1)S(1)} %get-tuple-element.45.resp_ref, bf16[2048,768]{1,0:T(8,128)(2,1)S(1)} %get-tuple-element.35.refs_3_.refs_1_.high_ref, ...), custom_call_target="tpu_custom_call" | custom-call | flops 10000000000 | bytes 100000000 | tf_op jit(solution)/shard_map/second_moments/pallas_call | solution.py:262
  53.1 2.1 %collective-permute-start.14 = (f32[384,128]{1,0:T(8,128)S(1)}, f32[384,128]{1,0:T(8,128)S(1)}, u32[]{:S(2)}, u32[]{:S(2)}) collective-permute-start(f32[384,128]{1,0:T(8,128)S(1)} %get-tuple-element.50), channel_id=1, source_target_pairs={{0,8},{4,12},{8,0},{12,4},{16,24},{20,28},{24,16},{28,20},{1,9},{5... | collective-permute-start | bytes 589832 | tf_op jit(solution)/shard_map/ppermute | solution.py:317
  56.2 6.0 %collective-permute-done.14 = f32[384,128]{1,0:T(8,128)S(1)} collective-permute-done((f32[384,128]{1,0:T(8,128)S(1)}, f32[384,128]{1,0:T(8,128)S(1)}, u32[]{:S(2)}, u32[]{:S(2)}) %collective-permute-start.14) | collective-permute-done | bytes 196640 | tf_op jit(solution)/shard_map/ppermute | solution.py:317
  63.1 1.2 %collective-permute-start.16 = (f32[384,128]{1,0:T(8,128)S(1)}, f32[384,128]{1,0:T(8,128)S(1)}, u32[]{:S(2)}, u32[]{:S(2)}) collective-permute-start(f32[384,128]{1,0:T(8,128)S(1)} %get-tuple-element.53), channel_id=1, source_target_pairs={{0,8},{4,12},{8,0},{12,4},{16,24},{20,28},{24,16},{28,20},{1,9},{5... | collective-permute-start | bytes 589832 | tf_op jit(solution)/shard_map/ppermute | solution.py:317
  65.6 9.3 %collective-permute-done.16.near_second_ref = f32[384,128]{1,0:T(8,128)S(1)} collective-permute-done((f32[384,128]{1,0:T(8,128)S(1)}, f32[384,128]{1,0:T(8,128)S(1)}, u32[]{:S(2)}, u32[]{:S(2)}) %collective-permute-start.16) | collective-permute-done | bytes 196640 | tf_op jit(solution)/shard_map/ppermute | solution.py:317
  (41 shorter events, 9.9 us)
Async XLA Ops:
  0.6 9.1 %collective-permute-start.2 = (f32[1024,768]{1,0:T(8,128)}, f32[1024,768]{1,0:T(8,128)S(1)}, u32[]{:S(2)}, u32[]{:S(2)}) collective-permute-start(f32[1024,768]{1,0:T(8,128)} %own_ref.1), channel_id=1, source_target_pairs={{0,4},{4,0},{8,12},{12,8},{16,20},{20,16},{24,28},{28,24},{1,5},{5... | collective-permute-start | bytes 9437192 | tf_op jit(solution)/shard_map/ppermute | solution.py:317
  1.1 13.9 %collective-permute-start.3 = (f32[64,768]{1,0:T(8,128)}, f32[64,768]{1,0:T(8,128)S(1)}, u32[]{:S(2)}, u32[]{:S(2)}) collective-permute-start(f32[64,768]{1,0:T(8,128)} %variances_ref.1), channel_id=1, source_target_pairs={{0,16},{4,20},{8,24},{12,28},{16,0},{20,4},{24,8},{28,12},{1,17},{... | collective-permute-start | bytes 589832 | tf_op jit(solution)/shard_map/ppermute | solution.py:317
  4.8 11.1 %collective-permute-start.5 = (f32[64,768]{1,0:T(8,128)}, f32[64,768]{1,0:T(8,128)S(1)}, u32[]{:S(2)}, u32[]{:S(2)}) collective-permute-start(f32[64,768]{1,0:T(8,128)} %variances_ref.1), channel_id=1, source_target_pairs={{0,8},{4,12},{8,0},{12,4},{16,24},{20,28},{24,16},{28,20},{1,9},{5... | collective-permute-start | bytes 589832 | tf_op jit(solution)/shard_map/ppermute | solution.py:317
  6.4 5.9 %copy-start = (f32[1024,768]{1,0:T(8,128)S(1)}, f32[1024,768]{1,0:T(8,128)}, u32[]{:S(2)}) copy-start(f32[1024,768]{1,0:T(8,128)} %own_ref.1) | copy-start | bytes 9437188
  7.7 24.9 %collective-permute-start.1 = (f32[392,128]{1,0:T(8,128)S(1)}, f32[392,128]{1,0:T(8,128)S(1)}, u32[]{:S(2)}, u32[]{:S(2)}) collective-permute-start(f32[392,128]{1,0:T(8,128)S(1)} %coefficients.1.refs_0_), channel_id=1, source_target_pairs={{0,24},{4,28},{8,16},{12,20},{16,8},{20,12},{24,0},{28,4},{1,25},{... | collective-permute-start | bytes 602120 | tf_op jit(solution)/shard_map/ppermute | solution.py:317
  7.8 24.8 %collective-permute-start = (f32[392,128]{1,0:T(8,128)S(1)}, f32[392,128]{1,0:T(8,128)S(1)}, u32[]{:S(2)}, u32[]{:S(2)}) collective-permute-start(f32[392,128]{1,0:T(8,128)S(1)} %coefficients.1.refs_0_), channel_id=1, source_target_pairs={{0,16},{4,20},{8,24},{12,28},{16,0},{20,4},{24,8},{28,12},{1,17},{... | collective-permute-start | bytes 602120 | tf_op jit(solution)/shard_map/ppermute | solution.py:317
  9.8 16.2 %collective-permute-start.7 = (f32[256,128]{1,0:T(8,128)S(1)}, f32[256,128]{1,0:T(8,128)S(1)}, u32[]{:S(2)}, u32[]{:S(2)}) collective-permute-start(f32[256,128]{1,0:T(8,128)S(1)} %slice.62), channel_id=1, source_target_pairs={{0,8},{4,12},{8,0},{12,4},{16,24},{20,28},{24,16},{28,20},{1,9},{5... | collective-permute-start | bytes 393224 | tf_op jit(solution)/shard_map/ppermute | solution.py:317
  15.0 15.1 %collective-permute-start.4 = (f32[64,768]{1,0:T(8,128)S(1)}, f32[64,768]{1,0:T(8,128)S(1)}, u32[]{:S(2)}, u32[]{:S(2)}) collective-permute-start(f32[64,768]{1,0:T(8,128)S(1)} %collective-permute-done.3.refs_1_), channel_id=1, source_target_pairs={{0,8},{4,12},{8,0},{12,4},{16,24},{20,28},{24,16},{28,20},{1,9},{5... | collective-permute-start | bytes 589832 | tf_op jit(solution)/shard_map/ppermute | solution.py:317
  18.0 17.1 %collective-permute-start.6 = (f32[136,128]{1,0:T(8,128)S(1)}, f32[136,128]{1,0:T(8,128)S(1)}, u32[]{:S(2)}, u32[]{:S(2)}) collective-permute-start(f32[136,128]{1,0:T(8,128)S(1)} %slice.61), channel_id=1, source_target_pairs={{0,8},{4,12},{8,0},{12,4},{16,24},{20,28},{24,16},{28,20},{1,9},{5... | collective-permute-start | bytes 208904 | tf_op jit(solution)/shard_map/ppermute | solution.py:317
  26.0 4.2 %copy-start.2 = (f32[64,768]{1,0:T(8,128)S(1)}, f32[64,768]{1,0:T(8,128)}, u32[]{:S(2)}) copy-start(f32[64,768]{1,0:T(8,128)} %variances_ref.1) | copy-start | bytes 589828
  35.9 1.2 %collective-permute-start.8 = (f32[2,2,1024]{2,1,0:T(2,128)S(1)}, f32[2,2,1024]{2,1,0:T(2,128)S(1)}, u32[]{:S(2)}, u32[]{:S(2)}) collective-permute-start(f32[2,2,1024]{2,1,0:T(2,128)S(1)} %get-tuple-element.41), channel_id=1, source_target_pairs={{0,4},{4,0},{8,12},{12,8},{16,20},{20,16},{24,28},{28,24},{1,5},{5... | collective-permute-start | bytes 49160 | tf_op jit(solution)/shard_map/ppermute | solution.py:317
  37.3 4.7 %collective-permute-start.11 = (f32[2,2,1024]{2,1,0:T(2,128)S(1)}, f32[2,2,1024]{2,1,0:T(2,128)S(1)}, u32[]{:S(2)}, u32[]{:S(2)}) collective-permute-start(f32[2,2,1024]{2,1,0:T(2,128)S(1)} %pad_maximum_fusion), channel_id=1, source_target_pairs={{0,3},{1,2},{2,1},{3,0},{4,7},{5,6},{6,5},{7,4},{8,11},{9,10},{10,... | collective-permute-start | bytes 49160 | tf_op jit(solution)/shard_map/ppermute | solution.py:317
  39.8 3.7 %collective-permute-start.10 = (f32[2,2,1024]{2,1,0:T(2,128)S(1)}, f32[2,2,1024]{2,1,0:T(2,128)S(1)}, u32[]{:S(2)}, u32[]{:S(2)}) collective-permute-start(f32[2,2,1024]{2,1,0:T(2,128)S(1)} %pad_maximum_fusion), channel_id=1, source_target_pairs={{0,2},{1,3},{2,0},{3,1},{4,6},{5,7},{6,4},{7,5},{8,10},{9,11},{10,... | collective-permute-start | bytes 49160 | tf_op jit(solution)/shard_map/ppermute | solution.py:317
  40.3 3.7 %collective-permute-start.9 = (f32[2,2,1024]{2,1,0:T(2,128)S(1)}, f32[2,2,1024]{2,1,0:T(2,128)S(1)}, u32[]{:S(2)}, u32[]{:S(2)}) collective-permute-start(f32[2,2,1024]{2,1,0:T(2,128)S(1)} %pad_maximum_fusion), channel_id=1, source_target_pairs={{0,1},{1,0},{2,3},{3,2},{4,5},{5,4},{6,7},{7,6},{8,9},{9,8},{10,11... | collective-permute-start | bytes 49160 | tf_op jit(solution)/shard_map/ppermute | solution.py:317
  46.8 6.2 %collective-permute-start.12 = (f32[392,128]{1,0:T(8,128)S(1)}, f32[392,128]{1,0:T(8,128)S(1)}, u32[]{:S(2)}, u32[]{:S(2)}) collective-permute-start(f32[392,128]{1,0:T(8,128)S(1)} %get-tuple-element.44), channel_id=1, source_target_pairs={{0,8},{4,12},{8,0},{12,4},{16,24},{20,28},{24,16},{28,20},{1,9},{5... | collective-permute-start | bytes 602120 | tf_op jit(solution)/shard_map/ppermute | solution.py:317
  49.4 25.6 %copy-start.1 = (f32[64,768]{1,0:T(8,128)S(1)}, f32[64,768]{1,0:T(8,128)}, u32[]{:S(2)}) copy-start(f32[64,768]{1,0:T(8,128)} %means_ref.1) | copy-start | bytes 589828
  49.4 25.6 %copy-start.3 = (f32[64]{0:T(128)S(1)}, f32[64]{0:T(128)}, u32[]{:S(2)}) copy-start(f32[64]{0:T(128)} %param.7) | copy-start | bytes 772
  53.1 9.1 %collective-permute-start.14 = (f32[384,128]{1,0:T(8,128)S(1)}, f32[384,128]{1,0:T(8,128)S(1)}, u32[]{:S(2)}, u32[]{:S(2)}) collective-permute-start(f32[384,128]{1,0:T(8,128)S(1)} %get-tuple-element.50), channel_id=1, source_target_pairs={{0,8},{4,12},{8,0},{12,4},{16,24},{20,28},{24,16},{28,20},{1,9},{5... | collective-permute-start | bytes 589832 | tf_op jit(solution)/shard_map/ppermute | solution.py:317
  55.2 10.4 %collective-permute-start.13 = (f32[392,128]{1,0:T(8,128)S(1)}, f32[392,128]{1,0:T(8,128)S(1)}, u32[]{:S(2)}, u32[]{:S(2)}) collective-permute-start(f32[392,128]{1,0:T(8,128)S(1)} %add.33), channel_id=1, source_target_pairs={{0,16},{4,20},{8,24},{12,28},{16,0},{20,4},{24,8},{28,12},{1,17},{... | collective-permute-start | bytes 602120 | tf_op jit(solution)/shard_map/ppermute | solution.py:317
  62.2 12.7 %collective-permute-start.15 = (f32[392,128]{1,0:T(8,128)S(1)}, f32[392,128]{1,0:T(8,128)S(1)}, u32[]{:S(2)}, u32[]{:S(2)}) collective-permute-start(f32[392,128]{1,0:T(8,128)S(1)} %get-tuple-element.51), channel_id=1, source_target_pairs={{0,8},{4,12},{8,0},{12,4},{16,24},{20,28},{24,16},{28,20},{1,9},{5... | collective-permute-start | bytes 602120 | tf_op jit(solution)/shard_map/ppermute | solution.py:317
  63.1 11.8 %collective-permute-start.16 = (f32[384,128]{1,0:T(8,128)S(1)}, f32[384,128]{1,0:T(8,128)S(1)}, u32[]{:S(2)}, u32[]{:S(2)}) collective-permute-start(f32[384,128]{1,0:T(8,128)S(1)} %get-tuple-element.53), channel_id=1, source_target_pairs={{0,8},{4,12},{8,0},{12,4},{16,24},{20,28},{24,16},{28,20},{1,9},{5... | collective-permute-start | bytes 589832 | tf_op jit(solution)/shard_map/ppermute | solution.py:317
  64.3 10.6 %collective-permute-start.17 = (f32[384,128]{1,0:T(8,128)S(1)}, f32[384,128]{1,0:T(8,128)S(1)}, u32[]{:S(2)}, u32[]{:S(2)}) collective-permute-start(f32[384,128]{1,0:T(8,128)S(1)} %add.35), channel_id=1, source_target_pairs={{0,16},{4,20},{8,24},{12,28},{16,0},{20,4},{24,8},{28,12},{1,17},{... | collective-permute-start | bytes 589832 | tf_op jit(solution)/shard_map/ppermute | solution.py:317

commit v7 on v5

--- a/solution.py
+++ b/solution.py
@@ -121,8 +121,6 @@
             high, low = split(pack[c * n : (c + 1) * n, :])
             weights[q * n : (q + 1) * n, lanes] = high
             weights[comps + q * n : comps + (q + 1) * n, lanes] = low
-    if packs[0].shape[0] == tiles * n:
-        return None
     return jnp.concatenate([to_column(pack[tiles * n : tiles * n + 1, :], n) for pack in packs])
 
 
@@ -151,6 +149,13 @@
     load_variances(variances, weights, n)
     for tile in row_tiles(high_ref.shape[0]):
         out_ref[:, tile] = product(weights[...], high_ref[tile, :], low_ref[tile, :], ACROSS)
+
+
+def linear_kernel(n, *refs):
+    *linear, high_ref, low_ref, out_ref, weights = refs
+    offset = load_packs(linear, weights, n)
+    for tile in row_tiles(high_ref.shape[0]):
+        out_ref[:, tile] = product(weights[...], high_ref[tile, :], low_ref[tile, :], ACROSS) + offset
 
 
 def stats_of(scores):
@@ -180,21 +185,21 @@
 
 
 def head_kernel(n, *refs):
-    *linear, high_ref, low_ref, quad_ref, out_ref, weights = refs
-    load_packs(linear, weights, n)
+    *variances, high_ref, low_ref, linear_ref, out_ref, weights = refs
+    load_variances(variances, weights, n)
     columns = slice(0, weights.shape[1])
     for tile in row_tiles(high_ref.shape[0]):
         scores = product(weights[...], high_ref[tile, columns], low_ref[tile, columns], ACROSS)
-        out_ref[:, tile] = quad_ref[:, tile] + scores
+        out_ref[:, tile] = linear_ref[:, tile] + scores
 
 
 def last_kernel(n, *refs):
-    *linear, high_ref, low_ref, quad_ref, early_ref, out_ref, stats_ref, weights = refs
-    offset = load_packs(linear, weights, n)
+    *variances, high_ref, low_ref, rest_ref, early_ref, out_ref, stats_ref, weights = refs
+    load_variances(variances, weights, n)
     columns = slice(high_ref.shape[1] - weights.shape[1], high_ref.shape[1])
     for tile, block, part in half_tiles(stats_ref.shape[2]):
         scores = product(weights[...], high_ref[tile, columns], low_ref[tile, columns], ACROSS)
-        scores = quad_ref[:, tile] + scores + offset
+        scores = rest_ref[:, tile] + scores
         out_ref[:, tile] = scores
         early = early_ref[0:1, tile], early_ref[1:2, tile]
         peak, total = joined(stats_of(scores), early)
@@ -317,21 +322,16 @@
     return lax.ppermute(value, axis, [(i, i ^ bit) for i in range(size)])
 
 
-def vmem(value):
-    return pltpu.with_memory_space_constraint(value, pltpu.VMEM)
-
-
 def after(value, *others):
     return lax.optimization_barrier((value, *others))[0]
 
 
-def gather_early(piece):
+def gather_even(piece):
     bit = lax.axis_size("dp") // 4
     held = {0: piece}
     while bit > 1:
         held.update({q ^ bit: swap(value, "dp", 2 * bit) for q, value in held.items()})
         bit //= 2
-    held[1] = swap(piece, "dp", 2)
     return held
 
 
@@ -363,60 +363,68 @@
     n = comp_means.shape[0]
     rows, width = embeddings.shape
     planes = lax.axis_size("dp") // 2
-    variances = gather_early(comp_variances)
-    linear = gather_early(coefficients(comp_means, comp_variances, comp_mass))
+    variances = gather_even(comp_variances)
+    variances[1] = swap(comp_variances, "dp", 2)
+    pack = coefficients(comp_means, comp_variances, comp_mass)
+    linear = {q: swap(pack, "dp", 2 * q) for q in range(planes - 1, 0, -1)} | {0: pack}
     other = swap(embeddings, "dp", 1)
-    order = sorted(linear)
-    late = [q for q in range(planes) if q not in linear]
     x_high, x_low, s_high, s_low = halves(embeddings, other)
-    for q in late:
-        variances[q] = swap(after(variances[q ^ 1], x_high), "dp", 2)
+    order = sorted(variances)
+    late = [q for q in range(planes) if q not in variances]
     n_early, n_late = n * len(order), n * len(late)
-
-    def quad_scores(group, name, cost=None):
-        comps = n * len(group)
-        operands = (*(vmem(variances[q]) for q in group), s_high, s_low)
-        body = functools.partial(quad_kernel, n)
-        return score_call(body, [(comps, 2 * rows)], [(2 * comps, width)], name, *operands, cost=cost)[0]
-
-    quad = quad_scores(order, "early_quad")
-    head = width // LANES * 2 // 3
-    heads, tails = [], []
-    for q in late:
-        source = after(linear[q ^ 1], quad)
-        heads.append(vmem(swap(source[: head * n], "dp", 2)))
-        tails.append(source[head * n :])
+    head = width // LANES * 2 // 3 * LANES
+    sources = [after(variances[q ^ 1], x_high) for q in late]
+    heads = [swap(source[:, :head], "dp", 2) for source in sources]
+    (quad,) = score_call(
+        functools.partial(quad_kernel, n),
+        [(n_early, 2 * rows)],
+        [(2 * n_early, width)],
+        "early_quad",
+        *(variances[q] for q in order),
+        s_high,
+        s_low,
+    )
+    tails = [swap(after(source[:, head:], quad), "dp", 2) for source in sources]
     early, early_stats = score_call(
         functools.partial(early_kernel, n),
         [(n_early, 2 * rows), (2, 2 * rows)],
         [(2 * n_early, width)],
         "early_scores",
-        *(vmem(linear[q]) for q in order),
+        *(linear[q] for q in order),
         x_high,
         x_low,
         quad,
         cost=LIGHT,
     )
-    tails = [vmem(swap(after(tail, early), "dp", 2)) for tail in tails]
+    (part,) = score_call(
+        functools.partial(linear_kernel, n),
+        [(n_late, 2 * rows)],
+        [(2 * n_late, width)],
+        "late_linear",
+        *(linear[q] for q in late),
+        x_high,
+        x_low,
+        cost=LIGHT,
+    )
     (part,) = score_call(
         functools.partial(head_kernel, n),
         [(n_late, 2 * rows)],
-        [(2 * n_late, head * LANES)],
+        [(2 * n_late, head)],
         "late_head",
         *heads,
-        x_high,
-        x_low,
-        quad_scores(late, "late_quad", LIGHT),
+        s_high,
+        s_low,
+        part,
         cost=LIGHT,
     )
     last, stats = score_call(
         functools.partial(last_kernel, n),
         [(n_late, 2 * rows), (2, 2, rows)],
-        [(2 * n_late, width - head * LANES)],
+        [(2 * n_late, width - head)],
         "last_scores",
         *tails,
-        x_high,
-        x_low,
+        s_high,
+        s_low,
         part,
         early_stats,
     )

time: 72.7 us -> 75.9 us (1.044)
  starting transfers between devices: 21.8 us -> 26.7 us
  waiting for transfers between devices: 30.6 us -> 29.1 us
    ppermute x18, starting transfers between devices: 21.8 us -> 26.7 us  [swap(): return lax.ppermute(value, axis, [(i, i ^ bit) for i in range(size)])]
    ppermute x18, waiting for transfers between devices: 30.6 us -> 29.1 us  [swap(): return lax.ppermute(value, axis, [(i, i ^ bit) for i in range(size)])]
  transfers between devices with their start and end apart: 18 -> 18, of which waited for: 13 -> 10; matrix products, arithmetic and copies ran while one was open for 0% -> 0% of each run, Pallas kernels for 20% -> 19%
where the time goes in v7:
time: 75.9 us; the launch traced here: 75.8 us
  waiting for transfers between devices  29.1 us (38%)
  starting transfers between devices  26.7 us (35%)
  Pallas kernels  19 us (25%)
  between operations  0.78 us (1%)
    ppermute x18, waiting for transfers between devices, swap(): return lax.ppermute(value, axis, [(i, i ^ bit) for i in range(size)])  29.1 us
    ppermute x18, starting transfers between devices, swap(): return lax.ppermute(value, axis, [(i, i ^ bit) for i in range(size)])  26.7 us
    pallas_call x5, Pallas kernels, score_call(): pl.pallas_call(body, out_shape=[jax.ShapeDtypeStruct(shape, F32) for shap...  9.23 us
    pallas_call x1, Pallas kernels, first_moments(): pl.pallas_call(functools.partial(first_kernel, n), out_shape=[pack] * (co...  2.67 us
    pallas_call x1, Pallas kernels, second_moments(): pl.pallas_call(functools.partial(second_kernel, n), out_shape=[pack] * (r...  2.58 us
    pallas_call x1, Pallas kernels, halves(): pl.pallas_call(halves_kernel, grid=(2 * steps,), in_specs=[pl.BlockSpec((...  2.25 us
  transfers between devices with their start and end apart: 18, of which 10 were waited for; matrix products, arithmetic and copies ran while one was open for 0% of the time, Pallas kernels for 19%

profile of v7, /device:TPU:0, one launch (start us, length us, event | category | flops | bytes accessed | tf_op | source)
XLA Modules:
  0.0 75.8 jit_solution(11173478808032651923)
XLA Ops:
  1.1 3.7 %collective-permute-start.4 = (f32[64,768]{1,0:T(8,128)}, f32[64,768]{1,0:T(8,128)S(1)}, u32[]{:S(2)}, u32[]{:S(2)}) collective-permute-start(f32[64,768]{1,0:T(8,128)} %variances_ref.1), channel_id=1, source_target_pairs={{0,16},{4,20},{8,24},{12,28},{16,0},{20,4},{24,8},{28,12},{1,17},{... | collective-permute-start | bytes 589832 | tf_op jit(solution)/shard_map/ppermute | solution.py:322
  4.8 1.6 %collective-permute-start.3 = (f32[64,768]{1,0:T(8,128)}, f32[64,768]{1,0:T(8,128)S(1)}, u32[]{:S(2)}, u32[]{:S(2)}) collective-permute-start(f32[64,768]{1,0:T(8,128)} %variances_ref.1), channel_id=1, source_target_pairs={{0,8},{4,12},{8,0},{12,4},{16,24},{20,28},{24,16},{28,20},{1,9},{5... | collective-permute-start | bytes 589832 | tf_op jit(solution)/shard_map/ppermute | solution.py:322
  6.4 1.3 %coefficients.1.refs_0_ = f32[392,128]{1,0:T(8,128)S(1)} custom-call(f32[64,768]{1,0:T(8,128)} %means_ref.1, f32[64,768]{1,0:T(8,128)} %variances_ref.1, f32[1,64]{1,0:T(1,128)} %bitcast.2), custom_call_target="tpu_custom_call" | custom-call | flops 10000000000 | bytes 100000000 | tf_op jit(solution)/shard_map/coefficients/pallas_call | solution.py:64
  7.8 1.9 %collective-permute-start.1 = (f32[392,128]{1,0:T(8,128)S(1)}, f32[392,128]{1,0:T(8,128)S(1)}, u32[]{:S(2)}, u32[]{:S(2)}) collective-permute-start(f32[392,128]{1,0:T(8,128)S(1)} %coefficients.1.refs_0_), channel_id=1, source_target_pairs={{0,16},{4,20},{8,24},{12,28},{16,0},{20,4},{24,8},{28,12},{1,17},{... | collective-permute-start | bytes 602120 | tf_op jit(solution)/shard_map/ppermute | solution.py:322
  9.7 2.5 %collective-permute-start = (f32[392,128]{1,0:T(8,128)S(1)}, f32[392,128]{1,0:T(8,128)S(1)}, u32[]{:S(2)}, u32[]{:S(2)}) collective-permute-start(f32[392,128]{1,0:T(8,128)S(1)} %coefficients.1.refs_0_), channel_id=1, source_target_pairs={{0,8},{4,12},{8,0},{12,4},{16,24},{20,28},{24,16},{28,20},{1,9},{5... | collective-permute-start | bytes 602120 | tf_op jit(solution)/shard_map/ppermute | solution.py:322
  12.2 2.2 %halves.1 = (bf16[2048,768]{1,0:T(8,128)(2,1)S(1)}, bf16[2048,768]{1,0:T(8,128)(2,1)S(1)}, bf16[2048,768]{1,0:T(8,128)(2,1)S(1)}, bf16[2048,768]{1,0:T(8,128)(2,1)S(1)}) custom-call(f32[1024,768]{1,0:T(8,128)S(1)} %copy-done, f32[1024,768]{1,0:T(8,128)S(1)} %collective-permute-done.2.other_ref), custom_call_target="tpu_custom_call" | custom-call | flops 10000000000 | bytes 100000000 | tf_op jit(solution)/shard_map/halves/pallas_call | solution.py:101
  16.0 2.4 %early_quad.1.refs_5_ = f32[192,2048]{1,0:T(8,128)S(1)} custom-call(f32[64,768]{1,0:T(8,128)S(1)} %copy-done.2, f32[64,768]{1,0:T(8,128)S(1)} %collective-permute-done.3.refs_1_, f32[64,768]{1,0:T(8,128)S(1)} %collective-permute-done.4.refs_2_, bf16[2048,768]{1,0:T(8,128)(2,1)S(1)} %get-tuple-element.34.refs_3_.refs_1_.high_ref, ...), custom_call_target="tpu_custom_call" | custom-call | flops 10000000000 | bytes 100000000 | tf_op jit(solution)/shard_map/early_quad/pallas_call | solution.py:211
  18.4 1.2 %collective-permute-start.5 = (f32[64,256]{1,0:T(8,128)S(1)}, f32[64,256]{1,0:T(8,128)S(1)}, u32[]{:S(2)}, u32[]{:S(2)}) collective-permute-start(f32[64,256]{1,0:T(8,128)S(1)} %slice.47), channel_id=1, source_target_pairs={{0,8},{4,12},{8,0},{12,4},{16,24},{20,28},{24,16},{28,20},{1,9},{5... | collective-permute-start | bytes 196616 | tf_op jit(solution)/shard_map/ppermute | solution.py:322
  20.7 2.1 %late_linear.1.refs_3_ = f32[64,2048]{1,0:T(8,128)S(1)} custom-call(f32[392,128]{1,0:T(8,128)S(1)} %collective-permute-done.7.refs_0_, bf16[2048,768]{1,0:T(8,128)(2,1)S(1)} %get-tuple-element.32.refs_3_.refs_1_.high_ref, bf16[2048,768]{1,0:T(8,128)(2,1)S(1)} %get-tuple-element.33.refs_4_.refs_2_.low_ref), custom_call_target="tpu_custom_call" | custom-call | flops 100000000 | bytes 1000000 | tf_op jit(solution)/shard_map/late_linear/pallas_call | solution.py:211
  22.8 9.3 %collective-permute-done.1.refs_2_ = f32[392,128]{1,0:T(8,128)S(1)} collective-permute-done((f32[392,128]{1,0:T(8,128)S(1)}, f32[392,128]{1,0:T(8,128)S(1)}, u32[]{:S(2)}, u32[]{:S(2)}) %collective-permute-start.1) | collective-permute-done | bytes 200736 | tf_op jit(solution)/shard_map/ppermute | solution.py:322
  32.1 2.5 %early_scores.1 = (f32[192,2048]{1,0:T(8,128)S(1)}, f32[2,2048]{1,0:T(2,128)S(1)}) custom-call(f32[392,128]{1,0:T(8,128)S(1)} %coefficients.1.refs_0_, f32[392,128]{1,0:T(8,128)S(1)} %collective-permute-done.refs_1_, f32[392,128]{1,0:T(8,128)S(1)} %collective-permute-done.1.refs_2_, bf16[2048,768]{1,0:T(8,128)(2,1)S(1)} %get-tuple-element.32.refs_3_.refs_1_.high_ref, ...), custom_call_target="tpu_custom_call" | custom-call | flops 100000000 | bytes 1000000 | tf_op jit(solution)/shard_map/early_scores/pallas_call | solution.py:211
  34.6 1.4 %late_head.1.refs_3_ = f32[64,2048]{1,0:T(8,128)S(1)} custom-call(f32[64,512]{1,0:T(8,128)S(1)} %collective-permute-done.6.refs_0_, bf16[2048,768]{1,0:T(8,128)(2,1)S(1)} %get-tuple-element.34.refs_3_.refs_1_.high_ref, bf16[2048,768]{1,0:T(8,128)(2,1)S(1)} %get-tuple-element.35.refs_4_.refs_2_.low_ref, f32[64,2048]{1,0:T(8,128)S(1)} %late_linear.1.refs_3_), custom_call_target="tpu_custom_call" | custom-call | flops 100000000 | bytes 1000000 | tf_op jit(solution)/shard_map/late_head/pallas_call | solution.py:211
  37.0 1.2 %collective-permute-done.8 = f32[2,2,1024]{2,1,0:T(2,128)S(1)} collective-permute-done((f32[2,2,1024]{2,1,0:T(2,128)S(1)}, f32[2,2,1024]{2,1,0:T(2,128)S(1)}, u32[]{:S(2)}, u32[]{:S(2)}) %collective-permute-start.8) | collective-permute-done | bytes 16416 | tf_op jit(solution)/shard_map/ppermute | solution.py:322
  38.2 2.6 %collective-permute-start.11 = (f32[2,2,1024]{2,1,0:T(2,128)S(1)}, f32[2,2,1024]{2,1,0:T(2,128)S(1)}, u32[]{:S(2)}, u32[]{:S(2)}) collective-permute-start(f32[2,2,1024]{2,1,0:T(2,128)S(1)} %pad_maximum_fusion), channel_id=1, source_target_pairs={{0,3},{1,2},{2,1},{3,0},{4,7},{5,6},{6,5},{7,4},{8,11},{9,10},{10,... | collective-permute-start | bytes 49160 | tf_op jit(solution)/shard_map/ppermute | solution.py:322
  41.8 1.1 %collective-permute-done.11 = f32[2,2,1024]{2,1,0:T(2,128)S(1)} collective-permute-done((f32[2,2,1024]{2,1,0:T(2,128)S(1)}, f32[2,2,1024]{2,1,0:T(2,128)S(1)}, u32[]{:S(2)}, u32[]{:S(2)}) %collective-permute-start.11) | collective-permute-done | bytes 16416 | tf_op jit(solution)/shard_map/ppermute | solution.py:322
  42.9 1.6 %collective-permute-done.10 = f32[2,2,1024]{2,1,0:T(2,128)S(1)} collective-permute-done((f32[2,2,1024]{2,1,0:T(2,128)S(1)}, f32[2,2,1024]{2,1,0:T(2,128)S(1)}, u32[]{:S(2)}, u32[]{:S(2)}) %collective-permute-start.10) | collective-permute-done | bytes 16416 | tf_op jit(solution)/shard_map/ppermute | solution.py:322
  45.1 2.7 %first_moments.1 = (f32[392,128]{1,0:T(8,128)S(1)}, f32[392,128]{1,0:T(8,128)S(1)}, f32[392,128]{1,0:T(8,128)S(1)}, f32[392,128]{1,0:T(8,128)S(1)}, bf16[512,2048]{1,0:T(8,128)(2,1)S(1)}) custom-call(f32[192,2048]{1,0:T(8,128)S(1)} %get-tuple-element.36.early_ref, f32[64,2048]{1,0:T(8,128)S(1)} %get-tuple-element.40.late_ref, ...), custom_call_target="tpu_custom_call" | custom-call | flops 10000000000 | bytes 100000000 | tf_op jit(solution)/shard_map/first_moments/pallas_call | solution.py:252
  48.5 2.6 %second_moments.1 = (f32[384,128]{1,0:T(8,128)S(1)}, f32[384,128]{1,0:T(8,128)S(1)}, f32[384,128]{1,0:T(8,128)S(1)}, f32[384,128]{1,0:T(8,128)S(1)}) custom-call(bf16[512,2048]{1,0:T(8,128)(2,1)S(1)} %get-tuple-element.45.resp_ref, bf16[2048,768]{1,0:T(8,128)(2,1)S(1)} %get-tuple-element.34.refs_3_.refs_1_.high_ref, ...), custom_call_target="tpu_custom_call" | custom-call | flops 10000000000 | bytes 100000000 | tf_op jit(solution)/shard_map/second_moments/pallas_call | solution.py:267
  51.1 2.5 %collective-permute-done.12 = f32[392,128]{1,0:T(8,128)S(1)} collective-permute-done((f32[392,128]{1,0:T(8,128)S(1)}, f32[392,128]{1,0:T(8,128)S(1)}, u32[]{:S(2)}, u32[]{:S(2)}) %collective-permute-start.12) | collective-permute-done | bytes 200736 | tf_op jit(solution)/shard_map/ppermute | solution.py:322
  54.3 3.4 %collective-permute-start.13 = (f32[392,128]{1,0:T(8,128)S(1)}, f32[392,128]{1,0:T(8,128)S(1)}, u32[]{:S(2)}, u32[]{:S(2)}) collective-permute-start(f32[392,128]{1,0:T(8,128)S(1)} %add.33), channel_id=1, source_target_pairs={{0,16},{4,20},{8,24},{12,28},{16,0},{20,4},{24,8},{28,12},{1,17},{... | collective-permute-start | bytes 602120 | tf_op jit(solution)/shard_map/ppermute | solution.py:322
  57.6 4.2 %collective-permute-done.14 = f32[384,128]{1,0:T(8,128)S(1)} collective-permute-done((f32[384,128]{1,0:T(8,128)S(1)}, f32[384,128]{1,0:T(8,128)S(1)}, u32[]{:S(2)}, u32[]{:S(2)}) %collective-permute-start.14) | collective-permute-done | bytes 196640 | tf_op jit(solution)/shard_map/ppermute | solution.py:322
  62.1 1.9 %collective-permute-start.16 = (f32[384,128]{1,0:T(8,128)S(1)}, f32[384,128]{1,0:T(8,128)S(1)}, u32[]{:S(2)}, u32[]{:S(2)}) collective-permute-start(f32[384,128]{1,0:T(8,128)S(1)} %get-tuple-element.53), channel_id=1, source_target_pairs={{0,8},{4,12},{8,0},{12,4},{16,24},{20,28},{24,16},{28,20},{1,9},{5... | collective-permute-start | bytes 589832 | tf_op jit(solution)/shard_map/ppermute | solution.py:322
  64.0 3.9 %collective-permute-start.17 = (f32[384,128]{1,0:T(8,128)S(1)}, f32[384,128]{1,0:T(8,128)S(1)}, u32[]{:S(2)}, u32[]{:S(2)}) collective-permute-start(f32[384,128]{1,0:T(8,128)S(1)} %add.35), channel_id=1, source_target_pairs={{0,16},{4,20},{8,24},{12,28},{16,0},{20,4},{24,8},{28,12},{1,17},{... | collective-permute-start | bytes 589832 | tf_op jit(solution)/shard_map/ppermute | solution.py:322
  67.9 6.9 %collective-permute-done.16.near_second_ref = f32[384,128]{1,0:T(8,128)S(1)} collective-permute-done((f32[384,128]{1,0:T(8,128)S(1)}, f32[384,128]{1,0:T(8,128)S(1)}, u32[]{:S(2)}, u32[]{:S(2)}) %collective-permute-start.16) | collective-permute-done | bytes 196640 | tf_op jit(solution)/shard_map/ppermute | solution.py:322
  (41 shorter events, 8.3 us)
Async XLA Ops:
  0.6 9.1 %collective-permute-start.2 = (f32[1024,768]{1,0:T(8,128)}, f32[1024,768]{1,0:T(8,128)S(1)}, u32[]{:S(2)}, u32[]{:S(2)}) collective-permute-start(f32[1024,768]{1,0:T(8,128)} %own_ref.1), channel_id=1, source_target_pairs={{0,4},{4,0},{8,12},{12,8},{16,20},{20,16},{24,28},{28,24},{1,5},{5... | collective-permute-start | bytes 9437192 | tf_op jit(solution)/shard_map/ppermute | solution.py:322
  1.1 13.9 %collective-permute-start.4 = (f32[64,768]{1,0:T(8,128)}, f32[64,768]{1,0:T(8,128)S(1)}, u32[]{:S(2)}, u32[]{:S(2)}) collective-permute-start(f32[64,768]{1,0:T(8,128)} %variances_ref.1), channel_id=1, source_target_pairs={{0,16},{4,20},{8,24},{12,28},{16,0},{20,4},{24,8},{28,12},{1,17},{... | collective-permute-start | bytes 589832 | tf_op jit(solution)/shard_map/ppermute | solution.py:322
  4.8 11.2 %collective-permute-start.3 = (f32[64,768]{1,0:T(8,128)}, f32[64,768]{1,0:T(8,128)S(1)}, u32[]{:S(2)}, u32[]{:S(2)}) collective-permute-start(f32[64,768]{1,0:T(8,128)} %variances_ref.1), channel_id=1, source_target_pairs={{0,8},{4,12},{8,0},{12,4},{16,24},{20,28},{24,16},{28,20},{1,9},{5... | collective-permute-start | bytes 589832 | tf_op jit(solution)/shard_map/ppermute | solution.py:322
  6.4 5.8 %copy-start = (f32[1024,768]{1,0:T(8,128)S(1)}, f32[1024,768]{1,0:T(8,128)}, u32[]{:S(2)}) copy-start(f32[1024,768]{1,0:T(8,128)} %own_ref.1) | copy-start | bytes 9437188
  7.7 8.3 %copy-start.2 = (f32[64,768]{1,0:T(8,128)S(1)}, f32[64,768]{1,0:T(8,128)}, u32[]{:S(2)}) copy-start(f32[64,768]{1,0:T(8,128)} %variances_ref.1) | copy-start | bytes 589828
  7.8 12.9 %collective-permute-start.7 = (f32[392,128]{1,0:T(8,128)S(1)}, f32[392,128]{1,0:T(8,128)S(1)}, u32[]{:S(2)}, u32[]{:S(2)}) collective-permute-start(f32[392,128]{1,0:T(8,128)S(1)} %coefficients.1.refs_0_), channel_id=1, source_target_pairs={{0,24},{4,28},{8,16},{12,20},{16,8},{20,12},{24,0},{28,4},{1,25},{... | collective-permute-start | bytes 602120 | tf_op jit(solution)/shard_map/ppermute | solution.py:322
  7.8 24.2 %collective-permute-start.1 = (f32[392,128]{1,0:T(8,128)S(1)}, f32[392,128]{1,0:T(8,128)S(1)}, u32[]{:S(2)}, u32[]{:S(2)}) collective-permute-start(f32[392,128]{1,0:T(8,128)S(1)} %coefficients.1.refs_0_), channel_id=1, source_target_pairs={{0,16},{4,20},{8,24},{12,28},{16,0},{20,4},{24,8},{28,12},{1,17},{... | collective-permute-start | bytes 602120 | tf_op jit(solution)/shard_map/ppermute | solution.py:322
  9.7 22.3 %collective-permute-start = (f32[392,128]{1,0:T(8,128)S(1)}, f32[392,128]{1,0:T(8,128)S(1)}, u32[]{:S(2)}, u32[]{:S(2)}) collective-permute-start(f32[392,128]{1,0:T(8,128)S(1)} %coefficients.1.refs_0_), channel_id=1, source_target_pairs={{0,8},{4,12},{8,0},{12,4},{16,24},{20,28},{24,16},{28,20},{1,9},{5... | collective-permute-start | bytes 602120 | tf_op jit(solution)/shard_map/ppermute | solution.py:322
  15.0 19.6 %collective-permute-start.6 = (f32[64,512]{1,0:T(8,128)S(1)}, f32[64,512]{1,0:T(8,128)S(1)}, u32[]{:S(2)}, u32[]{:S(2)}) collective-permute-start(f32[64,512]{1,0:T(8,128)S(1)} %slice.48), channel_id=1, source_target_pairs={{0,8},{4,12},{8,0},{12,4},{16,24},{20,28},{24,16},{28,20},{1,9},{5... | collective-permute-start | bytes 393224 | tf_op jit(solution)/shard_map/ppermute | solution.py:322
  18.4 17.6 %collective-permute-start.5 = (f32[64,256]{1,0:T(8,128)S(1)}, f32[64,256]{1,0:T(8,128)S(1)}, u32[]{:S(2)}, u32[]{:S(2)}) collective-permute-start(f32[64,256]{1,0:T(8,128)S(1)} %slice.47), channel_id=1, source_target_pairs={{0,8},{4,12},{8,0},{12,4},{16,24},{20,28},{24,16},{28,20},{1,9},{5... | collective-permute-start | bytes 196616 | tf_op jit(solution)/shard_map/ppermute | solution.py:322
  36.9 1.2 %collective-permute-start.8 = (f32[2,2,1024]{2,1,0:T(2,128)S(1)}, f32[2,2,1024]{2,1,0:T(2,128)S(1)}, u32[]{:S(2)}, u32[]{:S(2)}) collective-permute-start(f32[2,2,1024]{2,1,0:T(2,128)S(1)} %get-tuple-element.41), channel_id=1, source_target_pairs={{0,4},{4,0},{8,12},{12,8},{16,20},{20,16},{24,28},{28,24},{1,5},{5... | collective-permute-start | bytes 49160 | tf_op jit(solution)/shard_map/ppermute | solution.py:322
  38.2 4.7 %collective-permute-start.11 = (f32[2,2,1024]{2,1,0:T(2,128)S(1)}, f32[2,2,1024]{2,1,0:T(2,128)S(1)}, u32[]{:S(2)}, u32[]{:S(2)}) collective-permute-start(f32[2,2,1024]{2,1,0:T(2,128)S(1)} %pad_maximum_fusion), channel_id=1, source_target_pairs={{0,3},{1,2},{2,1},{3,0},{4,7},{5,6},{6,5},{7,4},{8,11},{9,10},{10,... | collective-permute-start | bytes 49160 | tf_op jit(solution)/shard_map/ppermute | solution.py:322
  40.8 3.7 %collective-permute-start.10 = (f32[2,2,1024]{2,1,0:T(2,128)S(1)}, f32[2,2,1024]{2,1,0:T(2,128)S(1)}, u32[]{:S(2)}, u32[]{:S(2)}) collective-permute-start(f32[2,2,1024]{2,1,0:T(2,128)S(1)} %pad_maximum_fusion), channel_id=1, source_target_pairs={{0,2},{1,3},{2,0},{3,1},{4,6},{5,7},{6,4},{7,5},{8,10},{9,11},{10,... | collective-permute-start | bytes 49160 | tf_op jit(solution)/shard_map/ppermute | solution.py:322
  41.3 3.7 %collective-permute-start.9 = (f32[2,2,1024]{2,1,0:T(2,128)S(1)}, f32[2,2,1024]{2,1,0:T(2,128)S(1)}, u32[]{:S(2)}, u32[]{:S(2)}) collective-permute-start(f32[2,2,1024]{2,1,0:T(2,128)S(1)} %pad_maximum_fusion), channel_id=1, source_target_pairs={{0,1},{1,0},{2,3},{3,2},{4,5},{5,4},{6,7},{7,6},{8,9},{9,8},{10,11... | collective-permute-start | bytes 49160 | tf_op jit(solution)/shard_map/ppermute | solution.py:322
  47.8 5.8 %collective-permute-start.12 = (f32[392,128]{1,0:T(8,128)S(1)}, f32[392,128]{1,0:T(8,128)S(1)}, u32[]{:S(2)}, u32[]{:S(2)}) collective-permute-start(f32[392,128]{1,0:T(8,128)S(1)} %get-tuple-element.44), channel_id=1, source_target_pairs={{0,8},{4,12},{8,0},{12,4},{16,24},{20,28},{24,16},{28,20},{1,9},{5... | collective-permute-start | bytes 602120 | tf_op jit(solution)/shard_map/ppermute | solution.py:322
  48.5 26.4 %copy-start.1 = (f32[64,768]{1,0:T(8,128)S(1)}, f32[64,768]{1,0:T(8,128)}, u32[]{:S(2)}) copy-start(f32[64,768]{1,0:T(8,128)} %means_ref.1) | copy-start | bytes 589828
  48.5 26.4 %copy-start.3 = (f32[64]{0:T(128)S(1)}, f32[64]{0:T(128)}, u32[]{:S(2)}) copy-start(f32[64]{0:T(128)} %param.7) | copy-start | bytes 772
  53.6 8.3 %collective-permute-start.14 = (f32[384,128]{1,0:T(8,128)S(1)}, f32[384,128]{1,0:T(8,128)S(1)}, u32[]{:S(2)}, u32[]{:S(2)}) collective-permute-start(f32[384,128]{1,0:T(8,128)S(1)} %get-tuple-element.50), channel_id=1, source_target_pairs={{0,8},{4,12},{8,0},{12,4},{16,24},{20,28},{24,16},{28,20},{1,9},{5... | collective-permute-start | bytes 589832 | tf_op jit(solution)/shard_map/ppermute | solution.py:322
  54.3 13.6 %collective-permute-start.13 = (f32[392,128]{1,0:T(8,128)S(1)}, f32[392,128]{1,0:T(8,128)S(1)}, u32[]{:S(2)}, u32[]{:S(2)}) collective-permute-start(f32[392,128]{1,0:T(8,128)S(1)} %add.33), channel_id=1, source_target_pairs={{0,16},{4,20},{8,24},{12,28},{16,0},{20,4},{24,8},{28,12},{1,17},{... | collective-permute-start | bytes 602120 | tf_op jit(solution)/shard_map/ppermute | solution.py:322
  61.9 12.9 %collective-permute-start.15 = (f32[392,128]{1,0:T(8,128)S(1)}, f32[392,128]{1,0:T(8,128)S(1)}, u32[]{:S(2)}, u32[]{:S(2)}) collective-permute-start(f32[392,128]{1,0:T(8,128)S(1)} %get-tuple-element.51), channel_id=1, source_target_pairs={{0,8},{4,12},{8,0},{12,4},{16,24},{20,28},{24,16},{28,20},{1,9},{5... | collective-permute-start | bytes 602120 | tf_op jit(solution)/shard_map/ppermute | solution.py:322
  62.1 12.8 %collective-permute-start.16 = (f32[384,128]{1,0:T(8,128)S(1)}, f32[384,128]{1,0:T(8,128)S(1)}, u32[]{:S(2)}, u32[]{:S(2)}) collective-permute-start(f32[384,128]{1,0:T(8,128)S(1)} %get-tuple-element.53), channel_id=1, source_target_pairs={{0,8},{4,12},{8,0},{12,4},{16,24},{20,28},{24,16},{28,20},{1,9},{5... | collective-permute-start | bytes 589832 | tf_op jit(solution)/shard_map/ppermute | solution.py:322
  64.0 10.8 %collective-permute-start.17 = (f32[384,128]{1,0:T(8,128)S(1)}, f32[384,128]{1,0:T(8,128)S(1)}, u32[]{:S(2)}, u32[]{:S(2)}) collective-permute-start(f32[384,128]{1,0:T(8,128)S(1)} %add.35), channel_id=1, source_target_pairs={{0,16},{4,20},{8,24},{12,28},{16,0},{20,4},{24,8},{28,12},{1,17},{... | collective-permute-start | bytes 589832 | tf_op jit(solution)/shard_map/ppermute | solution.py:322

commit v8 on v4

--- a/solution.py
+++ b/solution.py
@@ -338,6 +338,7 @@
 def scatter_planes(first, second):
     held = [dict(enumerate(parts)) for parts in (first, second)]
     totals, near = [[parts.pop(0)] for parts in held], []
+    near = [swap(after(held[0].pop(1), second[0]), "dp", 2)]
     planes, bit = len(first), 1
     while bit < planes:
         ready = []
@@ -345,9 +346,12 @@
             for q in sorted((q for q in parts if q & bit and q != bit), reverse=True):
                 parts[q ^ bit] = parts[q ^ bit] + swap(after(parts.pop(q), *ready), "dp", 2 * bit)
                 ready = [parts[q ^ bit]]
-        for total, parts in zip(totals, held):
-            part = swap(after(parts.pop(bit), *ready), "dp", 2 * bit)
-            (near if bit == 1 else total).append(part)
+        if bit == 1:
+            near.append(swap(after(held[1].pop(1), *ready), "dp", 2))
+            held[1] = {q: after(part, near[0]) for q, part in held[1].items()}
+        else:
+            for total, parts in zip(totals, held):
+                total.append(swap(after(parts.pop(bit), *ready), "dp", 2 * bit))
         bit *= 2
     return *lax.optimization_barrier(tuple(sum(t[1:], t[0]) for t in totals)), *near
 

time: 72.7 us -> 74.9 us (1.030)
  waiting for transfers between devices: 30.6 us -> 33.1 us
    ppermute x18, waiting for transfers between devices: 30.6 us -> 33.1 us  [swap(): return lax.ppermute(value, axis, [(i, i ^ bit) for i in range(size)])]
where the time goes in v8:
time: 74.9 us; the launch traced here: 74.7 us
  waiting for transfers between devices  33.1 us (44%)
  starting transfers between devices  21.4 us (29%)
  Pallas kernels  19 us (25%)
  between operations  0.75 us (1%)
    ppermute x18, waiting for transfers between devices, swap(): return lax.ppermute(value, axis, [(i, i ^ bit) for i in range(size)])  33.1 us
    ppermute x18, starting transfers between devices, swap(): return lax.ppermute(value, axis, [(i, i ^ bit) for i in range(size)])  21.4 us
    pallas_call x5, Pallas kernels, score_call(): pl.pallas_call(body, out_shape=[jax.ShapeDtypeStruct(shape, F32) for shap...  9.25 us
    pallas_call x1, Pallas kernels, first_moments(): pl.pallas_call(functools.partial(first_kernel, n), out_shape=[pack] * (co...  2.67 us
    pallas_call x1, Pallas kernels, second_moments(): pl.pallas_call(functools.partial(second_kernel, n), out_shape=[pack] * (r...  2.59 us
    pallas_call x1, Pallas kernels, halves(): pl.pallas_call(halves_kernel, grid=(2 * steps,), in_specs=[pl.BlockSpec((...  2.25 us
  transfers between devices with their start and end apart: 18, of which 14 were waited for; matrix products, arithmetic and copies ran while one was open for 0% of the time, Pallas kernels for 20%

profile of v8, /device:TPU:0, one launch (start us, length us, event | category | flops | bytes accessed | tf_op | source)
XLA Modules:
  0.0 74.7 jit_solution(13968019467236274453)
XLA Ops:
  1.1 3.7 %collective-permute-start.4 = (f32[64,768]{1,0:T(8,128)}, f32[64,768]{1,0:T(8,128)S(1)}, u32[]{:S(2)}, u32[]{:S(2)}) collective-permute-start(f32[64,768]{1,0:T(8,128)} %variances_ref.1), channel_id=1, source_target_pairs={{0,16},{4,20},{8,24},{12,28},{16,0},{20,4},{24,8},{28,12},{1,17},{... | collective-permute-start | bytes 589832 | tf_op jit(solution)/shard_map/ppermute | solution.py:317
  4.8 1.6 %collective-permute-start.3 = (f32[64,768]{1,0:T(8,128)}, f32[64,768]{1,0:T(8,128)S(1)}, u32[]{:S(2)}, u32[]{:S(2)}) collective-permute-start(f32[64,768]{1,0:T(8,128)} %variances_ref.1), channel_id=1, source_target_pairs={{0,8},{4,12},{8,0},{12,4},{16,24},{20,28},{24,16},{28,20},{1,9},{5... | collective-permute-start | bytes 589832 | tf_op jit(solution)/shard_map/ppermute | solution.py:317
  6.4 1.3 %coefficients.1.refs_0_ = f32[392,128]{1,0:T(8,128)S(1)} custom-call(f32[64,768]{1,0:T(8,128)} %means_ref.1, f32[64,768]{1,0:T(8,128)} %variances_ref.1, f32[1,64]{1,0:T(1,128)} %bitcast.2), custom_call_target="tpu_custom_call" | custom-call | flops 10000000000 | bytes 100000000 | tf_op jit(solution)/shard_map/coefficients/pallas_call | solution.py:64
  8.5 2.2 %halves.1 = (bf16[2048,768]{1,0:T(8,128)(2,1)S(1)}, bf16[2048,768]{1,0:T(8,128)(2,1)S(1)}, bf16[2048,768]{1,0:T(8,128)(2,1)S(1)}, bf16[2048,768]{1,0:T(8,128)(2,1)S(1)}) custom-call(f32[1024,768]{1,0:T(8,128)S(1)} %copy-done, f32[1024,768]{1,0:T(8,128)S(1)} %collective-permute-done.2.other_ref), custom_call_target="tpu_custom_call" | custom-call | flops 10000000000 | bytes 100000000 | tf_op jit(solution)/shard_map/halves/pallas_call | solution.py:101
  10.7 4.4 %collective-permute-done.4.refs_2_ = f32[64,768]{1,0:T(8,128)S(1)} collective-permute-done((f32[64,768]{1,0:T(8,128)}, f32[64,768]{1,0:T(8,128)S(1)}, u32[]{:S(2)}, u32[]{:S(2)}) %collective-permute-start.4) | collective-permute-done | bytes 196640 | tf_op jit(solution)/shard_map/ppermute | solution.py:317
  17.0 2.4 %early_quad.1.refs_5_ = f32[192,2048]{1,0:T(8,128)S(1)} custom-call(f32[64,768]{1,0:T(8,128)S(1)} %copy-done.2, f32[64,768]{1,0:T(8,128)S(1)} %collective-permute-done.3.refs_1_, f32[64,768]{1,0:T(8,128)S(1)} %collective-permute-done.4.refs_2_, bf16[2048,768]{1,0:T(8,128)(2,1)S(1)} %get-tuple-element.34.refs_3_.refs_1_.high_ref, ...), custom_call_target="tpu_custom_call" | custom-call | flops 10000000000 | bytes 100000000 | tf_op jit(solution)/shard_map/early_quad/pallas_call | solution.py:206
  19.4 4.1 %collective-permute-done.1.refs_2_ = f32[392,128]{1,0:T(8,128)S(1)} collective-permute-done((f32[392,128]{1,0:T(8,128)S(1)}, f32[392,128]{1,0:T(8,128)S(1)}, u32[]{:S(2)}, u32[]{:S(2)}) %collective-permute-start.1) | collective-permute-done | bytes 200736 | tf_op jit(solution)/shard_map/ppermute | solution.py:317
  24.4 2.5 %early_scores.1 = (f32[192,2048]{1,0:T(8,128)S(1)}, f32[2,2048]{1,0:T(2,128)S(1)}) custom-call(f32[392,128]{1,0:T(8,128)S(1)} %coefficients.1.refs_0_, f32[392,128]{1,0:T(8,128)S(1)} %collective-permute-done.refs_1_, f32[392,128]{1,0:T(8,128)S(1)} %collective-permute-done.1.refs_2_, bf16[2048,768]{1,0:T(8,128)(2,1)S(1)} %get-tuple-element.32.refs_3_.refs_1_.high_ref, ...), custom_call_target="tpu_custom_call" | custom-call | flops 100000000 | bytes 1000000 | tf_op jit(solution)/shard_map/early_scores/pallas_call | solution.py:206
  26.9 1.3 %collective-permute-start.5 = (f32[136,128]{1,0:T(8,128)S(1)}, f32[136,128]{1,0:T(8,128)S(1)}, u32[]{:S(2)}, u32[]{:S(2)}) collective-permute-start(f32[136,128]{1,0:T(8,128)S(1)} %slice.47), channel_id=1, source_target_pairs={{0,8},{4,12},{8,0},{12,4},{16,24},{20,28},{24,16},{28,20},{1,9},{5... | collective-permute-start | bytes 208904 | tf_op jit(solution)/shard_map/ppermute | solution.py:317
  28.6 2.1 %late_quad.1.refs_3_ = f32[64,2048]{1,0:T(8,128)S(1)} custom-call(f32[64,768]{1,0:T(8,128)S(1)} %collective-permute-done.7.refs_0_, bf16[2048,768]{1,0:T(8,128)(2,1)S(1)} %get-tuple-element.34.refs_3_.refs_1_.high_ref, bf16[2048,768]{1,0:T(8,128)(2,1)S(1)} %get-tuple-element.35.refs_4_.refs_2_.low_ref), custom_call_target="tpu_custom_call" | custom-call | flops 100000000 | bytes 1000000 | tf_op jit(solution)/shard_map/late_quad/pallas_call | solution.py:206
  31.4 1.4 %late_head.1.refs_3_ = f32[64,2048]{1,0:T(8,128)S(1)} custom-call(f32[256,128]{1,0:T(8,128)S(1)} %collective-permute-done.6.refs_0_, bf16[2048,768]{1,0:T(8,128)(2,1)S(1)} %get-tuple-element.32.refs_3_.refs_1_.high_ref, bf16[2048,768]{1,0:T(8,128)(2,1)S(1)} %get-tuple-element.33.refs_4_.refs_2_.low_ref, f32[64,2048]{1,0:T(8,128)S(1)} %late_quad.1.refs_3_), custom_call_target="tpu_custom_call" | custom-call | flops 100000000 | bytes 1000000 | tf_op jit(solution)/shard_map/late_head/pallas_call | solution.py:206
  33.7 1.2 %collective-permute-done.8 = f32[2,2,1024]{2,1,0:T(2,128)S(1)} collective-permute-done((f32[2,2,1024]{2,1,0:T(2,128)S(1)}, f32[2,2,1024]{2,1,0:T(2,128)S(1)}, u32[]{:S(2)}, u32[]{:S(2)}) %collective-permute-start.8) | collective-permute-done | bytes 16416 | tf_op jit(solution)/shard_map/ppermute | solution.py:317
  35.0 2.6 %collective-permute-start.11 = (f32[2,2,1024]{2,1,0:T(2,128)S(1)}, f32[2,2,1024]{2,1,0:T(2,128)S(1)}, u32[]{:S(2)}, u32[]{:S(2)}) collective-permute-start(f32[2,2,1024]{2,1,0:T(2,128)S(1)} %pad_maximum_fusion), channel_id=1, source_target_pairs={{0,3},{1,2},{2,1},{3,0},{4,7},{5,6},{6,5},{7,4},{8,11},{9,10},{10,... | collective-permute-start | bytes 49160 | tf_op jit(solution)/shard_map/ppermute | solution.py:317
  38.5 1.1 %collective-permute-done.11 = f32[2,2,1024]{2,1,0:T(2,128)S(1)} collective-permute-done((f32[2,2,1024]{2,1,0:T(2,128)S(1)}, f32[2,2,1024]{2,1,0:T(2,128)S(1)}, u32[]{:S(2)}, u32[]{:S(2)}) %collective-permute-start.11) | collective-permute-done | bytes 16416 | tf_op jit(solution)/shard_map/ppermute | solution.py:317
  39.7 1.6 %collective-permute-done.10 = f32[2,2,1024]{2,1,0:T(2,128)S(1)} collective-permute-done((f32[2,2,1024]{2,1,0:T(2,128)S(1)}, f32[2,2,1024]{2,1,0:T(2,128)S(1)}, u32[]{:S(2)}, u32[]{:S(2)}) %collective-permute-start.10) | collective-permute-done | bytes 16416 | tf_op jit(solution)/shard_map/ppermute | solution.py:317
  41.9 2.7 %first_moments.1 = (f32[392,128]{1,0:T(8,128)S(1)}, f32[392,128]{1,0:T(8,128)S(1)}, f32[392,128]{1,0:T(8,128)S(1)}, f32[392,128]{1,0:T(8,128)S(1)}, bf16[512,2048]{1,0:T(8,128)(2,1)S(1)}) custom-call(f32[192,2048]{1,0:T(8,128)S(1)} %get-tuple-element.36.early_ref, f32[64,2048]{1,0:T(8,128)S(1)} %get-tuple-element.41.late_ref, ...), custom_call_target="tpu_custom_call" | custom-call | flops 10000000000 | bytes 100000000 | tf_op jit(solution)/shard_map/first_moments/pallas_call | solution.py:247
  44.6 1.2 %collective-permute-start.12 = (f32[392,128]{1,0:T(8,128)S(1)}, f32[392,128]{1,0:T(8,128)S(1)}, u32[]{:S(2)}, u32[]{:S(2)}) collective-permute-start(f32[392,128]{1,0:T(8,128)S(1)} %get-tuple-element.45), channel_id=1, source_target_pairs={{0,8},{4,12},{8,0},{12,4},{16,24},{20,28},{24,16},{28,20},{1,9},{5... | collective-permute-start | bytes 602120 | tf_op jit(solution)/shard_map/ppermute | solution.py:317
  45.8 2.6 %second_moments.1 = (f32[384,128]{1,0:T(8,128)S(1)}, f32[384,128]{1,0:T(8,128)S(1)}, f32[384,128]{1,0:T(8,128)S(1)}, f32[384,128]{1,0:T(8,128)S(1)}) custom-call(bf16[512,2048]{1,0:T(8,128)(2,1)S(1)} %get-tuple-element.46.resp_ref, bf16[2048,768]{1,0:T(8,128)(2,1)S(1)} %get-tuple-element.34.refs_3_.refs_1_.high_ref, ...), custom_call_target="tpu_custom_call" | custom-call | flops 10000000000 | bytes 100000000 | tf_op jit(solution)/shard_map/second_moments/pallas_call | solution.py:262
  49.3 2.1 %collective-permute-done.12 = f32[392,128]{1,0:T(8,128)S(1)} collective-permute-done((f32[392,128]{1,0:T(8,128)S(1)}, f32[392,128]{1,0:T(8,128)S(1)}, u32[]{:S(2)}, u32[]{:S(2)}) %collective-permute-start.12) | collective-permute-done | bytes 200736 | tf_op jit(solution)/shard_map/ppermute | solution.py:317
  51.5 1.6 %collective-permute-start.14 = (f32[384,128]{1,0:T(8,128)S(1)}, f32[384,128]{1,0:T(8,128)S(1)}, u32[]{:S(2)}, u32[]{:S(2)}) collective-permute-start(f32[384,128]{1,0:T(8,128)S(1)} %get-tuple-element.50), channel_id=1, source_target_pairs={{0,8},{4,12},{8,0},{12,4},{16,24},{20,28},{24,16},{28,20},{1,9},{5... | collective-permute-start | bytes 589832 | tf_op jit(solution)/shard_map/ppermute | solution.py:317
  53.1 1.8 %collective-permute-start.13 = (f32[392,128]{1,0:T(8,128)S(1)}, f32[392,128]{1,0:T(8,128)S(1)}, u32[]{:S(2)}, u32[]{:S(2)}) collective-permute-start(f32[392,128]{1,0:T(8,128)S(1)} %add.33), channel_id=1, source_target_pairs={{0,16},{4,20},{8,24},{12,28},{16,0},{20,4},{24,8},{28,12},{1,17},{... | collective-permute-start | bytes 602120 | tf_op jit(solution)/shard_map/ppermute | solution.py:317
  54.9 8.3 %collective-permute-done.14 = f32[384,128]{1,0:T(8,128)S(1)} collective-permute-done((f32[384,128]{1,0:T(8,128)S(1)}, f32[384,128]{1,0:T(8,128)S(1)}, u32[]{:S(2)}, u32[]{:S(2)}) %collective-permute-start.14) | collective-permute-done | bytes 196640 | tf_op jit(solution)/shard_map/ppermute | solution.py:317
  63.7 2.5 %collective-permute-start.17 = (f32[384,128]{1,0:T(8,128)S(1)}, f32[384,128]{1,0:T(8,128)S(1)}, u32[]{:S(2)}, u32[]{:S(2)}) collective-permute-start(f32[384,128]{1,0:T(8,128)S(1)} %get-tuple-element.57), channel_id=1, source_target_pairs={{0,8},{4,12},{8,0},{12,4},{16,24},{20,28},{24,16},{28,20},{1,9},{5... | collective-permute-start | bytes 589832 | tf_op jit(solution)/shard_map/ppermute | solution.py:317
  66.2 7.4 %collective-permute-done.16 = f32[384,128]{1,0:T(8,128)S(1)} collective-permute-done((f32[384,128]{1,0:T(8,128)S(1)}, f32[384,128]{1,0:T(8,128)S(1)}, u32[]{:S(2)}, u32[]{:S(2)}) %collective-permute-start.16) | collective-permute-done | bytes 196640 | tf_op jit(solution)/shard_map/ppermute | solution.py:317
  (41 shorter events, 10.3 us)
Async XLA Ops:
  0.6 7.7 %collective-permute-start.2 = (f32[1024,768]{1,0:T(8,128)}, f32[1024,768]{1,0:T(8,128)S(1)}, u32[]{:S(2)}, u32[]{:S(2)}) collective-permute-start(f32[1024,768]{1,0:T(8,128)} %own_ref.1), channel_id=1, source_target_pairs={{0,4},{4,0},{8,12},{12,8},{16,20},{20,16},{24,28},{28,24},{1,5},{5... | collective-permute-start | bytes 9437192 | tf_op jit(solution)/shard_map/ppermute | solution.py:317
  1.1 13.9 %collective-permute-start.4 = (f32[64,768]{1,0:T(8,128)}, f32[64,768]{1,0:T(8,128)S(1)}, u32[]{:S(2)}, u32[]{:S(2)}) collective-permute-start(f32[64,768]{1,0:T(8,128)} %variances_ref.1), channel_id=1, source_target_pairs={{0,16},{4,20},{8,24},{12,28},{16,0},{20,4},{24,8},{28,12},{1,17},{... | collective-permute-start | bytes 589832 | tf_op jit(solution)/shard_map/ppermute | solution.py:317
  4.8 12.2 %collective-permute-start.3 = (f32[64,768]{1,0:T(8,128)}, f32[64,768]{1,0:T(8,128)S(1)}, u32[]{:S(2)}, u32[]{:S(2)}) collective-permute-start(f32[64,768]{1,0:T(8,128)} %variances_ref.1), channel_id=1, source_target_pairs={{0,8},{4,12},{8,0},{12,4},{16,24},{20,28},{24,16},{28,20},{1,9},{5... | collective-permute-start | bytes 589832 | tf_op jit(solution)/shard_map/ppermute | solution.py:317
  6.4 2.1 %copy-start = (f32[1024,768]{1,0:T(8,128)S(1)}, f32[1024,768]{1,0:T(8,128)}, u32[]{:S(2)}) copy-start(f32[1024,768]{1,0:T(8,128)} %own_ref.1) | copy-start | bytes 9437188
  7.7 9.2 %copy-start.2 = (f32[64,768]{1,0:T(8,128)S(1)}, f32[64,768]{1,0:T(8,128)}, u32[]{:S(2)}) copy-start(f32[64,768]{1,0:T(8,128)} %variances_ref.1) | copy-start | bytes 589828
  7.8 15.7 %collective-permute-start.1 = (f32[392,128]{1,0:T(8,128)S(1)}, f32[392,128]{1,0:T(8,128)S(1)}, u32[]{:S(2)}, u32[]{:S(2)}) collective-permute-start(f32[392,128]{1,0:T(8,128)S(1)} %coefficients.1.refs_0_), channel_id=1, source_target_pairs={{0,16},{4,20},{8,24},{12,28},{16,0},{20,4},{24,8},{28,12},{1,17},{... | collective-permute-start | bytes 602120 | tf_op jit(solution)/shard_map/ppermute | solution.py:317
  8.2 16.2 %collective-permute-start = (f32[392,128]{1,0:T(8,128)S(1)}, f32[392,128]{1,0:T(8,128)S(1)}, u32[]{:S(2)}, u32[]{:S(2)}) collective-permute-start(f32[392,128]{1,0:T(8,128)S(1)} %coefficients.1.refs_0_), channel_id=1, source_target_pairs={{0,8},{4,12},{8,0},{12,4},{16,24},{20,28},{24,16},{28,20},{1,9},{5... | collective-permute-start | bytes 602120 | tf_op jit(solution)/shard_map/ppermute | solution.py:317
  15.1 13.5 %collective-permute-start.7 = (f32[64,768]{1,0:T(8,128)S(1)}, f32[64,768]{1,0:T(8,128)S(1)}, u32[]{:S(2)}, u32[]{:S(2)}) collective-permute-start(f32[64,768]{1,0:T(8,128)S(1)} %collective-permute-done.4.refs_2_), channel_id=1, source_target_pairs={{0,8},{4,12},{8,0},{12,4},{16,24},{20,28},{24,16},{28,20},{1,9},{5... | collective-permute-start | bytes 589832 | tf_op jit(solution)/shard_map/ppermute | solution.py:317
  23.5 7.9 %collective-permute-start.6 = (f32[256,128]{1,0:T(8,128)S(1)}, f32[256,128]{1,0:T(8,128)S(1)}, u32[]{:S(2)}, u32[]{:S(2)}) collective-permute-start(f32[256,128]{1,0:T(8,128)S(1)} %slice.48), channel_id=1, source_target_pairs={{0,8},{4,12},{8,0},{12,4},{16,24},{20,28},{24,16},{28,20},{1,9},{5... | collective-permute-start | bytes 393224 | tf_op jit(solution)/shard_map/ppermute | solution.py:317
  26.9 5.9 %collective-permute-start.5 = (f32[136,128]{1,0:T(8,128)S(1)}, f32[136,128]{1,0:T(8,128)S(1)}, u32[]{:S(2)}, u32[]{:S(2)}) collective-permute-start(f32[136,128]{1,0:T(8,128)S(1)} %slice.47), channel_id=1, source_target_pairs={{0,8},{4,12},{8,0},{12,4},{16,24},{20,28},{24,16},{28,20},{1,9},{5... | collective-permute-start | bytes 208904 | tf_op jit(solution)/shard_map/ppermute | solution.py:317
  33.6 1.2 %collective-permute-start.8 = (f32[2,2,1024]{2,1,0:T(2,128)S(1)}, f32[2,2,1024]{2,1,0:T(2,128)S(1)}, u32[]{:S(2)}, u32[]{:S(2)}) collective-permute-start(f32[2,2,1024]{2,1,0:T(2,128)S(1)} %get-tuple-element.42), channel_id=1, source_target_pairs={{0,4},{4,0},{8,12},{12,8},{16,20},{20,16},{24,28},{28,24},{1,5},{5... | collective-permute-start | bytes 49160 | tf_op jit(solution)/shard_map/ppermute | solution.py:317
  35.0 4.7 %collective-permute-start.11 = (f32[2,2,1024]{2,1,0:T(2,128)S(1)}, f32[2,2,1024]{2,1,0:T(2,128)S(1)}, u32[]{:S(2)}, u32[]{:S(2)}) collective-permute-start(f32[2,2,1024]{2,1,0:T(2,128)S(1)} %pad_maximum_fusion), channel_id=1, source_target_pairs={{0,3},{1,2},{2,1},{3,0},{4,7},{5,6},{6,5},{7,4},{8,11},{9,10},{10,... | collective-permute-start | bytes 49160 | tf_op jit(solution)/shard_map/ppermute | solution.py:317
  37.6 3.7 %collective-permute-start.10 = (f32[2,2,1024]{2,1,0:T(2,128)S(1)}, f32[2,2,1024]{2,1,0:T(2,128)S(1)}, u32[]{:S(2)}, u32[]{:S(2)}) collective-permute-start(f32[2,2,1024]{2,1,0:T(2,128)S(1)} %pad_maximum_fusion), channel_id=1, source_target_pairs={{0,2},{1,3},{2,0},{3,1},{4,6},{5,7},{6,4},{7,5},{8,10},{9,11},{10,... | collective-permute-start | bytes 49160 | tf_op jit(solution)/shard_map/ppermute | solution.py:317
  38.1 3.7 %collective-permute-start.9 = (f32[2,2,1024]{2,1,0:T(2,128)S(1)}, f32[2,2,1024]{2,1,0:T(2,128)S(1)}, u32[]{:S(2)}, u32[]{:S(2)}) collective-permute-start(f32[2,2,1024]{2,1,0:T(2,128)S(1)} %pad_maximum_fusion), channel_id=1, source_target_pairs={{0,1},{1,0},{2,3},{3,2},{4,5},{5,4},{6,7},{7,6},{8,9},{9,8},{10,11... | collective-permute-start | bytes 49160 | tf_op jit(solution)/shard_map/ppermute | solution.py:317
  44.6 6.9 %collective-permute-start.12 = (f32[392,128]{1,0:T(8,128)S(1)}, f32[392,128]{1,0:T(8,128)S(1)}, u32[]{:S(2)}, u32[]{:S(2)}) collective-permute-start(f32[392,128]{1,0:T(8,128)S(1)} %get-tuple-element.45), channel_id=1, source_target_pairs={{0,8},{4,12},{8,0},{12,4},{16,24},{20,28},{24,16},{28,20},{1,9},{5... | collective-permute-start | bytes 602120 | tf_op jit(solution)/shard_map/ppermute | solution.py:317
  45.8 28.0 %copy-start.1 = (f32[64,768]{1,0:T(8,128)S(1)}, f32[64,768]{1,0:T(8,128)}, u32[]{:S(2)}) copy-start(f32[64,768]{1,0:T(8,128)} %means_ref.1) | copy-start | bytes 589828
  45.8 28.0 %copy-start.3 = (f32[64]{0:T(128)S(1)}, f32[64]{0:T(128)}, u32[]{:S(2)}) copy-start(f32[64]{0:T(128)} %param.7) | copy-start | bytes 772
  48.4 14.8 %collective-permute-start.15 = (f32[392,128]{1,0:T(8,128)S(1)}, f32[392,128]{1,0:T(8,128)S(1)}, u32[]{:S(2)}, u32[]{:S(2)}) collective-permute-start(f32[392,128]{1,0:T(8,128)S(1)} %get-tuple-element.52), channel_id=1, source_target_pairs={{0,8},{4,12},{8,0},{12,4},{16,24},{20,28},{24,16},{28,20},{1,9},{5... | collective-permute-start | bytes 602120 | tf_op jit(solution)/shard_map/ppermute | solution.py:317
  51.5 11.7 %collective-permute-start.14 = (f32[384,128]{1,0:T(8,128)S(1)}, f32[384,128]{1,0:T(8,128)S(1)}, u32[]{:S(2)}, u32[]{:S(2)}) collective-permute-start(f32[384,128]{1,0:T(8,128)S(1)} %get-tuple-element.50), channel_id=1, source_target_pairs={{0,8},{4,12},{8,0},{12,4},{16,24},{20,28},{24,16},{28,20},{1,9},{5... | collective-permute-start | bytes 589832 | tf_op jit(solution)/shard_map/ppermute | solution.py:317
  53.1 13.1 %collective-permute-start.13 = (f32[392,128]{1,0:T(8,128)S(1)}, f32[392,128]{1,0:T(8,128)S(1)}, u32[]{:S(2)}, u32[]{:S(2)}) collective-permute-start(f32[392,128]{1,0:T(8,128)S(1)} %add.33), channel_id=1, source_target_pairs={{0,16},{4,20},{8,24},{12,28},{16,0},{20,4},{24,8},{28,12},{1,17},{... | collective-permute-start | bytes 602120 | tf_op jit(solution)/shard_map/ppermute | solution.py:317
  63.2 10.4 %collective-permute-start.16 = (f32[384,128]{1,0:T(8,128)S(1)}, f32[384,128]{1,0:T(8,128)S(1)}, u32[]{:S(2)}, u32[]{:S(2)}) collective-permute-start(f32[384,128]{1,0:T(8,128)S(1)} %add.35), channel_id=1, source_target_pairs={{0,16},{4,20},{8,24},{12,28},{16,0},{20,4},{24,8},{28,12},{1,17},{... | collective-permute-start | bytes 589832 | tf_op jit(solution)/shard_map/ppermute | solution.py:317
  63.7 10.1 %collective-permute-start.17 = (f32[384,128]{1,0:T(8,128)S(1)}, f32[384,128]{1,0:T(8,128)S(1)}, u32[]{:S(2)}, u32[]{:S(2)}) collective-permute-start(f32[384,128]{1,0:T(8,128)S(1)} %get-tuple-element.57), channel_id=1, source_target_pairs={{0,8},{4,12},{8,0},{12,4},{16,24},{20,28},{24,16},{28,20},{1,9},{5... | collective-permute-start | bytes 589832 | tf_op jit(solution)/shard_map/ppermute | solution.py:317

commit v9 on v5

--- a/solution.py
+++ b/solution.py
@@ -343,7 +343,7 @@
         ready = []
         for parts in held:
             for q in sorted((q for q in parts if q & bit and q != bit), reverse=True):
-                parts[q ^ bit] = parts[q ^ bit] + swap(after(parts.pop(q), *ready), "dp", 2 * bit)
+                parts[q ^ bit] = after(parts[q ^ bit], *ready) + swap(parts.pop(q), "dp", 2 * bit)
                 ready = [parts[q ^ bit]]
         for total, parts in zip(totals, held):
             part = swap(after(parts.pop(bit), *ready), "dp", 2 * bit)

time: 72.7 us -> 74.4 us (1.023)
  waiting for transfers between devices: 30.6 us -> 34.8 us
  starting transfers between devices: 21.8 us -> 19.2 us
    ppermute x18, waiting for transfers between devices: 30.6 us -> 34.8 us  [swap(): return lax.ppermute(value, axis, [(i, i ^ bit) for i in range(size)])]
    ppermute x18, starting transfers between devices: 21.8 us -> 19.2 us  [swap(): return lax.ppermute(value, axis, [(i, i ^ bit) for i in range(size)])]
  transfers between devices with their start and end apart: 18 -> 18, of which waited for: 13 -> 14; matrix products, arithmetic and copies ran while one was open for 0% -> 0% of each run, Pallas kernels for 20% -> 20%
where the time goes in v9:
time: 74.4 us; the launch traced here: 74.3 us
  waiting for transfers between devices  34.8 us (47%)
  starting transfers between devices  19.2 us (26%)
  Pallas kernels  19 us (26%)
  between operations  0.76 us (1%)
    ppermute x18, waiting for transfers between devices, swap(): return lax.ppermute(value, axis, [(i, i ^ bit) for i in range(size)])  34.8 us
    ppermute x18, starting transfers between devices, swap(): return lax.ppermute(value, axis, [(i, i ^ bit) for i in range(size)])  19.2 us
    pallas_call x5, Pallas kernels, score_call(): pl.pallas_call(body, out_shape=[jax.ShapeDtypeStruct(shape, F32) for shap...  9.25 us
    pallas_call x1, Pallas kernels, first_moments(): pl.pallas_call(functools.partial(first_kernel, n), out_shape=[pack] * (co...  2.67 us
    pallas_call x1, Pallas kernels, second_moments(): pl.pallas_call(functools.partial(second_kernel, n), out_shape=[pack] * (r...  2.59 us
    pallas_call x1, Pallas kernels, halves(): pl.pallas_call(halves_kernel, grid=(2 * steps,), in_specs=[pl.BlockSpec((...  2.25 us
  transfers between devices with their start and end apart: 18, of which 14 were waited for; matrix products, arithmetic and copies ran while one was open for 0% of the time, Pallas kernels for 20%

profile of v9, /device:TPU:0, one launch (start us, length us, event | category | flops | bytes accessed | tf_op | source)
XLA Modules:
  0.0 74.3 jit_solution(7053502715444663370)
XLA Ops:
  1.1 3.7 %collective-permute-start.4 = (f32[64,768]{1,0:T(8,128)}, f32[64,768]{1,0:T(8,128)S(1)}, u32[]{:S(2)}, u32[]{:S(2)}) collective-permute-start(f32[64,768]{1,0:T(8,128)} %variances_ref.1), channel_id=1, source_target_pairs={{0,16},{4,20},{8,24},{12,28},{16,0},{20,4},{24,8},{28,12},{1,17},{... | collective-permute-start | bytes 589832 | tf_op jit(solution)/shard_map/ppermute | solution.py:317
  4.8 1.6 %collective-permute-start.3 = (f32[64,768]{1,0:T(8,128)}, f32[64,768]{1,0:T(8,128)S(1)}, u32[]{:S(2)}, u32[]{:S(2)}) collective-permute-start(f32[64,768]{1,0:T(8,128)} %variances_ref.1), channel_id=1, source_target_pairs={{0,8},{4,12},{8,0},{12,4},{16,24},{20,28},{24,16},{28,20},{1,9},{5... | collective-permute-start | bytes 589832 | tf_op jit(solution)/shard_map/ppermute | solution.py:317
  6.4 1.3 %coefficients.1.refs_0_ = f32[392,128]{1,0:T(8,128)S(1)} custom-call(f32[64,768]{1,0:T(8,128)} %means_ref.1, f32[64,768]{1,0:T(8,128)} %variances_ref.1, f32[1,64]{1,0:T(1,128)} %bitcast.2), custom_call_target="tpu_custom_call" | custom-call | flops 10000000000 | bytes 100000000 | tf_op jit(solution)/shard_map/coefficients/pallas_call | solution.py:64
  8.5 2.2 %halves.1 = (bf16[2048,768]{1,0:T(8,128)(2,1)S(1)}, bf16[2048,768]{1,0:T(8,128)(2,1)S(1)}, bf16[2048,768]{1,0:T(8,128)(2,1)S(1)}, bf16[2048,768]{1,0:T(8,128)(2,1)S(1)}) custom-call(f32[1024,768]{1,0:T(8,128)S(1)} %copy-done, f32[1024,768]{1,0:T(8,128)S(1)} %collective-permute-done.2.other_ref), custom_call_target="tpu_custom_call" | custom-call | flops 10000000000 | bytes 100000000 | tf_op jit(solution)/shard_map/halves/pallas_call | solution.py:101
  10.7 4.4 %collective-permute-done.4.refs_2_ = f32[64,768]{1,0:T(8,128)S(1)} collective-permute-done((f32[64,768]{1,0:T(8,128)}, f32[64,768]{1,0:T(8,128)S(1)}, u32[]{:S(2)}, u32[]{:S(2)}) %collective-permute-start.4) | collective-permute-done | bytes 196640 | tf_op jit(solution)/shard_map/ppermute | solution.py:317
  17.0 2.4 %early_quad.1.refs_5_ = f32[192,2048]{1,0:T(8,128)S(1)} custom-call(f32[64,768]{1,0:T(8,128)S(1)} %copy-done.2, f32[64,768]{1,0:T(8,128)S(1)} %collective-permute-done.3.refs_1_, f32[64,768]{1,0:T(8,128)S(1)} %collective-permute-done.4.refs_2_, bf16[2048,768]{1,0:T(8,128)(2,1)S(1)} %get-tuple-element.35.refs_3_.refs_1_.high_ref, ...), custom_call_target="tpu_custom_call" | custom-call | flops 10000000000 | bytes 100000000 | tf_op jit(solution)/shard_map/early_quad/pallas_call | solution.py:206
  19.4 4.1 %collective-permute-done.1.refs_2_ = f32[392,128]{1,0:T(8,128)S(1)} collective-permute-done((f32[392,128]{1,0:T(8,128)S(1)}, f32[392,128]{1,0:T(8,128)S(1)}, u32[]{:S(2)}, u32[]{:S(2)}) %collective-permute-start.1) | collective-permute-done | bytes 200736 | tf_op jit(solution)/shard_map/ppermute | solution.py:317
  24.4 2.5 %early_scores.1 = (f32[192,2048]{1,0:T(8,128)S(1)}, f32[2,2048]{1,0:T(2,128)S(1)}) custom-call(f32[392,128]{1,0:T(8,128)S(1)} %coefficients.1.refs_0_, f32[392,128]{1,0:T(8,128)S(1)} %collective-permute-done.refs_1_, f32[392,128]{1,0:T(8,128)S(1)} %collective-permute-done.1.refs_2_, bf16[2048,768]{1,0:T(8,128)(2,1)S(1)} %get-tuple-element.33.refs_3_.refs_1_.high_ref, ...), custom_call_target="tpu_custom_call" | custom-call | flops 100000000 | bytes 1000000 | tf_op jit(solution)/shard_map/early_scores/pallas_call | solution.py:206
  26.9 1.3 %collective-permute-start.5 = (f32[136,128]{1,0:T(8,128)S(1)}, f32[136,128]{1,0:T(8,128)S(1)}, u32[]{:S(2)}, u32[]{:S(2)}) collective-permute-start(f32[136,128]{1,0:T(8,128)S(1)} %slice.47), channel_id=1, source_target_pairs={{0,8},{4,12},{8,0},{12,4},{16,24},{20,28},{24,16},{28,20},{1,9},{5... | collective-permute-start | bytes 208904 | tf_op jit(solution)/shard_map/ppermute | solution.py:317
  28.6 2.1 %late_quad.1.refs_3_ = f32[64,2048]{1,0:T(8,128)S(1)} custom-call(f32[64,768]{1,0:T(8,128)S(1)} %collective-permute-done.7.refs_0_, bf16[2048,768]{1,0:T(8,128)(2,1)S(1)} %get-tuple-element.35.refs_3_.refs_1_.high_ref, bf16[2048,768]{1,0:T(8,128)(2,1)S(1)} %get-tuple-element.36.refs_4_.refs_2_.low_ref), custom_call_target="tpu_custom_call" | custom-call | flops 100000000 | bytes 1000000 | tf_op jit(solution)/shard_map/late_quad/pallas_call | solution.py:206
  31.4 1.4 %late_head.1.refs_3_ = f32[64,2048]{1,0:T(8,128)S(1)} custom-call(f32[256,128]{1,0:T(8,128)S(1)} %collective-permute-done.6.refs_0_, bf16[2048,768]{1,0:T(8,128)(2,1)S(1)} %get-tuple-element.33.refs_3_.refs_1_.high_ref, bf16[2048,768]{1,0:T(8,128)(2,1)S(1)} %get-tuple-element.34.refs_4_.refs_2_.low_ref, f32[64,2048]{1,0:T(8,128)S(1)} %late_quad.1.refs_3_), custom_call_target="tpu_custom_call" | custom-call | flops 100000000 | bytes 1000000 | tf_op jit(solution)/shard_map/late_head/pallas_call | solution.py:206
  33.7 1.2 %collective-permute-done.8 = f32[2,2,1024]{2,1,0:T(2,128)S(1)} collective-permute-done((f32[2,2,1024]{2,1,0:T(2,128)S(1)}, f32[2,2,1024]{2,1,0:T(2,128)S(1)}, u32[]{:S(2)}, u32[]{:S(2)}) %collective-permute-start.8) | collective-permute-done | bytes 16416 | tf_op jit(solution)/shard_map/ppermute | solution.py:317
  35.0 2.6 %collective-permute-start.11 = (f32[2,2,1024]{2,1,0:T(2,128)S(1)}, f32[2,2,1024]{2,1,0:T(2,128)S(1)}, u32[]{:S(2)}, u32[]{:S(2)}) collective-permute-start(f32[2,2,1024]{2,1,0:T(2,128)S(1)} %pad_maximum_fusion), channel_id=1, source_target_pairs={{0,3},{1,2},{2,1},{3,0},{4,7},{5,6},{6,5},{7,4},{8,11},{9,10},{10,... | collective-permute-start | bytes 49160 | tf_op jit(solution)/shard_map/ppermute | solution.py:317
  38.5 1.1 %collective-permute-done.11 = f32[2,2,1024]{2,1,0:T(2,128)S(1)} collective-permute-done((f32[2,2,1024]{2,1,0:T(2,128)S(1)}, f32[2,2,1024]{2,1,0:T(2,128)S(1)}, u32[]{:S(2)}, u32[]{:S(2)}) %collective-permute-start.11) | collective-permute-done | bytes 16416 | tf_op jit(solution)/shard_map/ppermute | solution.py:317
  39.7 1.6 %collective-permute-done.10 = f32[2,2,1024]{2,1,0:T(2,128)S(1)} collective-permute-done((f32[2,2,1024]{2,1,0:T(2,128)S(1)}, f32[2,2,1024]{2,1,0:T(2,128)S(1)}, u32[]{:S(2)}, u32[]{:S(2)}) %collective-permute-start.10) | collective-permute-done | bytes 16416 | tf_op jit(solution)/shard_map/ppermute | solution.py:317
  41.9 2.7 %first_moments.1 = (f32[392,128]{1,0:T(8,128)S(1)}, f32[392,128]{1,0:T(8,128)S(1)}, f32[392,128]{1,0:T(8,128)S(1)}, f32[392,128]{1,0:T(8,128)S(1)}, bf16[512,2048]{1,0:T(8,128)(2,1)S(1)}) custom-call(f32[192,2048]{1,0:T(8,128)S(1)} %get-tuple-element.37.early_ref, f32[64,2048]{1,0:T(8,128)S(1)} %get-tuple-element.42.late_ref, ...), custom_call_target="tpu_custom_call" | custom-call | flops 10000000000 | bytes 100000000 | tf_op jit(solution)/shard_map/first_moments/pallas_call | solution.py:247
  44.6 1.2 %collective-permute-start.12 = (f32[392,128]{1,0:T(8,128)S(1)}, f32[392,128]{1,0:T(8,128)S(1)}, u32[]{:S(2)}, u32[]{:S(2)}) collective-permute-start(f32[392,128]{1,0:T(8,128)S(1)} %get-tuple-element.46), channel_id=1, source_target_pairs={{0,8},{4,12},{8,0},{12,4},{16,24},{20,28},{24,16},{28,20},{1,9},{5... | collective-permute-start | bytes 602120 | tf_op jit(solution)/shard_map/ppermute | solution.py:317
  45.8 2.6 %second_moments.1 = (f32[384,128]{1,0:T(8,128)S(1)}, f32[384,128]{1,0:T(8,128)S(1)}, f32[384,128]{1,0:T(8,128)S(1)}, f32[384,128]{1,0:T(8,128)S(1)}) custom-call(bf16[512,2048]{1,0:T(8,128)(2,1)S(1)} %get-tuple-element.47.resp_ref, bf16[2048,768]{1,0:T(8,128)(2,1)S(1)} %get-tuple-element.35.refs_3_.refs_1_.high_ref, ...), custom_call_target="tpu_custom_call" | custom-call | flops 10000000000 | bytes 100000000 | tf_op jit(solution)/shard_map/second_moments/pallas_call | solution.py:262
  49.3 4.3 %collective-permute-done.12 = f32[392,128]{1,0:T(8,128)S(1)} collective-permute-done((f32[392,128]{1,0:T(8,128)S(1)}, f32[392,128]{1,0:T(8,128)S(1)}, u32[]{:S(2)}, u32[]{:S(2)}) %collective-permute-start.12) | collective-permute-done | bytes 200736 | tf_op jit(solution)/shard_map/ppermute | solution.py:317
  54.4 2.3 %collective-permute-done.14 = f32[384,128]{1,0:T(8,128)S(1)} collective-permute-done((f32[384,128]{1,0:T(8,128)S(1)}, f32[384,128]{1,0:T(8,128)S(1)}, u32[]{:S(2)}, u32[]{:S(2)}) %collective-permute-start.14) | collective-permute-done | bytes 196640 | tf_op jit(solution)/shard_map/ppermute | solution.py:317
  57.3 1.5 %collective-permute-start.16 = (f32[384,128]{1,0:T(8,128)S(1)}, f32[384,128]{1,0:T(8,128)S(1)}, u32[]{:S(2)}, u32[]{:S(2)}) collective-permute-start(f32[384,128]{1,0:T(8,128)S(1)} %get-tuple-element.55), channel_id=1, source_target_pairs={{0,8},{4,12},{8,0},{12,4},{16,24},{20,28},{24,16},{28,20},{1,9},{5... | collective-permute-start | bytes 589832 | tf_op jit(solution)/shard_map/ppermute | solution.py:317
  58.8 1.4 %collective-permute-start.17 = (f32[384,128]{1,0:T(8,128)S(1)}, f32[384,128]{1,0:T(8,128)S(1)}, u32[]{:S(2)}, u32[]{:S(2)}) collective-permute-start(f32[384,128]{1,0:T(8,128)S(1)} %add.35), channel_id=1, source_target_pairs={{0,16},{4,20},{8,24},{12,28},{16,0},{20,4},{24,8},{28,12},{1,17},{... | collective-permute-start | bytes 589832 | tf_op jit(solution)/shard_map/ppermute | solution.py:317
  60.2 3.2 %collective-permute-done.13 = f32[392,128]{1,0:T(8,128)S(1)} collective-permute-done((f32[392,128]{1,0:T(8,128)S(1)}, f32[392,128]{1,0:T(8,128)S(1)}, u32[]{:S(2)}, u32[]{:S(2)}) %collective-permute-start.13) | collective-permute-done | bytes 200736 | tf_op jit(solution)/shard_map/ppermute | solution.py:317
  63.4 9.9 %collective-permute-done.16.near_second_ref = f32[384,128]{1,0:T(8,128)S(1)} collective-permute-done((f32[384,128]{1,0:T(8,128)S(1)}, f32[384,128]{1,0:T(8,128)S(1)}, u32[]{:S(2)}, u32[]{:S(2)}) %collective-permute-start.16) | collective-permute-done | bytes 196640 | tf_op jit(solution)/shard_map/ppermute | solution.py:317
  (41 shorter events, 11.0 us)
Async XLA Ops:
  0.6 7.7 %collective-permute-start.2 = (f32[1024,768]{1,0:T(8,128)}, f32[1024,768]{1,0:T(8,128)S(1)}, u32[]{:S(2)}, u32[]{:S(2)}) collective-permute-start(f32[1024,768]{1,0:T(8,128)} %own_ref.1), channel_id=1, source_target_pairs={{0,4},{4,0},{8,12},{12,8},{16,20},{20,16},{24,28},{28,24},{1,5},{5... | collective-permute-start | bytes 9437192 | tf_op jit(solution)/shard_map/ppermute | solution.py:317
  1.1 13.9 %collective-permute-start.4 = (f32[64,768]{1,0:T(8,128)}, f32[64,768]{1,0:T(8,128)S(1)}, u32[]{:S(2)}, u32[]{:S(2)}) collective-permute-start(f32[64,768]{1,0:T(8,128)} %variances_ref.1), channel_id=1, source_target_pairs={{0,16},{4,20},{8,24},{12,28},{16,0},{20,4},{24,8},{28,12},{1,17},{... | collective-permute-start | bytes 589832 | tf_op jit(solution)/shard_map/ppermute | solution.py:317
  4.8 12.2 %collective-permute-start.3 = (f32[64,768]{1,0:T(8,128)}, f32[64,768]{1,0:T(8,128)S(1)}, u32[]{:S(2)}, u32[]{:S(2)}) collective-permute-start(f32[64,768]{1,0:T(8,128)} %variances_ref.1), channel_id=1, source_target_pairs={{0,8},{4,12},{8,0},{12,4},{16,24},{20,28},{24,16},{28,20},{1,9},{5... | collective-permute-start | bytes 589832 | tf_op jit(solution)/shard_map/ppermute | solution.py:317
  6.4 2.1 %copy-start = (f32[1024,768]{1,0:T(8,128)S(1)}, f32[1024,768]{1,0:T(8,128)}, u32[]{:S(2)}) copy-start(f32[1024,768]{1,0:T(8,128)} %own_ref.1) | copy-start | bytes 9437188
  7.7 9.2 %copy-start.2 = (f32[64,768]{1,0:T(8,128)S(1)}, f32[64,768]{1,0:T(8,128)}, u32[]{:S(2)}) copy-start(f32[64,768]{1,0:T(8,128)} %variances_ref.1) | copy-start | bytes 589828
  7.8 15.7 %collective-permute-start.1 = (f32[392,128]{1,0:T(8,128)S(1)}, f32[392,128]{1,0:T(8,128)S(1)}, u32[]{:S(2)}, u32[]{:S(2)}) collective-permute-start(f32[392,128]{1,0:T(8,128)S(1)} %coefficients.1.refs_0_), channel_id=1, source_target_pairs={{0,16},{4,20},{8,24},{12,28},{16,0},{20,4},{24,8},{28,12},{1,17},{... | collective-permute-start | bytes 602120 | tf_op jit(solution)/shard_map/ppermute | solution.py:317
  8.2 16.2 %collective-permute-start = (f32[392,128]{1,0:T(8,128)S(1)}, f32[392,128]{1,0:T(8,128)S(1)}, u32[]{:S(2)}, u32[]{:S(2)}) collective-permute-start(f32[392,128]{1,0:T(8,128)S(1)} %coefficients.1.refs_0_), channel_id=1, source_target_pairs={{0,8},{4,12},{8,0},{12,4},{16,24},{20,28},{24,16},{28,20},{1,9},{5... | collective-permute-start | bytes 602120 | tf_op jit(solution)/shard_map/ppermute | solution.py:317
  15.1 13.5 %collective-permute-start.7 = (f32[64,768]{1,0:T(8,128)S(1)}, f32[64,768]{1,0:T(8,128)S(1)}, u32[]{:S(2)}, u32[]{:S(2)}) collective-permute-start(f32[64,768]{1,0:T(8,128)S(1)} %collective-permute-done.4.refs_2_), channel_id=1, source_target_pairs={{0,8},{4,12},{8,0},{12,4},{16,24},{20,28},{24,16},{28,20},{1,9},{5... | collective-permute-start | bytes 589832 | tf_op jit(solution)/shard_map/ppermute | solution.py:317
  23.5 7.9 %collective-permute-start.6 = (f32[256,128]{1,0:T(8,128)S(1)}, f32[256,128]{1,0:T(8,128)S(1)}, u32[]{:S(2)}, u32[]{:S(2)}) collective-permute-start(f32[256,128]{1,0:T(8,128)S(1)} %slice.48), channel_id=1, source_target_pairs={{0,8},{4,12},{8,0},{12,4},{16,24},{20,28},{24,16},{28,20},{1,9},{5... | collective-permute-start | bytes 393224 | tf_op jit(solution)/shard_map/ppermute | solution.py:317
  26.9 5.9 %collective-permute-start.5 = (f32[136,128]{1,0:T(8,128)S(1)}, f32[136,128]{1,0:T(8,128)S(1)}, u32[]{:S(2)}, u32[]{:S(2)}) collective-permute-start(f32[136,128]{1,0:T(8,128)S(1)} %slice.47), channel_id=1, source_target_pairs={{0,8},{4,12},{8,0},{12,4},{16,24},{20,28},{24,16},{28,20},{1,9},{5... | collective-permute-start | bytes 208904 | tf_op jit(solution)/shard_map/ppermute | solution.py:317
  33.6 1.2 %collective-permute-start.8 = (f32[2,2,1024]{2,1,0:T(2,128)S(1)}, f32[2,2,1024]{2,1,0:T(2,128)S(1)}, u32[]{:S(2)}, u32[]{:S(2)}) collective-permute-start(f32[2,2,1024]{2,1,0:T(2,128)S(1)} %get-tuple-element.43), channel_id=1, source_target_pairs={{0,4},{4,0},{8,12},{12,8},{16,20},{20,16},{24,28},{28,24},{1,5},{5... | collective-permute-start | bytes 49160 | tf_op jit(solution)/shard_map/ppermute | solution.py:317
  35.0 4.7 %collective-permute-start.11 = (f32[2,2,1024]{2,1,0:T(2,128)S(1)}, f32[2,2,1024]{2,1,0:T(2,128)S(1)}, u32[]{:S(2)}, u32[]{:S(2)}) collective-permute-start(f32[2,2,1024]{2,1,0:T(2,128)S(1)} %pad_maximum_fusion), channel_id=1, source_target_pairs={{0,3},{1,2},{2,1},{3,0},{4,7},{5,6},{6,5},{7,4},{8,11},{9,10},{10,... | collective-permute-start | bytes 49160 | tf_op jit(solution)/shard_map/ppermute | solution.py:317
  37.6 3.7 %collective-permute-start.10 = (f32[2,2,1024]{2,1,0:T(2,128)S(1)}, f32[2,2,1024]{2,1,0:T(2,128)S(1)}, u32[]{:S(2)}, u32[]{:S(2)}) collective-permute-start(f32[2,2,1024]{2,1,0:T(2,128)S(1)} %pad_maximum_fusion), channel_id=1, source_target_pairs={{0,2},{1,3},{2,0},{3,1},{4,6},{5,7},{6,4},{7,5},{8,10},{9,11},{10,... | collective-permute-start | bytes 49160 | tf_op jit(solution)/shard_map/ppermute | solution.py:317
  38.1 3.7 %collective-permute-start.9 = (f32[2,2,1024]{2,1,0:T(2,128)S(1)}, f32[2,2,1024]{2,1,0:T(2,128)S(1)}, u32[]{:S(2)}, u32[]{:S(2)}) collective-permute-start(f32[2,2,1024]{2,1,0:T(2,128)S(1)} %pad_maximum_fusion), channel_id=1, source_target_pairs={{0,1},{1,0},{2,3},{3,2},{4,5},{5,4},{6,7},{7,6},{8,9},{9,8},{10,11... | collective-permute-start | bytes 49160 | tf_op jit(solution)/shard_map/ppermute | solution.py:317
  44.6 9.0 %collective-permute-start.12 = (f32[392,128]{1,0:T(8,128)S(1)}, f32[392,128]{1,0:T(8,128)S(1)}, u32[]{:S(2)}, u32[]{:S(2)}) collective-permute-start(f32[392,128]{1,0:T(8,128)S(1)} %get-tuple-element.46), channel_id=1, source_target_pairs={{0,8},{4,12},{8,0},{12,4},{16,24},{20,28},{24,16},{28,20},{1,9},{5... | collective-permute-start | bytes 602120 | tf_op jit(solution)/shard_map/ppermute | solution.py:317
  45.8 27.5 %copy-start.1 = (f32[64,768]{1,0:T(8,128)S(1)}, f32[64,768]{1,0:T(8,128)}, u32[]{:S(2)}) copy-start(f32[64,768]{1,0:T(8,128)} %means_ref.1) | copy-start | bytes 589828
  45.8 27.5 %copy-start.3 = (f32[64]{0:T(128)S(1)}, f32[64]{0:T(128)}, u32[]{:S(2)}) copy-start(f32[64]{0:T(128)} %param.7) | copy-start | bytes 772
  48.4 8.3 %collective-permute-start.14 = (f32[384,128]{1,0:T(8,128)S(1)}, f32[384,128]{1,0:T(8,128)S(1)}, u32[]{:S(2)}, u32[]{:S(2)}) collective-permute-start(f32[384,128]{1,0:T(8,128)S(1)} %get-tuple-element.52), channel_id=1, source_target_pairs={{0,8},{4,12},{8,0},{12,4},{16,24},{20,28},{24,16},{28,20},{1,9},{5... | collective-permute-start | bytes 589832 | tf_op jit(solution)/shard_map/ppermute | solution.py:317
  53.6 9.7 %collective-permute-start.13 = (f32[392,128]{1,0:T(8,128)S(1)}, f32[392,128]{1,0:T(8,128)S(1)}, u32[]{:S(2)}, u32[]{:S(2)}) collective-permute-start(f32[392,128]{1,0:T(8,128)S(1)} %add.33), channel_id=1, source_target_pairs={{0,16},{4,20},{8,24},{12,28},{16,0},{20,4},{24,8},{28,12},{1,17},{... | collective-permute-start | bytes 602120 | tf_op jit(solution)/shard_map/ppermute | solution.py:317
  56.8 16.5 %collective-permute-start.15 = (f32[392,128]{1,0:T(8,128)S(1)}, f32[392,128]{1,0:T(8,128)S(1)}, u32[]{:S(2)}, u32[]{:S(2)}) collective-permute-start(f32[392,128]{1,0:T(8,128)S(1)} %get-tuple-element.53), channel_id=1, source_target_pairs={{0,8},{4,12},{8,0},{12,4},{16,24},{20,28},{24,16},{28,20},{1,9},{5... | collective-permute-start | bytes 602120 | tf_op jit(solution)/shard_map/ppermute | solution.py:317
  57.3 16.0 %collective-permute-start.16 = (f32[384,128]{1,0:T(8,128)S(1)}, f32[384,128]{1,0:T(8,128)S(1)}, u32[]{:S(2)}, u32[]{:S(2)}) collective-permute-start(f32[384,128]{1,0:T(8,128)S(1)} %get-tuple-element.55), channel_id=1, source_target_pairs={{0,8},{4,12},{8,0},{12,4},{16,24},{20,28},{24,16},{28,20},{1,9},{5... | collective-permute-start | bytes 589832 | tf_op jit(solution)/shard_map/ppermute | solution.py:317
  58.8 14.4 %collective-permute-start.17 = (f32[384,128]{1,0:T(8,128)S(1)}, f32[384,128]{1,0:T(8,128)S(1)}, u32[]{:S(2)}, u32[]{:S(2)}) collective-permute-start(f32[384,128]{1,0:T(8,128)S(1)} %add.35), channel_id=1, source_target_pairs={{0,16},{4,20},{8,24},{12,28},{16,0},{20,4},{24,8},{28,12},{1,17},{... | collective-permute-start | bytes 589832 | tf_op jit(solution)/shard_map/ppermute | solution.py:317

commit v10 on v4

--- a/solution.py
+++ b/solution.py
@@ -213,27 +213,34 @@
     )(*operands)
 
 
-def moment_tiles(resp_ref, high_ref, low_ref, packs, n):
+def moment_tiles(resp_ref, high_ref, low_ref, packs, n, rows=slice(None), add=False):
     for c in range(0, high_ref.shape[1], 2 * LANES):
         columns = slice(c, c + 2 * LANES)
-        total = product(resp_ref[...], high_ref[:, columns], low_ref[:, columns], WITHIN)
+        total = product(resp_ref[:, rows], high_ref[rows, columns], low_ref[rows, columns], WITHIN)
         for q, pack in enumerate(packs):
             for k in range(2):
-                place = (c // LANES + k) * n
-                pack[place : place + n, :] = total[q * n : (q + 1) * n, k * LANES : (k + 1) * LANES]
-
-
-def first_kernel(n, early_ref, late_ref, stats_ref, high_ref, low_ref, *refs):
-    *packs, resp_ref = refs
+                tile = slice((c // LANES + k) * n, (c // LANES + k + 1) * n)
+                part = total[q * n : (q + 1) * n, k * LANES : (k + 1) * LANES]
+                pack[tile, :] = pack[tile, :] + part if add else part
+
+
+def first_kernel(n, sets, early_ref, late_ref, *refs):
+    stats, (high_ref, low_ref, *packs, resp_ref) = refs[:sets], refs[sets:]
     comps = resp_ref.shape[0] // 2
+    half = stats[0].shape[2]
     counts = jnp.zeros((comps, LANES), F32)
-    for tile, block, part in half_tiles(stats_ref.shape[2]):
-        peak, total = stats_ref[block, 0:1, part], stats_ref[block, 1:2, part]
-        scores = jnp.concatenate([early_ref[:, tile], late_ref[:, tile]])
-        resp = jnp.exp(scores - peak) * (1.0 / total)
-        resp_ref[:comps, tile], resp_ref[comps:, tile] = split(resp)
-        counts += sum(resp[:, c : c + LANES] for c in range(0, resp.shape[1], LANES))
-    moment_tiles(resp_ref, high_ref, low_ref, packs, n)
+    for block in range(2):
+        for part in row_tiles(half):
+            tile = slice(block * half + part.start, block * half + part.stop)
+            parts = [(ref[block, 0:1, part], ref[block, 1:2, part]) for ref in stats]
+            peak = functools.reduce(jnp.maximum, [p for p, _ in parts])
+            total = sum(t * jnp.exp(p - peak) for p, t in parts)
+            scores = jnp.concatenate([early_ref[:, tile], late_ref[:, tile]])
+            resp = jnp.exp(scores - peak) * (1.0 / total)
+            resp_ref[:comps, tile], resp_ref[comps:, tile] = split(resp)
+            counts += sum(resp[:, c : c + LANES] for c in range(0, resp.shape[1], LANES))
+        rows = slice(block * half, (block + 1) * half)
+        moment_tiles(resp_ref, high_ref, low_ref, packs, n, rows, block == 1)
     column = jnp.sum(counts, axis=1, keepdims=True)
     for q, pack in enumerate(packs):
         row = to_row(column[q * n : (q + 1) * n], LANES)
@@ -245,12 +252,12 @@
     comps = early.shape[0] + late.shape[0]
     pack = jax.ShapeDtypeStruct((width // LANES * n + 8, LANES), F32)
     return pl.pallas_call(
-        functools.partial(first_kernel, n),
+        functools.partial(first_kernel, n, len(stats)),
         out_shape=[pack] * (comps // n) + [jax.ShapeDtypeStruct((2 * comps, rows), BF16)],
         cost_estimate=HEAVY,
         compiler_params=params(24),
         name="first_moments",
-    )(early, late, stats, high, low)
+    )(early, late, *stats, high, low)
 
 
 def second_kernel(n, resp_ref, high_ref, low_ref, *packs):
@@ -420,7 +427,7 @@
         early_stats,
     )
     stats = merge([stats, swap(stats, "dp", 1)[::-1]])
-    stats = merge([stats] + [swap(stats, "comp", q) for q in range(1, lax.axis_size("comp"))])
+    stats = [stats] + [swap(stats, "comp", q) for q in range(1, lax.axis_size("comp"))]
 
     *first, resp = first_moments(early, last, stats, x_high, x_low, n)
     second = second_moments(resp, s_high, s_low, n)

time: 72.7 us -> 72.6 us (level)
  no operation moved by 1% of the time
where the time goes in v10:
time: 72.6 us; the launch traced here: 72.5 us
  waiting for transfers between devices  30.6 us (42%)
  starting transfers between devices  21.8 us (30%)
  Pallas kernels  19 us (26%)
  between operations  0.75 us (1%)
    ppermute x18, waiting for transfers between devices, swap(): return lax.ppermute(value, axis, [(i, i ^ bit) for i in range(size)])  30.6 us
    ppermute x18, starting transfers between devices, swap(): return lax.ppermute(value, axis, [(i, i ^ bit) for i in range(size)])  21.8 us
    pallas_call x5, Pallas kernels, score_call(): pl.pallas_call(body, out_shape=[jax.ShapeDtypeStruct(shape, F32) for shap...  9.25 us
    pallas_call x1, Pallas kernels, first_moments(): pl.pallas_call(functools.partial(first_kernel, n, len(stats)), out_shape=...  2.66 us
    pallas_call x1, Pallas kernels, second_moments(): pl.pallas_call(functools.partial(second_kernel, n), out_shape=[pack] * (r...  2.58 us
    pallas_call x1, Pallas kernels, halves(): pl.pallas_call(halves_kernel, grid=(2 * steps,), in_specs=[pl.BlockSpec((...  2.25 us
  transfers between devices with their start and end apart: 18, of which 14 were waited for; matrix products, arithmetic and copies ran while one was open for 0% of the time, Pallas kernels for 20%

profile of v10, /device:TPU:0, one launch (start us, length us, event | category | flops | bytes accessed | tf_op | source)
XLA Modules:
  0.0 72.5 jit_solution(12195174179683249754)
XLA Ops:
  1.1 3.7 %collective-permute-start.4 = (f32[64,768]{1,0:T(8,128)}, f32[64,768]{1,0:T(8,128)S(1)}, u32[]{:S(2)}, u32[]{:S(2)}) collective-permute-start(f32[64,768]{1,0:T(8,128)} %variances_ref.1), channel_id=1, source_target_pairs={{0,16},{4,20},{8,24},{12,28},{16,0},{20,4},{24,8},{28,12},{1,17},{... | collective-permute-start | bytes 589832 | tf_op jit(solution)/shard_map/ppermute | solution.py:324
  4.8 1.6 %collective-permute-start.3 = (f32[64,768]{1,0:T(8,128)}, f32[64,768]{1,0:T(8,128)S(1)}, u32[]{:S(2)}, u32[]{:S(2)}) collective-permute-start(f32[64,768]{1,0:T(8,128)} %variances_ref.1), channel_id=1, source_target_pairs={{0,8},{4,12},{8,0},{12,4},{16,24},{20,28},{24,16},{28,20},{1,9},{5... | collective-permute-start | bytes 589832 | tf_op jit(solution)/shard_map/ppermute | solution.py:324
  6.4 1.3 %coefficients.1.refs_0_ = f32[392,128]{1,0:T(8,128)S(1)} custom-call(f32[64,768]{1,0:T(8,128)} %means_ref.1, f32[64,768]{1,0:T(8,128)} %variances_ref.1, f32[1,64]{1,0:T(1,128)} %bitcast.2), custom_call_target="tpu_custom_call" | custom-call | flops 10000000000 | bytes 100000000 | tf_op jit(solution)/shard_map/coefficients/pallas_call | solution.py:64
  8.5 2.2 %halves.1 = (bf16[2048,768]{1,0:T(8,128)(2,1)S(1)}, bf16[2048,768]{1,0:T(8,128)(2,1)S(1)}, bf16[2048,768]{1,0:T(8,128)(2,1)S(1)}, bf16[2048,768]{1,0:T(8,128)(2,1)S(1)}) custom-call(f32[1024,768]{1,0:T(8,128)S(1)} %copy-done, f32[1024,768]{1,0:T(8,128)S(1)} %collective-permute-done.2.other_ref), custom_call_target="tpu_custom_call" | custom-call | flops 10000000000 | bytes 100000000 | tf_op jit(solution)/shard_map/halves/pallas_call | solution.py:101
  10.7 4.4 %collective-permute-done.4.refs_2_ = f32[64,768]{1,0:T(8,128)S(1)} collective-permute-done((f32[64,768]{1,0:T(8,128)}, f32[64,768]{1,0:T(8,128)S(1)}, u32[]{:S(2)}, u32[]{:S(2)}) %collective-permute-start.4) | collective-permute-done | bytes 196640 | tf_op jit(solution)/shard_map/ppermute | solution.py:324
  17.0 2.4 %early_quad.1.refs_5_ = f32[192,2048]{1,0:T(8,128)S(1)} custom-call(f32[64,768]{1,0:T(8,128)S(1)} %copy-done.2, f32[64,768]{1,0:T(8,128)S(1)} %collective-permute-done.3.refs_1_, f32[64,768]{1,0:T(8,128)S(1)} %collective-permute-done.4.refs_2_, bf16[2048,768]{1,0:T(8,128)(2,1)S(1)} %get-tuple-element.33.refs_3_.refs_1_.high_ref, ...), custom_call_target="tpu_custom_call" | custom-call | flops 10000000000 | bytes 100000000 | tf_op jit(solution)/shard_map/early_quad/pallas_call | solution.py:206
  19.4 4.1 %collective-permute-done.1.refs_2_ = f32[392,128]{1,0:T(8,128)S(1)} collective-permute-done((f32[392,128]{1,0:T(8,128)S(1)}, f32[392,128]{1,0:T(8,128)S(1)}, u32[]{:S(2)}, u32[]{:S(2)}) %collective-permute-start.1) | collective-permute-done | bytes 200736 | tf_op jit(solution)/shard_map/ppermute | solution.py:324
  24.4 2.5 %early_scores.1 = (f32[192,2048]{1,0:T(8,128)S(1)}, f32[2,2048]{1,0:T(2,128)S(1)}) custom-call(f32[392,128]{1,0:T(8,128)S(1)} %coefficients.1.refs_0_, f32[392,128]{1,0:T(8,128)S(1)} %collective-permute-done.refs_1_, f32[392,128]{1,0:T(8,128)S(1)} %collective-permute-done.1.refs_2_, bf16[2048,768]{1,0:T(8,128)(2,1)S(1)} %get-tuple-element.31.refs_3_.refs_1_.refs_4_, ...), custom_call_target="tpu_custom_call" | custom-call | flops 100000000 | bytes 1000000 | tf_op jit(solution)/shard_map/early_scores/pallas_call | solution.py:206
  26.9 1.3 %collective-permute-start.5 = (f32[136,128]{1,0:T(8,128)S(1)}, f32[136,128]{1,0:T(8,128)S(1)}, u32[]{:S(2)}, u32[]{:S(2)}) collective-permute-start(f32[136,128]{1,0:T(8,128)S(1)} %slice.26), channel_id=1, source_target_pairs={{0,8},{4,12},{8,0},{12,4},{16,24},{20,28},{24,16},{28,20},{1,9},{5... | collective-permute-start | bytes 208904 | tf_op jit(solution)/shard_map/ppermute | solution.py:324
  28.6 2.1 %late_quad.1.refs_3_ = f32[64,2048]{1,0:T(8,128)S(1)} custom-call(f32[64,768]{1,0:T(8,128)S(1)} %collective-permute-done.7.refs_0_, bf16[2048,768]{1,0:T(8,128)(2,1)S(1)} %get-tuple-element.33.refs_3_.refs_1_.high_ref, bf16[2048,768]{1,0:T(8,128)(2,1)S(1)} %get-tuple-element.34.refs_4_.refs_2_.low_ref), custom_call_target="tpu_custom_call" | custom-call | flops 100000000 | bytes 1000000 | tf_op jit(solution)/shard_map/late_quad/pallas_call | solution.py:206
  31.4 1.4 %late_head.1.refs_3_ = f32[64,2048]{1,0:T(8,128)S(1)} custom-call(f32[256,128]{1,0:T(8,128)S(1)} %collective-permute-done.6.refs_0_, bf16[2048,768]{1,0:T(8,128)(2,1)S(1)} %get-tuple-element.31.refs_3_.refs_1_.refs_4_, bf16[2048,768]{1,0:T(8,128)(2,1)S(1)} %get-tuple-element.32.refs_4_.refs_2_.refs_5_, f32[64,2048]{1,0:T(8,128)S(1)} %late_quad.1.refs_3_), custom_call_target="tpu_custom_call" | custom-call | flops 100000000 | bytes 1000000 | tf_op jit(solution)/shard_map/late_head/pallas_call | solution.py:206
  33.7 1.2 %collective-permute-done.8 = f32[2,2,1024]{2,1,0:T(2,128)S(1)} collective-permute-done((f32[2,2,1024]{2,1,0:T(2,128)S(1)}, f32[2,2,1024]{2,1,0:T(2,128)S(1)}, u32[]{:S(2)}, u32[]{:S(2)}) %collective-permute-start.8) | collective-permute-done | bytes 16416 | tf_op jit(solution)/shard_map/ppermute | solution.py:324
  35.0 2.6 %collective-permute-start.11 = (f32[2,2,1024]{2,1,0:T(2,128)S(1)}, f32[2,2,1024]{2,1,0:T(2,128)S(1)}, u32[]{:S(2)}, u32[]{:S(2)}) collective-permute-start(f32[2,2,1024]{2,1,0:T(2,128)S(1)} %pad_maximum_fusion.refs_0_), channel_id=1, source_target_pairs={{0,3},{1,2},{2,1},{3,0},{4,7},{5,6},{6,5},{7,4},{8,11},{9,10},{10,... | collective-permute-start | bytes 49160 | tf_op jit(solution)/shard_map/ppermute | solution.py:324
  39.7 1.6 %collective-permute-done.10.refs_2_ = f32[2,2,1024]{2,1,0:T(2,128)S(1)} collective-permute-done((f32[2,2,1024]{2,1,0:T(2,128)S(1)}, f32[2,2,1024]{2,1,0:T(2,128)S(1)}, u32[]{:S(2)}, u32[]{:S(2)}) %collective-permute-start.10) | collective-permute-done | bytes 16416 | tf_op jit(solution)/shard_map/ppermute | solution.py:324
  41.8 2.7 %first_moments.1 = (f32[392,128]{1,0:T(8,128)S(1)}, f32[392,128]{1,0:T(8,128)S(1)}, f32[392,128]{1,0:T(8,128)S(1)}, f32[392,128]{1,0:T(8,128)S(1)}, bf16[512,2048]{1,0:T(8,128)(2,1)S(1)}) custom-call(f32[192,2048]{1,0:T(8,128)S(1)} %get-tuple-element.35.early_ref, f32[64,2048]{1,0:T(8,128)S(1)} %get-tuple-element.40.late_ref, ...), custom_call_target="tpu_custom_call" | custom-call | flops 10000000000 | bytes 100000000 | tf_op jit(solution)/shard_map/first_moments/pallas_call | solution.py:254
  44.5 1.2 %collective-permute-start.12 = (f32[392,128]{1,0:T(8,128)S(1)}, f32[392,128]{1,0:T(8,128)S(1)}, u32[]{:S(2)}, u32[]{:S(2)}) collective-permute-start(f32[392,128]{1,0:T(8,128)S(1)} %get-tuple-element.44), channel_id=1, source_target_pairs={{0,8},{4,12},{8,0},{12,4},{16,24},{20,28},{24,16},{28,20},{1,9},{5... | collective-permute-start | bytes 602120 | tf_op jit(solution)/shard_map/ppermute | solution.py:324
  45.7 2.6 %second_moments.1 = (f32[384,128]{1,0:T(8,128)S(1)}, f32[384,128]{1,0:T(8,128)S(1)}, f32[384,128]{1,0:T(8,128)S(1)}, f32[384,128]{1,0:T(8,128)S(1)}) custom-call(bf16[512,2048]{1,0:T(8,128)(2,1)S(1)} %get-tuple-element.45.resp_ref, bf16[2048,768]{1,0:T(8,128)(2,1)S(1)} %get-tuple-element.33.refs_3_.refs_1_.high_ref, ...), custom_call_target="tpu_custom_call" | custom-call | flops 10000000000 | bytes 100000000 | tf_op jit(solution)/shard_map/second_moments/pallas_call | solution.py:269
  48.3 1.9 %collective-permute-done.12 = f32[392,128]{1,0:T(8,128)S(1)} collective-permute-done((f32[392,128]{1,0:T(8,128)S(1)}, f32[392,128]{1,0:T(8,128)S(1)}, u32[]{:S(2)}, u32[]{:S(2)}) %collective-permute-start.12) | collective-permute-done | bytes 200736 | tf_op jit(solution)/shard_map/ppermute | solution.py:324
  50.3 1.2 %collective-permute-start.14 = (f32[384,128]{1,0:T(8,128)S(1)}, f32[384,128]{1,0:T(8,128)S(1)}, u32[]{:S(2)}, u32[]{:S(2)}) collective-permute-start(f32[384,128]{1,0:T(8,128)S(1)} %get-tuple-element.49), channel_id=1, source_target_pairs={{0,8},{4,12},{8,0},{12,4},{16,24},{20,28},{24,16},{28,20},{1,9},{5... | collective-permute-start | bytes 589832 | tf_op jit(solution)/shard_map/ppermute | solution.py:324
  51.5 1.7 %collective-permute-start.13 = (f32[392,128]{1,0:T(8,128)S(1)}, f32[392,128]{1,0:T(8,128)S(1)}, u32[]{:S(2)}, u32[]{:S(2)}) collective-permute-start(f32[392,128]{1,0:T(8,128)S(1)} %add.17), channel_id=1, source_target_pairs={{0,16},{4,20},{8,24},{12,28},{16,0},{20,4},{24,8},{28,12},{1,17},{... | collective-permute-start | bytes 602120 | tf_op jit(solution)/shard_map/ppermute | solution.py:324
  53.3 6.0 %collective-permute-done.14 = f32[384,128]{1,0:T(8,128)S(1)} collective-permute-done((f32[384,128]{1,0:T(8,128)S(1)}, f32[384,128]{1,0:T(8,128)S(1)}, u32[]{:S(2)}, u32[]{:S(2)}) %collective-permute-start.14) | collective-permute-done | bytes 196640 | tf_op jit(solution)/shard_map/ppermute | solution.py:324
  59.4 4.5 %collective-permute-start.15 = (f32[384,128]{1,0:T(8,128)S(1)}, f32[384,128]{1,0:T(8,128)S(1)}, u32[]{:S(2)}, u32[]{:S(2)}) collective-permute-start(f32[384,128]{1,0:T(8,128)S(1)} %add.19), channel_id=1, source_target_pairs={{0,16},{4,20},{8,24},{12,28},{16,0},{20,4},{24,8},{28,12},{1,17},{... | collective-permute-start | bytes 589832 | tf_op jit(solution)/shard_map/ppermute | solution.py:324
  64.0 4.1 %collective-permute-done.15 = f32[384,128]{1,0:T(8,128)S(1)} collective-permute-done((f32[384,128]{1,0:T(8,128)S(1)}, f32[384,128]{1,0:T(8,128)S(1)}, u32[]{:S(2)}, u32[]{:S(2)}) %collective-permute-start.15) | collective-permute-done | bytes 196640 | tf_op jit(solution)/shard_map/ppermute | solution.py:324
  68.2 3.3 %collective-permute-done.17.near_second_ref = f32[384,128]{1,0:T(8,128)S(1)} collective-permute-done((f32[384,128]{1,0:T(8,128)S(1)}, f32[384,128]{1,0:T(8,128)S(1)}, u32[]{:S(2)}, u32[]{:S(2)}) %collective-permute-start.17) | collective-permute-done | bytes 196640 | tf_op jit(solution)/shard_map/ppermute | solution.py:324
  (39 shorter events, 10.0 us)
Async XLA Ops:
  0.6 7.7 %collective-permute-start.2 = (f32[1024,768]{1,0:T(8,128)}, f32[1024,768]{1,0:T(8,128)S(1)}, u32[]{:S(2)}, u32[]{:S(2)}) collective-permute-start(f32[1024,768]{1,0:T(8,128)} %own_ref.1), channel_id=1, source_target_pairs={{0,4},{4,0},{8,12},{12,8},{16,20},{20,16},{24,28},{28,24},{1,5},{5... | collective-permute-start | bytes 9437192 | tf_op jit(solution)/shard_map/ppermute | solution.py:324
  1.1 13.9 %collective-permute-start.4 = (f32[64,768]{1,0:T(8,128)}, f32[64,768]{1,0:T(8,128)S(1)}, u32[]{:S(2)}, u32[]{:S(2)}) collective-permute-start(f32[64,768]{1,0:T(8,128)} %variances_ref.1), channel_id=1, source_target_pairs={{0,16},{4,20},{8,24},{12,28},{16,0},{20,4},{24,8},{28,12},{1,17},{... | collective-permute-start | bytes 589832 | tf_op jit(solution)/shard_map/ppermute | solution.py:324
  4.8 12.2 %collective-permute-start.3 = (f32[64,768]{1,0:T(8,128)}, f32[64,768]{1,0:T(8,128)S(1)}, u32[]{:S(2)}, u32[]{:S(2)}) collective-permute-start(f32[64,768]{1,0:T(8,128)} %variances_ref.1), channel_id=1, source_target_pairs={{0,8},{4,12},{8,0},{12,4},{16,24},{20,28},{24,16},{28,20},{1,9},{5... | collective-permute-start | bytes 589832 | tf_op jit(solution)/shard_map/ppermute | solution.py:324
  6.4 2.1 %copy-start = (f32[1024,768]{1,0:T(8,128)S(1)}, f32[1024,768]{1,0:T(8,128)}, u32[]{:S(2)}) copy-start(f32[1024,768]{1,0:T(8,128)} %own_ref.1) | copy-start | bytes 9437188
  7.7 9.2 %copy-start.2 = (f32[64,768]{1,0:T(8,128)S(1)}, f32[64,768]{1,0:T(8,128)}, u32[]{:S(2)}) copy-start(f32[64,768]{1,0:T(8,128)} %variances_ref.1) | copy-start | bytes 589828
  7.8 15.7 %collective-permute-start.1 = (f32[392,128]{1,0:T(8,128)S(1)}, f32[392,128]{1,0:T(8,128)S(1)}, u32[]{:S(2)}, u32[]{:S(2)}) collective-permute-start(f32[392,128]{1,0:T(8,128)S(1)} %coefficients.1.refs_0_), channel_id=1, source_target_pairs={{0,16},{4,20},{8,24},{12,28},{16,0},{20,4},{24,8},{28,12},{1,17},{... | collective-permute-start | bytes 602120 | tf_op jit(solution)/shard_map/ppermute | solution.py:324
  8.2 16.2 %collective-permute-start = (f32[392,128]{1,0:T(8,128)S(1)}, f32[392,128]{1,0:T(8,128)S(1)}, u32[]{:S(2)}, u32[]{:S(2)}) collective-permute-start(f32[392,128]{1,0:T(8,128)S(1)} %coefficients.1.refs_0_), channel_id=1, source_target_pairs={{0,8},{4,12},{8,0},{12,4},{16,24},{20,28},{24,16},{28,20},{1,9},{5... | collective-permute-start | bytes 602120 | tf_op jit(solution)/shard_map/ppermute | solution.py:324
  15.1 13.5 %collective-permute-start.7 = (f32[64,768]{1,0:T(8,128)S(1)}, f32[64,768]{1,0:T(8,128)S(1)}, u32[]{:S(2)}, u32[]{:S(2)}) collective-permute-start(f32[64,768]{1,0:T(8,128)S(1)} %collective-permute-done.4.refs_2_), channel_id=1, source_target_pairs={{0,8},{4,12},{8,0},{12,4},{16,24},{20,28},{24,16},{28,20},{1,9},{5... | collective-permute-start | bytes 589832 | tf_op jit(solution)/shard_map/ppermute | solution.py:324
  23.5 7.9 %collective-permute-start.6 = (f32[256,128]{1,0:T(8,128)S(1)}, f32[256,128]{1,0:T(8,128)S(1)}, u32[]{:S(2)}, u32[]{:S(2)}) collective-permute-start(f32[256,128]{1,0:T(8,128)S(1)} %slice.27), channel_id=1, source_target_pairs={{0,8},{4,12},{8,0},{12,4},{16,24},{20,28},{24,16},{28,20},{1,9},{5... | collective-permute-start | bytes 393224 | tf_op jit(solution)/shard_map/ppermute | solution.py:324
  26.9 5.9 %collective-permute-start.5 = (f32[136,128]{1,0:T(8,128)S(1)}, f32[136,128]{1,0:T(8,128)S(1)}, u32[]{:S(2)}, u32[]{:S(2)}) collective-permute-start(f32[136,128]{1,0:T(8,128)S(1)} %slice.26), channel_id=1, source_target_pairs={{0,8},{4,12},{8,0},{12,4},{16,24},{20,28},{24,16},{28,20},{1,9},{5... | collective-permute-start | bytes 208904 | tf_op jit(solution)/shard_map/ppermute | solution.py:324
  33.6 1.2 %collective-permute-start.8 = (f32[2,2,1024]{2,1,0:T(2,128)S(1)}, f32[2,2,1024]{2,1,0:T(2,128)S(1)}, u32[]{:S(2)}, u32[]{:S(2)}) collective-permute-start(f32[2,2,1024]{2,1,0:T(2,128)S(1)} %get-tuple-element.41), channel_id=1, source_target_pairs={{0,4},{4,0},{8,12},{12,8},{16,20},{20,16},{24,28},{28,24},{1,5},{5... | collective-permute-start | bytes 49160 | tf_op jit(solution)/shard_map/ppermute | solution.py:324
  35.0 4.7 %collective-permute-start.11 = (f32[2,2,1024]{2,1,0:T(2,128)S(1)}, f32[2,2,1024]{2,1,0:T(2,128)S(1)}, u32[]{:S(2)}, u32[]{:S(2)}) collective-permute-start(f32[2,2,1024]{2,1,0:T(2,128)S(1)} %pad_maximum_fusion.refs_0_), channel_id=1, source_target_pairs={{0,3},{1,2},{2,1},{3,0},{4,7},{5,6},{6,5},{7,4},{8,11},{9,10},{10,... | collective-permute-start | bytes 49160 | tf_op jit(solution)/shard_map/ppermute | solution.py:324
  37.6 3.7 %collective-permute-start.10 = (f32[2,2,1024]{2,1,0:T(2,128)S(1)}, f32[2,2,1024]{2,1,0:T(2,128)S(1)}, u32[]{:S(2)}, u32[]{:S(2)}) collective-permute-start(f32[2,2,1024]{2,1,0:T(2,128)S(1)} %pad_maximum_fusion.refs_0_), channel_id=1, source_target_pairs={{0,2},{1,3},{2,0},{3,1},{4,6},{5,7},{6,4},{7,5},{8,10},{9,11},{10,... | collective-permute-start | bytes 49160 | tf_op jit(solution)/shard_map/ppermute | solution.py:324
  38.1 3.7 %collective-permute-start.9 = (f32[2,2,1024]{2,1,0:T(2,128)S(1)}, f32[2,2,1024]{2,1,0:T(2,128)S(1)}, u32[]{:S(2)}, u32[]{:S(2)}) collective-permute-start(f32[2,2,1024]{2,1,0:T(2,128)S(1)} %pad_maximum_fusion.refs_0_), channel_id=1, source_target_pairs={{0,1},{1,0},{2,3},{3,2},{4,5},{5,4},{6,7},{7,6},{8,9},{9,8},{10,11... | collective-permute-start | bytes 49160 | tf_op jit(solution)/shard_map/ppermute | solution.py:324
  44.5 5.8 %collective-permute-start.12 = (f32[392,128]{1,0:T(8,128)S(1)}, f32[392,128]{1,0:T(8,128)S(1)}, u32[]{:S(2)}, u32[]{:S(2)}) collective-permute-start(f32[392,128]{1,0:T(8,128)S(1)} %get-tuple-element.44), channel_id=1, source_target_pairs={{0,8},{4,12},{8,0},{12,4},{16,24},{20,28},{24,16},{28,20},{1,9},{5... | collective-permute-start | bytes 602120 | tf_op jit(solution)/shard_map/ppermute | solution.py:324
  45.7 25.8 %copy-start.1 = (f32[64,768]{1,0:T(8,128)S(1)}, f32[64,768]{1,0:T(8,128)}, u32[]{:S(2)}) copy-start(f32[64,768]{1,0:T(8,128)} %means_ref.1) | copy-start | bytes 589828
  45.7 25.8 %copy-start.3 = (f32[64]{0:T(128)S(1)}, f32[64]{0:T(128)}, u32[]{:S(2)}) copy-start(f32[64]{0:T(128)} %param.7) | copy-start | bytes 772
  50.3 9.0 %collective-permute-start.14 = (f32[384,128]{1,0:T(8,128)S(1)}, f32[384,128]{1,0:T(8,128)S(1)}, u32[]{:S(2)}, u32[]{:S(2)}) collective-permute-start(f32[384,128]{1,0:T(8,128)S(1)} %get-tuple-element.49), channel_id=1, source_target_pairs={{0,8},{4,12},{8,0},{12,4},{16,24},{20,28},{24,16},{28,20},{1,9},{5... | collective-permute-start | bytes 589832 | tf_op jit(solution)/shard_map/ppermute | solution.py:324
  51.5 12.5 %collective-permute-start.13 = (f32[392,128]{1,0:T(8,128)S(1)}, f32[392,128]{1,0:T(8,128)S(1)}, u32[]{:S(2)}, u32[]{:S(2)}) collective-permute-start(f32[392,128]{1,0:T(8,128)S(1)} %add.17), channel_id=1, source_target_pairs={{0,16},{4,20},{8,24},{12,28},{16,0},{20,4},{24,8},{28,12},{1,17},{... | collective-permute-start | bytes 602120 | tf_op jit(solution)/shard_map/ppermute | solution.py:324
  59.3 12.2 %collective-permute-start.16 = (f32[392,128]{1,0:T(8,128)S(1)}, f32[392,128]{1,0:T(8,128)S(1)}, u32[]{:S(2)}, u32[]{:S(2)}) collective-permute-start(f32[392,128]{1,0:T(8,128)S(1)} %get-tuple-element.53), channel_id=1, source_target_pairs={{0,8},{4,12},{8,0},{12,4},{16,24},{20,28},{24,16},{28,20},{1,9},{5... | collective-permute-start | bytes 602120 | tf_op jit(solution)/shard_map/ppermute | solution.py:324
  59.4 8.8 %collective-permute-start.15 = (f32[384,128]{1,0:T(8,128)S(1)}, f32[384,128]{1,0:T(8,128)S(1)}, u32[]{:S(2)}, u32[]{:S(2)}) collective-permute-start(f32[384,128]{1,0:T(8,128)S(1)} %add.19), channel_id=1, source_target_pairs={{0,16},{4,20},{8,24},{12,28},{16,0},{20,4},{24,8},{28,12},{1,17},{... | collective-permute-start | bytes 589832 | tf_op jit(solution)/shard_map/ppermute | solution.py:324
  63.9 7.6 %collective-permute-start.17 = (f32[384,128]{1,0:T(8,128)S(1)}, f32[384,128]{1,0:T(8,128)S(1)}, u32[]{:S(2)}, u32[]{:S(2)}) collective-permute-start(f32[384,128]{1,0:T(8,128)S(1)} %get-tuple-element.55), channel_id=1, source_target_pairs={{0,8},{4,12},{8,0},{12,4},{16,24},{20,28},{24,16},{28,20},{1,9},{5... | collective-permute-start | bytes 589832 | tf_op jit(solution)/shard_map/ppermute | solution.py:324

commit v11 on v10

--- a/solution.py
+++ b/solution.py
@@ -275,10 +275,45 @@
     )(resp, high, low)
 
 
+def kept_kernel(
+    means_hbm, variances_hbm, mass_hbm, first_ref, second_ref, means_ref, variances_ref, mass_ref, sems
+):
+    sources = (variances_hbm, means_hbm, mass_hbm)
+    targets = (variances_ref, means_ref, mass_ref)
+    copies = [pltpu.make_async_copy(s, t, sems.at[i]) for i, (s, t) in enumerate(zip(sources, targets))]
+    for copy in copies:
+        copy.start()
+    for copy in copies:
+        copy.wait()
+    means = means_ref[...]
+    kept = 0.4 * to_column(mass_ref[...], means.shape[0])
+    first_ref[...] = kept * means
+    second_ref[...] = kept * (variances_ref[...] + means * means)
+
+
+def kept_moments(means, variances, mass, ready):
+    n, width = means.shape
+    operands = (means, variances, after(mass.reshape(1, n), ready))
+    return pl.pallas_call(
+        kept_kernel,
+        in_specs=[pl.BlockSpec(memory_space=pl.ANY)] * 3,
+        out_shape=[jax.ShapeDtypeStruct((n, width), F32)] * 2,
+        scratch_shapes=[
+            pltpu.VMEM((n, width), F32),
+            pltpu.VMEM((n, width), F32),
+            pltpu.VMEM((1, n), F32),
+            pltpu.SemaphoreType.DMA((3,)),
+        ],
+        cost_estimate=HEAVY,
+        compiler_params=params(16),
+        name="kept_moments",
+    )(*(pltpu.with_memory_space_constraint(x, pltpu.HBM) for x in operands))
+
+
 def update_kernel(
     scale,
-    means_ref,
-    variances_ref,
+    kept_first_ref,
+    kept_second_ref,
     mass_ref,
     first_ref,
     second_ref,
@@ -288,34 +323,32 @@
     new_variances_ref,
     new_mass_ref,
 ):
-    n, width = means_ref.shape
+    n, width = kept_first_ref.shape
     tiles = width // LANES * n
     row = first_ref[tiles : tiles + 1, :n] + near_first_ref[tiles : tiles + 1, :n]
     new_row = 0.4 * mass_ref[...] + scale * row
     new_mass_ref[...] = new_row
     inverse = 1.0 / to_column(new_row, n)
-    kept = 0.4 * to_column(mass_ref[...], n)
     for c in range(width // LANES):
         lanes, tile = slice(c * LANES, (c + 1) * LANES), slice(c * n, (c + 1) * n)
-        means, variances = means_ref[:, lanes], variances_ref[:, lanes]
         first = first_ref[tile, :] + near_first_ref[tile, :]
         second = second_ref[tile, :] + near_second_ref[tile, :]
-        new_means = (kept * means + scale * first) * inverse
+        new_means = (kept_first_ref[:, lanes] + scale * first) * inverse
         new_means_ref[:, lanes] = new_means
-        second_moment = kept * (variances + means * means) + scale * second
+        second_moment = kept_second_ref[:, lanes] + scale * second
         new_variances_ref[:, lanes] = second_moment * inverse - new_means * new_means
 
 
-def update(scale, means, variances, mass, *sums):
+def update(scale, kept, mass, *sums):
     n = mass.shape[0]
-    block = jax.ShapeDtypeStruct(means.shape, F32)
+    block = jax.ShapeDtypeStruct(kept[0].shape, F32)
     new_means, new_variances, new_mass = pl.pallas_call(
         functools.partial(update_kernel, scale),
         out_shape=(block, block, jax.ShapeDtypeStruct((1, n), F32)),
         cost_estimate=HEAVY,
         compiler_params=params(16),
         name="update",
-    )(means, variances, mass.reshape(1, n), *sums)
+    )(*kept, mass.reshape(1, n), *sums)
     return new_means, new_variances, new_mass.reshape(n)
 
 
@@ -342,7 +375,7 @@
     return held
 
 
-def scatter_planes(first, second):
+def scatter_planes(first, second, beside):
     held = [dict(enumerate(parts)) for parts in (first, second)]
     totals, near = [[parts.pop(0)] for parts in held], []
     planes, bit = len(first), 1
@@ -352,11 +385,14 @@
             for q in sorted((q for q in parts if q & bit and q != bit), reverse=True):
                 parts[q ^ bit] = parts[q ^ bit] + swap(after(parts.pop(q), *ready), "dp", 2 * bit)
                 ready = [parts[q ^ bit]]
+            if bit == 1 and parts is held[0]:
+                made = beside(ready[0])
+                held[0] = {q: after(part, made[0]) if q == 2 else part for q, part in parts.items()}
         for total, parts in zip(totals, held):
             part = swap(after(parts.pop(bit), *ready), "dp", 2 * bit)
             (near if bit == 1 else total).append(part)
         bit *= 2
-    return *lax.optimization_barrier(tuple(sum(t[1:], t[0]) for t in totals)), *near
+    return made, *lax.optimization_barrier(tuple(sum(t[1:], t[0]) for t in totals)), *near
 
 
 def merge(stats):
@@ -433,12 +469,13 @@
     second = second_moments(resp, s_high, s_low, n)
     place = {q: i for i, q in enumerate(order + late)}
     first, second = ([parts[place[q]] for q in range(planes)] for parts in (first, second))
-    sums = scatter_planes(first, second)
+    olds = (comp_means, comp_variances, comp_mass)
+    kept, *sums = scatter_planes(first, second, lambda ready: kept_moments(*olds, ready))
 
     total_comps = n * lax.axis_size("dp") * lax.axis_size("comp")
     total_rows = embeddings.shape[0] * lax.axis_size("dp")
     scale = 0.6 * (total_comps / total_rows)
-    return update(scale, comp_means, comp_variances, comp_mass, *sums)
+    return update(scale, kept, comp_mass, *sums)
 
 
 def solution(mesh):

time: 72.6 us -> 73.7 us (1.015)
  starting transfers between devices: 21.8 us -> 20.3 us
  waiting for transfers between devices: 30.6 us -> 32 us
  Pallas kernels: 19 us -> 20.1 us
    ppermute x18, starting transfers between devices: 21.8 us -> 20.3 us  [swap(): return lax.ppermute(value, axis, [(i, i ^ bit) for i in range(size)])]
    ppermute x18, waiting for transfers between devices: 30.6 us -> 32 us  [swap(): return lax.ppermute(value, axis, [(i, i ^ bit) for i in range(size)])]
    pallas_call x0 -> x1, Pallas kernels: none -> 1.15 us  [kept_moments(): pl.pallas_call(kept_kernel, in_specs=[pl.BlockSpec(memory_space=pl.ANY)]...]
  transfers between devices with their start and end apart: 18 -> 18, of which waited for: 14 -> 15; matrix products, arithmetic and copies ran while one was open for 0% -> 0% of each run, Pallas kernels for 20% -> 21%
where the time goes in v11:
time: 73.7 us; the launch traced here: 73.6 us
  waiting for transfers between devices  32 us (43%)
  starting transfers between devices  20.3 us (28%)
  Pallas kernels  20.1 us (27%)
  between operations  0.76 us (1%)
    ppermute x18, waiting for transfers between devices, swap(): return lax.ppermute(value, axis, [(i, i ^ bit) for i in range(size)])  32 us
    ppermute x18, starting transfers between devices, swap(): return lax.ppermute(value, axis, [(i, i ^ bit) for i in range(size)])  20.3 us
    pallas_call x5, Pallas kernels, score_call(): pl.pallas_call(body, out_shape=[jax.ShapeDtypeStruct(shape, F32) for shap...  9.25 us
    pallas_call x1, Pallas kernels, first_moments(): pl.pallas_call(functools.partial(first_kernel, n, len(stats)), out_shape=...  2.66 us
    pallas_call x1, Pallas kernels, second_moments(): pl.pallas_call(functools.partial(second_kernel, n), out_shape=[pack] * (r...  2.58 us
    pallas_call x1, Pallas kernels, halves(): pl.pallas_call(halves_kernel, grid=(2 * steps,), in_specs=[pl.BlockSpec((...  2.25 us
  transfers between devices with their start and end apart: 18, of which 15 were waited for; matrix products, arithmetic and copies ran while one was open for 0% of the time, Pallas kernels for 21%

profile of v11, /device:TPU:0, one launch (start us, length us, event | category | flops | bytes accessed | tf_op | source)
XLA Modules:
  0.0 73.6 jit_solution(9231327046482314565)
XLA Ops:
  1.1 3.7 %collective-permute-start.4 = (f32[64,768]{1,0:T(8,128)}, f32[64,768]{1,0:T(8,128)S(1)}, u32[]{:S(2)}, u32[]{:S(2)}) collective-permute-start(f32[64,768]{1,0:T(8,128)} %variances_hbm.3), channel_id=1, source_target_pairs={{0,16},{4,20},{8,24},{12,28},{16,0},{20,4},{24,8},{28,12},{1,17},{... | collective-permute-start | bytes 589832 | tf_op jit(solution)/shard_map/ppermute | solution.py:357
  4.8 1.6 %collective-permute-start.3 = (f32[64,768]{1,0:T(8,128)}, f32[64,768]{1,0:T(8,128)S(1)}, u32[]{:S(2)}, u32[]{:S(2)}) collective-permute-start(f32[64,768]{1,0:T(8,128)} %variances_hbm.3), channel_id=1, source_target_pairs={{0,8},{4,12},{8,0},{12,4},{16,24},{20,28},{24,16},{28,20},{1,9},{5... | collective-permute-start | bytes 589832 | tf_op jit(solution)/shard_map/ppermute | solution.py:357
  6.4 1.3 %coefficients.1.refs_0_ = f32[392,128]{1,0:T(8,128)S(1)} custom-call(f32[64,768]{1,0:T(8,128)} %means_hbm.3, f32[64,768]{1,0:T(8,128)} %variances_hbm.3, f32[1,64]{1,0:T(1,128)} %bitcast.2), custom_call_target="tpu_custom_call" | custom-call | flops 10000000000 | bytes 100000000 | tf_op jit(solution)/shard_map/coefficients/pallas_call | solution.py:64
  8.5 2.2 %halves.1 = (bf16[2048,768]{1,0:T(8,128)(2,1)S(1)}, bf16[2048,768]{1,0:T(8,128)(2,1)S(1)}, bf16[2048,768]{1,0:T(8,128)(2,1)S(1)}, bf16[2048,768]{1,0:T(8,128)(2,1)S(1)}) custom-call(f32[1024,768]{1,0:T(8,128)S(1)} %copy-done, f32[1024,768]{1,0:T(8,128)S(1)} %collective-permute-done.2.other_ref), custom_call_target="tpu_custom_call" | custom-call | flops 10000000000 | bytes 100000000 | tf_op jit(solution)/shard_map/halves/pallas_call | solution.py:101
  10.7 4.4 %collective-permute-done.4.refs_2_ = f32[64,768]{1,0:T(8,128)S(1)} collective-permute-done((f32[64,768]{1,0:T(8,128)}, f32[64,768]{1,0:T(8,128)S(1)}, u32[]{:S(2)}, u32[]{:S(2)}) %collective-permute-start.4) | collective-permute-done | bytes 196640 | tf_op jit(solution)/shard_map/ppermute | solution.py:357
  17.0 2.4 %early_quad.1.refs_5_ = f32[192,2048]{1,0:T(8,128)S(1)} custom-call(f32[64,768]{1,0:T(8,128)S(1)} %copy-done.1, f32[64,768]{1,0:T(8,128)S(1)} %collective-permute-done.3.refs_1_, f32[64,768]{1,0:T(8,128)S(1)} %collective-permute-done.4.refs_2_, bf16[2048,768]{1,0:T(8,128)(2,1)S(1)} %get-tuple-element.37.refs_3_.refs_1_.high_ref, ...), custom_call_target="tpu_custom_call" | custom-call | flops 10000000000 | bytes 100000000 | tf_op jit(solution)/shard_map/early_quad/pallas_call | solution.py:206
  19.4 4.1 %collective-permute-done.1.refs_2_ = f32[392,128]{1,0:T(8,128)S(1)} collective-permute-done((f32[392,128]{1,0:T(8,128)S(1)}, f32[392,128]{1,0:T(8,128)S(1)}, u32[]{:S(2)}, u32[]{:S(2)}) %collective-permute-start.1) | collective-permute-done | bytes 200736 | tf_op jit(solution)/shard_map/ppermute | solution.py:357
  24.4 2.5 %early_scores.1 = (f32[192,2048]{1,0:T(8,128)S(1)}, f32[2,2048]{1,0:T(2,128)S(1)}) custom-call(f32[392,128]{1,0:T(8,128)S(1)} %coefficients.1.refs_0_, f32[392,128]{1,0:T(8,128)S(1)} %collective-permute-done.refs_1_, f32[392,128]{1,0:T(8,128)S(1)} %collective-permute-done.1.refs_2_, bf16[2048,768]{1,0:T(8,128)(2,1)S(1)} %get-tuple-element.35.refs_3_.refs_1_.refs_4_, ...), custom_call_target="tpu_custom_call" | custom-call | flops 100000000 | bytes 1000000 | tf_op jit(solution)/shard_map/early_scores/pallas_call | solution.py:206
  26.9 1.3 %collective-permute-start.5 = (f32[136,128]{1,0:T(8,128)S(1)}, f32[136,128]{1,0:T(8,128)S(1)}, u32[]{:S(2)}, u32[]{:S(2)}) collective-permute-start(f32[136,128]{1,0:T(8,128)S(1)} %slice.26), channel_id=1, source_target_pairs={{0,8},{4,12},{8,0},{12,4},{16,24},{20,28},{24,16},{28,20},{1,9},{5... | collective-permute-start | bytes 208904 | tf_op jit(solution)/shard_map/ppermute | solution.py:357
  28.6 2.1 %late_quad.1.refs_3_ = f32[64,2048]{1,0:T(8,128)S(1)} custom-call(f32[64,768]{1,0:T(8,128)S(1)} %collective-permute-done.7.refs_0_, bf16[2048,768]{1,0:T(8,128)(2,1)S(1)} %get-tuple-element.37.refs_3_.refs_1_.high_ref, bf16[2048,768]{1,0:T(8,128)(2,1)S(1)} %get-tuple-element.38.refs_4_.refs_2_.low_ref), custom_call_target="tpu_custom_call" | custom-call | flops 100000000 | bytes 1000000 | tf_op jit(solution)/shard_map/late_quad/pallas_call | solution.py:206
  31.4 1.4 %late_head.1.refs_3_ = f32[64,2048]{1,0:T(8,128)S(1)} custom-call(f32[256,128]{1,0:T(8,128)S(1)} %collective-permute-done.6.refs_0_, bf16[2048,768]{1,0:T(8,128)(2,1)S(1)} %get-tuple-element.35.refs_3_.refs_1_.refs_4_, bf16[2048,768]{1,0:T(8,128)(2,1)S(1)} %get-tuple-element.36.refs_4_.refs_2_.refs_5_, f32[64,2048]{1,0:T(8,128)S(1)} %late_quad.1.refs_3_), custom_call_target="tpu_custom_call" | custom-call | flops 100000000 | bytes 1000000 | tf_op jit(solution)/shard_map/late_head/pallas_call | solution.py:206
  35.0 2.6 %collective-permute-start.11 = (f32[2,2,1024]{2,1,0:T(2,128)S(1)}, f32[2,2,1024]{2,1,0:T(2,128)S(1)}, u32[]{:S(2)}, u32[]{:S(2)}) collective-permute-start(f32[2,2,1024]{2,1,0:T(2,128)S(1)} %pad_maximum_fusion.refs_0_), channel_id=1, source_target_pairs={{0,3},{1,2},{2,1},{3,0},{4,7},{5,6},{6,5},{7,4},{8,11},{9,10},{10,... | collective-permute-start | bytes 49160 | tf_op jit(solution)/shard_map/ppermute | solution.py:357
  39.7 1.6 %collective-permute-done.10.refs_2_ = f32[2,2,1024]{2,1,0:T(2,128)S(1)} collective-permute-done((f32[2,2,1024]{2,1,0:T(2,128)S(1)}, f32[2,2,1024]{2,1,0:T(2,128)S(1)}, u32[]{:S(2)}, u32[]{:S(2)}) %collective-permute-start.10) | collective-permute-done | bytes 16416 | tf_op jit(solution)/shard_map/ppermute | solution.py:357
  41.8 2.7 %first_moments.1 = (f32[392,128]{1,0:T(8,128)S(1)}, f32[392,128]{1,0:T(8,128)S(1)}, f32[392,128]{1,0:T(8,128)S(1)}, f32[392,128]{1,0:T(8,128)S(1)}, bf16[512,2048]{1,0:T(8,128)(2,1)S(1)}) custom-call(f32[192,2048]{1,0:T(8,128)S(1)} %get-tuple-element.39.early_ref, f32[64,2048]{1,0:T(8,128)S(1)} %get-tuple-element.44.late_ref, ...), custom_call_target="tpu_custom_call" | custom-call | flops 10000000000 | bytes 100000000 | tf_op jit(solution)/shard_map/first_moments/pallas_call | solution.py:254
  44.5 1.2 %collective-permute-start.12 = (f32[392,128]{1,0:T(8,128)S(1)}, f32[392,128]{1,0:T(8,128)S(1)}, u32[]{:S(2)}, u32[]{:S(2)}) collective-permute-start(f32[392,128]{1,0:T(8,128)S(1)} %get-tuple-element.47), channel_id=1, source_target_pairs={{0,8},{4,12},{8,0},{12,4},{16,24},{20,28},{24,16},{28,20},{1,9},{5... | collective-permute-start | bytes 602120 | tf_op jit(solution)/shard_map/ppermute | solution.py:357
  45.7 2.6 %second_moments.1 = (f32[384,128]{1,0:T(8,128)S(1)}, f32[384,128]{1,0:T(8,128)S(1)}, f32[384,128]{1,0:T(8,128)S(1)}, f32[384,128]{1,0:T(8,128)S(1)}) custom-call(bf16[512,2048]{1,0:T(8,128)(2,1)S(1)} %get-tuple-element.53.resp_ref, bf16[2048,768]{1,0:T(8,128)(2,1)S(1)} %get-tuple-element.37.refs_3_.refs_1_.high_ref, ...), custom_call_target="tpu_custom_call" | custom-call | flops 10000000000 | bytes 100000000 | tf_op jit(solution)/shard_map/second_moments/pallas_call | solution.py:269
  48.3 1.9 %collective-permute-done.12 = f32[392,128]{1,0:T(8,128)S(1)} collective-permute-done((f32[392,128]{1,0:T(8,128)S(1)}, f32[392,128]{1,0:T(8,128)S(1)}, u32[]{:S(2)}, u32[]{:S(2)}) %collective-permute-start.12) | collective-permute-done | bytes 200736 | tf_op jit(solution)/shard_map/ppermute | solution.py:357
  50.3 1.2 %collective-permute-start.14 = (f32[384,128]{1,0:T(8,128)S(1)}, f32[384,128]{1,0:T(8,128)S(1)}, u32[]{:S(2)}, u32[]{:S(2)}) collective-permute-start(f32[384,128]{1,0:T(8,128)S(1)} %get-tuple-element.57), channel_id=1, source_target_pairs={{0,8},{4,12},{8,0},{12,4},{16,24},{20,28},{24,16},{28,20},{1,9},{5... | collective-permute-start | bytes 589832 | tf_op jit(solution)/shard_map/ppermute | solution.py:357
  52.7 1.8 %collective-permute-start.13 = (f32[392,128]{1,0:T(8,128)S(1)}, f32[392,128]{1,0:T(8,128)S(1)}, u32[]{:S(2)}, u32[]{:S(2)}) collective-permute-start(f32[392,128]{1,0:T(8,128)S(1)} %add.17), channel_id=1, source_target_pairs={{0,16},{4,20},{8,24},{12,28},{16,0},{20,4},{24,8},{28,12},{1,17},{... | collective-permute-start | bytes 602120 | tf_op jit(solution)/shard_map/ppermute | solution.py:357
  54.5 6.9 %collective-permute-done.14 = f32[384,128]{1,0:T(8,128)S(1)} collective-permute-done((f32[384,128]{1,0:T(8,128)S(1)}, f32[384,128]{1,0:T(8,128)S(1)}, u32[]{:S(2)}, u32[]{:S(2)}) %collective-permute-start.14) | collective-permute-done | bytes 196640 | tf_op jit(solution)/shard_map/ppermute | solution.py:357
  61.6 3.0 %collective-permute-start.15 = (f32[384,128]{1,0:T(8,128)S(1)}, f32[384,128]{1,0:T(8,128)S(1)}, u32[]{:S(2)}, u32[]{:S(2)}) collective-permute-start(f32[384,128]{1,0:T(8,128)S(1)} %add.19), channel_id=1, source_target_pairs={{0,16},{4,20},{8,24},{12,28},{16,0},{20,4},{24,8},{28,12},{1,17},{... | collective-permute-start | bytes 589832 | tf_op jit(solution)/shard_map/ppermute | solution.py:357
  64.6 1.4 %collective-permute-done.13 = f32[392,128]{1,0:T(8,128)S(1)} collective-permute-done((f32[392,128]{1,0:T(8,128)S(1)}, f32[392,128]{1,0:T(8,128)S(1)}, u32[]{:S(2)}, u32[]{:S(2)}) %collective-permute-start.13) | collective-permute-done | bytes 200736 | tf_op jit(solution)/shard_map/ppermute | solution.py:357
  66.0 2.7 %collective-permute-done.15 = f32[384,128]{1,0:T(8,128)S(1)} collective-permute-done((f32[384,128]{1,0:T(8,128)S(1)}, f32[384,128]{1,0:T(8,128)S(1)}, u32[]{:S(2)}, u32[]{:S(2)}) %collective-permute-start.15) | collective-permute-done | bytes 196640 | tf_op jit(solution)/shard_map/ppermute | solution.py:357
  68.8 3.9 %collective-permute-done.17.near_second_ref = f32[384,128]{1,0:T(8,128)S(1)} collective-permute-done((f32[384,128]{1,0:T(8,128)S(1)}, f32[384,128]{1,0:T(8,128)S(1)}, u32[]{:S(2)}, u32[]{:S(2)}) %collective-permute-start.17) | collective-permute-done | bytes 196640 | tf_op jit(solution)/shard_map/ppermute | solution.py:357
  (38 shorter events, 12.2 us)
Async XLA Ops:
  0.6 7.7 %collective-permute-start.2 = (f32[1024,768]{1,0:T(8,128)}, f32[1024,768]{1,0:T(8,128)S(1)}, u32[]{:S(2)}, u32[]{:S(2)}) collective-permute-start(f32[1024,768]{1,0:T(8,128)} %own_ref.1), channel_id=1, source_target_pairs={{0,4},{4,0},{8,12},{12,8},{16,20},{20,16},{24,28},{28,24},{1,5},{5... | collective-permute-start | bytes 9437192 | tf_op jit(solution)/shard_map/ppermute | solution.py:357
  1.1 13.9 %collective-permute-start.4 = (f32[64,768]{1,0:T(8,128)}, f32[64,768]{1,0:T(8,128)S(1)}, u32[]{:S(2)}, u32[]{:S(2)}) collective-permute-start(f32[64,768]{1,0:T(8,128)} %variances_hbm.3), channel_id=1, source_target_pairs={{0,16},{4,20},{8,24},{12,28},{16,0},{20,4},{24,8},{28,12},{1,17},{... | collective-permute-start | bytes 589832 | tf_op jit(solution)/shard_map/ppermute | solution.py:357
  4.8 12.2 %collective-permute-start.3 = (f32[64,768]{1,0:T(8,128)}, f32[64,768]{1,0:T(8,128)S(1)}, u32[]{:S(2)}, u32[]{:S(2)}) collective-permute-start(f32[64,768]{1,0:T(8,128)} %variances_hbm.3), channel_id=1, source_target_pairs={{0,8},{4,12},{8,0},{12,4},{16,24},{20,28},{24,16},{28,20},{1,9},{5... | collective-permute-start | bytes 589832 | tf_op jit(solution)/shard_map/ppermute | solution.py:357
  6.4 2.1 %copy-start = (f32[1024,768]{1,0:T(8,128)S(1)}, f32[1024,768]{1,0:T(8,128)}, u32[]{:S(2)}) copy-start(f32[1024,768]{1,0:T(8,128)} %own_ref.1) | copy-start | bytes 9437188
  7.7 9.2 %copy-start.1 = (f32[64,768]{1,0:T(8,128)S(1)}, f32[64,768]{1,0:T(8,128)}, u32[]{:S(2)}) copy-start(f32[64,768]{1,0:T(8,128)} %variances_hbm.3) | copy-start | bytes 589828
  7.8 15.7 %collective-permute-start.1 = (f32[392,128]{1,0:T(8,128)S(1)}, f32[392,128]{1,0:T(8,128)S(1)}, u32[]{:S(2)}, u32[]{:S(2)}) collective-permute-start(f32[392,128]{1,0:T(8,128)S(1)} %coefficients.1.refs_0_), channel_id=1, source_target_pairs={{0,16},{4,20},{8,24},{12,28},{16,0},{20,4},{24,8},{28,12},{1,17},{... | collective-permute-start | bytes 602120 | tf_op jit(solution)/shard_map/ppermute | solution.py:357
  8.2 16.2 %collective-permute-start = (f32[392,128]{1,0:T(8,128)S(1)}, f32[392,128]{1,0:T(8,128)S(1)}, u32[]{:S(2)}, u32[]{:S(2)}) collective-permute-start(f32[392,128]{1,0:T(8,128)S(1)} %coefficients.1.refs_0_), channel_id=1, source_target_pairs={{0,8},{4,12},{8,0},{12,4},{16,24},{20,28},{24,16},{28,20},{1,9},{5... | collective-permute-start | bytes 602120 | tf_op jit(solution)/shard_map/ppermute | solution.py:357
  15.1 13.5 %collective-permute-start.7 = (f32[64,768]{1,0:T(8,128)S(1)}, f32[64,768]{1,0:T(8,128)S(1)}, u32[]{:S(2)}, u32[]{:S(2)}) collective-permute-start(f32[64,768]{1,0:T(8,128)S(1)} %collective-permute-done.4.refs_2_), channel_id=1, source_target_pairs={{0,8},{4,12},{8,0},{12,4},{16,24},{20,28},{24,16},{28,20},{1,9},{5... | collective-permute-start | bytes 589832 | tf_op jit(solution)/shard_map/ppermute | solution.py:357
  23.5 7.9 %collective-permute-start.6 = (f32[256,128]{1,0:T(8,128)S(1)}, f32[256,128]{1,0:T(8,128)S(1)}, u32[]{:S(2)}, u32[]{:S(2)}) collective-permute-start(f32[256,128]{1,0:T(8,128)S(1)} %slice.27), channel_id=1, source_target_pairs={{0,8},{4,12},{8,0},{12,4},{16,24},{20,28},{24,16},{28,20},{1,9},{5... | collective-permute-start | bytes 393224 | tf_op jit(solution)/shard_map/ppermute | solution.py:357
  26.9 5.9 %collective-permute-start.5 = (f32[136,128]{1,0:T(8,128)S(1)}, f32[136,128]{1,0:T(8,128)S(1)}, u32[]{:S(2)}, u32[]{:S(2)}) collective-permute-start(f32[136,128]{1,0:T(8,128)S(1)} %slice.26), channel_id=1, source_target_pairs={{0,8},{4,12},{8,0},{12,4},{16,24},{20,28},{24,16},{28,20},{1,9},{5... | collective-permute-start | bytes 208904 | tf_op jit(solution)/shard_map/ppermute | solution.py:357
  33.6 1.2 %collective-permute-start.8 = (f32[2,2,1024]{2,1,0:T(2,128)S(1)}, f32[2,2,1024]{2,1,0:T(2,128)S(1)}, u32[]{:S(2)}, u32[]{:S(2)}) collective-permute-start(f32[2,2,1024]{2,1,0:T(2,128)S(1)} %get-tuple-element.45), channel_id=1, source_target_pairs={{0,4},{4,0},{8,12},{12,8},{16,20},{20,16},{24,28},{28,24},{1,5},{5... | collective-permute-start | bytes 49160 | tf_op jit(solution)/shard_map/ppermute | solution.py:357
  35.0 4.7 %collective-permute-start.11 = (f32[2,2,1024]{2,1,0:T(2,128)S(1)}, f32[2,2,1024]{2,1,0:T(2,128)S(1)}, u32[]{:S(2)}, u32[]{:S(2)}) collective-permute-start(f32[2,2,1024]{2,1,0:T(2,128)S(1)} %pad_maximum_fusion.refs_0_), channel_id=1, source_target_pairs={{0,3},{1,2},{2,1},{3,0},{4,7},{5,6},{6,5},{7,4},{8,11},{9,10},{10,... | collective-permute-start | bytes 49160 | tf_op jit(solution)/shard_map/ppermute | solution.py:357
  37.6 3.7 %collective-permute-start.10 = (f32[2,2,1024]{2,1,0:T(2,128)S(1)}, f32[2,2,1024]{2,1,0:T(2,128)S(1)}, u32[]{:S(2)}, u32[]{:S(2)}) collective-permute-start(f32[2,2,1024]{2,1,0:T(2,128)S(1)} %pad_maximum_fusion.refs_0_), channel_id=1, source_target_pairs={{0,2},{1,3},{2,0},{3,1},{4,6},{5,7},{6,4},{7,5},{8,10},{9,11},{10,... | collective-permute-start | bytes 49160 | tf_op jit(solution)/shard_map/ppermute | solution.py:357
  38.1 3.7 %collective-permute-start.9 = (f32[2,2,1024]{2,1,0:T(2,128)S(1)}, f32[2,2,1024]{2,1,0:T(2,128)S(1)}, u32[]{:S(2)}, u32[]{:S(2)}) collective-permute-start(f32[2,2,1024]{2,1,0:T(2,128)S(1)} %pad_maximum_fusion.refs_0_), channel_id=1, source_target_pairs={{0,1},{1,0},{2,3},{3,2},{4,5},{5,4},{6,7},{7,6},{8,9},{9,8},{10,11... | collective-permute-start | bytes 49160 | tf_op jit(solution)/shard_map/ppermute | solution.py:357
  44.5 5.8 %collective-permute-start.12 = (f32[392,128]{1,0:T(8,128)S(1)}, f32[392,128]{1,0:T(8,128)S(1)}, u32[]{:S(2)}, u32[]{:S(2)}) collective-permute-start(f32[392,128]{1,0:T(8,128)S(1)} %get-tuple-element.47), channel_id=1, source_target_pairs={{0,8},{4,12},{8,0},{12,4},{16,24},{20,28},{24,16},{28,20},{1,9},{5... | collective-permute-start | bytes 602120 | tf_op jit(solution)/shard_map/ppermute | solution.py:357
  50.3 22.4 %copy-start.2 = (f32[64]{0:T(128)S(1)}, f32[64]{0:T(128)}, u32[]{:S(2)}) copy-start(f32[64]{0:T(128)} %param.7) | copy-start | bytes 772
  50.3 11.2 %collective-permute-start.14 = (f32[384,128]{1,0:T(8,128)S(1)}, f32[384,128]{1,0:T(8,128)S(1)}, u32[]{:S(2)}, u32[]{:S(2)}) collective-permute-start(f32[384,128]{1,0:T(8,128)S(1)} %get-tuple-element.57), channel_id=1, source_target_pairs={{0,8},{4,12},{8,0},{12,4},{16,24},{20,28},{24,16},{28,20},{1,9},{5... | collective-permute-start | bytes 589832 | tf_op jit(solution)/shard_map/ppermute | solution.py:357
  52.7 13.3 %collective-permute-start.13 = (f32[392,128]{1,0:T(8,128)S(1)}, f32[392,128]{1,0:T(8,128)S(1)}, u32[]{:S(2)}, u32[]{:S(2)}) collective-permute-start(f32[392,128]{1,0:T(8,128)S(1)} %add.17), channel_id=1, source_target_pairs={{0,16},{4,20},{8,24},{12,28},{16,0},{20,4},{24,8},{28,12},{1,17},{... | collective-permute-start | bytes 602120 | tf_op jit(solution)/shard_map/ppermute | solution.py:357
  61.5 11.2 %collective-permute-start.16 = (f32[392,128]{1,0:T(8,128)S(1)}, f32[392,128]{1,0:T(8,128)S(1)}, u32[]{:S(2)}, u32[]{:S(2)}) collective-permute-start(f32[392,128]{1,0:T(8,128)S(1)} %get-tuple-element.61), channel_id=1, source_target_pairs={{0,8},{4,12},{8,0},{12,4},{16,24},{20,28},{24,16},{28,20},{1,9},{5... | collective-permute-start | bytes 602120 | tf_op jit(solution)/shard_map/ppermute | solution.py:357
  61.6 7.2 %collective-permute-start.15 = (f32[384,128]{1,0:T(8,128)S(1)}, f32[384,128]{1,0:T(8,128)S(1)}, u32[]{:S(2)}, u32[]{:S(2)}) collective-permute-start(f32[384,128]{1,0:T(8,128)S(1)} %add.19), channel_id=1, source_target_pairs={{0,16},{4,20},{8,24},{12,28},{16,0},{20,4},{24,8},{28,12},{1,17},{... | collective-permute-start | bytes 589832 | tf_op jit(solution)/shard_map/ppermute | solution.py:357
  64.6 8.1 %collective-permute-start.17 = (f32[384,128]{1,0:T(8,128)S(1)}, f32[384,128]{1,0:T(8,128)S(1)}, u32[]{:S(2)}, u32[]{:S(2)}) collective-permute-start(f32[384,128]{1,0:T(8,128)S(1)} %get-tuple-element.63), channel_id=1, source_target_pairs={{0,8},{4,12},{8,0},{12,4},{16,24},{20,28},{24,16},{28,20},{1,9},{5... | collective-permute-start | bytes 589832 | tf_op jit(solution)/shard_map/ppermute | solution.py:357

commit v12 on v10

--- a/solution.py
+++ b/solution.py
@@ -275,10 +275,28 @@
     )(resp, high, low)
 
 
+def kept_kernel(means_ref, variances_ref, mass_ref, first_ref, second_ref):
+    means = means_ref[...]
+    kept = 0.4 * to_column(mass_ref[...], means.shape[0])
+    first_ref[...] = kept * means
+    second_ref[...] = kept * (variances_ref[...] + means * means)
+
+
+def kept_moments(means, variances, mass, ready):
+    block = jax.ShapeDtypeStruct(means.shape, F32)
+    return pl.pallas_call(
+        kept_kernel,
+        out_shape=(block, block),
+        cost_estimate=HEAVY,
+        compiler_params=params(16),
+        name="kept_moments",
+    )(means, variances, after(mass.reshape(1, -1), ready))
+
+
 def update_kernel(
     scale,
-    means_ref,
-    variances_ref,
+    kept_first_ref,
+    kept_second_ref,
     mass_ref,
     first_ref,
     second_ref,
@@ -288,34 +306,32 @@
     new_variances_ref,
     new_mass_ref,
 ):
-    n, width = means_ref.shape
+    n, width = kept_first_ref.shape
     tiles = width // LANES * n
     row = first_ref[tiles : tiles + 1, :n] + near_first_ref[tiles : tiles + 1, :n]
     new_row = 0.4 * mass_ref[...] + scale * row
     new_mass_ref[...] = new_row
     inverse = 1.0 / to_column(new_row, n)
-    kept = 0.4 * to_column(mass_ref[...], n)
     for c in range(width // LANES):
         lanes, tile = slice(c * LANES, (c + 1) * LANES), slice(c * n, (c + 1) * n)
-        means, variances = means_ref[:, lanes], variances_ref[:, lanes]
         first = first_ref[tile, :] + near_first_ref[tile, :]
         second = second_ref[tile, :] + near_second_ref[tile, :]
-        new_means = (kept * means + scale * first) * inverse
+        new_means = (kept_first_ref[:, lanes] + scale * first) * inverse
         new_means_ref[:, lanes] = new_means
-        second_moment = kept * (variances + means * means) + scale * second
+        second_moment = kept_second_ref[:, lanes] + scale * second
         new_variances_ref[:, lanes] = second_moment * inverse - new_means * new_means
 
 
-def update(scale, means, variances, mass, *sums):
+def update(scale, kept, mass, *sums):
     n = mass.shape[0]
-    block = jax.ShapeDtypeStruct(means.shape, F32)
+    block = jax.ShapeDtypeStruct(kept[0].shape, F32)
     new_means, new_variances, new_mass = pl.pallas_call(
         functools.partial(update_kernel, scale),
         out_shape=(block, block, jax.ShapeDtypeStruct((1, n), F32)),
         cost_estimate=HEAVY,
         compiler_params=params(16),
         name="update",
-    )(means, variances, mass.reshape(1, n), *sums)
+    )(*kept, mass.reshape(1, n), *sums)
     return new_means, new_variances, new_mass.reshape(n)
 
 
@@ -433,12 +449,13 @@
     second = second_moments(resp, s_high, s_low, n)
     place = {q: i for i, q in enumerate(order + late)}
     first, second = ([parts[place[q]] for q in range(planes)] for parts in (first, second))
+    kept = kept_moments(comp_means, comp_variances, comp_mass, resp)
     sums = scatter_planes(first, second)
 
     total_comps = n * lax.axis_size("dp") * lax.axis_size("comp")
     total_rows = embeddings.shape[0] * lax.axis_size("dp")
     scale = 0.6 * (total_comps / total_rows)
-    return update(scale, comp_means, comp_variances, comp_mass, *sums)
+    return update(scale, kept, comp_mass, *sums)
 
 
 def solution(mesh):

time: 72.6 us -> 72.5 us (level)
  transfers between devices with their start and end apart: 18 -> 18, of which waited for: 14 -> 15; matrix products, arithmetic and copies ran while one was open for 0% -> 0% of each run, Pallas kernels for 20% -> 20%
where the time goes in v12:
time: 72.5 us; the launch traced here: 72.4 us
  waiting for transfers between devices  30.5 us (42%)
  starting transfers between devices  21.7 us (30%)
  Pallas kernels  19.1 us (26%)
  between operations  0.76 us (1%)
    ppermute x18, waiting for transfers between devices, swap(): return lax.ppermute(value, axis, [(i, i ^ bit) for i in range(size)])  30.5 us
    ppermute x18, starting transfers between devices, swap(): return lax.ppermute(value, axis, [(i, i ^ bit) for i in range(size)])  21.7 us
    pallas_call x5, Pallas kernels, score_call(): pl.pallas_call(body, out_shape=[jax.ShapeDtypeStruct(shape, F32) for shap...  9.25 us
    pallas_call x1, Pallas kernels, first_moments(): pl.pallas_call(functools.partial(first_kernel, n, len(stats)), out_shape=...  2.66 us
    pallas_call x1, Pallas kernels, second_moments(): pl.pallas_call(functools.partial(second_kernel, n), out_shape=[pack] * (r...  2.58 us
    pallas_call x1, Pallas kernels, halves(): pl.pallas_call(halves_kernel, grid=(2 * steps,), in_specs=[pl.BlockSpec((...  2.25 us
  transfers between devices with their start and end apart: 18, of which 15 were waited for; matrix products, arithmetic and copies ran while one was open for 0% of the time, Pallas kernels for 20%

profile of v12, /device:TPU:0, one launch (start us, length us, event | category | flops | bytes accessed | tf_op | source)
XLA Modules:
  0.0 72.4 jit_solution(10316699363963355463)
XLA Ops:
  1.1 3.7 %collective-permute-start.4 = (f32[64,768]{1,0:T(8,128)}, f32[64,768]{1,0:T(8,128)S(1)}, u32[]{:S(2)}, u32[]{:S(2)}) collective-permute-start(f32[64,768]{1,0:T(8,128)} %variances_ref.1), channel_id=1, source_target_pairs={{0,16},{4,20},{8,24},{12,28},{16,0},{20,4},{24,8},{28,12},{1,17},{... | collective-permute-start | bytes 589832 | tf_op jit(solution)/shard_map/ppermute | solution.py:340
  4.8 1.6 %collective-permute-start.3 = (f32[64,768]{1,0:T(8,128)}, f32[64,768]{1,0:T(8,128)S(1)}, u32[]{:S(2)}, u32[]{:S(2)}) collective-permute-start(f32[64,768]{1,0:T(8,128)} %variances_ref.1), channel_id=1, source_target_pairs={{0,8},{4,12},{8,0},{12,4},{16,24},{20,28},{24,16},{28,20},{1,9},{5... | collective-permute-start | bytes 589832 | tf_op jit(solution)/shard_map/ppermute | solution.py:340
  6.4 1.3 %coefficients.1.refs_0_ = f32[392,128]{1,0:T(8,128)S(1)} custom-call(f32[64,768]{1,0:T(8,128)} %means_ref.1, f32[64,768]{1,0:T(8,128)} %variances_ref.1, f32[1,64]{1,0:T(1,128)} %bitcast.2), custom_call_target="tpu_custom_call" | custom-call | flops 10000000000 | bytes 100000000 | tf_op jit(solution)/shard_map/coefficients/pallas_call | solution.py:64
  8.5 2.2 %halves.1 = (bf16[2048,768]{1,0:T(8,128)(2,1)S(1)}, bf16[2048,768]{1,0:T(8,128)(2,1)S(1)}, bf16[2048,768]{1,0:T(8,128)(2,1)S(1)}, bf16[2048,768]{1,0:T(8,128)(2,1)S(1)}) custom-call(f32[1024,768]{1,0:T(8,128)S(1)} %copy-done, f32[1024,768]{1,0:T(8,128)S(1)} %collective-permute-done.2.other_ref), custom_call_target="tpu_custom_call" | custom-call | flops 10000000000 | bytes 100000000 | tf_op jit(solution)/shard_map/halves/pallas_call | solution.py:101
  10.7 4.4 %collective-permute-done.4.refs_2_ = f32[64,768]{1,0:T(8,128)S(1)} collective-permute-done((f32[64,768]{1,0:T(8,128)}, f32[64,768]{1,0:T(8,128)S(1)}, u32[]{:S(2)}, u32[]{:S(2)}) %collective-permute-start.4) | collective-permute-done | bytes 196640 | tf_op jit(solution)/shard_map/ppermute | solution.py:340
  17.0 2.4 %early_quad.1.refs_5_ = f32[192,2048]{1,0:T(8,128)S(1)} custom-call(f32[64,768]{1,0:T(8,128)S(1)} %copy-done.2, f32[64,768]{1,0:T(8,128)S(1)} %collective-permute-done.3.refs_1_, f32[64,768]{1,0:T(8,128)S(1)} %collective-permute-done.4.refs_2_, bf16[2048,768]{1,0:T(8,128)(2,1)S(1)} %get-tuple-element.36.refs_3_.refs_1_.high_ref, ...), custom_call_target="tpu_custom_call" | custom-call | flops 10000000000 | bytes 100000000 | tf_op jit(solution)/shard_map/early_quad/pallas_call | solution.py:206
  19.4 4.1 %collective-permute-done.1.refs_2_ = f32[392,128]{1,0:T(8,128)S(1)} collective-permute-done((f32[392,128]{1,0:T(8,128)S(1)}, f32[392,128]{1,0:T(8,128)S(1)}, u32[]{:S(2)}, u32[]{:S(2)}) %collective-permute-start.1) | collective-permute-done | bytes 200736 | tf_op jit(solution)/shard_map/ppermute | solution.py:340
  24.4 2.5 %early_scores.1 = (f32[192,2048]{1,0:T(8,128)S(1)}, f32[2,2048]{1,0:T(2,128)S(1)}) custom-call(f32[392,128]{1,0:T(8,128)S(1)} %coefficients.1.refs_0_, f32[392,128]{1,0:T(8,128)S(1)} %collective-permute-done.refs_1_, f32[392,128]{1,0:T(8,128)S(1)} %collective-permute-done.1.refs_2_, bf16[2048,768]{1,0:T(8,128)(2,1)S(1)} %get-tuple-element.34.refs_3_.refs_1_.refs_4_, ...), custom_call_target="tpu_custom_call" | custom-call | flops 100000000 | bytes 1000000 | tf_op jit(solution)/shard_map/early_scores/pallas_call | solution.py:206
  26.9 1.3 %collective-permute-start.5 = (f32[136,128]{1,0:T(8,128)S(1)}, f32[136,128]{1,0:T(8,128)S(1)}, u32[]{:S(2)}, u32[]{:S(2)}) collective-permute-start(f32[136,128]{1,0:T(8,128)S(1)} %slice.26), channel_id=1, source_target_pairs={{0,8},{4,12},{8,0},{12,4},{16,24},{20,28},{24,16},{28,20},{1,9},{5... | collective-permute-start | bytes 208904 | tf_op jit(solution)/shard_map/ppermute | solution.py:340
  28.6 2.1 %late_quad.1.refs_3_ = f32[64,2048]{1,0:T(8,128)S(1)} custom-call(f32[64,768]{1,0:T(8,128)S(1)} %collective-permute-done.7.refs_0_, bf16[2048,768]{1,0:T(8,128)(2,1)S(1)} %get-tuple-element.36.refs_3_.refs_1_.high_ref, bf16[2048,768]{1,0:T(8,128)(2,1)S(1)} %get-tuple-element.37.refs_4_.refs_2_.low_ref), custom_call_target="tpu_custom_call" | custom-call | flops 100000000 | bytes 1000000 | tf_op jit(solution)/shard_map/late_quad/pallas_call | solution.py:206
  31.4 1.4 %late_head.1.refs_3_ = f32[64,2048]{1,0:T(8,128)S(1)} custom-call(f32[256,128]{1,0:T(8,128)S(1)} %collective-permute-done.6.refs_0_, bf16[2048,768]{1,0:T(8,128)(2,1)S(1)} %get-tuple-element.34.refs_3_.refs_1_.refs_4_, bf16[2048,768]{1,0:T(8,128)(2,1)S(1)} %get-tuple-element.35.refs_4_.refs_2_.refs_5_, f32[64,2048]{1,0:T(8,128)S(1)} %late_quad.1.refs_3_), custom_call_target="tpu_custom_call" | custom-call | flops 100000000 | bytes 1000000 | tf_op jit(solution)/shard_map/late_head/pallas_call | solution.py:206
  35.0 2.6 %collective-permute-start.11 = (f32[2,2,1024]{2,1,0:T(2,128)S(1)}, f32[2,2,1024]{2,1,0:T(2,128)S(1)}, u32[]{:S(2)}, u32[]{:S(2)}) collective-permute-start(f32[2,2,1024]{2,1,0:T(2,128)S(1)} %pad_maximum_fusion.refs_0_), channel_id=1, source_target_pairs={{0,3},{1,2},{2,1},{3,0},{4,7},{5,6},{6,5},{7,4},{8,11},{9,10},{10,... | collective-permute-start | bytes 49160 | tf_op jit(solution)/shard_map/ppermute | solution.py:340
  39.7 1.6 %collective-permute-done.10.refs_2_ = f32[2,2,1024]{2,1,0:T(2,128)S(1)} collective-permute-done((f32[2,2,1024]{2,1,0:T(2,128)S(1)}, f32[2,2,1024]{2,1,0:T(2,128)S(1)}, u32[]{:S(2)}, u32[]{:S(2)}) %collective-permute-start.10) | collective-permute-done | bytes 16416 | tf_op jit(solution)/shard_map/ppermute | solution.py:340
  41.8 2.7 %first_moments.1 = (f32[392,128]{1,0:T(8,128)S(1)}, f32[392,128]{1,0:T(8,128)S(1)}, f32[392,128]{1,0:T(8,128)S(1)}, f32[392,128]{1,0:T(8,128)S(1)}, bf16[512,2048]{1,0:T(8,128)(2,1)S(1)}) custom-call(f32[192,2048]{1,0:T(8,128)S(1)} %get-tuple-element.38.early_ref, f32[64,2048]{1,0:T(8,128)S(1)} %get-tuple-element.43.late_ref, ...), custom_call_target="tpu_custom_call" | custom-call | flops 10000000000 | bytes 100000000 | tf_op jit(solution)/shard_map/first_moments/pallas_call | solution.py:254
  44.5 1.2 %collective-permute-start.12 = (f32[392,128]{1,0:T(8,128)S(1)}, f32[392,128]{1,0:T(8,128)S(1)}, u32[]{:S(2)}, u32[]{:S(2)}) collective-permute-start(f32[392,128]{1,0:T(8,128)S(1)} %get-tuple-element.51), channel_id=1, source_target_pairs={{0,8},{4,12},{8,0},{12,4},{16,24},{20,28},{24,16},{28,20},{1,9},{5... | collective-permute-start | bytes 602120 | tf_op jit(solution)/shard_map/ppermute | solution.py:340
  45.7 2.6 %second_moments.1 = (f32[384,128]{1,0:T(8,128)S(1)}, f32[384,128]{1,0:T(8,128)S(1)}, f32[384,128]{1,0:T(8,128)S(1)}, f32[384,128]{1,0:T(8,128)S(1)}) custom-call(bf16[512,2048]{1,0:T(8,128)(2,1)S(1)} %get-tuple-element.45.resp_ref, bf16[2048,768]{1,0:T(8,128)(2,1)S(1)} %get-tuple-element.36.refs_3_.refs_1_.high_ref, ...), custom_call_target="tpu_custom_call" | custom-call | flops 10000000000 | bytes 100000000 | tf_op jit(solution)/shard_map/second_moments/pallas_call | solution.py:269
  48.3 1.9 %collective-permute-done.12 = f32[392,128]{1,0:T(8,128)S(1)} collective-permute-done((f32[392,128]{1,0:T(8,128)S(1)}, f32[392,128]{1,0:T(8,128)S(1)}, u32[]{:S(2)}, u32[]{:S(2)}) %collective-permute-start.12) | collective-permute-done | bytes 200736 | tf_op jit(solution)/shard_map/ppermute | solution.py:340
  50.3 1.2 %collective-permute-start.14 = (f32[384,128]{1,0:T(8,128)S(1)}, f32[384,128]{1,0:T(8,128)S(1)}, u32[]{:S(2)}, u32[]{:S(2)}) collective-permute-start(f32[384,128]{1,0:T(8,128)S(1)} %get-tuple-element.55), channel_id=1, source_target_pairs={{0,8},{4,12},{8,0},{12,4},{16,24},{20,28},{24,16},{28,20},{1,9},{5... | collective-permute-start | bytes 589832 | tf_op jit(solution)/shard_map/ppermute | solution.py:340
  51.5 1.7 %collective-permute-start.13 = (f32[392,128]{1,0:T(8,128)S(1)}, f32[392,128]{1,0:T(8,128)S(1)}, u32[]{:S(2)}, u32[]{:S(2)}) collective-permute-start(f32[392,128]{1,0:T(8,128)S(1)} %add.17), channel_id=1, source_target_pairs={{0,16},{4,20},{8,24},{12,28},{16,0},{20,4},{24,8},{28,12},{1,17},{... | collective-permute-start | bytes 602120 | tf_op jit(solution)/shard_map/ppermute | solution.py:340
  53.3 6.0 %collective-permute-done.14 = f32[384,128]{1,0:T(8,128)S(1)} collective-permute-done((f32[384,128]{1,0:T(8,128)S(1)}, f32[384,128]{1,0:T(8,128)S(1)}, u32[]{:S(2)}, u32[]{:S(2)}) %collective-permute-start.14) | collective-permute-done | bytes 196640 | tf_op jit(solution)/shard_map/ppermute | solution.py:340
  59.4 4.5 %collective-permute-start.15 = (f32[384,128]{1,0:T(8,128)S(1)}, f32[384,128]{1,0:T(8,128)S(1)}, u32[]{:S(2)}, u32[]{:S(2)}) collective-permute-start(f32[384,128]{1,0:T(8,128)S(1)} %add.19), channel_id=1, source_target_pairs={{0,16},{4,20},{8,24},{12,28},{16,0},{20,4},{24,8},{28,12},{1,17},{... | collective-permute-start | bytes 589832 | tf_op jit(solution)/shard_map/ppermute | solution.py:340
  64.1 4.0 %collective-permute-done.15 = f32[384,128]{1,0:T(8,128)S(1)} collective-permute-done((f32[384,128]{1,0:T(8,128)S(1)}, f32[384,128]{1,0:T(8,128)S(1)}, u32[]{:S(2)}, u32[]{:S(2)}) %collective-permute-start.15) | collective-permute-done | bytes 196640 | tf_op jit(solution)/shard_map/ppermute | solution.py:340
  68.2 1.2 %collective-permute-done.17.near_second_ref = f32[384,128]{1,0:T(8,128)S(1)} collective-permute-done((f32[384,128]{1,0:T(8,128)S(1)}, f32[384,128]{1,0:T(8,128)S(1)}, u32[]{:S(2)}, u32[]{:S(2)}) %collective-permute-start.17) | collective-permute-done | bytes 196640 | tf_op jit(solution)/shard_map/ppermute | solution.py:340
  69.4 2.1 %collective-permute-done.16.near_first_ref = f32[392,128]{1,0:T(8,128)S(1)} collective-permute-done((f32[392,128]{1,0:T(8,128)S(1)}, f32[392,128]{1,0:T(8,128)S(1)}, u32[]{:S(2)}, u32[]{:S(2)}) %collective-permute-start.16) | collective-permute-done | bytes 200736 | tf_op jit(solution)/shard_map/ppermute | solution.py:340
  (40 shorter events, 11.2 us)
Async XLA Ops:
  0.6 7.7 %collective-permute-start.2 = (f32[1024,768]{1,0:T(8,128)}, f32[1024,768]{1,0:T(8,128)S(1)}, u32[]{:S(2)}, u32[]{:S(2)}) collective-permute-start(f32[1024,768]{1,0:T(8,128)} %own_ref.1), channel_id=1, source_target_pairs={{0,4},{4,0},{8,12},{12,8},{16,20},{20,16},{24,28},{28,24},{1,5},{5... | collective-permute-start | bytes 9437192 | tf_op jit(solution)/shard_map/ppermute | solution.py:340
  1.1 13.9 %collective-permute-start.4 = (f32[64,768]{1,0:T(8,128)}, f32[64,768]{1,0:T(8,128)S(1)}, u32[]{:S(2)}, u32[]{:S(2)}) collective-permute-start(f32[64,768]{1,0:T(8,128)} %variances_ref.1), channel_id=1, source_target_pairs={{0,16},{4,20},{8,24},{12,28},{16,0},{20,4},{24,8},{28,12},{1,17},{... | collective-permute-start | bytes 589832 | tf_op jit(solution)/shard_map/ppermute | solution.py:340
  4.8 12.2 %collective-permute-start.3 = (f32[64,768]{1,0:T(8,128)}, f32[64,768]{1,0:T(8,128)S(1)}, u32[]{:S(2)}, u32[]{:S(2)}) collective-permute-start(f32[64,768]{1,0:T(8,128)} %variances_ref.1), channel_id=1, source_target_pairs={{0,8},{4,12},{8,0},{12,4},{16,24},{20,28},{24,16},{28,20},{1,9},{5... | collective-permute-start | bytes 589832 | tf_op jit(solution)/shard_map/ppermute | solution.py:340
  6.4 2.1 %copy-start = (f32[1024,768]{1,0:T(8,128)S(1)}, f32[1024,768]{1,0:T(8,128)}, u32[]{:S(2)}) copy-start(f32[1024,768]{1,0:T(8,128)} %own_ref.1) | copy-start | bytes 9437188
  7.7 9.2 %copy-start.2 = (f32[64,768]{1,0:T(8,128)S(1)}, f32[64,768]{1,0:T(8,128)}, u32[]{:S(2)}) copy-start(f32[64,768]{1,0:T(8,128)} %variances_ref.1) | copy-start | bytes 589828
  7.8 15.7 %collective-permute-start.1 = (f32[392,128]{1,0:T(8,128)S(1)}, f32[392,128]{1,0:T(8,128)S(1)}, u32[]{:S(2)}, u32[]{:S(2)}) collective-permute-start(f32[392,128]{1,0:T(8,128)S(1)} %coefficients.1.refs_0_), channel_id=1, source_target_pairs={{0,16},{4,20},{8,24},{12,28},{16,0},{20,4},{24,8},{28,12},{1,17},{... | collective-permute-start | bytes 602120 | tf_op jit(solution)/shard_map/ppermute | solution.py:340
  8.2 16.2 %collective-permute-start = (f32[392,128]{1,0:T(8,128)S(1)}, f32[392,128]{1,0:T(8,128)S(1)}, u32[]{:S(2)}, u32[]{:S(2)}) collective-permute-start(f32[392,128]{1,0:T(8,128)S(1)} %coefficients.1.refs_0_), channel_id=1, source_target_pairs={{0,8},{4,12},{8,0},{12,4},{16,24},{20,28},{24,16},{28,20},{1,9},{5... | collective-permute-start | bytes 602120 | tf_op jit(solution)/shard_map/ppermute | solution.py:340
  15.1 13.5 %collective-permute-start.7 = (f32[64,768]{1,0:T(8,128)S(1)}, f32[64,768]{1,0:T(8,128)S(1)}, u32[]{:S(2)}, u32[]{:S(2)}) collective-permute-start(f32[64,768]{1,0:T(8,128)S(1)} %collective-permute-done.4.refs_2_), channel_id=1, source_target_pairs={{0,8},{4,12},{8,0},{12,4},{16,24},{20,28},{24,16},{28,20},{1,9},{5... | collective-permute-start | bytes 589832 | tf_op jit(solution)/shard_map/ppermute | solution.py:340
  23.5 7.9 %collective-permute-start.6 = (f32[256,128]{1,0:T(8,128)S(1)}, f32[256,128]{1,0:T(8,128)S(1)}, u32[]{:S(2)}, u32[]{:S(2)}) collective-permute-start(f32[256,128]{1,0:T(8,128)S(1)} %slice.27), channel_id=1, source_target_pairs={{0,8},{4,12},{8,0},{12,4},{16,24},{20,28},{24,16},{28,20},{1,9},{5... | collective-permute-start | bytes 393224 | tf_op jit(solution)/shard_map/ppermute | solution.py:340
  26.9 5.9 %collective-permute-start.5 = (f32[136,128]{1,0:T(8,128)S(1)}, f32[136,128]{1,0:T(8,128)S(1)}, u32[]{:S(2)}, u32[]{:S(2)}) collective-permute-start(f32[136,128]{1,0:T(8,128)S(1)} %slice.26), channel_id=1, source_target_pairs={{0,8},{4,12},{8,0},{12,4},{16,24},{20,28},{24,16},{28,20},{1,9},{5... | collective-permute-start | bytes 208904 | tf_op jit(solution)/shard_map/ppermute | solution.py:340
  33.6 1.2 %collective-permute-start.8 = (f32[2,2,1024]{2,1,0:T(2,128)S(1)}, f32[2,2,1024]{2,1,0:T(2,128)S(1)}, u32[]{:S(2)}, u32[]{:S(2)}) collective-permute-start(f32[2,2,1024]{2,1,0:T(2,128)S(1)} %get-tuple-element.44), channel_id=1, source_target_pairs={{0,4},{4,0},{8,12},{12,8},{16,20},{20,16},{24,28},{28,24},{1,5},{5... | collective-permute-start | bytes 49160 | tf_op jit(solution)/shard_map/ppermute | solution.py:340
  35.0 4.7 %collective-permute-start.11 = (f32[2,2,1024]{2,1,0:T(2,128)S(1)}, f32[2,2,1024]{2,1,0:T(2,128)S(1)}, u32[]{:S(2)}, u32[]{:S(2)}) collective-permute-start(f32[2,2,1024]{2,1,0:T(2,128)S(1)} %pad_maximum_fusion.refs_0_), channel_id=1, source_target_pairs={{0,3},{1,2},{2,1},{3,0},{4,7},{5,6},{6,5},{7,4},{8,11},{9,10},{10,... | collective-permute-start | bytes 49160 | tf_op jit(solution)/shard_map/ppermute | solution.py:340
  37.6 3.7 %collective-permute-start.10 = (f32[2,2,1024]{2,1,0:T(2,128)S(1)}, f32[2,2,1024]{2,1,0:T(2,128)S(1)}, u32[]{:S(2)}, u32[]{:S(2)}) collective-permute-start(f32[2,2,1024]{2,1,0:T(2,128)S(1)} %pad_maximum_fusion.refs_0_), channel_id=1, source_target_pairs={{0,2},{1,3},{2,0},{3,1},{4,6},{5,7},{6,4},{7,5},{8,10},{9,11},{10,... | collective-permute-start | bytes 49160 | tf_op jit(solution)/shard_map/ppermute | solution.py:340
  38.1 3.7 %collective-permute-start.9 = (f32[2,2,1024]{2,1,0:T(2,128)S(1)}, f32[2,2,1024]{2,1,0:T(2,128)S(1)}, u32[]{:S(2)}, u32[]{:S(2)}) collective-permute-start(f32[2,2,1024]{2,1,0:T(2,128)S(1)} %pad_maximum_fusion.refs_0_), channel_id=1, source_target_pairs={{0,1},{1,0},{2,3},{3,2},{4,5},{5,4},{6,7},{7,6},{8,9},{9,8},{10,11... | collective-permute-start | bytes 49160 | tf_op jit(solution)/shard_map/ppermute | solution.py:340
  44.5 5.8 %collective-permute-start.12 = (f32[392,128]{1,0:T(8,128)S(1)}, f32[392,128]{1,0:T(8,128)S(1)}, u32[]{:S(2)}, u32[]{:S(2)}) collective-permute-start(f32[392,128]{1,0:T(8,128)S(1)} %get-tuple-element.51), channel_id=1, source_target_pairs={{0,8},{4,12},{8,0},{12,4},{16,24},{20,28},{24,16},{28,20},{1,9},{5... | collective-permute-start | bytes 602120 | tf_op jit(solution)/shard_map/ppermute | solution.py:340
  45.7 18.2 %copy-start.1 = (f32[64,768]{1,0:T(8,128)S(1)}, f32[64,768]{1,0:T(8,128)}, u32[]{:S(2)}) copy-start(f32[64,768]{1,0:T(8,128)} %means_ref.1) | copy-start | bytes 589828
  45.7 18.2 %copy-start.3 = (f32[64]{0:T(128)S(1)}, f32[64]{0:T(128)}, u32[]{:S(2)}) copy-start(f32[64]{0:T(128)} %param.7) | copy-start | bytes 772
  50.3 9.0 %collective-permute-start.14 = (f32[384,128]{1,0:T(8,128)S(1)}, f32[384,128]{1,0:T(8,128)S(1)}, u32[]{:S(2)}, u32[]{:S(2)}) collective-permute-start(f32[384,128]{1,0:T(8,128)S(1)} %get-tuple-element.55), channel_id=1, source_target_pairs={{0,8},{4,12},{8,0},{12,4},{16,24},{20,28},{24,16},{28,20},{1,9},{5... | collective-permute-start | bytes 589832 | tf_op jit(solution)/shard_map/ppermute | solution.py:340
  51.5 12.6 %collective-permute-start.13 = (f32[392,128]{1,0:T(8,128)S(1)}, f32[392,128]{1,0:T(8,128)S(1)}, u32[]{:S(2)}, u32[]{:S(2)}) collective-permute-start(f32[392,128]{1,0:T(8,128)S(1)} %add.17), channel_id=1, source_target_pairs={{0,16},{4,20},{8,24},{12,28},{16,0},{20,4},{24,8},{28,12},{1,17},{... | collective-permute-start | bytes 602120 | tf_op jit(solution)/shard_map/ppermute | solution.py:340
  59.3 10.0 %collective-permute-start.17 = (f32[384,128]{1,0:T(8,128)S(1)}, f32[384,128]{1,0:T(8,128)S(1)}, u32[]{:S(2)}, u32[]{:S(2)}) collective-permute-start(f32[384,128]{1,0:T(8,128)S(1)} %get-tuple-element.61), channel_id=1, source_target_pairs={{0,8},{4,12},{8,0},{12,4},{16,24},{20,28},{24,16},{28,20},{1,9},{5... | collective-permute-start | bytes 589832 | tf_op jit(solution)/shard_map/ppermute | solution.py:340
  59.4 8.7 %collective-permute-start.15 = (f32[384,128]{1,0:T(8,128)S(1)}, f32[384,128]{1,0:T(8,128)S(1)}, u32[]{:S(2)}, u32[]{:S(2)}) collective-permute-start(f32[384,128]{1,0:T(8,128)S(1)} %add.19), channel_id=1, source_target_pairs={{0,16},{4,20},{8,24},{12,28},{16,0},{20,4},{24,8},{28,12},{1,17},{... | collective-permute-start | bytes 589832 | tf_op jit(solution)/shard_map/ppermute | solution.py:340
  63.9 7.6 %collective-permute-start.16 = (f32[392,128]{1,0:T(8,128)S(1)}, f32[392,128]{1,0:T(8,128)S(1)}, u32[]{:S(2)}, u32[]{:S(2)}) collective-permute-start(f32[392,128]{1,0:T(8,128)S(1)} %get-tuple-element.59), channel_id=1, source_target_pairs={{0,8},{4,12},{8,0},{12,4},{16,24},{20,28},{24,16},{28,20},{1,9},{5... | collective-permute-start | bytes 602120 | tf_op jit(solution)/shard_map/ppermute | solution.py:340

commit v13 on v10

--- a/solution.py
+++ b/solution.py
@@ -386,7 +386,7 @@
         return score_call(body, [(comps, 2 * rows)], [(2 * comps, width)], name, *operands, cost=cost)[0]
 
     quad = quad_scores(order, "early_quad")
-    head = width // LANES * 2 // 3
+    head = width // LANES // 2
     heads, tails = [], []
     for q in late:
         source = after(linear[q ^ 1], quad)

time: 72.6 us -> 73.4 us (1.011)
  waiting for transfers between devices: 30.6 us -> 33 us
  starting transfers between devices: 21.8 us -> 20.1 us
    ppermute x18, waiting for transfers between devices: 30.6 us -> 33 us  [swap(): return lax.ppermute(value, axis, [(i, i ^ bit) for i in range(size)])]
    ppermute x18, starting transfers between devices: 21.8 us -> 20.1 us  [swap(): return lax.ppermute(value, axis, [(i, i ^ bit) for i in range(size)])]
where the time goes in v13:
time: 73.4 us; the launch traced here: 73.2 us
  waiting for transfers between devices  33 us (45%)
  starting transfers between devices  20.1 us (27%)
  Pallas kernels  19 us (26%)
  between operations  0.76 us (1%)
    ppermute x18, waiting for transfers between devices, swap(): return lax.ppermute(value, axis, [(i, i ^ bit) for i in range(size)])  33 us
    ppermute x18, starting transfers between devices, swap(): return lax.ppermute(value, axis, [(i, i ^ bit) for i in range(size)])  20.1 us
    pallas_call x5, Pallas kernels, score_call(): pl.pallas_call(body, out_shape=[jax.ShapeDtypeStruct(shape, F32) for shap...  9.25 us
    pallas_call x1, Pallas kernels, first_moments(): pl.pallas_call(functools.partial(first_kernel, n, len(stats)), out_shape=...  2.66 us
    pallas_call x1, Pallas kernels, second_moments(): pl.pallas_call(functools.partial(second_kernel, n), out_shape=[pack] * (r...  2.58 us
    pallas_call x1, Pallas kernels, halves(): pl.pallas_call(halves_kernel, grid=(2 * steps,), in_specs=[pl.BlockSpec((...  2.25 us
  transfers between devices with their start and end apart: 18, of which 14 were waited for; matrix products, arithmetic and copies ran while one was open for 0% of the time, Pallas kernels for 20%

profile of v13, /device:TPU:0, one launch (start us, length us, event | category | flops | bytes accessed | tf_op | source)
XLA Modules:
  0.0 73.2 jit_solution(13811247351831342035)
XLA Ops:
  1.1 3.7 %collective-permute-start.4 = (f32[64,768]{1,0:T(8,128)}, f32[64,768]{1,0:T(8,128)S(1)}, u32[]{:S(2)}, u32[]{:S(2)}) collective-permute-start(f32[64,768]{1,0:T(8,128)} %variances_ref.1), channel_id=1, source_target_pairs={{0,16},{4,20},{8,24},{12,28},{16,0},{20,4},{24,8},{28,12},{1,17},{... | collective-permute-start | bytes 589832 | tf_op jit(solution)/shard_map/ppermute | solution.py:324
  4.8 1.6 %collective-permute-start.3 = (f32[64,768]{1,0:T(8,128)}, f32[64,768]{1,0:T(8,128)S(1)}, u32[]{:S(2)}, u32[]{:S(2)}) collective-permute-start(f32[64,768]{1,0:T(8,128)} %variances_ref.1), channel_id=1, source_target_pairs={{0,8},{4,12},{8,0},{12,4},{16,24},{20,28},{24,16},{28,20},{1,9},{5... | collective-permute-start | bytes 589832 | tf_op jit(solution)/shard_map/ppermute | solution.py:324
  6.4 1.3 %coefficients.1.refs_0_ = f32[392,128]{1,0:T(8,128)S(1)} custom-call(f32[64,768]{1,0:T(8,128)} %means_ref.1, f32[64,768]{1,0:T(8,128)} %variances_ref.1, f32[1,64]{1,0:T(1,128)} %bitcast.2), custom_call_target="tpu_custom_call" | custom-call | flops 10000000000 | bytes 100000000 | tf_op jit(solution)/shard_map/coefficients/pallas_call | solution.py:64
  8.5 2.2 %halves.1 = (bf16[2048,768]{1,0:T(8,128)(2,1)S(1)}, bf16[2048,768]{1,0:T(8,128)(2,1)S(1)}, bf16[2048,768]{1,0:T(8,128)(2,1)S(1)}, bf16[2048,768]{1,0:T(8,128)(2,1)S(1)}) custom-call(f32[1024,768]{1,0:T(8,128)S(1)} %copy-done, f32[1024,768]{1,0:T(8,128)S(1)} %collective-permute-done.2.other_ref), custom_call_target="tpu_custom_call" | custom-call | flops 10000000000 | bytes 100000000 | tf_op jit(solution)/shard_map/halves/pallas_call | solution.py:101
  10.7 4.4 %collective-permute-done.4.refs_2_ = f32[64,768]{1,0:T(8,128)S(1)} collective-permute-done((f32[64,768]{1,0:T(8,128)}, f32[64,768]{1,0:T(8,128)S(1)}, u32[]{:S(2)}, u32[]{:S(2)}) %collective-permute-start.4) | collective-permute-done | bytes 196640 | tf_op jit(solution)/shard_map/ppermute | solution.py:324
  17.0 2.4 %early_quad.1.refs_5_ = f32[192,2048]{1,0:T(8,128)S(1)} custom-call(f32[64,768]{1,0:T(8,128)S(1)} %copy-done.2, f32[64,768]{1,0:T(8,128)S(1)} %collective-permute-done.3.refs_1_, f32[64,768]{1,0:T(8,128)S(1)} %collective-permute-done.4.refs_2_, bf16[2048,768]{1,0:T(8,128)(2,1)S(1)} %get-tuple-element.33.refs_3_.refs_1_.high_ref, ...), custom_call_target="tpu_custom_call" | custom-call | flops 10000000000 | bytes 100000000 | tf_op jit(solution)/shard_map/early_quad/pallas_call | solution.py:206
  19.4 4.1 %collective-permute-done.1.refs_2_ = f32[392,128]{1,0:T(8,128)S(1)} collective-permute-done((f32[392,128]{1,0:T(8,128)S(1)}, f32[392,128]{1,0:T(8,128)S(1)}, u32[]{:S(2)}, u32[]{:S(2)}) %collective-permute-start.1) | collective-permute-done | bytes 200736 | tf_op jit(solution)/shard_map/ppermute | solution.py:324
  24.4 2.5 %early_scores.1 = (f32[192,2048]{1,0:T(8,128)S(1)}, f32[2,2048]{1,0:T(2,128)S(1)}) custom-call(f32[392,128]{1,0:T(8,128)S(1)} %coefficients.1.refs_0_, f32[392,128]{1,0:T(8,128)S(1)} %collective-permute-done.refs_1_, f32[392,128]{1,0:T(8,128)S(1)} %collective-permute-done.1.refs_2_, bf16[2048,768]{1,0:T(8,128)(2,1)S(1)} %get-tuple-element.31.refs_3_.refs_1_.refs_4_, ...), custom_call_target="tpu_custom_call" | custom-call | flops 100000000 | bytes 1000000 | tf_op jit(solution)/shard_map/early_scores/pallas_call | solution.py:206
  26.9 1.3 %collective-permute-start.5 = (f32[200,128]{1,0:T(8,128)S(1)}, f32[200,128]{1,0:T(8,128)S(1)}, u32[]{:S(2)}, u32[]{:S(2)}) collective-permute-start(f32[200,128]{1,0:T(8,128)S(1)} %slice.26), channel_id=1, source_target_pairs={{0,8},{4,12},{8,0},{12,4},{16,24},{20,28},{24,16},{28,20},{1,9},{5... | collective-permute-start | bytes 307208 | tf_op jit(solution)/shard_map/ppermute | solution.py:324
  28.6 2.1 %late_quad.1.refs_3_ = f32[64,2048]{1,0:T(8,128)S(1)} custom-call(f32[64,768]{1,0:T(8,128)S(1)} %collective-permute-done.7.refs_0_, bf16[2048,768]{1,0:T(8,128)(2,1)S(1)} %get-tuple-element.33.refs_3_.refs_1_.high_ref, bf16[2048,768]{1,0:T(8,128)(2,1)S(1)} %get-tuple-element.34.refs_4_.refs_2_.low_ref), custom_call_target="tpu_custom_call" | custom-call | flops 100000000 | bytes 1000000 | tf_op jit(solution)/shard_map/late_quad/pallas_call | solution.py:206
  33.4 1.2 %collective-permute-done.8 = f32[2,2,1024]{2,1,0:T(2,128)S(1)} collective-permute-done((f32[2,2,1024]{2,1,0:T(2,128)S(1)}, f32[2,2,1024]{2,1,0:T(2,128)S(1)}, u32[]{:S(2)}, u32[]{:S(2)}) %collective-permute-start.8) | collective-permute-done | bytes 16416 | tf_op jit(solution)/shard_map/ppermute | solution.py:324
  34.6 2.6 %collective-permute-start.11 = (f32[2,2,1024]{2,1,0:T(2,128)S(1)}, f32[2,2,1024]{2,1,0:T(2,128)S(1)}, u32[]{:S(2)}, u32[]{:S(2)}) collective-permute-start(f32[2,2,1024]{2,1,0:T(2,128)S(1)} %pad_maximum_fusion.refs_0_), channel_id=1, source_target_pairs={{0,3},{1,2},{2,1},{3,0},{4,7},{5,6},{6,5},{7,4},{8,11},{9,10},{10,... | collective-permute-start | bytes 49160 | tf_op jit(solution)/shard_map/ppermute | solution.py:324
  38.2 1.1 %collective-permute-done.11.refs_3_ = f32[2,2,1024]{2,1,0:T(2,128)S(1)} collective-permute-done((f32[2,2,1024]{2,1,0:T(2,128)S(1)}, f32[2,2,1024]{2,1,0:T(2,128)S(1)}, u32[]{:S(2)}, u32[]{:S(2)}) %collective-permute-start.11) | collective-permute-done | bytes 16416 | tf_op jit(solution)/shard_map/ppermute | solution.py:324
  39.3 1.6 %collective-permute-done.10.refs_2_ = f32[2,2,1024]{2,1,0:T(2,128)S(1)} collective-permute-done((f32[2,2,1024]{2,1,0:T(2,128)S(1)}, f32[2,2,1024]{2,1,0:T(2,128)S(1)}, u32[]{:S(2)}, u32[]{:S(2)}) %collective-permute-start.10) | collective-permute-done | bytes 16416 | tf_op jit(solution)/shard_map/ppermute | solution.py:324
  41.4 2.7 %first_moments.1 = (f32[392,128]{1,0:T(8,128)S(1)}, f32[392,128]{1,0:T(8,128)S(1)}, f32[392,128]{1,0:T(8,128)S(1)}, f32[392,128]{1,0:T(8,128)S(1)}, bf16[512,2048]{1,0:T(8,128)(2,1)S(1)}) custom-call(f32[192,2048]{1,0:T(8,128)S(1)} %get-tuple-element.35.early_ref, f32[64,2048]{1,0:T(8,128)S(1)} %get-tuple-element.40.late_ref, ...), custom_call_target="tpu_custom_call" | custom-call | flops 10000000000 | bytes 100000000 | tf_op jit(solution)/shard_map/first_moments/pallas_call | solution.py:254
  44.1 1.5 %collective-permute-start.12 = (f32[392,128]{1,0:T(8,128)S(1)}, f32[392,128]{1,0:T(8,128)S(1)}, u32[]{:S(2)}, u32[]{:S(2)}) collective-permute-start(f32[392,128]{1,0:T(8,128)S(1)} %get-tuple-element.44), channel_id=1, source_target_pairs={{0,8},{4,12},{8,0},{12,4},{16,24},{20,28},{24,16},{28,20},{1,9},{5... | collective-permute-start | bytes 602120 | tf_op jit(solution)/shard_map/ppermute | solution.py:324
  45.7 2.6 %second_moments.1 = (f32[384,128]{1,0:T(8,128)S(1)}, f32[384,128]{1,0:T(8,128)S(1)}, f32[384,128]{1,0:T(8,128)S(1)}, f32[384,128]{1,0:T(8,128)S(1)}) custom-call(bf16[512,2048]{1,0:T(8,128)(2,1)S(1)} %get-tuple-element.45.resp_ref, bf16[2048,768]{1,0:T(8,128)(2,1)S(1)} %get-tuple-element.33.refs_3_.refs_1_.high_ref, ...), custom_call_target="tpu_custom_call" | custom-call | flops 10000000000 | bytes 100000000 | tf_op jit(solution)/shard_map/second_moments/pallas_call | solution.py:269
  48.3 1.6 %collective-permute-done.12 = f32[392,128]{1,0:T(8,128)S(1)} collective-permute-done((f32[392,128]{1,0:T(8,128)S(1)}, f32[392,128]{1,0:T(8,128)S(1)}, u32[]{:S(2)}, u32[]{:S(2)}) %collective-permute-start.12) | collective-permute-done | bytes 200736 | tf_op jit(solution)/shard_map/ppermute | solution.py:324
  49.9 1.5 %collective-permute-start.14 = (f32[384,128]{1,0:T(8,128)S(1)}, f32[384,128]{1,0:T(8,128)S(1)}, u32[]{:S(2)}, u32[]{:S(2)}) collective-permute-start(f32[384,128]{1,0:T(8,128)S(1)} %get-tuple-element.49), channel_id=1, source_target_pairs={{0,8},{4,12},{8,0},{12,4},{16,24},{20,28},{24,16},{28,20},{1,9},{5... | collective-permute-start | bytes 589832 | tf_op jit(solution)/shard_map/ppermute | solution.py:324
  51.5 1.8 %collective-permute-start.13 = (f32[392,128]{1,0:T(8,128)S(1)}, f32[392,128]{1,0:T(8,128)S(1)}, u32[]{:S(2)}, u32[]{:S(2)}) collective-permute-start(f32[392,128]{1,0:T(8,128)S(1)} %add.17), channel_id=1, source_target_pairs={{0,16},{4,20},{8,24},{12,28},{16,0},{20,4},{24,8},{28,12},{1,17},{... | collective-permute-start | bytes 602120 | tf_op jit(solution)/shard_map/ppermute | solution.py:324
  53.3 9.0 %collective-permute-done.14 = f32[384,128]{1,0:T(8,128)S(1)} collective-permute-done((f32[384,128]{1,0:T(8,128)S(1)}, f32[384,128]{1,0:T(8,128)S(1)}, u32[]{:S(2)}, u32[]{:S(2)}) %collective-permute-start.14) | collective-permute-done | bytes 196640 | tf_op jit(solution)/shard_map/ppermute | solution.py:324
  62.4 2.2 %collective-permute-start.15 = (f32[384,128]{1,0:T(8,128)S(1)}, f32[384,128]{1,0:T(8,128)S(1)}, u32[]{:S(2)}, u32[]{:S(2)}) collective-permute-start(f32[384,128]{1,0:T(8,128)S(1)} %add.19), channel_id=1, source_target_pairs={{0,16},{4,20},{8,24},{12,28},{16,0},{20,4},{24,8},{28,12},{1,17},{... | collective-permute-start | bytes 589832 | tf_op jit(solution)/shard_map/ppermute | solution.py:324
  64.7 4.4 %collective-permute-done.15 = f32[384,128]{1,0:T(8,128)S(1)} collective-permute-done((f32[384,128]{1,0:T(8,128)S(1)}, f32[384,128]{1,0:T(8,128)S(1)}, u32[]{:S(2)}, u32[]{:S(2)}) %collective-permute-start.15) | collective-permute-done | bytes 196640 | tf_op jit(solution)/shard_map/ppermute | solution.py:324
  69.1 3.1 %collective-permute-done.17.near_second_ref = f32[384,128]{1,0:T(8,128)S(1)} collective-permute-done((f32[384,128]{1,0:T(8,128)S(1)}, f32[384,128]{1,0:T(8,128)S(1)}, u32[]{:S(2)}, u32[]{:S(2)}) %collective-permute-start.17) | collective-permute-done | bytes 196640 | tf_op jit(solution)/shard_map/ppermute | solution.py:324
  (39 shorter events, 9.9 us)
Async XLA Ops:
  0.6 7.7 %collective-permute-start.2 = (f32[1024,768]{1,0:T(8,128)}, f32[1024,768]{1,0:T(8,128)S(1)}, u32[]{:S(2)}, u32[]{:S(2)}) collective-permute-start(f32[1024,768]{1,0:T(8,128)} %own_ref.1), channel_id=1, source_target_pairs={{0,4},{4,0},{8,12},{12,8},{16,20},{20,16},{24,28},{28,24},{1,5},{5... | collective-permute-start | bytes 9437192 | tf_op jit(solution)/shard_map/ppermute | solution.py:324
  1.1 13.9 %collective-permute-start.4 = (f32[64,768]{1,0:T(8,128)}, f32[64,768]{1,0:T(8,128)S(1)}, u32[]{:S(2)}, u32[]{:S(2)}) collective-permute-start(f32[64,768]{1,0:T(8,128)} %variances_ref.1), channel_id=1, source_target_pairs={{0,16},{4,20},{8,24},{12,28},{16,0},{20,4},{24,8},{28,12},{1,17},{... | collective-permute-start | bytes 589832 | tf_op jit(solution)/shard_map/ppermute | solution.py:324
  4.8 12.2 %collective-permute-start.3 = (f32[64,768]{1,0:T(8,128)}, f32[64,768]{1,0:T(8,128)S(1)}, u32[]{:S(2)}, u32[]{:S(2)}) collective-permute-start(f32[64,768]{1,0:T(8,128)} %variances_ref.1), channel_id=1, source_target_pairs={{0,8},{4,12},{8,0},{12,4},{16,24},{20,28},{24,16},{28,20},{1,9},{5... | collective-permute-start | bytes 589832 | tf_op jit(solution)/shard_map/ppermute | solution.py:324
  6.4 2.1 %copy-start = (f32[1024,768]{1,0:T(8,128)S(1)}, f32[1024,768]{1,0:T(8,128)}, u32[]{:S(2)}) copy-start(f32[1024,768]{1,0:T(8,128)} %own_ref.1) | copy-start | bytes 9437188
  7.7 9.2 %copy-start.2 = (f32[64,768]{1,0:T(8,128)S(1)}, f32[64,768]{1,0:T(8,128)}, u32[]{:S(2)}) copy-start(f32[64,768]{1,0:T(8,128)} %variances_ref.1) | copy-start | bytes 589828
  7.8 15.7 %collective-permute-start.1 = (f32[392,128]{1,0:T(8,128)S(1)}, f32[392,128]{1,0:T(8,128)S(1)}, u32[]{:S(2)}, u32[]{:S(2)}) collective-permute-start(f32[392,128]{1,0:T(8,128)S(1)} %coefficients.1.refs_0_), channel_id=1, source_target_pairs={{0,16},{4,20},{8,24},{12,28},{16,0},{20,4},{24,8},{28,12},{1,17},{... | collective-permute-start | bytes 602120 | tf_op jit(solution)/shard_map/ppermute | solution.py:324
  8.2 16.2 %collective-permute-start = (f32[392,128]{1,0:T(8,128)S(1)}, f32[392,128]{1,0:T(8,128)S(1)}, u32[]{:S(2)}, u32[]{:S(2)}) collective-permute-start(f32[392,128]{1,0:T(8,128)S(1)} %coefficients.1.refs_0_), channel_id=1, source_target_pairs={{0,8},{4,12},{8,0},{12,4},{16,24},{20,28},{24,16},{28,20},{1,9},{5... | collective-permute-start | bytes 602120 | tf_op jit(solution)/shard_map/ppermute | solution.py:324
  15.1 13.5 %collective-permute-start.7 = (f32[64,768]{1,0:T(8,128)S(1)}, f32[64,768]{1,0:T(8,128)S(1)}, u32[]{:S(2)}, u32[]{:S(2)}) collective-permute-start(f32[64,768]{1,0:T(8,128)S(1)} %collective-permute-done.4.refs_2_), channel_id=1, source_target_pairs={{0,8},{4,12},{8,0},{12,4},{16,24},{20,28},{24,16},{28,20},{1,9},{5... | collective-permute-start | bytes 589832 | tf_op jit(solution)/shard_map/ppermute | solution.py:324
  23.5 7.2 %collective-permute-start.6 = (f32[192,128]{1,0:T(8,128)S(1)}, f32[192,128]{1,0:T(8,128)S(1)}, u32[]{:S(2)}, u32[]{:S(2)}) collective-permute-start(f32[192,128]{1,0:T(8,128)S(1)} %slice.27), channel_id=1, source_target_pairs={{0,8},{4,12},{8,0},{12,4},{16,24},{20,28},{24,16},{28,20},{1,9},{5... | collective-permute-start | bytes 294920 | tf_op jit(solution)/shard_map/ppermute | solution.py:324
  26.9 5.2 %collective-permute-start.5 = (f32[200,128]{1,0:T(8,128)S(1)}, f32[200,128]{1,0:T(8,128)S(1)}, u32[]{:S(2)}, u32[]{:S(2)}) collective-permute-start(f32[200,128]{1,0:T(8,128)S(1)} %slice.26), channel_id=1, source_target_pairs={{0,8},{4,12},{8,0},{12,4},{16,24},{20,28},{24,16},{28,20},{1,9},{5... | collective-permute-start | bytes 307208 | tf_op jit(solution)/shard_map/ppermute | solution.py:324
  33.3 1.2 %collective-permute-start.8 = (f32[2,2,1024]{2,1,0:T(2,128)S(1)}, f32[2,2,1024]{2,1,0:T(2,128)S(1)}, u32[]{:S(2)}, u32[]{:S(2)}) collective-permute-start(f32[2,2,1024]{2,1,0:T(2,128)S(1)} %get-tuple-element.41), channel_id=1, source_target_pairs={{0,4},{4,0},{8,12},{12,8},{16,20},{20,16},{24,28},{28,24},{1,5},{5... | collective-permute-start | bytes 49160 | tf_op jit(solution)/shard_map/ppermute | solution.py:324
  34.6 4.7 %collective-permute-start.11 = (f32[2,2,1024]{2,1,0:T(2,128)S(1)}, f32[2,2,1024]{2,1,0:T(2,128)S(1)}, u32[]{:S(2)}, u32[]{:S(2)}) collective-permute-start(f32[2,2,1024]{2,1,0:T(2,128)S(1)} %pad_maximum_fusion.refs_0_), channel_id=1, source_target_pairs={{0,3},{1,2},{2,1},{3,0},{4,7},{5,6},{6,5},{7,4},{8,11},{9,10},{10,... | collective-permute-start | bytes 49160 | tf_op jit(solution)/shard_map/ppermute | solution.py:324
  37.2 3.7 %collective-permute-start.10 = (f32[2,2,1024]{2,1,0:T(2,128)S(1)}, f32[2,2,1024]{2,1,0:T(2,128)S(1)}, u32[]{:S(2)}, u32[]{:S(2)}) collective-permute-start(f32[2,2,1024]{2,1,0:T(2,128)S(1)} %pad_maximum_fusion.refs_0_), channel_id=1, source_target_pairs={{0,2},{1,3},{2,0},{3,1},{4,6},{5,7},{6,4},{7,5},{8,10},{9,11},{10,... | collective-permute-start | bytes 49160 | tf_op jit(solution)/shard_map/ppermute | solution.py:324
  37.7 3.7 %collective-permute-start.9 = (f32[2,2,1024]{2,1,0:T(2,128)S(1)}, f32[2,2,1024]{2,1,0:T(2,128)S(1)}, u32[]{:S(2)}, u32[]{:S(2)}) collective-permute-start(f32[2,2,1024]{2,1,0:T(2,128)S(1)} %pad_maximum_fusion.refs_0_), channel_id=1, source_target_pairs={{0,1},{1,0},{2,3},{3,2},{4,5},{5,4},{6,7},{7,6},{8,9},{9,8},{10,11... | collective-permute-start | bytes 49160 | tf_op jit(solution)/shard_map/ppermute | solution.py:324
  44.1 5.8 %collective-permute-start.12 = (f32[392,128]{1,0:T(8,128)S(1)}, f32[392,128]{1,0:T(8,128)S(1)}, u32[]{:S(2)}, u32[]{:S(2)}) collective-permute-start(f32[392,128]{1,0:T(8,128)S(1)} %get-tuple-element.44), channel_id=1, source_target_pairs={{0,8},{4,12},{8,0},{12,4},{16,24},{20,28},{24,16},{28,20},{1,9},{5... | collective-permute-start | bytes 602120 | tf_op jit(solution)/shard_map/ppermute | solution.py:324
  45.7 26.6 %copy-start.1 = (f32[64,768]{1,0:T(8,128)S(1)}, f32[64,768]{1,0:T(8,128)}, u32[]{:S(2)}) copy-start(f32[64,768]{1,0:T(8,128)} %means_ref.1) | copy-start | bytes 589828
  45.7 26.6 %copy-start.3 = (f32[64]{0:T(128)S(1)}, f32[64]{0:T(128)}, u32[]{:S(2)}) copy-start(f32[64]{0:T(128)} %param.7) | copy-start | bytes 772
  49.9 12.3 %collective-permute-start.14 = (f32[384,128]{1,0:T(8,128)S(1)}, f32[384,128]{1,0:T(8,128)S(1)}, u32[]{:S(2)}, u32[]{:S(2)}) collective-permute-start(f32[384,128]{1,0:T(8,128)S(1)} %get-tuple-element.49), channel_id=1, source_target_pairs={{0,8},{4,12},{8,0},{12,4},{16,24},{20,28},{24,16},{28,20},{1,9},{5... | collective-permute-start | bytes 589832 | tf_op jit(solution)/shard_map/ppermute | solution.py:324
  51.5 13.2 %collective-permute-start.13 = (f32[392,128]{1,0:T(8,128)S(1)}, f32[392,128]{1,0:T(8,128)S(1)}, u32[]{:S(2)}, u32[]{:S(2)}) collective-permute-start(f32[392,128]{1,0:T(8,128)S(1)} %add.17), channel_id=1, source_target_pairs={{0,16},{4,20},{8,24},{12,28},{16,0},{20,4},{24,8},{28,12},{1,17},{... | collective-permute-start | bytes 602120 | tf_op jit(solution)/shard_map/ppermute | solution.py:324
  62.3 10.0 %collective-permute-start.16 = (f32[392,128]{1,0:T(8,128)S(1)}, f32[392,128]{1,0:T(8,128)S(1)}, u32[]{:S(2)}, u32[]{:S(2)}) collective-permute-start(f32[392,128]{1,0:T(8,128)S(1)} %get-tuple-element.53), channel_id=1, source_target_pairs={{0,8},{4,12},{8,0},{12,4},{16,24},{20,28},{24,16},{28,20},{1,9},{5... | collective-permute-start | bytes 602120 | tf_op jit(solution)/shard_map/ppermute | solution.py:324
  62.4 6.7 %collective-permute-start.15 = (f32[384,128]{1,0:T(8,128)S(1)}, f32[384,128]{1,0:T(8,128)S(1)}, u32[]{:S(2)}, u32[]{:S(2)}) collective-permute-start(f32[384,128]{1,0:T(8,128)S(1)} %add.19), channel_id=1, source_target_pairs={{0,16},{4,20},{8,24},{12,28},{16,0},{20,4},{24,8},{28,12},{1,17},{... | collective-permute-start | bytes 589832 | tf_op jit(solution)/shard_map/ppermute | solution.py:324
  64.6 7.7 %collective-permute-start.17 = (f32[384,128]{1,0:T(8,128)S(1)}, f32[384,128]{1,0:T(8,128)S(1)}, u32[]{:S(2)}, u32[]{:S(2)}) collective-permute-start(f32[384,128]{1,0:T(8,128)S(1)} %get-tuple-element.55), channel_id=1, source_target_pairs={{0,8},{4,12},{8,0},{12,4},{16,24},{20,28},{24,16},{28,20},{1,9},{5... | collective-permute-start | bytes 589832 | tf_op jit(solution)/shard_map/ppermute | solution.py:324
